TPU v7x, 32 devices: a whole 2x2x4 slice. The times are simulated.
32 devices in a mesh: expert: 8 (over z, y), dp: 4 (over x, core).
Axes of the slice: x: 2, y: 2, z: 4, core: 2. Of those that a mesh axis runs over, the one named last changes fastest.
Arguments:
- tokens: bfloat16 [32768, 1024], P(('expert', 'dp')), may hold values from -6 to 6
- documents: int32 [32768], P(('expert', 'dp')), may hold values from 0 to 8, as said below
- routes: int32 [32768, 1], P(('expert', 'dp')), may hold values from 0 to 7; in each aligned block of 1024 rows (0 to 1023, 1024 to 2047, ...) at most 192 rows name the same one
- out_grad: bfloat16 [32768, 1024], P(('expert', 'dp')), may hold values from -6 to 6
- norm_params: float32 [4, 1024], P(None, ('expert', 'dp'))
- qkv_weight: float32 [1024, 3072], P(('expert', 'dp')), may hold values from -0.09375 to 0.09375
- proj_weight: float32 [1024, 1024], P(('expert', 'dp')), may hold values from -0.5 to 0.5
- centroids: float32 [8, 1024], P('expert', 'dp'), may hold values from -0.0625 to 0.0625
- expert_in: float32 [8, 1024, 4096], P('expert', 'dp'), may hold values from -0.09375 to 0.09375
- expert_out: float32 [8, 4096, 1024], P('expert', None, 'dp'), may hold values from -0.25 to 0.25
- norm_moment: float32 [4, 1024], P(None, ('expert', 'dp')), may hold values from -0.015625 to 0.015625
- qkv_moment: float32 [1024, 3072], P(('expert', 'dp')), may hold values from -0.0014648438 to 0.0014648438
- proj_moment: float32 [1024, 1024], P(('expert', 'dp')), may hold values from -0.0014648438 to 0.0014648438
- centroid_moment: float32 [8, 1024], P('expert', 'dp'), may hold values from -0.0014648438 to 0.0014648438
- in_moment: float32 [8, 1024, 4096], P('expert', 'dp'), may hold values from -0.0014648438 to 0.0014648438
- out_moment: float32 [8, 4096, 1024], P('expert', None, 'dp'), may hold values from -0.0014648438 to 0.0014648438
- norm_average: float32 [4, 1024], P(None, ('expert', 'dp')), may hold values from 0.5 to 1.5
- qkv_average: float32 [1024, 3072], P(('expert', 'dp')), may hold values from -0.09375 to 0.09375
- proj_average: float32 [1024, 1024], P(('expert', 'dp')), may hold values from -0.5 to 0.5
- centroid_average: float32 [8, 1024], P('expert', 'dp'), may hold values from -0.0625 to 0.0625
- in_average: float32 [8, 1024, 4096], P('expert', 'dp'), may hold values from -0.09375 to 0.09375
- out_average: float32 [8, 4096, 1024], P('expert', None, 'dp'), may hold values from -0.25 to 0.25
Outputs:
- activations: bfloat16 [32768, 1024], P(('expert', 'dp'))
- input_grad: float32 [32768, 1024], P(('expert', 'dp'))
- grad_norm: float32 [], replicated
- new_norm_params: float32 [4, 1024], P(None, ('expert', 'dp'))
- new_qkv_weight: float32 [1024, 3072], P(('expert', 'dp'))
- new_proj_weight: float32 [1024, 1024], P(('expert', 'dp'))
- new_centroids: float32 [8, 1024], P('expert', 'dp')
- new_expert_in: float32 [8, 1024, 4096], P('expert', 'dp')
- new_expert_out: float32 [8, 4096, 1024], P('expert', None, 'dp')
- new_norm_moment: float32 [4, 1024], P(None, ('expert', 'dp'))
- new_qkv_moment: float32 [1024, 3072], P(('expert', 'dp'))
- new_proj_moment: float32 [1024, 1024], P(('expert', 'dp'))
- new_centroid_moment: float32 [8, 1024], P('expert', 'dp')
- new_in_moment: float32 [8, 1024, 4096], P('expert', 'dp')
- new_out_moment: float32 [8, 4096, 1024], P('expert', None, 'dp')
- new_norm_average: float32 [4, 1024], P(None, ('expert', 'dp'))
- new_qkv_average: float32 [1024, 3072], P(('expert', 'dp'))
- new_proj_average: float32 [1024, 1024], P(('expert', 'dp'))
- new_centroid_average: float32 [8, 1024], P('expert', 'dp')
- new_in_average: float32 [8, 1024, 4096], P('expert', 'dp')
- new_out_average: float32 [8, 4096, 1024], P('expert', None, 'dp')
Inputs may be any that keep to these rules, and one draw needn't show every extreme that they name: Each row of 1024 tokens holds 2 to 9 documents numbered 0, 1, ... in order, never falling; some row holds 9 and some row 2. `routes`: of one device's 1024 tokens at most 192 name the same expert; some expert is named by exactly 192 of some device's tokens.
All inputs are finite; a program needn't handle non-finite values.
Results may differ from a plain program's by a relative error of at most 0.014.
The roundings to bfloat16 on the way count: a program that leaves them out, or rounds other values in their place, can miss the bound.
Values may be sent and summed in bfloat16 or wider, within the bound.
No kernel may reach another device: no remote copies, remote signals or barrier semaphores. Data moves between devices by JAX's collectives and lax.ppermute only.
A program may use at most 320 MiB of HBM per device.

v0:
```python
import jax
import jax.numpy as jnp
from jax import lax
from jax.sharding import PartitionSpec as P

HEAD_DIM = 64
SEQ = 1024


eps = 1e-05
scale_qk = 0.125
momentum_rate = 0.9
learn_rate = 100.0
norm_rate = 500.0
average_rate = 0.9
clip_limit = 1.0
group_heads = 4
highest = lax.Precision.HIGHEST


def layer_norm(values, norm_gain, norm_bias):
    centre = values - jnp.mean(values, axis=-1, keepdims=True)
    spread = jnp.mean(centre * centre, axis=-1, keepdims=True)
    return centre * lax.rsqrt(spread + eps) * norm_gain + norm_bias


def exact_gelu(values):
    return jax.nn.gelu(values, approximate=False)


def masks_for(doc_row):
    places = jnp.arange(doc_row.shape[0])
    return (doc_row[:, None] == doc_row[None, :]) & (places[:, None] >= places[None, :])


def to_blocks(flat_cols, rows_here, members):
    groups = flat_cols.shape[1] // (members * group_heads * HEAD_DIM)
    shaped = flat_cols.reshape(rows_here, SEQ, members, groups, group_heads, HEAD_DIM)
    return shaped.transpose(2, 0, 3, 4, 1, 5).reshape(
        members, rows_here * groups, group_heads, SEQ, HEAD_DIM
    )


def from_blocks(blocks, rows_here):
    members = blocks.shape[0]
    groups = blocks.shape[1] // rows_here
    shaped = blocks.reshape(members, rows_here, groups, group_heads, SEQ, HEAD_DIM)
    return shaped.transpose(1, 4, 0, 2, 3, 5).reshape(
        rows_here * SEQ, members * groups * group_heads * HEAD_DIM
    )


def masked_scores(query_blk, key_blk, doc_row):
    scores = (
        jnp.einsum("hqd,hkd->hqk", query_blk, key_blk, preferred_element_type=jnp.float32)
        * scale_qk
    )
    return jnp.where(masks_for(doc_row)[None], scores, -1000000000.0)


def head_forward(block_items):
    query_blk, key_blk, value_blk, doc_row = block_items
    scores = masked_scores(query_blk, key_blk, doc_row)
    top_score = jnp.max(scores, axis=-1, keepdims=True)
    exponent = jnp.exp(scores - top_score)
    totals = jnp.sum(exponent, axis=-1, keepdims=True)
    attn_weights = (exponent / totals).astype(jnp.bfloat16)
    mixed_heads = jnp.einsum(
        "hqk,hkd->hqd", attn_weights, value_blk, preferred_element_type=jnp.float32
    )
    log_total = top_score[..., 0] + jnp.log(totals[..., 0])
    return (mixed_heads.astype(jnp.bfloat16), log_total)


def head_backward(block_items):
    query_blk, key_blk, value_blk, grad_mixed, log_total, doc_row = block_items
    scores = masked_scores(query_blk, key_blk, doc_row)
    attn_weights = jnp.exp(scores - log_total[..., None])
    grad_weights = jnp.einsum(
        "hqd,hkd->hqk", grad_mixed, value_blk, preferred_element_type=jnp.float32
    )
    grad_values = jnp.einsum(
        "hqk,hqd->hkd",
        attn_weights.astype(jnp.bfloat16),
        grad_mixed,
        preferred_element_type=jnp.float32,
    )
    inner_sum = jnp.sum(attn_weights * grad_weights, axis=-1, keepdims=True)
    grad_scores = (attn_weights * (grad_weights - inner_sum)).astype(jnp.bfloat16)
    grad_queries = (
        jnp.einsum("hqk,hkd->hqd", grad_scores, key_blk, preferred_element_type=jnp.float32)
        * scale_qk
    )
    grad_keys = (
        jnp.einsum("hqk,hqd->hkd", grad_scores, query_blk, preferred_element_type=jnp.float32)
        * scale_qk
    )
    return (
        grad_queries.astype(jnp.bfloat16),
        grad_keys.astype(jnp.bfloat16),
        grad_values.astype(jnp.bfloat16),
    )


def update(weight, moment, average, gradient, factor, rate):
    clipped = gradient * factor
    moment_new = momentum_rate * moment + clipped
    weight_new = weight - rate * (clipped + momentum_rate * moment_new)
    average_new = average_rate * average + (1.0 - average_rate) * weight_new
    return (weight_new, moment_new, average_new)


def shards(
    tokens,
    documents,
    routes,
    out_grad,
    norm_params,
    qkv_weight,
    proj_weight,
    centroids,
    expert_in,
    expert_out,
    norm_moment,
    qkv_moment,
    proj_moment,
    centroid_moment,
    in_moment,
    out_moment,
    norm_average,
    qkv_average,
    proj_average,
    centroid_average,
    in_average,
    out_average,
):
    local_tokens = tokens.shape[0]
    model_width = tokens.shape[1]
    rows_here = local_tokens // SEQ
    experts_all = lax.axis_size("expert")
    slot_cap = max(2, 3 * local_tokens // (2 * experts_all))
    slot_count = experts_all * slot_cap
    dense_low = (
        lax.all_gather(qkv_weight.astype(jnp.bfloat16), ("expert", "dp"), axis=0, tiled=True),
        lax.all_gather(proj_weight.astype(jnp.bfloat16), ("expert", "dp"), axis=0, tiled=True),
        lax.all_gather(norm_params.astype(jnp.bfloat16), ("expert", "dp"), axis=1, tiled=True),
        lax.all_gather(
            centroids.reshape(-1).astype(jnp.bfloat16), ("expert", "dp"), axis=0, tiled=True
        ),
    )
    qkv_full = dense_low[0]
    proj_full = dense_low[1]
    norm_values = dense_low[2].astype(jnp.float32)
    centre_table = dense_low[3].reshape(experts_all, model_width)
    expert_low = (
        lax.all_gather(expert_in.astype(jnp.bfloat16), "dp", axis=1, tiled=True),
        lax.all_gather(expert_out.astype(jnp.bfloat16), "dp", axis=2, tiled=True),
    )
    weight_in = expert_low[0][0]
    weight_out = expert_low[1][0]
    x_in = tokens.astype(jnp.float32)
    normed_one, norm_back_one = jax.vjp(layer_norm, x_in, norm_values[0], norm_values[1])
    normed_low = normed_one.astype(jnp.bfloat16)
    packed = jnp.dot(normed_low, qkv_full, preferred_element_type=jnp.float32).astype(jnp.bfloat16)
    split_qkv = to_blocks(packed, rows_here, 3)
    groups = split_qkv.shape[1] // rows_here
    doc_rows = jnp.repeat(documents.reshape(rows_here, SEQ), groups, axis=0)
    mixed_blocks, log_totals = lax.map(
        head_forward, (split_qkv[0], split_qkv[1], split_qkv[2], doc_rows)
    )
    mixed_low = from_blocks(mixed_blocks[None], rows_here)
    attended = jnp.dot(mixed_low, proj_full, preferred_element_type=jnp.float32)
    after_attn = x_in + attended
    normed_two, norm_back_two = jax.vjp(layer_norm, after_attn, norm_values[2], norm_values[3])
    sent_low = normed_two.astype(jnp.bfloat16)
    route_ids = routes[:, 0]
    onehot = route_ids[:, None] == jnp.arange(experts_all, dtype=jnp.int32)[None, :]
    picked_centre = jnp.dot(
        onehot.astype(jnp.bfloat16), centre_table, preferred_element_type=jnp.float32
    )
    logits = jnp.sum(sent_low.astype(jnp.float32) * picked_centre, axis=-1)
    gate_value = jax.nn.sigmoid(logits)
    running = jnp.cumsum(onehot.astype(jnp.int32), axis=0)
    within = jnp.sum(running * onehot.astype(jnp.int32), axis=1) - 1
    slot_index = route_ids * slot_cap + within
    slot_token = (
        jnp.zeros((slot_count,), jnp.int32)
        .at[slot_index]
        .set(jnp.arange(local_tokens, dtype=jnp.int32))
    )
    slot_live = jnp.zeros((slot_count,), jnp.bfloat16).at[slot_index].set(1)
    outgoing = (sent_low[slot_token] * slot_live[:, None]).reshape(
        experts_all, slot_cap, model_width
    )
    arrived = lax.all_to_all(outgoing, "expert", split_axis=0, concat_axis=0, tiled=True)
    preact = jnp.einsum("skd,df->skf", arrived, weight_in, preferred_element_type=jnp.float32)
    hidden = exact_gelu(preact).astype(jnp.bfloat16)
    result = jnp.einsum(
        "skf,fd->skd", hidden, weight_out, preferred_element_type=jnp.float32
    ).astype(jnp.bfloat16)
    dispatched = (result, arrived, preact)
    returned = lax.all_to_all(dispatched[0], "expert", split_axis=0, concat_axis=0, tiled=True)
    expert_rows = returned.reshape(slot_count, model_width)[slot_index]
    activations = (after_attn + gate_value[:, None] * expert_rows.astype(jnp.float32)).astype(
        jnp.bfloat16
    )
    grad_out = out_grad.astype(jnp.float32)
    grad_logits = (
        jnp.sum(grad_out * expert_rows.astype(jnp.float32), axis=-1)
        * gate_value
        * (1.0 - gate_value)
    )
    grad_rows = (gate_value[:, None] * grad_out).astype(jnp.bfloat16)
    grad_outgoing = (grad_rows[slot_token] * slot_live[:, None]).reshape(
        experts_all, slot_cap, model_width
    )
    grad_arrived = lax.all_to_all(grad_outgoing, "expert", split_axis=0, concat_axis=0, tiled=True)
    arrived = dispatched[1]
    preact = dispatched[2]
    hidden_full, gelu_back = jax.vjp(exact_gelu, preact)
    hidden_low = hidden_full.astype(jnp.bfloat16)
    grad_hidden = jnp.einsum(
        "skd,fd->skf", grad_arrived, weight_out, preferred_element_type=jnp.float32
    )
    grad_preact = gelu_back(grad_hidden)[0].astype(jnp.bfloat16)
    grad_input_rows = jnp.einsum(
        "skf,df->skd", grad_preact, weight_in, preferred_element_type=jnp.float32
    ).astype(jnp.bfloat16)
    grad_weight_in = jnp.einsum(
        "skd,skf->df", arrived, grad_preact, preferred_element_type=jnp.float32
    )
    grad_weight_out = jnp.einsum(
        "skf,skd->fd", hidden_low, grad_arrived, preferred_element_type=jnp.float32
    )
    grad_back = lax.all_to_all(grad_input_rows, "expert", split_axis=0, concat_axis=0, tiled=True)
    grad_sent = grad_back.reshape(slot_count, model_width)[slot_index].astype(jnp.float32)
    grad_normed_two = grad_sent + grad_logits[:, None] * picked_centre
    grad_centre = jnp.einsum(
        "te,td->ed",
        onehot.astype(jnp.float32),
        grad_logits[:, None] * sent_low.astype(jnp.float32),
        precision=highest,
    )
    grad_after, grad_gain_two, grad_bias_two = norm_back_two(grad_normed_two)
    grad_after = grad_after + grad_out
    grad_attended = grad_after.astype(jnp.bfloat16)
    grad_proj = jnp.einsum(
        "td,te->de", mixed_low, grad_attended, preferred_element_type=jnp.float32
    )
    grad_mixed = jnp.einsum(
        "te,de->td", grad_attended, proj_full, preferred_element_type=jnp.float32
    ).astype(jnp.bfloat16)
    grad_blocks = to_blocks(grad_mixed, rows_here, 1)[0]
    grad_parts = lax.map(
        head_backward, (split_qkv[0], split_qkv[1], split_qkv[2], grad_blocks, log_totals, doc_rows)
    )
    grad_packed = from_blocks(jnp.stack(grad_parts), rows_here)
    grad_qkv = jnp.einsum("td,te->de", normed_low, grad_packed, preferred_element_type=jnp.float32)
    grad_normed_one = jnp.einsum(
        "te,de->td", grad_packed, qkv_full, preferred_element_type=jnp.float32
    )
    grad_x_norm, grad_gain_one, grad_bias_one = norm_back_one(grad_normed_one)
    input_grad = grad_after + grad_x_norm
    grad_norm_rows = jnp.stack([grad_gain_one, grad_bias_one, grad_gain_two, grad_bias_two])
    reduced = (
        lax.psum_scatter(grad_qkv, ("expert", "dp"), scatter_dimension=0, tiled=True),
        lax.psum_scatter(grad_proj, ("expert", "dp"), scatter_dimension=0, tiled=True),
        lax.psum_scatter(grad_norm_rows, ("expert", "dp"), scatter_dimension=1, tiled=True),
        lax.psum_scatter(
            grad_centre.reshape(-1), ("expert", "dp"), scatter_dimension=0, tiled=True
        ),
    )
    expert_reduced = (
        lax.psum_scatter(
            grad_weight_in[None].astype(jnp.bfloat16), "dp", scatter_dimension=1, tiled=True
        ).astype(jnp.float32),
        lax.psum_scatter(
            grad_weight_out[None].astype(jnp.bfloat16), "dp", scatter_dimension=2, tiled=True
        ).astype(jnp.float32),
    )
    qkv_grad = reduced[0]
    proj_grad = reduced[1]
    norm_grad = reduced[2]
    centre_grad = reduced[3].reshape(centroids.shape)
    in_grad = expert_reduced[0]
    out_grad_w = expert_reduced[1]
    square_sum = (
        jnp.sum(qkv_grad * qkv_grad)
        + jnp.sum(proj_grad * proj_grad)
        + jnp.sum(norm_grad * norm_grad)
        + jnp.sum(centre_grad * centre_grad)
        + jnp.sum(in_grad * in_grad)
        + jnp.sum(out_grad_w * out_grad_w)
    )
    grad_norm = jnp.sqrt(lax.psum(square_sum, ("expert", "dp")))
    factor = clip_limit / jnp.maximum(grad_norm, clip_limit)
    norm_new = update(norm_params, norm_moment, norm_average, norm_grad, factor, norm_rate)
    qkv_new = update(qkv_weight, qkv_moment, qkv_average, qkv_grad, factor, learn_rate)
    proj_new = update(proj_weight, proj_moment, proj_average, proj_grad, factor, learn_rate)
    centre_new = update(
        centroids, centroid_moment, centroid_average, centre_grad, factor, learn_rate
    )
    in_new = update(expert_in, in_moment, in_average, in_grad, factor, learn_rate)
    out_new = update(expert_out, out_moment, out_average, out_grad_w, factor, learn_rate)
    return (
        activations,
        input_grad,
        grad_norm,
        norm_new[0],
        qkv_new[0],
        proj_new[0],
        centre_new[0],
        in_new[0],
        out_new[0],
        norm_new[1],
        qkv_new[1],
        proj_new[1],
        centre_new[1],
        in_new[1],
        out_new[1],
        norm_new[2],
        qkv_new[2],
        proj_new[2],
        centre_new[2],
        in_new[2],
        out_new[2],
    )


def solution(mesh):
    placed = (
        P(("expert", "dp"), None),
        P(("expert", "dp")),
        P(("expert", "dp"), None),
        P(("expert", "dp"), None),
        P(None, ("expert", "dp")),
        P(("expert", "dp"), None),
        P(("expert", "dp"), None),
        P("expert", "dp"),
        P("expert", "dp", None),
        P("expert", None, "dp"),
        P(None, ("expert", "dp")),
        P(("expert", "dp"), None),
        P(("expert", "dp"), None),
        P("expert", "dp"),
        P("expert", "dp", None),
        P("expert", None, "dp"),
        P(None, ("expert", "dp")),
        P(("expert", "dp"), None),
        P(("expert", "dp"), None),
        P("expert", "dp"),
        P("expert", "dp", None),
        P("expert", None, "dp"),
    )
    return jax.shard_map(
        shards,
        mesh=mesh,
        in_specs=placed,
        out_specs=(
            P(("expert", "dp"), None),
            P(("expert", "dp"), None),
            P(),
            P(None, ("expert", "dp")),
            P(("expert", "dp"), None),
            P(("expert", "dp"), None),
            P("expert", "dp"),
            P("expert", "dp", None),
            P("expert", None, "dp"),
            P(None, ("expert", "dp")),
            P(("expert", "dp"), None),
            P(("expert", "dp"), None),
            P("expert", "dp"),
            P("expert", "dp", None),
            P("expert", None, "dp"),
            P(None, ("expert", "dp")),
            P(("expert", "dp"), None),
            P(("expert", "dp"), None),
            P("expert", "dp"),
            P("expert", "dp", None),
            P("expert", None, "dp"),
        ),
        check_vma=False,
    )
```

profile of v0, /device:TPU:0, one launch (start us, length us, event | category | flops | bytes accessed | tf_op | source)
XLA Modules:
  0.0 1673.3 jit_solution(5144450814290929143)
XLA Ops:
  18.4 43.4 %all-gather.1 = bf16[32,32,4]{1,2,0:T(4,128)(2,1)S(1)} all-gather(bf16[1,32,4]{1,2,0:T(4,128)(2,1)S(1)} %convert_bitcast_fusion), channel_id=1, replica_groups=mesh['expert'=8,'dp'=4] {'expert','dp'}, dimensions={0}, use_global_device_ids=true | all-gather | bytes 8448 | tf_op jit(solution)/shard_map/all_gather | solution.py:146
  62.5 36.8 %all-gather = bf16[1,8192]{1,0:T(2,128)(2,1)S(1)} all-gather(bf16[1,256]{1,0:T(2,128)(2,1)S(1)} %convert_element_type.131), channel_id=2, replica_groups=mesh['expert'=8,'dp'=4] {'expert','dp'}, dimensions={1}, use_global_device_ids=true | all-gather | bytes 16896 | tf_op jit(solution)/shard_map/all_gather | solution.py:147
  144.5 64.2 %while.26 = (s32[]{:T(128)}, bf16[4,4,1024,64]{2,3,1,0:T(8,128)(2,1)}, f32[4,4,1024]{2,1,0:T(4,128)}, s32[4,1024]{1,0:T(4,128)S(1)}, bf16[4,4,1024,64]{2,3,1,0:T...) while((s32[]{:T(128)}, ...), condition=%wide.region_5.6_spmd, body=%wide.region_2.5_spmd.sunk | while | flops 1127477248 | bytes 56769112 | solution.py:168
  238.2 67.7 %all-to-all-done = bf16[8,192,1024]{2,1,0:T(8,128)(2,1)S(1)} async-done(((bf16[8,192,1024]{2,1,0:T(8,128)(2,1)}), bf16[8,192,1024]{2,1,0:T(8,128)(2,1)S(1)}, u32[]{:S(2)}, u32[]{:S(2)}) %all-to-all-start) | async-done | bytes 3145760 | tf_op jit(solution)/shard_map/all_to_all | solution.py:195
  305.9 27.6 %fusion.79 = (u8[192,4096]{1,0:T(8,128)(4,1)S(1)}, u8[192,4096]{1,0:T(8,128)(4,1)S(1)}, f32[8,192,4096]{2,1,0:T(8,128)}) fusion(bf16[8,192,1024]{2,1,0:T(8,128)(2,1)S(1)} %all-to-all-done, bf16[1,1024,4096]{2,1,0:T(8,128)(2,1)} %all-gather.11.cloned.1.call-done), kind=kOutput, calls=%fused_computation.117 | convolution fusion | flops 12965117952 | bytes 38273024 | tf_op jit(solution)/shard_map/skd,df->skf/dot_general | solution.py:196
  333.5 59.0 %multiply_convert_fusion.1 = (bf16[8,192,4096]{2,1,0:T(8,128)(2,1)}, f32[8,192,4096]{2,1,0:T(8,128)}) fusion(f32[8,192,4096]{2,1,0:T(8,128)} %get-tuple-element.284, u8[192,4096]{1,0:T(8,128)(4,1)S(1)} %get-tuple-element.203, u8[192,4096]{1,0:T(8,128)(4,1)S(1)} %get-tuple-element.202), kind=kLoop, calls=%fused_computation.78 | loop fusion | flops 440401920 | bytes 64487424 | tf_op jit(solution)/shard_map/convert_element_type | solution.py:197
  392.5 19.3 %fusion.107 = bf16[8,192,1024]{2,1,0:T(8,128)(2,1)} fusion(bf16[8,192,4096]{2,1,0:T(8,128)(2,1)} %get-tuple-element.265, bf16[1,4096,1024]{2,1,0:T(8,128)(2,1)} %all-gather.13.cloned.1.call-done), kind=kOutput, calls=%fused_computation.159 | convolution fusion | flops 12886474752 | bytes 24117248 | tf_op jit(solution)/shard_map/skf,fd->skd/dot_general | solution.py:198
  419.6 66.9 %all-to-all-done.1 = bf16[8,192,1024]{2,1,0:T(8,128)(2,1)S(1)} async-done(((bf16[8,192,1024]{2,1,0:T(8,128)(2,1)}), bf16[8,192,1024]{2,1,0:T(8,128)(2,1)S(1)}, u32[]{:S(2)}, u32[]{:S(2)}) %all-to-all-start.1) | async-done | bytes 3145760 | tf_op jit(solution)/shard_map/all_to_all | solution.py:202
  510.7 74.5 %all_to_all.20 = bf16[8,192,1024]{2,1,0:T(8,128)(2,1)S(1)} all-to-all(bf16[8,192,1024]{2,1,0:T(8,128)(2,1)S(1)} %broadcast_multiply_fusion), channel_id=1, replica_groups=mesh['expert'=8,'dp'=4] {'expert'}, dimensions={0} | all-to-all | bytes 6291456 | tf_op jit(solution)/shard_map/all_to_all | solution.py:217
  585.2 32.2 %add_convert_fusion = bf16[8,192,4096]{2,1,0:T(8,128)(2,1)} fusion(f32[8,192,4096]{2,1,0:T(8,128)} %get-tuple-element.266, f32[8,192,4096]{2,1,0:T(8,128)} %get-tuple-element.284, bf16[8,192,1024]{2,1,0:T(8,128)(2,1)S(1)} %all_to_all.20, bf16[1,4096,1024]{2,1,0:T(8,128)(2,1)} %all-gather.13.cloned.1.call-done), kind=kOutput, calls=%fused_computation.77 | convolution fusion | flops 12972982272 | bytes 74448896 | tf_op jit(solution)/shard_map/skd,fd->skf/dot_general | solution.py:222
  617.4 19.2 %fusion.104 = bf16[8,192,1024]{2,1,0:T(8,128)(2,1)} fusion(bf16[8,192,4096]{2,1,0:T(8,128)(2,1)} %add_convert_fusion, bf16[1,1024,4096]{2,1,0:T(8,128)(2,1)} %all-gather.11.cloned.1.call-done), kind=kOutput, calls=%fused_computation.158 | convolution fusion | flops 12886474752 | bytes 24117248 | tf_op jit(solution)/shard_map/skf,df->skd/dot_general | solution.py:226
  640.3 70.3 %all-to-all-done.3 = bf16[8,192,1024]{2,1,0:T(8,128)(2,1)S(1)} async-done(((bf16[8,192,1024]{2,1,0:T(8,128)(2,1)}), bf16[8,192,1024]{2,1,0:T(8,128)(2,1)S(1)}, u32[]{:S(2)}, u32[]{:S(2)}) %all-to-all-start.3) | async-done | bytes 3145760 | tf_op jit(solution)/shard_map/all_to_all | solution.py:235
  739.5 243.7 %while.27 = (s32[]{:T(128)}, bf16[4,4,1024,64]{2,3,1,0:T(8,128)(2,1)}, bf16[4,4,1024,64]{2,3,1,0:T(8,128)(2,1)}, bf16[4,4,1024,64]{2,3,1,0:T(8,128)(2,1)}, s32[4...) while((s32[]{:T(128)}, ...), condition=%wide.region_19.20_spmd, body=%wide.region_17.19_spmd.sunk | while | flops 2726555648 | bytes 250709232 | solution.py:254
  752.2 12.5 multiply_reduce_fusion.9
  764.7 16.3 multiply_convert_fusion.3
  813.0 12.5 multiply_reduce_fusion.9
  825.5 16.3 multiply_convert_fusion.3
  873.8 12.5 multiply_reduce_fusion.9
  886.3 16.3 multiply_convert_fusion.3
  934.6 12.5 multiply_reduce_fusion.9
  947.1 16.3 multiply_convert_fusion.3
  1015.3 19.3 %fusion.73 = bf16[1,4096,1024]{2,1,0:T(8,128)(2,1)} fusion(bf16[8,192,4096]{2,1,0:T(8,128)(2,1)} %get-tuple-element.265, bf16[8,192,1024]{2,1,0:T(8,128)(2,1)} %copy-done.18), kind=kOutput, calls=%fused_computation.102 | convolution fusion | flops 12889096192 | bytes 24117248 | tf_op jit(solution)/shard_map/skf,skd->fd/dot_general | solution.py:232
  1034.6 19.6 %fusion.72 = bf16[1,1024,4096]{2,1,0:T(8,128)(2,1)} fusion(bf16[8,192,1024]{2,1,0:T(8,128)(2,1)} %copy-done.17, bf16[8,192,4096]{2,1,0:T(8,128)(2,1)} %add_convert_fusion), kind=kOutput, calls=%fused_computation.101 | convolution fusion | flops 12889096192 | bytes 24117248 | tf_op jit(solution)/shard_map/skd,skf->df/dot_general | solution.py:229
  1054.8 12.7 fusion.126
  1072.1 38.4 %all-reduce = f32[8192]{0:T(1024)S(1)} all-reduce(f32[8192]{0:T(1024)S(1)} %bitcast.239), channel_id=6, replica_groups=mesh['expert'=8,'dp'=4] {'expert','dp'}, use_global_device_ids=true, to_apply=%region_32.33.clone | all-reduce | flops 8192 | bytes 65536
  1123.0 18.9 %reduce-scatter.16.cloned.1.call-done = f32[32,4]{1,0:T(8,128)} async-done(((f32[1024,4]{1,0:T(8,128)}), f32[32,4]{1,0:T(8,128)}) %reduce-scatter.16.cloned.1.call-update) | async-done | bytes 528
  1143.3 138.5 %reduce-scatter.10.cloned.1.call-done = f32[32,1024]{1,0:T(8,128)} async-done(((f32[1024,1024]{1,0:T(8,128)}), f32[32,1024]{1,0:T(8,128)}) %reduce-scatter.10.cloned.1.call-update) | async-done | bytes 131088 | tf_op jit(solution)/shard_map/reduce_scatter | solution.py:267
  1283.4 68.8 %reduce-scatter.14.cloned.1.call-done = bf16[1,4096,256]{2,1,0:T(8,128)(2,1)} async-done(((bf16[1,4096,1024]{2,1,0:T(8,128)(2,1)}), bf16[1,4096,256]{2,1,0:T(8,128)(2,1)}) %reduce-scatter.14.cloned.1.call-update) | async-done | bytes 2097168 | tf_op jit(solution)/shard_map/reduce_scatter | solution.py:277
  1355.7 70.9 %reduce-scatter.12.cloned.1.call-done = bf16[1,256,4096]{2,1,0:T(8,128)(2,1)} async-done(((bf16[1,1024,4096]{2,1,0:T(8,128)(2,1)}), bf16[1,256,4096]{2,1,0:T(8,128)(2,1)}) %reduce-scatter.12.cloned.1.call-update) | async-done | bytes 2097168 | tf_op jit(solution)/shard_map/reduce_scatter | solution.py:274
  1429.8 159.6 %reduce-scatter.8.cloned.1.call-done = f32[32,3072]{1,0:T(8,128)} async-done(((f32[1024,3072]{1,0:T(8,128)}), f32[32,3072]{1,0:T(8,128)}) %reduce-scatter.8.cloned.1.call-update) | async-done | bytes 393232 | tf_op jit(solution)/shard_map/reduce_scatter | solution.py:266
  1599.0 39.7 %psum.7 = f32[]{:T(128)} all-reduce(f32[]{:T(128)S(6)} %add.212), channel_id=1, replica_groups=mesh['expert'=8,'dp'=4] {'expert','dp'}, use_global_device_ids=true, to_apply=%region_38.39 | all-reduce | flops 1 | bytes 8 | tf_op jit(solution)/shard_map/psum | solution.py:295
  1651.2 12.0 multiply_add_fusion.1
  (341 shorter events, 421.3 us)
Async XLA Ops:
  7.2 109.2 %all-gather.7.cloned.1.call-start = ((), (), s32[]{:S(2)}) async-start(), calls=%async_computation.9 | async-start | bytes 6488064 | tf_op jit(solution)/shard_map/all_gather | solution.py:144
  9.0 199.8 %all-gather.9.cloned.1.call-start = ((), (), s32[]{:S(2)}) async-start(), calls=%async_computation.10 | async-start | bytes 2162688 | tf_op jit(solution)/shard_map/all_gather | solution.py:145
  10.6 227.6 %all-gather.11.cloned.1.call-start = ((), (), s32[]{:S(2)}) async-start(), calls=%async_computation.11 | async-start | bytes 10485760 | tf_op jit(solution)/shard_map/all_gather | solution.py:156
  14.5 48.1 %copy-start.63 = (f32[1,256]{1,0:T(1,128)S(1)}, f32[1,256]{1,0:T(1,128)}, u32[]{:S(2)}) copy-start(f32[1,256]{1,0:T(1,128)} %param.33) | copy-start | bytes 3076
  14.5 85.6 %copy-start.29 = (s32[1024,1]{0,1:T(1,128)S(1)}, s32[1024,1]{0,1:T(1,128)}, u32[]{:S(2)}) copy-start(s32[1024,1]{0,1:T(1,128)} %param.28) | copy-start | bytes 12292
  17.4 111.0 %copy-start.2 = (bf16[1024,1024]{0,1:T(8,128)(2,1)}, bf16[1024,1024]{0,1:T(8,128)(2,1)S(1)}, u32[]{:S(2)}) copy-start(bf16[1024,1024]{0,1:T(8,128)(2,1)S(1)} %copy.97) | copy-start | bytes 6291460
  17.7 110.6 %copy-start.32 = (f32[1024]{0:T(1024)}, f32[1024]{0:T(1024)S(1)}, u32[]{:S(2)}) copy-start(f32[1024]{0:T(1024)S(1)} %broadcast_multiply_fusion.3) | copy-start | bytes 12292
  18.4 43.4 %copy-start.50 = (f32[1024]{0:T(1024)}, f32[1024]{0:T(1024)S(1)}, u32[]{:S(2)}) copy-start(f32[1024]{0:T(1024)S(1)} %fusion.99) | copy-start | bytes 12292
  18.4 110.0 %copy-start.46 = (f32[1024]{0:T(1024)}, f32[1024]{0:T(1024)S(1)}, u32[]{:S(2)}) copy-start(f32[1024]{0:T(1024)S(1)} %fusion.121) | copy-start | bytes 12292
  62.5 65.8 %copy-start.38 = (f32[1,1024]{1,0:T(1,128)}, f32[1,1024]{1,0:T(1,128)S(1)}, u32[]{:S(2)}) copy-start(f32[1,1024]{1,0:T(1,128)S(1)} %get-tuple-element.280) | copy-start | bytes 12292
  62.5 65.9 %copy-start.65 = (f32[1,1024]{1,0:T(1,128)}, f32[1,1024]{1,0:T(1,128)S(1)}, u32[]{:S(2)}) copy-start(f32[1,1024]{1,0:T(1,128)S(1)} %get-tuple-element.279) | copy-start | bytes 12292
  144.5 64.2 %copy-start.3 = (bf16[1024,1024]{0,1:T(8,128)(2,1)S(1)}, bf16[1024,1024]{0,1:T(8,128)(2,1)}, u32[]{:S(2)}) copy-start(bf16[1024,1024]{0,1:T(8,128)(2,1)} %copy-done.2) | copy-start | bytes 6291460
  230.7 75.2 %all-to-all-start = ((bf16[8,192,1024]{2,1,0:T(8,128)(2,1)}), bf16[8,192,1024]{2,1,0:T(8,128)(2,1)S(1)}, u32[]{:S(2)}, u32[]{:S(2)}) async-start(bf16[8,192,1024]{2,1,0:T(8,128)(2,1)} %broadcast_multiply_fusion.1), calls=%async_computation | async-start | bytes 6291456 | tf_op jit(solution)/shard_map/all_to_all | solution.py:195
  234.4 158.1 %all-gather.13.cloned.1.call-start = ((), (), s32[]{:S(2)}) async-start(), calls=%async_computation.12 | async-start | bytes 10485760 | tf_op jit(solution)/shard_map/all_gather | solution.py:157
  305.9 27.6 %copy-start.17 = (bf16[8,192,1024]{2,1,0:T(8,128)(2,1)}, bf16[8,192,1024]{2,1,0:T(8,128)(2,1)S(1)}, u32[]{:S(2)}) copy-start(bf16[8,192,1024]{2,1,0:T(8,128)(2,1)S(1)} %all-to-all-done) | copy-start | bytes 9437188
  411.8 74.7 %all-to-all-start.1 = ((bf16[8,192,1024]{2,1,0:T(8,128)(2,1)}), bf16[8,192,1024]{2,1,0:T(8,128)(2,1)S(1)}, u32[]{:S(2)}, u32[]{:S(2)}) async-start(bf16[8,192,1024]{2,1,0:T(8,128)(2,1)} %fusion.107), calls=%async_computation.1 | async-start | bytes 6291456 | tf_op jit(solution)/shard_map/all_to_all | solution.py:202
  585.2 32.2 %copy-start.18 = (bf16[8,192,1024]{2,1,0:T(8,128)(2,1)}, bf16[8,192,1024]{2,1,0:T(8,128)(2,1)S(1)}, u32[]{:S(2)}) copy-start(bf16[8,192,1024]{2,1,0:T(8,128)(2,1)S(1)} %all_to_all.20) | copy-start | bytes 9437188
  636.6 74.0 %all-to-all-start.3 = ((bf16[8,192,1024]{2,1,0:T(8,128)(2,1)}), bf16[8,192,1024]{2,1,0:T(8,128)(2,1)S(1)}, u32[]{:S(2)}, u32[]{:S(2)}) async-start(bf16[8,192,1024]{2,1,0:T(8,128)(2,1)} %fusion.104), calls=%async_computation.3 | async-start | bytes 6291456 | tf_op jit(solution)/shard_map/all_to_all | solution.py:235
  640.3 501.7 %reduce-scatter.16.cloned.1.call-start = ((), (), s32[]{:S(2)}) async-start(), calls=%async_computation.17 | async-start | bytes 540672
  640.3 84.2 %copy-start.40 = (f32[1024]{0:T(1024)}, f32[1024]{0:T(1024)S(1)}, u32[]{:S(2)}) copy-start(f32[1024]{0:T(1024)S(1)} %subtract_multiply_fusion) | copy-start | bytes 12292
  1008.5 273.3 %reduce-scatter.10.cloned.1.call-start = ((), (), s32[]{:S(2)}) async-start(), calls=%async_computation.14 | async-start | bytes 4325376 | tf_op jit(solution)/shard_map/reduce_scatter | solution.py:267
  1015.2 337.0 %reduce-scatter.14.cloned.1.call-start = ((), (), s32[]{:S(2)}) async-start(), calls=%async_computation.16 | async-start | bytes 10485760 | tf_op jit(solution)/shard_map/reduce_scatter | solution.py:277
  1034.5 392.0 %reduce-scatter.12.cloned.1.call-start = ((), (), s32[]{:S(2)}) async-start(), calls=%async_computation.15 | async-start | bytes 10485760 | tf_op jit(solution)/shard_map/reduce_scatter | solution.py:274
  1054.2 535.3 %reduce-scatter.8.cloned.1.call-start = ((), (), s32[]{:S(2)}) async-start(), calls=%async_computation.13 | async-start | bytes 12976128 | tf_op jit(solution)/shard_map/reduce_scatter | solution.py:266
  1067.5 43.6 %copy-start.49 = (f32[1024]{0:T(1024)S(1)}, f32[1024]{0:T(1024)}, u32[]{:S(2)}) copy-start(f32[1024]{0:T(1024)} %copy-done.48) | copy-start | bytes 12292
  1283.4 356.2 %copy-start.61 = (f32[4,32]{1,0:T(4,128)S(1)}, f32[4,32]{1,0:T(4,128)}, u32[]{:S(2)}) copy-start(f32[4,32]{1,0:T(4,128)} %param.30) | copy-start | bytes 1540
  1283.4 356.2 %copy-start.67 = (f32[4,32]{1,0:T(4,128)S(1)}, f32[4,32]{1,0:T(4,128)}, u32[]{:S(2)}) copy-start(f32[4,32]{1,0:T(4,128)} %param.42) | copy-start | bytes 1540
  1283.4 356.2 %copy-start.68 = (f32[4,32]{1,0:T(4,128)S(1)}, f32[4,32]{1,0:T(4,128)}, u32[]{:S(2)}) copy-start(f32[4,32]{1,0:T(4,128)} %param.36) | copy-start | bytes 1540
  1283.4 356.7 %copy-start.64 = (f32[1,256]{1,0:T(1,128)S(1)}, f32[1,256]{1,0:T(1,128)}, u32[]{:S(2)}) copy-start(f32[1,256]{1,0:T(1,128)} %param.33) | copy-start | bytes 3076
  1283.4 356.7 %copy-start.69 = (f32[1,256]{1,0:T(1,128)S(1)}, f32[1,256]{1,0:T(1,128)}, u32[]{:S(2)}) copy-start(f32[1,256]{1,0:T(1,128)} %param.45) | copy-start | bytes 3076
  1283.4 356.7 %copy-start.70 = (f32[1,256]{1,0:T(1,128)S(1)}, f32[1,256]{1,0:T(1,128)}, u32[]{:S(2)}) copy-start(f32[1,256]{1,0:T(1,128)} %param.39) | copy-start | bytes 3076
  1352.2 288.5 %copy-start.15 = (bf16[1,4096,256]{2,1,0:T(8,128)(2,1)S(1)}, bf16[1,4096,256]{2,1,0:T(8,128)(2,1)}, u32[]{:S(2)}) copy-start(bf16[1,4096,256]{2,1,0:T(8,128)(2,1)} %reduce-scatter.14.cloned.1.call-done) | copy-start | bytes 6291460
  (65 other events, 419.1 us)
Sparse Core Ops, SparseCore 0:
  11.5 72.3 all-gather.6
  87.3 54.9 all-gather.8
  144.4 57.1 all-gather.10
  238.3 60.9 all-gather.12
  1008.6 133.2 reduce-scatter.15
  1144.8 137.0 reduce-scatter.9
  1284.6 67.6 reduce-scatter.13
  1354.8 71.7 reduce-scatter.11
  1433.6 155.7 reduce-scatter.7
where the time goes:
time: 1680 us; the launch traced here: 1670 us
  waiting for transfers between devices  662 us (39%)
  matrix products  404 us (24%)
  other arithmetic  233 us (14%)
  blocking collectives  233 us (14%)
  local copies, waits for them, and re-layouts  109 us (6%)
  between operations  20.9 us (1%)
    reduce_scatter x1, waiting for transfers between devices, shards(): lax.psum_scatter(grad_qkv, ('expert', 'dp'), scatter_dimension=0, tiled=T...  160 us
    reduce_scatter x1, waiting for transfers between devices, shards(): lax.psum_scatter(grad_proj, ('expert', 'dp'), scatter_dimension=0, tiled=...  138 us
    all_to_all x1, blocking collectives, shards(): lax.all_to_all(grad_outgoing, 'expert', split_axis=0, concat_axis=0, tile...  74.5 us
    reduce_scatter x1, waiting for transfers between devices, shards(): lax.psum_scatter(grad_weight_in[None].astype(jnp.bfloat16), 'dp', scatter...  70.9 us
    all_to_all x1, waiting for transfers between devices, shards(): lax.all_to_all(grad_input_rows, 'expert', split_axis=0, concat_axis=0, ti...  70.3 us
    reduce_scatter x1, waiting for transfers between devices, shards(): lax.psum_scatter(grad_weight_out[None].astype(jnp.bfloat16), 'dp', scatte...  68.8 us
    all_to_all x1, waiting for transfers between devices, shards(): lax.all_to_all(outgoing, 'expert', split_axis=0, concat_axis=0, tiled=True)  67.7 us
    dot_general x8, matrix products, masked_scores(): jnp.einsum('hqd,hkd->hqk', query_blk, key_blk, preferred_element_type=jnp...  67.6 us
  transfers between devices with their start and end apart: 12, of which 8 were waited for; matrix products, arithmetic and copies ran while one was open for 19% of the time, Pallas kernels for 0%

commit v1 on v0

v1 whole, which is shorter than its diff:
```python
import functools
import math

import jax
import jax.numpy as jnp
from jax import lax
from jax.experimental import pallas as pl
from jax.experimental.pallas import tpu as pltpu
from jax.sharding import PartitionSpec as P

HEAD_DIM = 64
SEQ = 1024
LANES = 128
BLOCK = 256

eps = 1e-05
scale_qk = 0.125
momentum_rate = 0.9
learn_rate = 100.0
norm_rate = 500.0
average_rate = 0.9
clip_limit = 1.0
masked_score = -1000000000.0
everywhere = ("expert", "dp")
low = jnp.bfloat16
f32 = jnp.float32

erfc_point = 0.4
erfc_terms = (
    0.11596270714310389,
    0.08090178846816841,
    0.2341610172367065,
    -0.1854824771652721,
    0.35459055762612957,
    -0.10013360714943426,
)


def dot_rows(left, right):
    return lax.dot_general(left, right, (((1,), (0,)), ((), ())), preferred_element_type=f32)


def dot_cols(left, right):
    return lax.dot_general(left, right, (((1,), (1,)), ((), ())), preferred_element_type=f32)


def layer_norm(values, norm_gain, norm_bias):
    centre = values - jnp.mean(values, axis=-1, keepdims=True)
    spread = jnp.mean(centre * centre, axis=-1, keepdims=True)
    return centre * lax.rsqrt(spread + eps) * norm_gain + norm_bias


def fill_bias(bias, doc_of_rows, doc_of_cols, rows_are_keys):
    for block in range(0, SEQ, BLOCK):
        rows = lax.broadcasted_iota(jnp.int32, (BLOCK, SEQ), 0) + block
        cols = lax.broadcasted_iota(jnp.int32, (BLOCK, SEQ), 1)
        causal = (rows <= cols) if rows_are_keys else (rows >= cols)
        same = doc_of_rows[block : block + BLOCK, :] == doc_of_cols[...]
        bias[block : block + BLOCK, :] = jnp.where(same & causal, 3.0e38, masked_score)


def in_head(shape, head, axis):
    return lax.broadcasted_iota(jnp.int32, shape, axis) // HEAD_DIM == head


def keep_head(values, head):
    return jnp.where(in_head(values.shape, head, 1), values, jnp.zeros_like(values))


def attend_kernel(q_ref, k_ref, v_ref, doc_col, doc_row, mixed_ref, lse_ref, bias):
    @pl.when(pl.program_id(1) == 0)
    def _():
        fill_bias(bias, doc_col, doc_row, False)

    for block in range(0, SEQ, BLOCK):
        seen = block + BLOCK
        query = q_ref[block:seen, :] * jnp.asarray(scale_qk, low)
        outs, stats = [], []
        for head in range(2):
            scores = dot_cols(keep_head(query, head), k_ref[:seen, :])
            scores = jnp.minimum(scores, bias[block:seen, :seen])
            top = jnp.max(scores, axis=-1, keepdims=True)
            exponent = jnp.exp(scores - top)
            total = jnp.sum(exponent, axis=-1, keepdims=True)
            outs.append(dot_rows(exponent.astype(low), v_ref[:seen, :]) / total)
            stats.append(top + jnp.log(total))
        first = in_head((BLOCK, LANES), 0, 1)
        mixed_ref[block:seen, :] = jnp.where(first, outs[0], outs[1]).astype(low)
        lane = lax.broadcasted_iota(jnp.int32, (BLOCK, LANES), 1)
        both = jnp.where(lane == 0, stats[0], stats[1])
        lse_ref[:, block:seen] = both.T[:8, :]


def attend(packed, doc_col, doc_row):
    count, wide = packed.shape
    width = wide // 3
    pairs = width // LANES

    def part(which):
        return pl.BlockSpec((SEQ, LANES), lambda r, p, w=which: (r, w * pairs + p))

    return pl.pallas_call(
        attend_kernel,
        grid=(count // SEQ, pairs),
        in_specs=[
            part(0),
            part(1),
            part(2),
            pl.BlockSpec((SEQ, 1), lambda r, p: (r, 0)),
            pl.BlockSpec((1, SEQ), lambda r, p: (0, r)),
        ],
        out_specs=[
            pl.BlockSpec((SEQ, LANES), lambda r, p: (r, p)),
            pl.BlockSpec((8, SEQ), lambda r, p: (p, r)),
        ],
        out_shape=[
            jax.ShapeDtypeStruct((count, width), low),
            jax.ShapeDtypeStruct((8 * pairs, count), f32),
        ],
        scratch_shapes=[pltpu.VMEM((SEQ, SEQ), f32)],
        compiler_params=pltpu.CompilerParams(vmem_limit_bytes=48 * 2**20),
        cost_estimate=pl.CostEstimate(
            flops=4 * count * SEQ * width, bytes_accessed=8 * count * width, transcendentals=0
        ),
        name="attend",
    )(packed, packed, packed, doc_col, doc_row)


def attend_back_kernel(
    q_ref, k_ref, v_ref, grad_ref, mixed_ref, lse_ref, doc_col, doc_row, out_ref, bias, grad_q_t
):
    @pl.when(pl.program_id(1) == 0)
    def _():
        fill_bias(bias, doc_col, doc_row, True)

    query = q_ref[...] * jnp.asarray(scale_qk, low)
    grad = grad_ref[...]
    product = grad.astype(f32) * mixed_ref[...].astype(f32)
    upper = product.astype(low)
    lower = (product - upper.astype(f32)).astype(low)
    chooser = (
        lax.broadcasted_iota(jnp.int32, (8, LANES), 0)
        == lax.broadcasted_iota(jnp.int32, (8, LANES), 1) // HEAD_DIM
    ).astype(low)
    inner = dot_cols(chooser, upper) + dot_cols(chooser, lower)
    key_t = k_ref[...].T
    for block in range(0, SEQ, BLOCK):
        after = block + BLOCK
        key = k_ref[block:after, :]
        value = v_ref[block:after, :]
        grad_k, grad_v = [], []
        for head in range(2):
            scores = dot_cols(keep_head(key, head), query[block:, :])
            scores = jnp.minimum(scores, bias[block:after, block:])
            weights = jnp.exp(scores - lse_ref[head : head + 1, block:])
            grad_w = dot_cols(keep_head(value, head), grad[block:, :])
            grad_s = (weights * (grad_w - inner[head : head + 1, block:])).astype(low)
            grad_v.append(dot_rows(weights.astype(low), grad[block:, :]))
            grad_k.append(dot_rows(grad_s, query[block:, :]))
            rows = slice(head * HEAD_DIM, (head + 1) * HEAD_DIM)
            moved = dot_rows(key_t[rows, block:after], grad_s)
            if block == 0:
                grad_q_t[rows, :] = moved
            else:
                grad_q_t[rows, block:] += moved
        first = in_head((BLOCK, LANES), 0, 1)
        out_ref[1, block:after, :] = jnp.where(first, grad_k[0], grad_k[1]).astype(low)
        out_ref[2, block:after, :] = jnp.where(first, grad_v[0], grad_v[1]).astype(low)
    out_ref[0] = (grad_q_t[...] * scale_qk).T.astype(low)


def attend_back(packed, grad_mixed, mixed, lse, doc_col, doc_row, first, pairs_here):
    count, wide = packed.shape
    width = wide // 3
    pairs = width // LANES

    def part(which):
        return pl.BlockSpec((SEQ, LANES), lambda r, p, w=which: (r, w * pairs + first + p))

    same = pl.BlockSpec((SEQ, LANES), lambda r, p: (r, first + p))
    return pl.pallas_call(
        attend_back_kernel,
        grid=(count // SEQ, pairs_here),
        in_specs=[
            part(0),
            part(1),
            part(2),
            same,
            same,
            pl.BlockSpec((8, SEQ), lambda r, p: (first + p, r)),
            pl.BlockSpec((SEQ, 1), lambda r, p: (r, 0)),
            pl.BlockSpec((1, SEQ), lambda r, p: (0, r)),
        ],
        out_specs=pl.BlockSpec((3, SEQ, LANES), lambda r, p: (0, r, p)),
        out_shape=jax.ShapeDtypeStruct((3, count, pairs_here * LANES), low),
        scratch_shapes=[pltpu.VMEM((SEQ, SEQ), f32), pltpu.VMEM((LANES, SEQ), f32)],
        compiler_params=pltpu.CompilerParams(vmem_limit_bytes=48 * 2**20),
        cost_estimate=pl.CostEstimate(
            flops=10 * count * SEQ * pairs_here * LANES,
            bytes_accessed=16 * count * pairs_here * LANES,
            transcendentals=0,
        ),
        name="attend_back",
    )(packed, packed, packed, grad_mixed, mixed, lse, doc_col, doc_row)


def gelu_and_slope(x):
    point = 1.0 / (1.0 + (erfc_point * math.sqrt(0.5)) * jnp.abs(x))
    bell = jnp.exp(-0.5 * x * x)
    tail = erfc_terms[-1]
    for term in erfc_terms[-2::-1]:
        tail = tail * point + term
    tail = tail * point * bell
    below = jnp.where(x >= 0.0, 1.0 - tail, tail)
    return x * below, below + x * bell * (1.0 / math.sqrt(2.0 * math.pi))


def expert_kernel(x_ref, in_ref, out_ref, hidden_ref, slope_ref, result_ref, total):
    step = pl.program_id(0)

    @pl.when(step == 0)
    def _():
        total[...] = jnp.zeros_like(total)

    for row in range(0, x_ref.shape[0], BLOCK):
        rows = slice(row, row + BLOCK)
        preact = dot_rows(x_ref[rows, :], in_ref[...])
        value, slope = gelu_and_slope(preact)
        hidden = value.astype(low)
        hidden_ref[rows, :] = hidden
        slope_ref[rows, :] = slope.astype(low)
        total[rows, :] += dot_rows(hidden, out_ref[...])

    @pl.when(step == pl.num_programs(0) - 1)
    def _():
        result_ref[...] = total[...].astype(low)


def expert_forward(arrived, weight_in, weight_out, tile=512):
    slots, width = arrived.shape
    inner = weight_in.shape[1]
    whole = pl.BlockSpec((slots, width), lambda j: (0, 0))
    strip = pl.BlockSpec((slots, tile), lambda j: (0, j))
    return pl.pallas_call(
        expert_kernel,
        grid=(inner // tile,),
        in_specs=[
            whole,
            pl.BlockSpec((width, tile), lambda j: (0, j)),
            pl.BlockSpec((tile, width), lambda j: (j, 0)),
        ],
        out_specs=[strip, strip, whole],
        out_shape=[
            jax.ShapeDtypeStruct((slots, inner), low),
            jax.ShapeDtypeStruct((slots, inner), low),
            jax.ShapeDtypeStruct((slots, width), low),
        ],
        scratch_shapes=[pltpu.VMEM((slots, width), f32)],
        compiler_params=pltpu.CompilerParams(vmem_limit_bytes=56 * 2**20),
        cost_estimate=pl.CostEstimate(
            flops=4 * slots * width * inner,
            bytes_accessed=4 * (slots + width) * inner,
            transcendentals=0,
        ),
        name="expert_forward",
    )(arrived, weight_in, weight_out)


def expert_back_kernel(
    grad_ref,
    slope_ref,
    in_ref,
    out_ref,
    x_ref,
    result_ref,
    centre_ref,
    grad_preact_ref,
    grad_rows_ref,
    grad_centre_ref,
    total,
):
    step = pl.program_id(0)

    @pl.when(step == 0)
    def _():
        total[...] = jnp.zeros_like(total)

    for row in range(0, grad_ref.shape[0], BLOCK):
        rows = slice(row, row + BLOCK)
        grad_hidden = dot_cols(grad_ref[rows, :], out_ref[...])
        grad_preact = (grad_hidden * slope_ref[rows, :].astype(f32)).astype(low)
        grad_preact_ref[rows, :] = grad_preact
        total[rows, :] += dot_cols(grad_preact, in_ref[...])

    @pl.when(step == pl.num_programs(0) - 1)
    def _():
        centre = centre_ref[...].astype(f32)
        grad_centre = jnp.zeros(grad_centre_ref.shape, f32)
        for row in range(0, grad_ref.shape[0], BLOCK):
            rows = slice(row, row + BLOCK)
            x = x_ref[rows, :].astype(f32)
            gate = jax.nn.sigmoid(jnp.sum(x * centre, axis=-1, keepdims=True))
            moved = grad_ref[rows, :].astype(f32) * result_ref[rows, :].astype(f32)
            grad_logit = jnp.sum(moved, axis=-1, keepdims=True) * (1.0 - gate)
            grad_rows_ref[rows, :] = (total[rows, :] + grad_logit * centre).astype(low)
            by_slot = (grad_logit * x).reshape(-1, 8, x.shape[1])
            grad_centre = grad_centre + jnp.sum(by_slot, axis=0)
        grad_centre_ref[...] = grad_centre


def expert_back(grad_arrived, slope, weight_in, weight_out, arrived, result, centre, tile=512):
    slots, width = arrived.shape
    inner = weight_in.shape[1]
    whole = pl.BlockSpec((slots, width), lambda j: (0, 0))
    strip = pl.BlockSpec((slots, tile), lambda j: (0, j))
    return pl.pallas_call(
        expert_back_kernel,
        grid=(inner // tile,),
        in_specs=[
            whole,
            strip,
            pl.BlockSpec((width, tile), lambda j: (0, j)),
            pl.BlockSpec((tile, width), lambda j: (j, 0)),
            whole,
            whole,
            pl.BlockSpec((1, width), lambda j: (0, 0)),
        ],
        out_specs=[strip, whole, pl.BlockSpec((8, width), lambda j: (0, 0))],
        out_shape=[
            jax.ShapeDtypeStruct((slots, inner), low),
            jax.ShapeDtypeStruct((slots, width), low),
            jax.ShapeDtypeStruct((8, width), f32),
        ],
        scratch_shapes=[pltpu.VMEM((slots, width), f32)],
        compiler_params=pltpu.CompilerParams(vmem_limit_bytes=56 * 2**20),
        cost_estimate=pl.CostEstimate(
            flops=4 * slots * width * inner,
            bytes_accessed=4 * (slots + width) * inner,
            transcendentals=0,
        ),
        name="expert_back",
    )(grad_arrived, slope, weight_in, weight_out, arrived, result, centre)


def swap(values, axis, distance):
    size = lax.axis_size(axis)
    return lax.ppermute(values, axis, [(i, i ^ distance) for i in range(size)])


def scatter_over_dp(values):
    me = lax.axis_index("dp")
    distance = 1
    held = values
    while distance < lax.axis_size("dp"):
        bit = (me // distance) % 2
        pairs = held.reshape((held.shape[0] // 2, 2) + held.shape[1:])
        mine = lax.dynamic_index_in_dim(pairs, bit, 1, keepdims=False)
        theirs = lax.dynamic_index_in_dim(pairs, 1 - bit, 1, keepdims=False)
        held = (mine.astype(f32) + swap(theirs, "dp", distance).astype(f32)).astype(low)
        distance *= 2
    return held[0]


def sum_everywhere(value):
    held = value.reshape(1, 1)
    for axis in ("dp", "expert"):
        distance = 1
        while distance < lax.axis_size(axis):
            held = held + swap(held, axis, distance)
            distance *= 2
    return held[0, 0]


def update(weight, moment, average, gradient, factor, rate):
    clipped = gradient * factor
    moment_new = momentum_rate * moment + clipped
    weight_new = weight - rate * (clipped + momentum_rate * moment_new)
    average_new = average_rate * average + (1.0 - average_rate) * weight_new
    return (weight_new, moment_new, average_new)


def shards(
    tokens,
    documents,
    routes,
    out_grad,
    norm_params,
    qkv_weight,
    proj_weight,
    centroids,
    expert_in,
    expert_out,
    norm_moment,
    qkv_moment,
    proj_moment,
    centroid_moment,
    in_moment,
    out_moment,
    norm_average,
    qkv_average,
    proj_average,
    centroid_average,
    in_average,
    out_average,
):
    local_tokens, width = tokens.shape
    experts = lax.axis_size("expert")
    dp = lax.axis_size("dp")
    devices = experts * dp
    slot_cap = max(2, 3 * local_tokens // (2 * experts))
    slots = experts * slot_cap
    rows_own = qkv_weight.shape[0]
    norm_own = norm_params.shape[1]
    centre_own = centroids.shape[1]

    small = jnp.concatenate([norm_params.reshape(-1), centroids.reshape(-1)]).astype(low)
    small = jnp.pad(small, (0, rows_own * LANES - small.shape[0])).reshape(rows_own, LANES)
    dense = jnp.concatenate([qkv_weight.astype(low), proj_weight.astype(low), small], axis=1)
    dense = lax.all_gather(dense, everywhere, axis=0, tiled=True)
    weight_in = lax.all_gather(expert_in.astype(low), "dp", axis=1, tiled=True)[0]
    weight_out = lax.all_gather(expert_out.astype(low), "dp", axis=2, tiled=True)[0]

    route_ids = routes[:, 0]
    onehot = route_ids[:, None] == jnp.arange(experts, dtype=jnp.int32)[None, :]
    running = jnp.cumsum(onehot.astype(jnp.int32), axis=0)
    within = jnp.sum(running * onehot.astype(jnp.int32), axis=1) - 1
    slot_index = route_ids * slot_cap + within

    qkv_full = dense[:, : 3 * width]
    proj_full = dense[:, 3 * width : 4 * width]
    small_full = dense[:, 4 * width :].reshape(devices, rows_own * LANES)
    norm_values = (
        small_full[:, : 4 * norm_own].reshape(devices, 4, norm_own).transpose(1, 0, 2)
    ).reshape(4, width).astype(f32)
    centre_table = small_full[:, 4 * norm_own : 4 * norm_own + centre_own].reshape(experts, width)

    x_in = tokens.astype(f32)
    normed_one, norm_back_one = jax.vjp(layer_norm, x_in, norm_values[0], norm_values[1])
    normed_low = normed_one.astype(low)
    packed = jnp.dot(normed_low, qkv_full, preferred_element_type=f32).astype(low)
    doc_col = documents[:, None]
    doc_row = documents[None, :]
    mixed_low, lse = attend(packed, doc_col, doc_row)
    attended = jnp.dot(mixed_low, proj_full, preferred_element_type=f32)
    after_attn = x_in + attended
    normed_two, norm_back_two = jax.vjp(layer_norm, after_attn, norm_values[2], norm_values[3])
    sent_low = normed_two.astype(low)
    picked_centre = jnp.dot(onehot.astype(low), centre_table, preferred_element_type=f32)
    logits = jnp.sum(sent_low.astype(f32) * picked_centre, axis=-1)
    gate_value = jax.nn.sigmoid(logits)
    grad_out = out_grad.astype(f32)
    grad_rows = (gate_value[:, None] * grad_out).astype(low)

    place = jnp.arange(slots, dtype=jnp.int32)[:, None] == slot_index[None, :]
    place = place.astype(low)

    def dispatch(rows):
        out = jnp.dot(place, rows, preferred_element_type=f32).astype(low)
        out = out.reshape(experts, slot_cap, width)
        out = lax.all_to_all(out, "expert", split_axis=0, concat_axis=0, tiled=True)
        return out.reshape(slots, width)

    def send_back(rows):
        rows = rows.reshape(experts, slot_cap, width)
        rows = lax.all_to_all(rows, "expert", split_axis=0, concat_axis=0, tiled=True)
        return rows.reshape(slots, width)

    def collect(rows):
        return lax.dot_general(
            place, rows, (((0,), (0,)), ((), ())), preferred_element_type=f32
        )

    arrived = dispatch(sent_low)
    grad_arrived = dispatch(grad_rows)
    hidden, slope, result = expert_forward(arrived, weight_in, weight_out)
    grad_weight_out = lax.dot_general(
        hidden, grad_arrived, (((0,), (0,)), ((), ())), preferred_element_type=f32
    ).astype(low)
    centre_own_row = lax.dynamic_slice_in_dim(centre_table, lax.axis_index("expert"), 1, 0)
    grad_preact, grad_input_rows, grad_centre = expert_back(
        grad_arrived, slope, weight_in, weight_out, arrived, result, centre_own_row
    )
    out_grad_w = lax.psum_scatter(
        grad_weight_out[None], "dp", scatter_dimension=2, tiled=True
    ).astype(f32)
    grad_back = send_back(grad_input_rows)
    grad_weight_in = lax.dot_general(
        arrived, grad_preact, (((0,), (0,)), ((), ())), preferred_element_type=f32
    ).astype(low)
    in_grad = lax.psum_scatter(
        grad_weight_in[None], "dp", scatter_dimension=1, tiled=True
    ).astype(f32)
    returned = send_back(result)

    grad_normed_two = collect(grad_back)
    grad_after, grad_gain_two, grad_bias_two = norm_back_two(grad_normed_two)
    grad_after = grad_after + grad_out
    grad_attended = grad_after.astype(low)
    grad_mixed = dot_cols(grad_attended, proj_full).astype(low)
    grad_proj = lax.dot_general(
        mixed_low, grad_attended, (((0,), (0,)), ((), ())), preferred_element_type=f32
    ).astype(low)

    pairs = width // LANES
    groups = 2
    each = pairs // groups
    grad_parts, grad_qkv = [], []
    grad_normed_one = jnp.zeros((local_tokens, width), f32)
    for group in range(groups):
        part = attend_back(
            packed, grad_mixed, mixed_low, lse, doc_col, doc_row, group * each, each
        )
        wide = each * LANES
        columns = [
            qkv_full[:, s * width + group * wide : s * width + (group + 1) * wide]
            for s in range(3)
        ]
        flat = jnp.concatenate([part[0], part[1], part[2]], axis=1)
        grad_parts.append(flat)
        grad_qkv.append(
            lax.dot_general(
                normed_low, flat, (((0,), (0,)), ((), ())), preferred_element_type=f32
            ).astype(low)
        )
        grad_normed_one = grad_normed_one + dot_cols(flat, jnp.concatenate(columns, axis=1))
    grad_x_norm, grad_gain_one, grad_bias_one = norm_back_one(grad_normed_one)
    input_grad = grad_after + grad_x_norm
    activations = (after_attn + gate_value[:, None] * collect(returned)).astype(low)

    def to_owners(values):
        columns = values.shape[1]
        held = values.reshape(experts, dp, rows_own, columns).transpose(1, 0, 2, 3)
        held = scatter_over_dp(held)
        held = lax.all_to_all(held, "expert", split_axis=0, concat_axis=0, tiled=True)
        return jnp.sum(held.astype(f32), axis=0)

    grad_norm_rows = jnp.stack([grad_gain_one, grad_bias_one, grad_gain_two, grad_bias_two])
    norm_flat = grad_norm_rows.reshape(4, devices, norm_own).transpose(1, 0, 2)
    norm_flat = norm_flat.reshape(devices, 4 * norm_own).astype(low)
    norm_flat = jnp.pad(norm_flat, ((0, 0), (0, rows_own * LANES - 4 * norm_own)))
    norm_flat = norm_flat.reshape(devices * rows_own, LANES)
    first_part = to_owners(jnp.concatenate([grad_proj, grad_qkv[0]], axis=1))
    second_part = to_owners(jnp.concatenate([grad_qkv[1], norm_flat], axis=1))
    proj_grad = first_part[:, :width]
    halves = [first_part[:, width:], second_part[:, : 3 * width // 2]]
    wide = each * LANES
    qkv_grad = jnp.concatenate(
        [half[:, s * wide : (s + 1) * wide] for s in range(3) for half in halves], axis=1
    )
    norm_grad = second_part[:, 3 * width // 2 :].reshape(-1)[: 4 * norm_own].reshape(4, norm_own)
    centre_sum = jnp.sum(grad_centre, axis=0).reshape(dp, centre_own)
    centre_grad = lax.psum_scatter(centre_sum, "dp", scatter_dimension=0, tiled=True)
    square_sum = (
        jnp.sum(qkv_grad * qkv_grad)
        + jnp.sum(proj_grad * proj_grad)
        + jnp.sum(norm_grad * norm_grad)
        + jnp.sum(centre_grad * centre_grad)
        + jnp.sum(in_grad * in_grad)
        + jnp.sum(out_grad_w * out_grad_w)
    )
    grad_norm = jnp.sqrt(sum_everywhere(square_sum))
    factor = clip_limit / jnp.maximum(grad_norm, clip_limit)
    norm_new = update(norm_params, norm_moment, norm_average, norm_grad, factor, norm_rate)
    qkv_new = update(qkv_weight, qkv_moment, qkv_average, qkv_grad, factor, learn_rate)
    proj_new = update(proj_weight, proj_moment, proj_average, proj_grad, factor, learn_rate)
    centre_new = update(
        centroids, centroid_moment, centroid_average, centre_grad, factor, learn_rate
    )
    in_new = update(expert_in, in_moment, in_average, in_grad, factor, learn_rate)
    out_new = update(expert_out, out_moment, out_average, out_grad_w, factor, learn_rate)
    return (
        activations,
        input_grad,
        grad_norm,
        norm_new[0],
        qkv_new[0],
        proj_new[0],
        centre_new[0],
        in_new[0],
        out_new[0],
        norm_new[1],
        qkv_new[1],
        proj_new[1],
        centre_new[1],
        in_new[1],
        out_new[1],
        norm_new[2],
        qkv_new[2],
        proj_new[2],
        centre_new[2],
        in_new[2],
        out_new[2],
    )


def solution(mesh):
    placed = (
        P(("expert", "dp"), None),
        P(("expert", "dp")),
        P(("expert", "dp"), None),
        P(("expert", "dp"), None),
        P(None, ("expert", "dp")),
        P(("expert", "dp"), None),
        P(("expert", "dp"), None),
        P("expert", "dp"),
        P("expert", "dp", None),
        P("expert", None, "dp"),
        P(None, ("expert", "dp")),
        P(("expert", "dp"), None),
        P(("expert", "dp"), None),
        P("expert", "dp"),
        P("expert", "dp", None),
        P("expert", None, "dp"),
        P(None, ("expert", "dp")),
        P(("expert", "dp"), None),
        P(("expert", "dp"), None),
        P("expert", "dp"),
        P("expert", "dp", None),
        P("expert", None, "dp"),
    )
    return jax.shard_map(
        shards,
        mesh=mesh,
        in_specs=placed,
        out_specs=(
            P(("expert", "dp"), None),
            P(("expert", "dp"), None),
            P(),
            P(None, ("expert", "dp")),
            P(("expert", "dp"), None),
            P(("expert", "dp"), None),
            P("expert", "dp"),
            P("expert", "dp", None),
            P("expert", None, "dp"),
            P(None, ("expert", "dp")),
            P(("expert", "dp"), None),
            P(("expert", "dp"), None),
            P("expert", "dp"),
            P("expert", "dp", None),
            P("expert", None, "dp"),
            P(None, ("expert", "dp")),
            P(("expert", "dp"), None),
            P(("expert", "dp"), None),
            P("expert", "dp"),
            P("expert", "dp", None),
            P("expert", None, "dp"),
        ),
        check_vma=False,
    )
```

time: 1680 us -> 721 us (0.43)
  waiting for transfers between devices: 662 us -> 222 us
  matrix products: 404 us -> 110 us
  blocking collectives: 233 us -> 5.98 us
  Pallas kernels: 0 us -> 165 us
  other arithmetic: 233 us -> 81.4 us
  local copies, waits for them, and re-layouts: 109 us -> 57 us
  starting transfers between devices: 11.5 us -> 47.7 us
    reduce_scatter x4 -> x2, waiting for transfers between devices: 438 us -> 0.04 us  [the longest x1 0.02 us: shards(): lax.psum_scatter(grad_weight_in[None], 'dp', scatter_dimension=1, tiled=T...]
    dot_general x42 -> x15, matrix products: 404 us -> 110 us  [the longest x1 20.6 us: shards(): lax.dot_general(hidden, grad_arrived, (((0,), (0,)), ((), ())), preferred...]
    pallas_call x0 -> x5, Pallas kernels: none -> 165 us  [the longest x1 56 us: expert_forward(): pl.pallas_call(expert_kernel, grid=(inner // tile,), in_specs=[whole, pl....]
    convert_element_type x13 -> x10, other arithmetic: 140 us -> 16.7 us  [the longest x2 5.65 us: scatter_over_dp(): (mine.astype(f32) + swap(theirs, 'dp', distance).astype(f32)).astype(low)]
    all_to_all x3 -> x6, waiting for transfers between devices: 205 us -> 118 us  [the longest x2 74.5 us: dispatch(): out = lax.all_to_all(out, 'expert', split_axis=0, concat_axis=0, tiled=True)]
    all_gather x2 -> x0, blocking collectives: 80.2 us -> none  [the longest x1 43.4 us: shards(): lax.all_gather(norm_params.astype(jnp.bfloat16), ('expert', 'dp'), axis=1...]
    all_to_all x1 -> x0, blocking collectives: 74.5 us -> none  [shards(): lax.all_to_all(grad_outgoing, 'expert', split_axis=0, concat_axis=0, tile...]
    all_gather x4 -> x3, waiting for transfers between devices: 0.04 us -> 66.1 us  [the longest x1 66.1 us: shards(): dense = lax.all_gather(dense, everywhere, axis=0, tiled=True)]
  transfers between devices with their start and end apart: 12 -> 20, of which waited for: 8 -> 12; matrix products, arithmetic and copies ran while one was open for 19% -> 25% of each run, Pallas kernels for 0% -> 17%
where the time goes in v1:
time: 721 us; the launch traced here: 713 us
  waiting for transfers between devices  222 us (31%)
  Pallas kernels  165 us (23%)
  matrix products  110 us (15%)
  other arithmetic  81.4 us (11%)
  local copies, waits for them, and re-layouts  57 us (8%)
  starting transfers between devices  47.7 us (7%)
  between operations  23.8 us (3%)
    all_to_all x2, waiting for transfers between devices, dispatch(): out = lax.all_to_all(out, 'expert', split_axis=0, concat_axis=0, tiled=True)  74.5 us
    all_gather x1, waiting for transfers between devices, shards(): dense = lax.all_gather(dense, everywhere, axis=0, tiled=True)  66.1 us
    pallas_call x1, Pallas kernels, expert_forward(): pl.pallas_call(expert_kernel, grid=(inner // tile,), in_specs=[whole, pl....  56 us
    all_to_all x2, waiting for transfers between devices, send_back(): lax.all_to_all(rows, 'expert', split_axis=0, concat_axis=0, tiled=True)  43.1 us
    pallas_call x1, Pallas kernels, expert_back(): pl.pallas_call(expert_back_kernel, grid=(inner // tile,), in_specs=[whole...  42.8 us
    ppermute x9, waiting for transfers between devices, swap(): return lax.ppermute(values, axis, [(i, i ^ distance) for i in range(size)])  37.8 us
    pallas_call x2, Pallas kernels, attend_back(): pl.pallas_call(attend_back_kernel, grid=(count // SEQ, pairs_here), in_sp...  37.1 us
    unnamed x148, local copies, waits for them, and re-layouts  32.4 us
  transfers between devices with their start and end apart: 20, of which 12 were waited for; matrix products, arithmetic and copies ran while one was open for 25% of the time, Pallas kernels for 17%

profile of v1, /device:TPU:0, one launch (start us, length us, event | category | flops | bytes accessed | tf_op | source)
XLA Modules:
  0.0 712.6 jit_solution(13230286248188098562)
XLA Ops:
  26.7 66.1 %all-gather.4.cloned.1.call-done = bf16[1024,4224]{1,0:T(8,128)(2,1)} async-done(((bf16[32,4224]{1,0:T(8,128)(2,1)}), bf16[1024,4224]{1,0:T(8,128)(2,1)}) %all-gather.4.cloned.1.call-update) | async-done | bytes 8650768 | tf_op jit(solution)/shard_map/all_gather | solution.py:419
  94.4 12.0 %fusion.10.q_ref.k_ref.v_ref = bf16[1024,3072]{1,0:T(8,128)(2,1)} fusion(bf16[1024,4224]{1,0:T(8,128)(2,1)} %all-gather.4.cloned.1.call-done, bf16[1024,1024]{0,1:T(8,128)(2,1)S(1)} %copy.80, f32[1024]{0:T(1024)S(1)} %add.217, f32[1024]{0:T(1024)S(1)} %mul.327, f32[1024]{0:T(1024)S(1)} %fusion.70, f32[1024]{0:T(1024)S(1)} %broadcast_multiply_fusion.1), kind=kOutput, calls=%fused_computation.18 | convolution fusion | flops 6451888128 | bytes 14696448 | tf_op jit(solution)/shard_map/dot_general | solution.py:440
  106.4 29.4 %attend.1 = (bf16[1024,1024]{1,0:T(8,128)(2,1)S(1)}, f32[64,1024]{1,0:T(8,128)S(1)}) custom-call(bf16[1024,3072]{1,0:T(8,128)(2,1)} %fusion.10.q_ref.k_ref.v_ref, bf16[1024,3072]{1,0:T(8,128)(2,1)} %fusion.10.q_ref.k_ref.v_ref, bf16[1024,3072]{1,0:T(8,128)(2,1)} %fusion.10.q_ref.k_ref.v_ref, s32[1024,1]{1,0:T(8,128)S(1)} %copy.81.doc_col, s32[1,1024]{1,0:T(1,128)S(1)} %bitcast.93), custom_call_target="tpu_custom_call" | custom-call | flops 4294967296 | bytes 8388608 | tf_op jit(solution)/shard_map/attend/pallas_call | solution.py:102
  135.9 4.8 fusion.85
  142.7 4.8 fusion.32
  158.0 4.8 fusion.33
  162.8 60.6 %all-to-all-done = bf16[8,192,1024]{2,1,0:T(8,128)(2,1)} async-done(((bf16[8,192,1024]{2,1,0:T(8,128)(2,1)}), bf16[8,192,1024]{2,1,0:T(8,128)(2,1)}, u32[]{:S(2)}, u32[]{:S(2)}) %all-to-all-start) | async-done | bytes 3145760 | tf_op jit(solution)/shard_map/all_to_all | solution.py:460
  228.5 56.0 %expert_forward.1 = (bf16[1536,4096]{1,0:T(8,128)(2,1)}, bf16[1536,4096]{1,0:T(8,128)(2,1)}, bf16[1536,1024]{1,0:T(8,128)(2,1)}) custom-call(bf16[1536,1024]{1,0:T(8,128)(2,1)} %bitcast.8.x_ref, bf16[1024,4096]{1,0:T(8,128)(2,1)} %bitcast.113, bf16[4096,1024]{1,0:T(8,128)(2,1)} %bitcast.111), custom_call_target="tpu_custom_call" | custom-call | flops 25769803776 | bytes 41943040 | tf_op jit(solution)/shard_map/expert_forward/pallas_call | solution.py:244
  284.6 13.9 %all-to-all-done.2 = bf16[8,192,1024]{2,1,0:T(8,128)(2,1)} async-done(((bf16[8,192,1024]{2,1,0:T(8,128)(2,1)}), bf16[8,192,1024]{2,1,0:T(8,128)(2,1)}, u32[]{:S(2)}, u32[]{:S(2)}) %all-to-all-start.2) | async-done | bytes 3145760 | tf_op jit(solution)/shard_map/all_to_all | solution.py:460
  298.5 42.8 %expert_back.1 = (bf16[1536,4096]{1,0:T(8,128)(2,1)}, bf16[1536,1024]{1,0:T(8,128)(2,1)}, f32[8,1024]{1,0:T(8,128)}) custom-call(bf16[1536,1024]{1,0:T(8,128)(2,1)} %bitcast.14.grad_ref, bf16[1536,4096]{1,0:T(8,128)(2,1)} %get-tuple-element.31.slope_ref, bf16[1024,4096]{1,0:T(8,128)(2,1)} %bitcast.114, bf16[4096,1024]{1,0:T(8,128)(2,1)} %bitcast.112, ...), custom_call_target="tpu_custom_call" | custom-call | flops 25769803776 | bytes 41943040 | tf_op jit(solution)/shard_map/expert_back/pallas_call | solution.py:316
  341.2 19.6 %convert_bitcast_fusion.1 = bf16[1,1024,4096]{2,1,0:T(8,128)(2,1)} fusion(bf16[1536,1024]{1,0:T(8,128)(2,1)} %bitcast.8.x_ref, bf16[1536,4096]{1,0:T(8,128)(2,1)} %get-tuple-element.35), kind=kOutput, calls=%fused_computation.1 | convolution fusion | flops 12889096192 | bytes 24117248 | tf_op jit(solution)/shard_map/dot_general | solution.py:487
  365.4 6.4 fusion.84
  371.8 20.6 %convert_bitcast_fusion = bf16[1,4096,1024]{2,1,0:T(8,128)(2,1)} fusion(bf16[1536,4096]{1,0:T(8,128)(2,1)} %get-tuple-element.36, bf16[1536,1024]{1,0:T(8,128)(2,1)} %bitcast.14.grad_ref), kind=kOutput, calls=%fused_computation | convolution fusion | flops 12889096192 | bytes 24117248 | tf_op jit(solution)/shard_map/dot_general | solution.py:476
  392.4 43.1 %all-to-all-done.3 = bf16[8,192,1024]{2,1,0:T(8,128)(2,1)} async-done(((bf16[8,192,1024]{2,1,0:T(8,128)(2,1)}), bf16[8,192,1024]{2,1,0:T(8,128)(2,1)}, u32[]{:S(2)}, u32[]{:S(2)}) %all-to-all-start.3) | async-done | bytes 3145760 | tf_op jit(solution)/shard_map/all_to_all | solution.py:465
  435.5 4.9 all-to-all-start.1
  440.3 7.0 fusion.86
  447.4 5.8 copy.84
  453.2 4.8 multiply_reduce_fusion
  467.7 18.4 %attend_back.3 = bf16[3,1024,512]{2,1,0:T(8,128)(2,1)} custom-call(bf16[1024,3072]{1,0:T(8,128)(2,1)} %fusion.10.q_ref.k_ref.v_ref, bf16[1024,3072]{1,0:T(8,128)(2,1)} %fusion.10.q_ref.k_ref.v_ref, bf16[1024,3072]{1,0:T(8,128)(2,1)} %fusion.10.q_ref.k_ref.v_ref, bf16[1024,1024]{1,0:T(8,128)(2,1)S(1)} %convolution_convert_fusion.3.grad_ref, ...), custom_call_target="tpu_custom_call" | custom-call | flops 5368709120 | bytes 8388608 | tf_op jit(solution)/shard_map/attend_back/pallas_call | solution.py:181
  486.1 18.7 %attend_back.2 = bf16[3,1024,512]{2,1,0:T(8,128)(2,1)} custom-call(bf16[1024,3072]{1,0:T(8,128)(2,1)} %fusion.10.q_ref.k_ref.v_ref, bf16[1024,3072]{1,0:T(8,128)(2,1)} %fusion.10.q_ref.k_ref.v_ref, bf16[1024,3072]{1,0:T(8,128)(2,1)} %fusion.10.q_ref.k_ref.v_ref, bf16[1024,1024]{1,0:T(8,128)(2,1)S(1)} %convolution_convert_fusion.3.grad_ref, ...), custom_call_target="tpu_custom_call" | custom-call | flops 5368709120 | bytes 8388608 | tf_op jit(solution)/shard_map/attend_back/pallas_call | solution.py:181
  521.3 5.2 convolution_convert_fusion.2
  530.9 5.2 convolution_convert_fusion.1
  562.2 13.6 %collective-permute-done.3 = bf16[1,8,32,1664]{3,2,0,1:T(8,128)(2,1)} collective-permute-done((bf16[1,8,32,1664]{3,2,0,1:T(8,128)(2,1)S(1)}, bf16[1,8,32,1664]{3,2,0,1:T(8,128)(2,1)}, u32[]{:S(2)}, u32[]{:S(2)}) %collective-permute-start.3) | collective-permute-done | bytes 852000 | tf_op jit(solution)/shard_map/ppermute | solution.py:347
  578.4 6.2 all-to-all-start.5
  584.6 18.6 %collective-permute-done.1 = bf16[1,8,32,2560]{3,2,0,1:T(8,128)(2,1)} collective-permute-done((bf16[1,8,32,2560]{3,2,0,1:T(8,128)(2,1)}, bf16[1,8,32,2560]{3,2,0,1:T(8,128)(2,1)}, u32[]{:S(2)}, u32[]{:S(2)}) %collective-permute-start.1) | collective-permute-done | bytes 1310752 | tf_op jit(solution)/shard_map/ppermute | solution.py:347
  607.2 6.0 all-to-all-start.4
  613.8 6.0 all-reduce.2
  621.0 6.7 add_add_fusion.2
  627.8 5.3 copy.93
  633.1 7.3 %add_convert_fusion = bf16[1024,1024]{0,1:T(8,128)(2,1)} fusion(f32[1024,1024]{0,1:T(8,128)} %copy-done.6, f32[1024]{0:T(1024)S(1)} %copy-done.61, bf16[1536,1024]{1,0:T(8,128)(2,1)} %bitcast.12, s32[1024]{0:T(1024)S(1)} %add_add_fusion.3), kind=kOutput, calls=%fused_computation.51 | convolution fusion | flops 3225944064 | bytes 9445376 | tf_op jit(solution)/shard_map/dot_general | solution.py:469
  682.0 11.2 %multiply_add_fusion = (f32[1,4096,256]{2,1,0:T(8,128)}, f32[1,4096,256]{2,1,0:T(8,128)}, f32[1,4096,256]{2,1,0:T(8,128)}) fusion(f32[1,4096,256]{2,1,0:T(8,128)} %param.43, f32[1,4096,256]{2,1,0:T(8,128)} %param.31, f32[]{:T(128)S(6)} %div.71, bf16[1,4096,256]{2,1,0:T(8,128)(2,1)} %reduce-scatter.5.cloned.1.call-done, f32[1,4096,256]{2,1,0:T(8,128)} %param.37), kind=kLoop, calls=%fused_computation.46 | loop fusion | flops 11534336 | bytes 27262980 | tf_op jit(solution)/shard_map/add | solution.py:378
  693.2 11.3 %multiply_add_fusion.1 = (f32[1,256,4096]{2,1,0:T(8,128)}, f32[1,256,4096]{2,1,0:T(8,128)}, f32[1,256,4096]{2,1,0:T(8,128)}) fusion(f32[1,256,4096]{2,1,0:T(8,128)} %param.42, f32[1,256,4096]{2,1,0:T(8,128)} %param.30, f32[]{:T(128)S(6)} %div.71, bf16[1,256,4096]{2,1,0:T(8,128)(2,1)S(1)} %copy-done.20, f32[1,256,4096]{2,1,0:T(8,128)} %param.36), kind=kLoop, calls=%fused_computation.47 | loop fusion | flops 11534336 | bytes 27262980 | tf_op jit(solution)/shard_map/add | solution.py:378
  (270 shorter events, 141.7 us)
Async XLA Ops:
  7.2 85.5 %all-gather.4.cloned.1.call-start = ((), (), s32[]{:S(2)}) async-start(), calls=%async_computation.8 | async-start | bytes 8921088 | tf_op jit(solution)/shard_map/all_gather | solution.py:419
  11.4 217.1 %all-gather.8.cloned.1.call-start = ((), (), s32[]{:S(2)}) async-start(), calls=%async_computation.10 | async-start | bytes 10485760 | tf_op jit(solution)/shard_map/all_gather | solution.py:421
  15.2 213.3 %all-gather.6.cloned.1.call-start = ((), (), s32[]{:S(2)}) async-start(), calls=%async_computation.9 | async-start | bytes 10485760 | tf_op jit(solution)/shard_map/all_gather | solution.py:420
  22.0 113.9 %copy-start.8 = (bf16[1024,1024]{0,1:T(8,128)(2,1)}, bf16[1024,1024]{0,1:T(8,128)(2,1)S(1)}, u32[]{:S(2)}) copy-start(bf16[1024,1024]{0,1:T(8,128)(2,1)S(1)} %copy.80) | copy-start | bytes 6291460
  22.3 84.1 %copy-start.47 = (f32[1024]{0:T(1024)}, f32[1024]{0:T(1024)S(1)}, u32[]{:S(2)}) copy-start(f32[1024]{0:T(1024)S(1)} %broadcast_multiply_fusion.1) | copy-start | bytes 12292
  23.6 82.9 %copy-start.51 = (f32[1024]{0:T(1024)}, f32[1024]{0:T(1024)S(1)}, u32[]{:S(2)}) copy-start(f32[1024]{0:T(1024)S(1)} %fusion.70) | copy-start | bytes 12292
  23.8 82.7 %copy-start.2 = (s32[1024,1]{1,0:T(8,128)}, s32[1024,1]{1,0:T(8,128)S(1)}, u32[]{:S(2)}) copy-start(s32[1024,1]{1,0:T(8,128)S(1)} %copy.81.doc_col) | copy-start | bytes 12292
  147.5 75.9 %all-to-all-start = ((bf16[8,192,1024]{2,1,0:T(8,128)(2,1)}), bf16[8,192,1024]{2,1,0:T(8,128)(2,1)}, u32[]{:S(2)}, u32[]{:S(2)}) async-start(bf16[8,192,1024]{2,1,0:T(8,128)(2,1)} %bitcast.7), calls=%async_computation | async-start | bytes 6291456 | tf_op jit(solution)/shard_map/all_to_all | solution.py:460
  154.9 306.0 %copy-start.14 = (bf16[1024,1024]{0,1:T(8,128)(2,1)}, bf16[1024,1024]{0,1:T(8,128)(2,1)S(1)}, u32[]{:S(2)}) copy-start(bf16[1024,1024]{0,1:T(8,128)(2,1)S(1)} %copy.83) | copy-start | bytes 6291460
  223.4 75.1 %all-to-all-start.2 = ((bf16[8,192,1024]{2,1,0:T(8,128)(2,1)}), bf16[8,192,1024]{2,1,0:T(8,128)(2,1)}, u32[]{:S(2)}, u32[]{:S(2)}) async-start(bf16[8,192,1024]{2,1,0:T(8,128)(2,1)} %bitcast.102), calls=%async_computation.2 | async-start | bytes 6291456 | tf_op jit(solution)/shard_map/all_to_all | solution.py:460
  227.9 421.6 %reduce-scatter.3.cloned.1.call-start = ((), (), s32[]{:S(2)}) async-start(), calls=%async_computation.11 | async-start | bytes 10485760 | tf_op jit(solution)/shard_map/reduce_scatter | solution.py:490
  360.8 74.6 %all-to-all-start.3 = ((bf16[8,192,1024]{2,1,0:T(8,128)(2,1)}), bf16[8,192,1024]{2,1,0:T(8,128)(2,1)}, u32[]{:S(2)}, u32[]{:S(2)}) async-start(bf16[8,192,1024]{2,1,0:T(8,128)(2,1)} %bitcast.101), calls=%async_computation.3 | async-start | bytes 6291456 | tf_op jit(solution)/shard_map/all_to_all | solution.py:465
  365.3 288.1 %reduce-scatter.5.cloned.1.call-start = ((), (), s32[]{:S(2)}) async-start(), calls=%async_computation.12 | async-start | bytes 10485760 | tf_op jit(solution)/shard_map/reduce_scatter | solution.py:483
  435.5 142.9 %all-to-all-start.1 = ((bf16[8,192,1024]{2,1,0:T(8,128)(2,1)}), bf16[8,192,1024]{2,1,0:T(8,128)(2,1)}, u32[]{:S(2)}, u32[]{:S(2)}) async-start(bf16[8,192,1024]{2,1,0:T(8,128)(2,1)} %bitcast.100), calls=%async_computation.1 | async-start | bytes 6291456 | tf_op jit(solution)/shard_map/all_to_all | solution.py:465
  538.2 17.1 %collective-permute-start = (bf16[2,8,32,2560]{3,2,0,1:T(8,128)(2,1)}, bf16[2,8,32,2560]{3,2,0,1:T(8,128)(2,1)}, u32[]{:S(2)}, u32[]{:S(2)}) collective-permute-start(bf16[2,8,32,2560]{3,2,0,1:T(8,128)(2,1)} %dynamic-slice_bitcast_fusion), channel_id=1, source_target_pairs={{0,1},{1,0},{2,3},{3,2},{4,5},{5,4},{6,7},{7,6},{8,9},{9,8},{10,11... | collective-permute-start | bytes 7864328 | tf_op jit(solution)/shard_map/ppermute | solution.py:347
  547.5 3.9 collective-permute-start.2
  553.9 22.0 %collective-permute-start.3 = (bf16[1,8,32,1664]{3,2,0,1:T(8,128)(2,1)S(1)}, bf16[1,8,32,1664]{3,2,0,1:T(8,128)(2,1)}, u32[]{:S(2)}, u32[]{:S(2)}) collective-permute-start(bf16[1,8,32,1664]{3,2,0,1:T(8,128)(2,1)S(1)} %constant_dynamic-slice_fusion), channel_id=1, source_target_pairs={{0,2},{1,3},{2,0},{3,1},{4,6},{5,7},{6,4},{7,5},{8,10},{9,11},{10,... | collective-permute-start | bytes 2555912 | tf_op jit(solution)/shard_map/ppermute | solution.py:347
  561.2 41.9 %collective-permute-start.1 = (bf16[1,8,32,2560]{3,2,0,1:T(8,128)(2,1)}, bf16[1,8,32,2560]{3,2,0,1:T(8,128)(2,1)}, u32[]{:S(2)}, u32[]{:S(2)}) collective-permute-start(bf16[1,8,32,2560]{3,2,0,1:T(8,128)(2,1)} %constant_dynamic-slice_fusion.1), channel_id=1, source_target_pairs={{0,2},{1,3},{2,0},{3,1},{4,6},{5,7},{6,4},{7,5},{8,10},{9,11},{10,... | collective-permute-start | bytes 3932168 | tf_op jit(solution)/shard_map/ppermute | solution.py:347
  578.4 34.8 %copy-start.67 = (u32[32]{0:T(128)S(1)}, u32[32]{0:T(128)}, u32[]{:S(2)}) copy-start(u32[32]{0:T(128)} %constant.150) | copy-start | bytes 388
  578.4 35.4 %copy-start.56 = (f32[8,1024]{1,0:T(8,128)S(1)}, f32[8,1024]{1,0:T(8,128)}, u32[]{:S(2)}) copy-start(f32[8,1024]{1,0:T(8,128)} %get-tuple-element.34) | copy-start | bytes 98308
  578.4 27.9 %all-to-all-start.5 = ((bf16[8,32,1664]{2,1,0:T(8,128)(2,1)}), bf16[8,32,1664]{2,1,0:T(8,128)(2,1)S(1)}, u32[]{:S(2)}, u32[]{:S(2)}) async-start(bf16[8,32,1664]{2,1,0:T(8,128)(2,1)} %fusion.60), calls=%async_computation.5 | async-start | bytes 1703936 | tf_op jit(solution)/shard_map/all_to_all | solution.py:534
  607.2 38.0 %all-to-all-start.4 = ((bf16[8,32,2560]{2,1,0:T(8,128)(2,1)}), bf16[8,32,2560]{2,1,0:T(8,128)(2,1)S(1)}, u32[]{:S(2)}, u32[]{:S(2)}) async-start(bf16[8,32,2560]{2,1,0:T(8,128)(2,1)} %fusion.59), calls=%async_computation.4 | async-start | bytes 2621440 | tf_op jit(solution)/shard_map/all_to_all | solution.py:534
  644.6 34.7 %copy-start.27 = (f32[32,3072]{1,0:T(8,128)S(1)}, f32[32,3072]{1,0:T(8,128)}, u32[]{:S(2)}) copy-start(f32[32,3072]{1,0:T(8,128)} %param.27) | copy-start | bytes 1179652
  644.6 34.7 %copy-start.44 = (f32[32,3072]{1,0:T(8,128)S(1)}, f32[32,3072]{1,0:T(8,128)}, u32[]{:S(2)}) copy-start(f32[32,3072]{1,0:T(8,128)} %param.39) | copy-start | bytes 1179652
  646.1 35.3 %copy-start.57 = (f32[4,32]{1,0:T(4,128)S(1)}, f32[4,32]{1,0:T(4,128)}, u32[]{:S(2)}) copy-start(f32[4,32]{1,0:T(4,128)} %param.26) | copy-start | bytes 1540
  646.1 35.3 %copy-start.62 = (f32[4,32]{1,0:T(4,128)S(1)}, f32[4,32]{1,0:T(4,128)}, u32[]{:S(2)}) copy-start(f32[4,32]{1,0:T(4,128)} %param.38) | copy-start | bytes 1540
  646.1 35.3 %copy-start.63 = (f32[4,32]{1,0:T(4,128)S(1)}, f32[4,32]{1,0:T(4,128)}, u32[]{:S(2)}) copy-start(f32[4,32]{1,0:T(4,128)} %param.32) | copy-start | bytes 1540
  657.3 1.2 collective-permute-start.4
  659.2 3.6 collective-permute-start.5
  663.4 3.6 collective-permute-start.6
  667.7 3.6 collective-permute-start.7
  671.9 4.5 collective-permute-start.8
  (56 other events, 447.6 us)
Sparse Core Ops, SparseCore 0:
  11.5 81.1 all-gather.3
  94.9 58.0 all-gather.7
  155.0 58.2 all-gather.5
  360.9 70.6 reduce-scatter.2
  434.3 71.6 reduce-scatter.4

commit v2 on v1

v2 whole, which is shorter than its diff:
```python
import functools
import math

import jax
import jax.numpy as jnp
from jax import lax
from jax.experimental import pallas as pl
from jax.experimental.pallas import tpu as pltpu
from jax.sharding import PartitionSpec as P

HEAD_DIM = 64
SEQ = 1024
LANES = 128
BLOCK = 256

eps = 1e-05
scale_qk = 0.125
momentum_rate = 0.9
learn_rate = 100.0
norm_rate = 500.0
average_rate = 0.9
clip_limit = 1.0
masked_score = -1000000000.0
everywhere = ("expert", "dp")
low = jnp.bfloat16
f32 = jnp.float32

erfc_point = 0.4
erfc_terms = (
    0.11596270714310389,
    0.08090178846816841,
    0.2341610172367065,
    -0.1854824771652721,
    0.35459055762612957,
    -0.10013360714943426,
)


def dot_rows(left, right):
    return lax.dot_general(left, right, (((1,), (0,)), ((), ())), preferred_element_type=f32)


def dot_cols(left, right):
    return lax.dot_general(left, right, (((1,), (1,)), ((), ())), preferred_element_type=f32)


def layer_norm(values, norm_gain, norm_bias):
    centre = values - jnp.mean(values, axis=-1, keepdims=True)
    spread = jnp.mean(centre * centre, axis=-1, keepdims=True)
    return centre * lax.rsqrt(spread + eps) * norm_gain + norm_bias


def fill_bias(bias, doc_of_rows, doc_of_cols, rows_are_keys):
    for block in range(0, SEQ, BLOCK):
        rows = lax.broadcasted_iota(jnp.int32, (BLOCK, SEQ), 0) + block
        cols = lax.broadcasted_iota(jnp.int32, (BLOCK, SEQ), 1)
        causal = (rows <= cols) if rows_are_keys else (rows >= cols)
        same = doc_of_rows[block : block + BLOCK, :] == doc_of_cols[...]
        bias[block : block + BLOCK, :] = jnp.where(same & causal, 3.0e38, masked_score)


def in_head(shape, head, axis):
    return lax.broadcasted_iota(jnp.int32, shape, axis) // HEAD_DIM == head


def keep_head(values, head):
    return jnp.where(in_head(values.shape, head, 1), values, jnp.zeros_like(values))


def attend_kernel(q_ref, k_ref, v_ref, doc_col, doc_row, mixed_ref, lse_ref, bias):
    @pl.when(pl.program_id(1) == 0)
    def _():
        fill_bias(bias, doc_col, doc_row, False)

    for block in range(0, SEQ, BLOCK):
        seen = block + BLOCK
        query = q_ref[block:seen, :] * jnp.asarray(scale_qk, low)
        outs, stats = [], []
        for head in range(2):
            scores = dot_cols(keep_head(query, head), k_ref[:seen, :])
            scores = jnp.minimum(scores, bias[block:seen, :seen])
            top = jnp.max(scores, axis=-1, keepdims=True)
            exponent = jnp.exp(scores - top)
            total = jnp.sum(exponent, axis=-1, keepdims=True)
            outs.append(dot_rows(exponent.astype(low), v_ref[:seen, :]) / total)
            stats.append(top + jnp.log(total))
        first = in_head((BLOCK, LANES), 0, 1)
        mixed_ref[block:seen, :] = jnp.where(first, outs[0], outs[1]).astype(low)
        lane = lax.broadcasted_iota(jnp.int32, (BLOCK, LANES), 1)
        both = jnp.where(lane == 0, stats[0], stats[1])
        lse_ref[:, block:seen] = both.T[:8, :]


def attend(packed, doc_col, doc_row):
    count, wide = packed.shape
    width = wide // 3
    pairs = width // LANES

    def part(which):
        return pl.BlockSpec((SEQ, LANES), lambda r, p, w=which: (r, w * pairs + p))

    return pl.pallas_call(
        attend_kernel,
        grid=(count // SEQ, pairs),
        in_specs=[
            part(0),
            part(1),
            part(2),
            pl.BlockSpec((SEQ, 1), lambda r, p: (r, 0)),
            pl.BlockSpec((1, SEQ), lambda r, p: (0, r)),
        ],
        out_specs=[
            pl.BlockSpec((SEQ, LANES), lambda r, p: (r, p)),
            pl.BlockSpec((8, SEQ), lambda r, p: (p, r)),
        ],
        out_shape=[
            jax.ShapeDtypeStruct((count, width), low),
            jax.ShapeDtypeStruct((8 * pairs, count), f32),
        ],
        scratch_shapes=[pltpu.VMEM((SEQ, SEQ), f32)],
        compiler_params=pltpu.CompilerParams(vmem_limit_bytes=48 * 2**20),
        cost_estimate=pl.CostEstimate(
            flops=4 * count * SEQ * width, bytes_accessed=8 * count * width, transcendentals=0
        ),
        name="attend",
    )(packed, packed, packed, doc_col, doc_row)


def attend_back_kernel(
    q_ref, k_ref, v_ref, grad_ref, mixed_ref, lse_ref, doc_col, doc_row, out_ref, bias, grad_q_t
):
    pair = pl.program_id(1)

    @pl.when(pair == 0)
    def _():
        fill_bias(bias, doc_col, doc_row, True)

    wide = out_ref.shape[1] // 3
    place = [pl.ds(pl.multiple_of(s * wide + pair * LANES, LANES), LANES) for s in range(3)]
    query = q_ref[...] * jnp.asarray(scale_qk, low)
    grad = grad_ref[...]
    product = grad.astype(f32) * mixed_ref[...].astype(f32)
    upper = product.astype(low)
    lower = (product - upper.astype(f32)).astype(low)
    chooser = (
        lax.broadcasted_iota(jnp.int32, (8, LANES), 0)
        == lax.broadcasted_iota(jnp.int32, (8, LANES), 1) // HEAD_DIM
    ).astype(low)
    inner = dot_cols(chooser, upper) + dot_cols(chooser, lower)
    key_t = k_ref[...].T
    for block in range(0, SEQ, BLOCK):
        after = block + BLOCK
        key = k_ref[block:after, :]
        value = v_ref[block:after, :]
        grad_k, grad_v = [], []
        for head in range(2):
            scores = dot_cols(keep_head(key, head), query[block:, :])
            scores = jnp.minimum(scores, bias[block:after, block:])
            weights = jnp.exp(scores - lse_ref[head : head + 1, block:])
            grad_w = dot_cols(keep_head(value, head), grad[block:, :])
            grad_s = (weights * (grad_w - inner[head : head + 1, block:])).astype(low)
            grad_v.append(dot_rows(weights.astype(low), grad[block:, :]))
            grad_k.append(dot_rows(grad_s, query[block:, :]))
            rows = slice(head * HEAD_DIM, (head + 1) * HEAD_DIM)
            moved = dot_rows(key_t[rows, block:after], grad_s)
            if block == 0:
                grad_q_t[rows, :] = moved
            else:
                grad_q_t[rows, block:] += moved
        first = in_head((BLOCK, LANES), 0, 1)
        out_ref[block:after, place[1]] = jnp.where(first, grad_k[0], grad_k[1]).astype(low)
        out_ref[block:after, place[2]] = jnp.where(first, grad_v[0], grad_v[1]).astype(low)
    out_ref[:, place[0]] = (grad_q_t[...] * scale_qk).T.astype(low)


def attend_back(packed, grad_mixed, mixed, lse, doc_col, doc_row, first, count):
    tokens, wide = packed.shape
    pairs = wide // 3 // LANES

    def part(which):
        return pl.BlockSpec((SEQ, LANES), lambda r, p, w=which: (r, w * pairs + first + p))

    return pl.pallas_call(
        attend_back_kernel,
        grid=(tokens // SEQ, count),
        in_specs=[
            part(0),
            part(1),
            part(2),
            pl.BlockSpec((SEQ, LANES), lambda r, p: (r, first + p)),
            pl.BlockSpec((SEQ, LANES), lambda r, p: (r, first + p)),
            pl.BlockSpec((8, SEQ), lambda r, p: (first + p, r)),
            pl.BlockSpec((SEQ, 1), lambda r, p: (r, 0)),
            pl.BlockSpec((1, SEQ), lambda r, p: (0, r)),
        ],
        out_specs=pl.BlockSpec((SEQ, 3 * count * LANES), lambda r, p: (r, 0)),
        out_shape=jax.ShapeDtypeStruct((tokens, 3 * count * LANES), low),
        scratch_shapes=[pltpu.VMEM((SEQ, SEQ), f32), pltpu.VMEM((LANES, SEQ), f32)],
        compiler_params=pltpu.CompilerParams(vmem_limit_bytes=48 * 2**20),
        cost_estimate=pl.CostEstimate(
            flops=20 * tokens * SEQ * count * LANES,
            bytes_accessed=16 * tokens * count * LANES,
            transcendentals=0,
        ),
        name="attend_back",
    )(packed, packed, packed, grad_mixed, mixed, lse, doc_col, doc_row)


def norm_parts(values):
    centre = values - jnp.mean(values, axis=-1, keepdims=True)
    spread = jnp.mean(centre * centre, axis=-1, keepdims=True)
    scale = lax.rsqrt(spread + eps)
    return centre * scale, scale


def norm_back(grad, normal, scale, gain):
    moved = grad * gain
    return scale * (
        moved
        - jnp.mean(moved, axis=-1, keepdims=True)
        - normal * jnp.mean(moved * normal, axis=-1, keepdims=True)
    )


def sum_slabs(values):
    return jnp.sum(values.reshape(-1, 8, values.shape[1]), axis=0)


def after_attend_kernel(
    mixed_refs, proj_ref, x_ref, grad_ref, norm_ref, centre_ref, route_ref, slot_ref, outs, sent
):
    after_ref, grad_rows_ref, gate_ref, out_refs = outs[0], outs[1], outs[2], outs[3:]
    step = pl.program_id(0)
    attended = 0.0
    depth = 0
    for mixed in mixed_refs:
        wide = mixed.shape[1]
        attended = attended + dot_rows(mixed[...], proj_ref[depth : depth + wide, :])
        depth += wide
    after = x_ref[...].astype(f32) + attended
    after_ref[...] = after
    normal, _ = norm_parts(after)
    sent_low = (normal * norm_ref[2:3, :] + norm_ref[3:4, :]).astype(low)
    sent[pl.ds(pl.multiple_of(step * BLOCK, BLOCK), BLOCK), :] = sent_low
    experts = centre_ref.shape[0]
    onehot = route_ref[...] == lax.broadcasted_iota(jnp.int32, (BLOCK, experts), 1)
    picked = dot_rows(onehot.astype(low), centre_ref[...])
    gate = jax.nn.sigmoid(jnp.sum(sent_low.astype(f32) * picked, axis=-1, keepdims=True))
    grad_rows_ref[...] = (gate * grad_ref[...].astype(f32)).astype(low)
    gate_ref[...] = jnp.broadcast_to(gate, gate_ref.shape)

    @pl.when(step == pl.num_programs(0) - 1)
    def _():
        base = 0
        for out_ref in out_refs:
            for row in range(0, out_ref.shape[0], BLOCK):
                slots = lax.broadcasted_iota(jnp.int32, (BLOCK, sent.shape[0]), 0) + base
                place = (slots == slot_ref[...]).astype(low)
                out_ref[row : row + BLOCK, :] = dot_rows(place, sent[...]).astype(low)
                base += BLOCK


def after_attend(mixed, proj, tokens, out_grad, norms, centres, routes, slot_row, chunk_rows):
    count, width = tokens.shape
    chunks = len(chunk_rows)
    tile = pl.BlockSpec((BLOCK, width), lambda i: (i, 0))

    def kernel(*refs):
        n = len(mixed)
        after_attend_kernel(refs[:n], *refs[n : n + 7], refs[n + 7 : -1], refs[-1])

    return pl.pallas_call(
        kernel,
        grid=(count // BLOCK,),
        in_specs=[pl.BlockSpec((BLOCK, m.shape[1]), lambda i: (i, 0)) for m in mixed]
        + [
            pl.BlockSpec((width, width), lambda i: (0, 3)),
            tile,
            tile,
            pl.BlockSpec(norms.shape, lambda i: (0, 0)),
            pl.BlockSpec(centres.shape, lambda i: (0, 0)),
            pl.BlockSpec((BLOCK, 1), lambda i: (i, 0)),
            pl.BlockSpec((1, count), lambda i: (0, 0)),
        ],
        out_specs=[tile, tile, pl.BlockSpec((BLOCK, LANES), lambda i: (i, 0))]
        + [pl.BlockSpec((rows, width), lambda i: (0, 0)) for rows in chunk_rows],
        out_shape=[
            jax.ShapeDtypeStruct((count, width), f32),
            jax.ShapeDtypeStruct((count, width), low),
            jax.ShapeDtypeStruct((count, LANES), f32),
        ]
        + [jax.ShapeDtypeStruct((rows, width), low) for rows in chunk_rows],
        scratch_shapes=[pltpu.VMEM((count, width), low)],
        compiler_params=pltpu.CompilerParams(vmem_limit_bytes=48 * 2**20),
        cost_estimate=pl.CostEstimate(
            flops=2 * count * width * (width + sum(chunk_rows)),
            bytes_accessed=12 * count * width,
            transcendentals=0,
        ),
        name="after_attend",
    )(*mixed, proj, tokens, out_grad, norms, centres, routes, slot_row)


def picked_rows(slot_ref, row_refs):
    base, total = 0, 0.0
    for rows in row_refs:
        slots = lax.broadcasted_iota(jnp.int32, (BLOCK, rows.shape[0]), 1) + base
        place = (slots == slot_ref[...]).astype(low)
        total = total + dot_rows(place, rows[...])
        base += rows.shape[0]
    return total


def before_attend_back_kernel(
    row_refs, slot_ref, after_ref, grad_ref, norm_ref, proj_ref, outs
):
    grad_after_ref, grad_low_ref, grad_mixed_ref, sums_ref = outs
    grad_normed = picked_rows(slot_ref, row_refs)
    normal, scale = norm_parts(after_ref[...])
    grad_after = grad_ref[...].astype(f32) + norm_back(
        grad_normed, normal, scale, norm_ref[2:3, :]
    )
    grad_after_ref[...] = grad_after
    grad_low = grad_after.astype(low)
    grad_low_ref[...] = grad_low
    grad_mixed_ref[...] = dot_cols(grad_low, proj_ref[...]).astype(low)
    sums = jnp.concatenate([sum_slabs(grad_normed * normal), sum_slabs(grad_normed)], axis=0)

    @pl.when(pl.program_id(0) == 0)
    def _():
        sums_ref[...] = sums

    @pl.when(pl.program_id(0) > 0)
    def _():
        sums_ref[...] += sums


def before_attend_back(rows, slot_col, after, out_grad, norms, proj):
    count, width = after.shape
    tile = pl.BlockSpec((BLOCK, width), lambda i: (i, 0))

    def kernel(*refs):
        n = len(rows)
        before_attend_back_kernel(refs[:n], *refs[n : n + 5], refs[n + 5 :])

    return pl.pallas_call(
        kernel,
        grid=(count // BLOCK,),
        in_specs=[pl.BlockSpec(r.shape, lambda i: (0, 0)) for r in rows]
        + [
            pl.BlockSpec((BLOCK, 1), lambda i: (i, 0)),
            tile,
            tile,
            pl.BlockSpec(norms.shape, lambda i: (0, 0)),
            pl.BlockSpec((width, width), lambda i: (0, 3)),
        ],
        out_specs=[tile, tile, tile, pl.BlockSpec((16, width), lambda i: (0, 0))],
        out_shape=[
            jax.ShapeDtypeStruct((count, width), f32),
            jax.ShapeDtypeStruct((count, width), low),
            jax.ShapeDtypeStruct((count, width), low),
            jax.ShapeDtypeStruct((16, width), f32),
        ],
        compiler_params=pltpu.CompilerParams(vmem_limit_bytes=48 * 2**20),
        cost_estimate=pl.CostEstimate(
            flops=5 * count * width * width, bytes_accessed=16 * count * width, transcendentals=0
        ),
        name="before_attend_back",
    )(*rows, slot_col, after, out_grad, norms, proj)


def input_grad_kernel(plan, grad_refs, weight_ref, x_ref, norm_ref, grad_after_ref, outs):
    out_ref, sums_ref = outs
    grad_normed = 0.0
    each = weight_ref.shape[1] // 3
    for grad, (offset, wide) in zip(grad_refs, plan):
        for s in range(3):
            start = s * each + offset
            grad_normed = grad_normed + dot_cols(
                grad[:, s * wide : (s + 1) * wide], weight_ref[:, start : start + wide]
            )
    normal, scale = norm_parts(x_ref[...].astype(f32))
    out_ref[...] = grad_after_ref[...] + norm_back(grad_normed, normal, scale, norm_ref[0:1, :])
    sums = jnp.concatenate([sum_slabs(grad_normed * normal), sum_slabs(grad_normed)], axis=0)

    @pl.when(pl.program_id(0) == 0)
    def _():
        sums_ref[...] = sums

    @pl.when(pl.program_id(0) > 0)
    def _():
        sums_ref[...] += sums


def input_gradient(plan, grads, dense, tokens, norms, grad_after):
    count, width = tokens.shape
    tile = pl.BlockSpec((BLOCK, width), lambda i: (i, 0))

    def kernel(*refs):
        n = len(grads)
        input_grad_kernel(plan, refs[:n], *refs[n : n + 4], refs[n + 4 :])

    return pl.pallas_call(
        kernel,
        grid=(count // BLOCK,),
        in_specs=[pl.BlockSpec((BLOCK, g.shape[1]), lambda i: (i, 0)) for g in grads]
        + [
            pl.BlockSpec((width, 3 * width), lambda i: (0, 0)),
            tile,
            pl.BlockSpec(norms.shape, lambda i: (0, 0)),
            tile,
        ],
        out_specs=[tile, pl.BlockSpec((16, width), lambda i: (0, 0))],
        out_shape=[
            jax.ShapeDtypeStruct((count, width), f32),
            jax.ShapeDtypeStruct((16, width), f32),
        ],
        compiler_params=pltpu.CompilerParams(vmem_limit_bytes=48 * 2**20),
        cost_estimate=pl.CostEstimate(
            flops=6 * count * width * width, bytes_accessed=16 * count * width, transcendentals=0
        ),
        name="input_gradient",
    )(*grads, dense, tokens, norms, grad_after)


def activations_of(rows, slot_col, gate, after):
    count, width = after.shape
    tile = pl.BlockSpec((BLOCK, width), lambda i: (i, 0))

    def kernel(*refs):
        n = len(rows)
        slot_ref, gate_ref, after_ref, out_ref = refs[n:]
        found = picked_rows(slot_ref, refs[:n])
        out_ref[...] = (after_ref[...] + gate_ref[:, :1] * found).astype(low)

    return pl.pallas_call(
        kernel,
        grid=(count // BLOCK,),
        in_specs=[pl.BlockSpec(r.shape, lambda i: (0, 0)) for r in rows]
        + [
            pl.BlockSpec((BLOCK, 1), lambda i: (i, 0)),
            pl.BlockSpec((BLOCK, LANES), lambda i: (i, 0)),
            tile,
        ],
        out_specs=tile,
        out_shape=jax.ShapeDtypeStruct((count, width), low),
        compiler_params=pltpu.CompilerParams(vmem_limit_bytes=48 * 2**20),
        cost_estimate=pl.CostEstimate(
            flops=3 * count * width * width, bytes_accessed=10 * count * width, transcendentals=0
        ),
        name="activations_of",
    )(*rows, slot_col, gate, after)


def gelu_and_slope(x):
    point = 1.0 / (1.0 + (erfc_point * math.sqrt(0.5)) * jnp.abs(x))
    bell = jnp.exp(-0.5 * x * x)
    tail = erfc_terms[-1]
    for term in erfc_terms[-2::-1]:
        tail = tail * point + term
    tail = tail * point * bell
    below = jnp.where(x >= 0.0, 1.0 - tail, tail)
    return x * below, below + x * bell * (1.0 / math.sqrt(2.0 * math.pi))


def row_groups(experts, each):
    group = max(g for g in range(1, experts + 1) if experts % g == 0 and g * each <= BLOCK)
    return group, group * each


def expert_kernel(x_ref, in_ref, *rest):
    hidden_ref, slope_ref = rest[-2:]
    experts, each, width = x_ref.shape
    group, size = row_groups(experts, each)
    for e in range(0, experts, group):
        preact = dot_rows(x_ref[e : e + group].reshape(size, width), in_ref[...])
        value, slope = gelu_and_slope(preact)
        hidden_ref[e : e + group] = value.astype(low).reshape(group, each, -1)
        slope_ref[e : e + group] = slope.astype(low).reshape(group, each, -1)


def expert_forward(arrived, weight_in, chunk, chunks, buffer=None, tile=512):
    experts, each, width = arrived.shape
    inner = weight_in.shape[1]
    return pl.pallas_call(
        expert_kernel,
        grid=(inner // tile,),
        in_specs=[
            pl.BlockSpec((experts, each, width), lambda j: (0, 0, 0)),
            pl.BlockSpec((width, tile), lambda j: (0, j)),
        ]
        + ([] if buffer is None else [pl.BlockSpec(memory_space=pl.ANY)]),
        out_specs=[
            pl.BlockSpec((experts, each, tile), lambda j: (0, chunk, j)),
            pl.BlockSpec((experts, each, tile), lambda j: (0, 0, j)),
        ],
        out_shape=[
            jax.ShapeDtypeStruct((experts, chunks * each, inner), low),
            jax.ShapeDtypeStruct((experts, each, inner), low),
        ],
        input_output_aliases={} if buffer is None else {2: 0},
        compiler_params=pltpu.CompilerParams(vmem_limit_bytes=56 * 2**20),
        cost_estimate=pl.CostEstimate(
            flops=4 * experts * each * width * inner,
            bytes_accessed=4 * (experts * each + width) * inner,
            transcendentals=0,
        ),
        name="expert_forward",
    )(arrived, weight_in, *([] if buffer is None else [buffer]))


def expert_back_kernel(
    grad_ref, slope_ref, in_ref, out_ref, x_ref, result_ref, centre_ref, *rest
):
    grad_preact_ref, grad_rows_ref, grad_centre_ref, strips, grad_logit_ref = rest[-5:]
    step = pl.program_id(0)
    count, size, tile = strips.shape
    each = grad_ref.shape[1]

    @pl.when(step < count)
    def _():
        grad_hidden = dot_cols(grad_ref[...].reshape(size, -1), out_ref[...])
        grad_preact = (grad_hidden * slope_ref[...].reshape(size, tile).astype(f32)).astype(low)
        strips[step] = grad_preact
        grad_preact_ref[...] = grad_preact.reshape(-1, each, tile)

    @pl.when(step == count)
    def _():
        centre = centre_ref[...].astype(f32)
        grad_centre = jnp.zeros(grad_centre_ref.shape, f32)
        group, rows = row_groups(grad_ref.shape[0], each)
        for e in range(0, grad_ref.shape[0], group):
            x = x_ref[e : e + group].reshape(rows, -1).astype(f32)
            gate = jax.nn.sigmoid(jnp.sum(x * centre, axis=-1, keepdims=True))
            grad = grad_ref[e : e + group].reshape(rows, -1).astype(f32)
            moved = grad * result_ref[e : e + group].reshape(rows, -1).astype(f32)
            grad_logit = jnp.sum(moved, axis=-1, keepdims=True) * (1.0 - gate)
            grad_logit_ref[e * each : e * each + rows, :] = jnp.broadcast_to(
                grad_logit, (rows, LANES)
            )
            grad_centre = grad_centre + sum_slabs(grad_logit * x)
        grad_centre_ref[...] = grad_centre

    @pl.when(step >= count)
    def _():
        columns = grad_rows_ref.shape[2]
        start = pl.multiple_of((step - count) * columns, columns)
        centre = centre_ref[:, pl.ds(start, columns)].astype(f32)
        total = grad_logit_ref[:, :1] * centre
        for k in range(count):
            total = total + dot_cols(strips[k], in_ref[:, k * tile : (k + 1) * tile])
        grad_rows_ref[...] = total.astype(low).reshape(-1, each, columns)


def expert_back(
    grad_arrived,
    slope,
    weight_in,
    weight_out,
    arrived,
    result,
    centre,
    chunk,
    chunks,
    buffer=None,
    tile=1024,
    columns=256,
):
    experts, each, width = grad_arrived.shape
    inner = weight_in.shape[1]
    count = inner // tile
    alone = pl.BlockSpec((experts, each, width), lambda j: (0, 0, 0))

    def strip(j):
        return jnp.minimum(j, count - 1)

    def part(j):
        return jnp.maximum(j - count, 0)

    return pl.pallas_call(
        expert_back_kernel,
        grid=(count + width // columns,),
        in_specs=[
            alone,
            pl.BlockSpec((experts, each, tile), lambda j: (0, 0, strip(j))),
            pl.BlockSpec((columns, inner), lambda j: (part(j), 0)),
            pl.BlockSpec((tile, width), lambda j: (strip(j), 0)),
            alone,
            pl.BlockSpec((experts, each, width), lambda j: (0, chunk, 0)),
            pl.BlockSpec((1, width), lambda j: (0, 0)),
        ]
        + ([] if buffer is None else [pl.BlockSpec(memory_space=pl.ANY)]),
        out_specs=[
            pl.BlockSpec((experts, each, tile), lambda j: (0, chunk, strip(j))),
            pl.BlockSpec((experts, each, columns), lambda j: (0, 0, part(j))),
            pl.BlockSpec((8, width), lambda j: (0, 0)),
        ],
        out_shape=[
            jax.ShapeDtypeStruct((experts, chunks * each, inner), low),
            jax.ShapeDtypeStruct((experts, each, width), low),
            jax.ShapeDtypeStruct((8, width), f32),
        ],
        scratch_shapes=[
            pltpu.VMEM((count, experts * each, tile), low),
            pltpu.VMEM((experts * each, LANES), f32),
        ],
        input_output_aliases={} if buffer is None else {7: 0},
        compiler_params=pltpu.CompilerParams(vmem_limit_bytes=58 * 2**20),
        cost_estimate=pl.CostEstimate(
            flops=4 * experts * each * width * inner,
            bytes_accessed=4 * (experts * each + width) * inner,
            transcendentals=0,
        ),
        name="expert_back",
    )(
        grad_arrived,
        slope,
        weight_in,
        weight_out,
        arrived,
        result,
        centre,
        *([] if buffer is None else [buffer]),
    )


def swap(values, axis, distance):
    size = lax.axis_size(axis)
    return lax.ppermute(values, axis, [(i, i ^ distance) for i in range(size)])


def sum_over_cores(held):
    bit = lax.axis_index("dp") % 2
    halves = held.reshape((held.shape[0], held.shape[1] // 2, 2) + held.shape[2:])
    mine = lax.dynamic_index_in_dim(halves, bit, 2, keepdims=False)
    theirs = lax.dynamic_index_in_dim(halves, 1 - bit, 2, keepdims=False)
    return (mine.astype(f32) + swap(theirs, "dp", 1).astype(f32)).astype(low)


def sum_over_pairs(held, partners, keep):
    experts, dp = lax.axis_size("expert"), lax.axis_size("dp")
    total = lax.dynamic_index_in_dim(held, keep, 0, keepdims=False).astype(f32)
    for offset, (far, near) in enumerate(partners, 1):
        block = lax.dynamic_index_in_dim(held, jnp.bitwise_xor(keep, offset), 0, keepdims=False)
        perm = [
            (e * dp + d, (e ^ far) * dp + (d ^ near)) for e in range(experts) for d in range(dp)
        ]
        total = total + lax.ppermute(block, everywhere, perm).astype(f32)
    return total


def sum_near(held):
    far = held.shape[1]
    held = held.reshape((held.shape[0] // 2, 2 * far) + held.shape[2:]).swapaxes(0, 1)
    partners = [(i // far, i % far * 2) for i in range(1, 2 * far)]
    keep = lax.axis_index("expert") % 2 * far + lax.axis_index("dp") // 2
    return sum_over_pairs(held, partners, keep).astype(low)


def sum_far(held):
    partners = [(2 * i, 0) for i in range(1, held.shape[0])]
    return sum_over_pairs(held, partners, lax.axis_index("expert") // 2)


def in_order(*values):
    return lax.optimization_barrier(values)


def sum_everywhere(value):
    held = value.reshape(1, 1)
    for axis in ("dp", "expert"):
        distance = 1
        while distance < lax.axis_size(axis):
            held = held + swap(held, axis, distance)
            distance *= 2
    return held[0, 0]


def update(weight, moment, average, gradient, factor, rate):
    clipped = gradient * factor
    moment_new = momentum_rate * moment + clipped
    weight_new = weight - rate * (clipped + momentum_rate * moment_new)
    average_new = average_rate * average + (1.0 - average_rate) * weight_new
    return (weight_new, moment_new, average_new)


def shards(
    tokens,
    documents,
    routes,
    out_grad,
    norm_params,
    qkv_weight,
    proj_weight,
    centroids,
    expert_in,
    expert_out,
    norm_moment,
    qkv_moment,
    proj_moment,
    centroid_moment,
    in_moment,
    out_moment,
    norm_average,
    qkv_average,
    proj_average,
    centroid_average,
    in_average,
    out_average,
):
    local_tokens, width = tokens.shape
    experts = lax.axis_size("expert")
    dp = lax.axis_size("dp")
    devices = experts * dp
    slot_cap = max(2, 3 * local_tokens // (2 * experts))
    slots = experts * slot_cap
    chunks = 2 if slot_cap % 32 == 0 else 1
    half_cap = slot_cap // chunks
    rows_own = qkv_weight.shape[0]
    norm_own = norm_params.shape[1]
    centre_own = centroids.shape[1]
    groups = 4

    small = jnp.concatenate([norm_params.reshape(-1), centroids.reshape(-1)]).astype(low)
    small = jnp.pad(small, (0, rows_own * LANES - small.shape[0])).reshape(rows_own, LANES)
    dense = jnp.concatenate([qkv_weight.astype(low), proj_weight.astype(low), small], axis=1)
    dense = lax.all_gather(dense, everywhere, axis=0, tiled=True)
    weight_in = lax.all_gather(expert_in.astype(low), "dp", axis=1, tiled=True)[0]
    weight_out = lax.all_gather(expert_out.astype(low), "dp", axis=2, tiled=True)[0]

    small_full = dense[:, 4 * width :].reshape(devices, rows_own * LANES)
    norms = (
        small_full[:, : 4 * norm_own].reshape(devices, 4, norm_own).transpose(1, 0, 2)
    ).reshape(4, width).astype(f32)
    centre_table = small_full[:, 4 * norm_own : 4 * norm_own + centre_own].reshape(experts, width)

    route_ids = routes[:, 0]
    onehot = route_ids[:, None] == jnp.arange(experts, dtype=jnp.int32)[None, :]
    running = jnp.cumsum(onehot.astype(jnp.int32), axis=0)
    within = jnp.sum(running * onehot.astype(jnp.int32), axis=1) - 1
    slot_index = route_ids * slot_cap + within
    chunked = (within // half_cap * experts + route_ids) * half_cap + within % half_cap
    slot_row, slot_col = slot_index[None, :], slot_index[:, None]
    chunked_row, chunked_col = chunked[None, :], chunked[:, None]
    doc_col = documents[:, None]
    doc_row = documents[None, :]

    normed_low = layer_norm(tokens.astype(f32), norms[0], norms[1]).astype(low)
    packed = jnp.dot(normed_low, dense[:, : 3 * width], preferred_element_type=f32).astype(low)
    mixed, lse = attend(packed, doc_col, doc_row)
    after, grad_rows, gate, *outgoing = after_attend(
        [mixed],
        dense,
        tokens,
        out_grad,
        norms,
        centre_table,
        routes,
        chunked_row,
        [slots // chunks] * chunks,
    )

    def exchange(rows):
        rows = rows.reshape(experts, -1, width)
        return lax.all_to_all(rows, "expert", split_axis=0, concat_axis=0, tiled=True)

    grad_outgoing = []
    for c in range(chunks):
        own = jnp.arange(slots // chunks, dtype=jnp.int32)[:, None] + c * (slots // chunks)
        place = (own == chunked_row).astype(low)
        grad_outgoing.append(jnp.dot(place, grad_rows, preferred_element_type=f32).astype(low))
    arrived, slope, hidden = [], [], None
    for c in range(chunks):
        if c:
            arrived[c - 1], outgoing[c] = in_order(arrived[c - 1], outgoing[c])
        arrived.append(exchange(outgoing[c]))
    for c in range(chunks):
        if c == chunks - 1:
            arrived[c], grad_outgoing[0] = in_order(arrived[c], grad_outgoing[0])
        hidden, slope_c = expert_forward(arrived[c], weight_in, c, chunks, hidden)
        slope.append(slope_c)
        if c == 0 and chunks > 1:
            hidden, grad_outgoing[0] = in_order(hidden, grad_outgoing[0])
    grad_arrived = [exchange(grad_outgoing[0])]
    hidden = hidden.reshape(slots, -1)
    result = jnp.dot(hidden, weight_out, preferred_element_type=f32).astype(low)
    result = result.reshape(experts, slot_cap, width)
    for c in range(1, chunks):
        grad_arrived[c - 1], grad_outgoing[c], result = in_order(
            grad_arrived[c - 1], grad_outgoing[c], result
        )
        grad_arrived.append(exchange(grad_outgoing[c]))
    centre_row = lax.dynamic_slice_in_dim(centre_table, lax.axis_index("expert"), 1, 0)
    grad_preact = grad_weight_out = None
    grad_input, grad_centre = [], 0.0
    for c in range(chunks):
        last = c == chunks - 1
        if last:
            grad_weight_out = lax.dot_general(
                hidden,
                jnp.concatenate(grad_arrived, axis=1).reshape(slots, width),
                (((0,), (0,)), ((), ())),
                preferred_element_type=f32,
            ).astype(low)
            grad_arrived[c], grad_weight_out = in_order(grad_arrived[c], grad_weight_out)
        grad_preact, rows_c, centre_c = expert_back(
            grad_arrived[c],
            slope[c],
            weight_in,
            weight_out,
            arrived[c],
            result,
            centre_row,
            c,
            chunks,
            grad_preact,
        )
        if not last:
            rows_c, grad_arrived[c + 1] = in_order(rows_c, grad_arrived[c + 1])
        elif grad_input:
            rows_c, grad_input[-1] = in_order(rows_c, grad_input[-1])
        grad_input.append(exchange(rows_c).reshape(slots // chunks, width))
        grad_centre = grad_centre + jnp.sum(centre_c, axis=0)
    out_grad_w = lax.psum_scatter(grad_weight_out[None], "dp", scatter_dimension=2, tiled=True)
    arrived = jnp.concatenate(arrived, axis=1)
    grad_weight_in = lax.dot_general(
        arrived.reshape(slots, width),
        grad_preact.reshape(slots, -1),
        (((0,), (0,)), ((), ())),
        preferred_element_type=f32,
    ).astype(low)
    out_grad_w = out_grad_w.astype(f32)
    result, grad_input[-1], grad_weight_in = in_order(result, grad_input[-1], grad_weight_in)
    in_grad = lax.psum_scatter(grad_weight_in[None], "dp", scatter_dimension=1, tiled=True)
    in_grad = in_grad.astype(f32)
    returned = exchange(result).reshape(slots, width)

    grad_after, grad_low, grad_mixed, sums_two = before_attend_back(
        grad_input, chunked_col, after, out_grad, norms, dense
    )

    grad_proj = lax.dot_general(
        mixed, grad_low, (((0,), (0,)), ((), ())), preferred_element_type=f32
    ).astype(low)
    norm_two = jnp.sum(sums_two.reshape(2, 8, width), axis=1)
    norm_two = norm_two.reshape(2, devices, norm_own).transpose(1, 0, 2).reshape(devices, -1)
    mine = jnp.arange(experts)[:, None, None] == lax.axis_index("expert")
    centre_flat = jnp.where(mine, grad_centre.reshape(1, dp, centre_own), 0.0)
    extra = jnp.concatenate([norm_two, centre_flat.reshape(devices, centre_own)], axis=1)
    extra = jnp.pad(extra, ((0, 0), (0, rows_own * LANES - extra.shape[1]))).astype(low)
    extra = extra.reshape(devices * rows_own, LANES)
    each = width // LANES // groups
    wide = each * LANES

    def begin(parts):
        joined = jnp.concatenate(parts, axis=1)
        return joined.reshape(experts, dp, rows_own, joined.shape[1])

    def back_group(g):
        part = attend_back(packed, grad_mixed, mixed, lse, doc_col, doc_row, g * each, each)
        grad = lax.dot_general(
            normed_low, part, (((0,), (0,)), ((), ())), preferred_element_type=f32
        )
        return part, grad.astype(low)

    parts, grads = [], []
    rest = begin([grad_proj, extra])
    for g in range(groups):
        if g == 1:
            rest = sum_over_cores(rest)
            rest, grad_mixed = in_order(rest, grad_mixed)
        if g == groups - 1:
            first = sum_over_cores(begin(grads[: groups // 2]))
            rest = sum_near(rest)
            rest, first, grad_mixed, returned = in_order(rest, first, grad_mixed, returned)
        part, grad = back_group(g)
        grad, grad_mixed = in_order(grad, grad_mixed)
        parts.append(part)
        grads.append(grad)
    first = sum_near(first)
    second = sum_over_cores(begin(grads[groups // 2 :]))
    first, second, grad_after = in_order(first, second, grad_after)
    second = sum_near(second)
    input_grad, sums_one = input_gradient(
        [(g * wide, wide) for g in range(groups)], parts, dense, tokens, norms, grad_after
    )
    rest, first = sum_far(rest), sum_far(first)
    rest, first, second, sums_one, gate = in_order(rest, first, second, sums_one, gate)
    activations = activations_of([returned], slot_col, gate, after)
    second = sum_far(second)
    norm_one = jnp.sum(sums_one.reshape(2, 8, width), axis=1)
    norm_one = norm_one.reshape(2, devices, norm_own).transpose(1, 0, 2).reshape(devices, -1)
    norm_one = lax.all_to_all(norm_one, everywhere, split_axis=0, concat_axis=0, tiled=True)
    norm_one = jnp.sum(norm_one, axis=0).reshape(2, norm_own)

    proj_grad = rest[:, :width]
    extra = rest[:, width:].reshape(-1)
    norm_grad = jnp.concatenate([norm_one, extra[: 2 * norm_own].reshape(2, norm_own)], axis=0)
    centre_grad = extra[2 * norm_own : 2 * norm_own + centre_own].reshape(centroids.shape)
    owned = [first, second]
    qkv_grad = jnp.concatenate(
        [
            half[:, (3 * k + s) * wide : (3 * k + s + 1) * wide]
            for s in range(3)
            for half in owned
            for k in range(groups // 2)
        ],
        axis=1,
    )
    square_sum = (
        jnp.sum(qkv_grad * qkv_grad)
        + jnp.sum(proj_grad * proj_grad)
        + jnp.sum(norm_grad * norm_grad)
        + jnp.sum(centre_grad * centre_grad)
        + jnp.sum(in_grad * in_grad)
        + jnp.sum(out_grad_w * out_grad_w)
    )
    grad_norm = jnp.sqrt(sum_everywhere(square_sum))
    factor = clip_limit / jnp.maximum(grad_norm, clip_limit)
    norm_new = update(norm_params, norm_moment, norm_average, norm_grad, factor, norm_rate)
    qkv_new = update(qkv_weight, qkv_moment, qkv_average, qkv_grad, factor, learn_rate)
    proj_new = update(proj_weight, proj_moment, proj_average, proj_grad, factor, learn_rate)
    centre_new = update(
        centroids, centroid_moment, centroid_average, centre_grad, factor, learn_rate
    )
    in_new = update(expert_in, in_moment, in_average, in_grad, factor, learn_rate)
    out_new = update(expert_out, out_moment, out_average, out_grad_w, factor, learn_rate)
    return (
        activations,
        input_grad,
        grad_norm,
        norm_new[0],
        qkv_new[0],
        proj_new[0],
        centre_new[0],
        in_new[0],
        out_new[0],
        norm_new[1],
        qkv_new[1],
        proj_new[1],
        centre_new[1],
        in_new[1],
        out_new[1],
        norm_new[2],
        qkv_new[2],
        proj_new[2],
        centre_new[2],
        in_new[2],
        out_new[2],
    )


def solution(mesh):
    placed = (
        P(("expert", "dp"), None),
        P(("expert", "dp")),
        P(("expert", "dp"), None),
        P(("expert", "dp"), None),
        P(None, ("expert", "dp")),
        P(("expert", "dp"), None),
        P(("expert", "dp"), None),
        P("expert", "dp"),
        P("expert", "dp", None),
        P("expert", None, "dp"),
        P(None, ("expert", "dp")),
        P(("expert", "dp"), None),
        P(("expert", "dp"), None),
        P("expert", "dp"),
        P("expert", "dp", None),
        P("expert", None, "dp"),
        P(None, ("expert", "dp")),
        P(("expert", "dp"), None),
        P(("expert", "dp"), None),
        P("expert", "dp"),
        P("expert", "dp", None),
        P("expert", None, "dp"),
    )
    return jax.shard_map(
        shards,
        mesh=mesh,
        in_specs=placed,
        out_specs=(
            P(("expert", "dp"), None),
            P(("expert", "dp"), None),
            P(),
            P(None, ("expert", "dp")),
            P(("expert", "dp"), None),
            P(("expert", "dp"), None),
            P("expert", "dp"),
            P("expert", "dp", None),
            P("expert", None, "dp"),
            P(None, ("expert", "dp")),
            P(("expert", "dp"), None),
            P(("expert", "dp"), None),
            P("expert", "dp"),
            P("expert", "dp", None),
            P("expert", None, "dp"),
            P(None, ("expert", "dp")),
            P(("expert", "dp"), None),
            P(("expert", "dp"), None),
            P("expert", "dp"),
            P("expert", "dp", None),
            P("expert", None, "dp"),
        ),
        check_vma=False,
    )
```

time: 721 us -> 692 us (0.960)
  waiting for transfers between devices: 222 us -> 170 us
  Pallas kernels: 165 us -> 205 us
  local copies, waits for them, and re-layouts: 57 us -> 18.8 us
  blocking collectives: 5.98 us -> 41.1 us
  starting transfers between devices: 47.7 us -> 69.2 us
  matrix products: 110 us -> 91.1 us
  other arithmetic: 81.4 us -> 65.1 us
    all_to_all x6 -> x7, waiting for transfers between devices: 118 us -> 57.1 us  [the longest x6 57.1 us: exchange(): lax.all_to_all(rows, 'expert', split_axis=0, concat_axis=0, tiled=True)]
    all_to_all x0 -> x1, blocking collectives: none -> 41.1 us  [exchange(): lax.all_to_all(rows, 'expert', split_axis=0, concat_axis=0, tiled=True)]
    ppermute x0 -> x18, waiting for transfers between devices: none -> 40.1 us  [sum_over_pairs(): total = total + lax.ppermute(block, everywhere, perm).astype(f32)]
    pallas_call x4 -> x12, Pallas kernels: 136 us -> 176 us  [the longest x2 47.7 us: expert_back(): pl.pallas_call(expert_back_kernel, grid=(count + width // columns,), in_s...]
    ppermute x9 -> x8, waiting for transfers between devices: 37.8 us -> 3 us  [swap(): return lax.ppermute(values, axis, [(i, i ^ distance) for i in range(size)])]
    ppermute x0 -> x18, starting transfers between devices: none -> 24.9 us  [sum_over_pairs(): total = total + lax.ppermute(block, everywhere, perm).astype(f32)]
    unnamed x148 -> x121, local copies, waits for them, and re-layouts: 32.4 us -> 9.86 us
    dot_general x15 -> x11, matrix products: 110 us -> 91.1 us  [the longest x1 19.5 us: shards(): lax.dot_general(arrived.reshape(slots, width), grad_preact.reshape(slots,...]
  transfers between devices with their start and end apart: 20 -> 38, of which waited for: 12 -> 17; matrix products, arithmetic and copies ran while one was open for 25% -> 16% of each run, Pallas kernels for 17% -> 30%
where the time goes in v2:
time: 692 us; the launch traced here: 683 us
  Pallas kernels  205 us (30%)
  waiting for transfers between devices  170 us (25%)
  matrix products  91.1 us (13%)
  starting transfers between devices  69.2 us (10%)
  other arithmetic  65.1 us (9%)
  blocking collectives  41.1 us (6%)
  between operations  23.4 us (3%)
  local copies, waits for them, and re-layouts  18.8 us (3%)
    all_gather x1, waiting for transfers between devices, shards(): dense = lax.all_gather(dense, everywhere, axis=0, tiled=True)  69.2 us
    all_to_all x6, waiting for transfers between devices, exchange(): lax.all_to_all(rows, 'expert', split_axis=0, concat_axis=0, tiled=True)  57.1 us
    pallas_call x2, Pallas kernels, expert_back(): pl.pallas_call(expert_back_kernel, grid=(count + width // columns,), in_s...  47.7 us
    pallas_call x2, Pallas kernels, expert_forward(): pl.pallas_call(expert_kernel, grid=(inner // tile,), in_specs=[pl.BlockSp...  42.5 us
    all_to_all x1, blocking collectives, exchange(): lax.all_to_all(rows, 'expert', split_axis=0, concat_axis=0, tiled=True)  41.1 us
    ppermute x18, waiting for transfers between devices, sum_over_pairs(): total = total + lax.ppermute(block, everywhere, perm).astype(f32)  40.1 us
    pallas_call x4, Pallas kernels, attend_back(): pl.pallas_call(attend_back_kernel, grid=(tokens // SEQ, count), in_specs=...  39 us
    pallas_call x1, Pallas kernels, attend(): pl.pallas_call(attend_kernel, grid=(count // SEQ, pairs), in_specs=[part(...  29.2 us
  transfers between devices with their start and end apart: 38, of which 17 were waited for; matrix products, arithmetic and copies ran while one was open for 16% of the time, Pallas kernels for 30%

profile of v2, /device:TPU:0, one launch (start us, length us, event | category | flops | bytes accessed | tf_op | source)
XLA Modules:
  0.0 683.2 jit_solution(1942566504204340295)
XLA Ops:
  23.6 69.2 %all-gather.4.cloned.1.call-done.refs_1_.refs_6_.refs_4_ = bf16[1024,4224]{1,0:T(8,128)(2,1)} async-done(((bf16[32,4224]{1,0:T(8,128)(2,1)}), bf16[1024,4224]{1,0:T(8,128)(2,1)}) %all-gather.4.cloned.1.call-update) | async-done | bytes 8650768 | tf_op jit(solution)/shard_map/all_gather | solution.py:727
  97.2 12.7 %fusion.2.q_ref.k_ref.v_ref = bf16[1024,3072]{1,0:T(8,128)(2,1)} fusion(bf16[1024,1024]{1,0:T(8,128)(2,1)S(1)} %fusion.18, bf16[1024,4224]{1,0:T(8,128)(2,1)} %all-gather.4.cloned.1.call-done.refs_1_.refs_6_.refs_4_), kind=kOutput, calls=%fused_computation.4 | convolution fusion | flops 6445596672 | bytes 14680064 | tf_op jit(solution)/shard_map/dot_general | solution.py:749
  110.0 29.2 %attend.1 = (bf16[1024,1024]{1,0:T(8,128)(2,1)S(1)}, f32[64,1024]{1,0:T(8,128)S(1)}) custom-call(bf16[1024,3072]{1,0:T(8,128)(2,1)} %fusion.2.q_ref.k_ref.v_ref, bf16[1024,3072]{1,0:T(8,128)(2,1)} %fusion.2.q_ref.k_ref.v_ref, bf16[1024,3072]{1,0:T(8,128)(2,1)} %fusion.2.q_ref.k_ref.v_ref, s32[1024,1]{1,0:T(8,128)S(1)} %copy.122.doc_col, s32[1,1024]{1,0:T(1,128)S(1)} %bitcast.172), custom_call_target="tpu_custom_call" | custom-call | flops 4294967296 | bytes 8388608 | tf_op jit(solution)/shard_map/attend/pallas_call | solution.py:102
  140.4 13.3 %after_attend.1 = (f32[1024,1024]{1,0:T(8,128)}, bf16[1024,1024]{1,0:T(8,128)(2,1)}, f32[1024,128]{1,0:T(8,128)S(1)}, bf16[768,1024]{1,0:T(8,128)(2,1)S(1)}, bf16[768,1024]{1,0:T(8,128)(2,1)}) custom-call(bf16[1024,1024]{1,0:T(8,128)(2,1)} %copy-done, bf16[1024,4224]{1,0:T(8,128)(2,1)} %all-gather.4.cloned.1.call-done.refs_1_.refs_6_.refs_4_, ...), custom_call_target="tpu_custom_call" | custom-call | flops 5368709120 | bytes 12582912 | tf_op jit(solution)/shard_map/after_attend/pallas_call | solution.py:272
  153.7 41.1 %all_to_all.44.x_ref = bf16[8,96,1024]{2,1,0:T(8,128)(2,1)} all-to-all(bf16[8,96,1024]{2,1,0:T(8,128)(2,1)S(1)} %bitcast.170), channel_id=1, replica_groups=mesh['expert'=8,'dp'=4] {'expert'}, dimensions={0} | all-to-all | bytes 3145728 | tf_op jit(solution)/shard_map/all_to_all | solution.py:765
  206.2 21.2 %expert_forward.2 = (bf16[8,192,4096]{2,1,0:T(8,128)(2,1)}, bf16[8,96,4096]{2,1,0:T(8,128)(2,1)}) custom-call(bf16[8,96,1024]{2,1,0:T(8,128)(2,1)} %all_to_all.44.x_ref, bf16[1024,4096]{1,0:T(8,128)(2,1)} %bitcast.211), custom_call_target="tpu_custom_call" | custom-call | flops 12884901888 | bytes 29360128 | tf_op jit(solution)/shard_map/expert_forward/pallas_call | solution.py:485
  227.4 8.0 %all-to-all-done.1.x_ref = bf16[8,96,1024]{2,1,0:T(8,128)(2,1)S(1)} async-done(((bf16[8,96,1024]{2,1,0:T(8,128)(2,1)}), bf16[8,96,1024]{2,1,0:T(8,128)(2,1)S(1)}, u32[]{:S(2)}, u32[]{:S(2)}) %all-to-all-start.1) | async-done | bytes 1572896 | tf_op jit(solution)/shard_map/all_to_all | solution.py:765
  239.8 21.3 %expert_forward.3 = (bf16[8,192,4096]{2,1,0:T(8,128)(2,1)}, bf16[8,96,4096]{2,1,0:T(8,128)(2,1)}) custom-call(bf16[8,96,1024]{2,1,0:T(8,128)(2,1)} %copy-done.29, bf16[1024,4096]{1,0:T(8,128)(2,1)} %bitcast.212, bf16[8,192,4096]{2,1,0:T(8,128)(2,1)} %get-tuple-element.93.rest_0_), custom_call_target="tpu_custom_call", output_to_operand_aliasing={{0}: (2, {})} | custom-call | flops 12884901888 | bytes 29360128 | tf_op jit(solution)/shard_map/expert_forward/pallas_call | solution.py:485
  261.0 19.1 %convolution_convert_fusion = bf16[1536,1024]{1,0:T(8,128)(2,1)} fusion(bf16[1536,4096]{1,0:T(8,128)(2,1)} %bitcast.217, bf16[1,4096,1024]{2,1,0:T(8,128)(2,1)} %all-gather.8.cloned.1.call-done), kind=kOutput, calls=%fused_computation.29 | convolution fusion | flops 12886474752 | bytes 24117248 | tf_op jit(solution)/shard_map/dot_general | solution.py:786
  280.2 5.9 all-to-all-start.3
  286.7 22.8 %expert_back.2 = (bf16[8,192,4096]{2,1,0:T(8,128)(2,1)}, bf16[8,96,1024]{2,1,0:T(8,128)(2,1)}, f32[8,1024]{1,0:T(8,128)}) custom-call(bf16[8,96,1024]{2,1,0:T(8,128)(2,1)} %all-to-all-done.2.grad_ref, bf16[8,96,4096]{2,1,0:T(8,128)(2,1)} %get-tuple-element.96.slope_ref, bf16[1024,4096]{1,0:T(8,128)(2,1)} %bitcast.213, bf16[4096,1024]{1,0:T(8,128)(2,1)} %bitcast.215, ...), custom_call_target="tpu_custom_call" | custom-call | flops 12884901888 | bytes 29360128 | tf_op jit(solution)/shard_map/expert_back/pallas_call | solution.py:580
  309.5 12.7 %all-to-all-done.3.grad_ref = bf16[8,96,1024]{2,1,0:T(8,128)(2,1)S(1)} async-done(((bf16[8,96,1024]{2,1,0:T(8,128)(2,1)}), bf16[8,96,1024]{2,1,0:T(8,128)(2,1)S(1)}, u32[]{:S(2)}, u32[]{:S(2)}) %all-to-all-start.3) | async-done | bytes 1572896 | tf_op jit(solution)/shard_map/all_to_all | solution.py:765
  322.2 19.4 %bitcast_convert_fusion.1 = bf16[4096,1024]{1,0:T(8,128)(2,1)} fusion(bf16[8,192,4096]{2,1,0:T(8,128)(2,1)} %get-tuple-element.94, bf16[8,96,1024]{2,1,0:T(8,128)(2,1)S(1)} %all-to-all-done.3.grad_ref, bf16[8,96,1024]{2,1,0:T(8,128)(2,1)} %all-to-all-done.2.grad_ref), kind=kOutput, calls=%fused_computation.1 | convolution fusion | flops 12895387648 | bytes 24117248 | tf_op jit(solution)/shard_map/dot_general | solution.py:799
  347.4 24.9 %expert_back.3 = (bf16[8,192,4096]{2,1,0:T(8,128)(2,1)}, bf16[8,96,1024]{2,1,0:T(8,128)(2,1)}, f32[8,1024]{1,0:T(8,128)}) custom-call(bf16[8,96,1024]{2,1,0:T(8,128)(2,1)} %copy-done.30, bf16[8,96,4096]{2,1,0:T(8,128)(2,1)} %get-tuple-element.102.slope_ref, bf16[1024,4096]{1,0:T(8,128)(2,1)} %bitcast.214, ...), custom_call_target="tpu_custom_call", output_to_operand_aliasing={{0}: (7, {})} | custom-call | flops 12884901888 | bytes 29360128 | tf_op jit(solution)/shard_map/expert_back/pallas_call | solution.py:580
  372.4 10.1 %all-to-all-done.4 = bf16[8,96,1024]{2,1,0:T(8,128)(2,1)S(1)} async-done(((bf16[8,96,1024]{2,1,0:T(8,128)(2,1)}), bf16[8,96,1024]{2,1,0:T(8,128)(2,1)S(1)}, u32[]{:S(2)}, u32[]{:S(2)}) %all-to-all-start.4) | async-done | bytes 1572896 | tf_op jit(solution)/shard_map/all_to_all | solution.py:765
  388.3 19.5 %bitcast_convert_fusion = bf16[1024,4096]{1,0:T(8,128)(2,1)} fusion(bf16[8,192,4096]{2,1,0:T(8,128)(2,1)} %get-tuple-element.108, bf16[8,96,1024]{2,1,0:T(8,128)(2,1)} %copy-done.29, bf16[8,96,1024]{2,1,0:T(8,128)(2,1)} %all_to_all.44.x_ref), kind=kOutput, calls=%fused_computation | convolution fusion | flops 12895387648 | bytes 24117248 | tf_op jit(solution)/shard_map/dot_general | solution.py:826
  407.9 15.5 %all-to-all-done.5 = bf16[8,96,1024]{2,1,0:T(8,128)(2,1)} async-done(((bf16[8,96,1024]{2,1,0:T(8,128)(2,1)}), bf16[8,96,1024]{2,1,0:T(8,128)(2,1)}, u32[]{:S(2)}, u32[]{:S(2)}) %all-to-all-start.5) | async-done | bytes 1572896 | tf_op jit(solution)/shard_map/all_to_all | solution.py:765
  423.4 11.9 %before_attend_back.1 = (f32[1024,1024]{1,0:T(8,128)}, bf16[1024,1024]{1,0:T(8,128)(2,1)S(1)}, bf16[1024,1024]{1,0:T(8,128)(2,1)}, f32[16,1024]{1,0:T(8,128)S(1)}) custom-call(bf16[768,1024]{1,0:T(8,128)(2,1)S(1)} %bitcast.169, bf16[768,1024]{1,0:T(8,128)(2,1)} %bitcast.20.refs_1_, s32[1024,1]{1,0:T(8,128)S(1)} %fusion.53.refs_2_, ...), custom_call_target="tpu_custom_call" | custom-call | flops 5368709120 | bytes 16777216 | tf_op jit(solution)/shard_map/before_attend_back/pallas_call | solution.py:346
  445.2 5.0 all-to-all-start.6
  450.3 9.9 %attend_back.4.refs_0_ = bf16[1024,768]{1,0:T(8,128)(2,1)S(1)} custom-call(bf16[1024,3072]{1,0:T(8,128)(2,1)} %fusion.2.q_ref.k_ref.v_ref, bf16[1024,3072]{1,0:T(8,128)(2,1)} %fusion.2.q_ref.k_ref.v_ref, bf16[1024,3072]{1,0:T(8,128)(2,1)} %fusion.2.q_ref.k_ref.v_ref, bf16[1024,1024]{1,0:T(8,128)(2,1)S(1)} %copy-done.2, bf16[1024,1024]{1,0:T(8,128)(2,1)} %copy-done, ...), custom_call_target="tpu_custom_call" | custom-call | flops 5368709120 | bytes 4194304 | tf_op jit(solution)/shard_map/attend_back/pallas_call | solution.py:183
  464.2 9.9 %attend_back.5.refs_1_ = bf16[1024,768]{1,0:T(8,128)(2,1)S(1)} custom-call(bf16[1024,3072]{1,0:T(8,128)(2,1)} %fusion.2.q_ref.k_ref.v_ref, bf16[1024,3072]{1,0:T(8,128)(2,1)} %fusion.2.q_ref.k_ref.v_ref, bf16[1024,3072]{1,0:T(8,128)(2,1)} %fusion.2.q_ref.k_ref.v_ref, bf16[1024,1024]{1,0:T(8,128)(2,1)S(1)} %copy-done.2, bf16[1024,1024]{1,0:T(8,128)(2,1)} %copy-done, ...), custom_call_target="tpu_custom_call" | custom-call | flops 5368709120 | bytes 4194304 | tf_op jit(solution)/shard_map/attend_back/pallas_call | solution.py:183
  480.4 9.5 %attend_back.6.refs_2_ = bf16[1024,768]{1,0:T(8,128)(2,1)S(1)} custom-call(bf16[1024,3072]{1,0:T(8,128)(2,1)} %fusion.2.q_ref.k_ref.v_ref, bf16[1024,3072]{1,0:T(8,128)(2,1)} %fusion.2.q_ref.k_ref.v_ref, bf16[1024,3072]{1,0:T(8,128)(2,1)} %fusion.2.q_ref.k_ref.v_ref, bf16[1024,1024]{1,0:T(8,128)(2,1)S(1)} %copy-done.2, bf16[1024,1024]{1,0:T(8,128)(2,1)} %copy-done, ...), custom_call_target="tpu_custom_call" | custom-call | flops 5368709120 | bytes 4194304 | tf_op jit(solution)/shard_map/attend_back/pallas_call | solution.py:183
  493.0 15.3 %collective-permute-done.2 = bf16[4,32,1152]{2,1,0:T(8,128)(2,1)S(1)} collective-permute-done((bf16[4,32,1152]{2,1,0:T(8,128)(2,1)S(1)}, bf16[4,32,1152]{2,1,0:T(8,128)(2,1)S(1)}, u32[]{:S(2)}, u32[]{:S(2)}) %collective-permute-start.2) | collective-permute-done | bytes 294944 | tf_op jit(solution)/shard_map/ppermute | solution.py:648
  510.8 10.8 %all-to-all-done.6 = bf16[8,192,1024]{2,1,0:T(8,128)(2,1)} async-done(((bf16[8,192,1024]{2,1,0:T(8,128)(2,1)}), bf16[8,192,1024]{2,1,0:T(8,128)(2,1)}, u32[]{:S(2)}, u32[]{:S(2)}) %all-to-all-start.6) | async-done | bytes 3145760 | tf_op jit(solution)/shard_map/all_to_all | solution.py:765
  521.6 9.7 %attend_back.7.refs_3_ = bf16[1024,768]{1,0:T(8,128)(2,1)S(1)} custom-call(bf16[1024,3072]{1,0:T(8,128)(2,1)} %fusion.2.q_ref.k_ref.v_ref, bf16[1024,3072]{1,0:T(8,128)(2,1)} %fusion.2.q_ref.k_ref.v_ref, bf16[1024,3072]{1,0:T(8,128)(2,1)} %fusion.2.q_ref.k_ref.v_ref, bf16[1024,1024]{1,0:T(8,128)(2,1)S(1)} %copy-done.2, bf16[1024,1024]{1,0:T(8,128)(2,1)} %copy-done, ...), custom_call_target="tpu_custom_call" | custom-call | flops 5368709120 | bytes 4194304 | tf_op jit(solution)/shard_map/attend_back/pallas_call | solution.py:183
  547.8 6.6 collective-permute-done.10
  554.4 7.2 %collective-permute-done.8 = bf16[4,32,1536]{2,1,0:T(8,128)(2,1)S(1)} collective-permute-done((bf16[4,32,1536]{2,1,0:T(8,128)(2,1)S(1)}, bf16[4,32,1536]{2,1,0:T(8,128)(2,1)S(1)}, u32[]{:S(2)}, u32[]{:S(2)}) %collective-permute-start.8) | collective-permute-done | bytes 393248 | tf_op jit(solution)/shard_map/ppermute | solution.py:648
  571.2 13.8 %input_gradient.1 = (f32[1024,1024]{1,0:T(8,128)}, f32[16,1024]{1,0:T(8,128)S(1)}) custom-call(bf16[1024,768]{1,0:T(8,128)(2,1)S(1)} %copy-done.6, bf16[1024,768]{1,0:T(8,128)(2,1)S(1)} %copy-done.8, bf16[1024,768]{1,0:T(8,128)(2,1)S(1)} %copy-done.10, bf16[1024,768]{1,0:T(8,128)(2,1)} %copy-done.11, ...), custom_call_target="tpu_custom_call" | custom-call | flops 6442450944 | bytes 16777216 | tf_op jit(solution)/shard_map/input_gradient/pallas_call | solution.py:403
  586.7 8.9 %collective-permute-done.17 = bf16[4,32,1536]{2,1,0:T(8,128)(2,1)S(1)} collective-permute-done((bf16[4,32,1536]{2,1,0:T(8,128)(2,1)S(1)}, bf16[4,32,1536]{2,1,0:T(8,128)(2,1)S(1)}, u32[]{:S(2)}, u32[]{:S(2)}) %collective-permute-start.17) | collective-permute-done | bytes 393248 | tf_op jit(solution)/shard_map/ppermute | solution.py:648
  606.8 7.7 %activations_of.1 = bf16[1024,1024]{1,0:T(8,128)(2,1)} custom-call(bf16[1536,1024]{1,0:T(8,128)(2,1)} %bitcast.36.refs_0_, s32[1024,1]{1,0:T(8,128)S(1)} %copy.141.refs_1_, f32[1024,128]{1,0:T(8,128)S(1)} %get-tuple-element.137.refs_2_, f32[1024,1024]{1,0:T(8,128)} %get-tuple-element.110.refs_3_), custom_call_target="tpu_custom_call" | custom-call | flops 3221225472 | bytes 10485760 | tf_op jit(solution)/shard_map/activations_of/pallas_call | solution.py:436
  652.9 10.5 %multiply_add_fusion = (f32[1,4096,256]{2,1,0:T(8,128)}, f32[1,4096,256]{2,1,0:T(8,128)}, f32[1,4096,256]{2,1,0:T(8,128)}) fusion(f32[1,4096,256]{2,1,0:T(8,128)} %param.43, f32[1,4096,256]{2,1,0:T(8,128)} %param.31, f32[]{:T(128)S(6)} %div.65, bf16[1,4096,256]{2,1,0:T(8,128)(2,1)S(1)} %copy-done.20, f32[1,4096,256]{2,1,0:T(8,128)} %param.37), kind=kLoop, calls=%fused_computation.27 | loop fusion | flops 11534336 | bytes 27262980 | tf_op jit(solution)/shard_map/add | solution.py:683
  663.4 11.9 %multiply_add_fusion.1 = (f32[1,256,4096]{2,1,0:T(8,128)}, f32[1,256,4096]{2,1,0:T(8,128)}, f32[1,256,4096]{2,1,0:T(8,128)}) fusion(f32[1,256,4096]{2,1,0:T(8,128)} %param.42, f32[1,256,4096]{2,1,0:T(8,128)} %param.30, f32[]{:T(128)S(6)} %div.65, bf16[1,256,4096]{2,1,0:T(8,128)(2,1)} %reduce-scatter.3.cloned.1.call-done, f32[1,256,4096]{2,1,0:T(8,128)} %param.36), kind=kLoop, calls=%fused_computation.28 | loop fusion | flops 11534336 | bytes 27262980 | tf_op jit(solution)/shard_map/add | solution.py:683
  (297 shorter events, 145.3 us)
Async XLA Ops:
  7.2 85.5 %all-gather.4.cloned.1.call-start = ((), (), s32[]{:S(2)}) async-start(), calls=%async_computation.10 | async-start | bytes 8921088 | tf_op jit(solution)/shard_map/all_gather | solution.py:727
  11.4 194.8 %all-gather.6.cloned.1.call-start = ((), (), s32[]{:S(2)}) async-start(), calls=%async_computation.11 | async-start | bytes 10485760 | tf_op jit(solution)/shard_map/all_gather | solution.py:728
  15.3 245.7 %all-gather.8.cloned.1.call-start = ((), (), s32[]{:S(2)}) async-start(), calls=%async_computation.12 | async-start | bytes 10485760 | tf_op jit(solution)/shard_map/all_gather | solution.py:729
  194.8 40.6 %all-to-all-start.1 = ((bf16[8,96,1024]{2,1,0:T(8,128)(2,1)}), bf16[8,96,1024]{2,1,0:T(8,128)(2,1)S(1)}, u32[]{:S(2)}, u32[]{:S(2)}) async-start(bf16[8,96,1024]{2,1,0:T(8,128)(2,1)} %bitcast.11), calls=%async_computation.1 | async-start | bytes 3145728 | tf_op jit(solution)/shard_map/all_to_all | solution.py:765
  235.4 44.7 %all-to-all-start.2 = ((bf16[8,96,1024]{2,1,0:T(8,128)(2,1)}), bf16[8,96,1024]{2,1,0:T(8,128)(2,1)}, u32[]{:S(2)}, u32[]{:S(2)}) async-start(bf16[8,96,1024]{2,1,0:T(8,128)(2,1)} %bitcast.197), calls=%async_computation.2 | async-start | bytes 3145728 | tf_op jit(solution)/shard_map/all_to_all | solution.py:765
  280.2 42.1 %all-to-all-start.3 = ((bf16[8,96,1024]{2,1,0:T(8,128)(2,1)}), bf16[8,96,1024]{2,1,0:T(8,128)(2,1)S(1)}, u32[]{:S(2)}, u32[]{:S(2)}) async-start(bf16[8,96,1024]{2,1,0:T(8,128)(2,1)} %bitcast.196), calls=%async_computation.3 | async-start | bytes 3145728 | tf_op jit(solution)/shard_map/all_to_all | solution.py:765
  286.1 333.5 %reduce-scatter.5.cloned.1.call-start = ((), (), s32[]{:S(2)}) async-start(), calls=%async_computation.14 | async-start | bytes 10485760 | tf_op jit(solution)/shard_map/reduce_scatter | solution.py:824
  341.7 40.8 %all-to-all-start.4 = ((bf16[8,96,1024]{2,1,0:T(8,128)(2,1)}), bf16[8,96,1024]{2,1,0:T(8,128)(2,1)S(1)}, u32[]{:S(2)}, u32[]{:S(2)}) async-start(bf16[8,96,1024]{2,1,0:T(8,128)(2,1)} %get-tuple-element.105), calls=%async_computation.4 | async-start | bytes 3145728 | tf_op jit(solution)/shard_map/all_to_all | solution.py:765
  382.5 40.9 %all-to-all-start.5 = ((bf16[8,96,1024]{2,1,0:T(8,128)(2,1)}), bf16[8,96,1024]{2,1,0:T(8,128)(2,1)}, u32[]{:S(2)}, u32[]{:S(2)}) async-start(bf16[8,96,1024]{2,1,0:T(8,128)(2,1)} %get-tuple-element.107), calls=%async_computation.5 | async-start | bytes 3145728 | tf_op jit(solution)/shard_map/all_to_all | solution.py:765
  386.8 236.0 %reduce-scatter.3.cloned.1.call-start = ((), (), s32[]{:S(2)}) async-start(), calls=%async_computation.13 | async-start | bytes 10485760 | tf_op jit(solution)/shard_map/reduce_scatter | solution.py:834
  445.2 16.9 %collective-permute-start = (bf16[8,2,32,1152]{3,2,1,0:T(8,128)(2,1)}, bf16[8,2,32,1152]{3,2,1,0:T(8,128)(2,1)}, u32[]{:S(2)}, u32[]{:S(2)}) collective-permute-start(bf16[8,2,32,1152]{3,2,1,0:T(8,128)(2,1)} %fusion.41), channel_id=1, source_target_pairs={{0,1},{1,0},{2,3},{3,2},{4,5},{5,4},{6,7},{7,6},{8,9},{9,8},{10,11... | collective-permute-start | bytes 3538952 | tf_op jit(solution)/shard_map/ppermute | solution.py:629
  445.2 76.4 %all-to-all-start.6 = ((bf16[8,192,1024]{2,1,0:T(8,128)(2,1)}), bf16[8,192,1024]{2,1,0:T(8,128)(2,1)}, u32[]{:S(2)}, u32[]{:S(2)}) async-start(bf16[8,192,1024]{2,1,0:T(8,128)(2,1)} %bitcast.193), calls=%async_computation.6 | async-start | bytes 6291456 | tf_op jit(solution)/shard_map/all_to_all | solution.py:765
  476.4 32.9 %collective-permute-start.4 = (bf16[8,2,32,1536]{3,2,1,0:T(8,128)(2,1)S(1)}, bf16[8,2,32,1536]{3,2,1,0:T(8,128)(2,1)S(1)}, u32[]{:S(2)}, u32[]{:S(2)}) collective-permute-start(bf16[8,2,32,1536]{3,2,1,0:T(8,128)(2,1)S(1)} %dynamic-slice_bitcast_fusion.1), channel_id=1, source_target_pairs={{0,1},{1,0},{2,3},{3,2},{4,5},{5,4},{6,7},{7,6},{8,9},{9,8},{10,11... | collective-permute-start | bytes 4718600 | tf_op jit(solution)/shard_map/ppermute | solution.py:629
  476.8 16.2 %collective-permute-start.1 = (bf16[4,32,1152]{2,1,0:T(8,128)(2,1)S(1)}, bf16[4,32,1152]{2,1,0:T(8,128)(2,1)S(1)}, u32[]{:S(2)}, u32[]{:S(2)}) collective-permute-start(bf16[4,32,1152]{2,1,0:T(8,128)(2,1)S(1)} %get-tuple-element.171), channel_id=1, source_target_pairs={{0,2},{1,3},{2,0},{3,1},{4,6},{5,7},{6,4},{7,5},{8,10},{9,11},{10,... | collective-permute-start | bytes 884744 | tf_op jit(solution)/shard_map/ppermute | solution.py:648
  478.2 30.1 %collective-permute-start.2 = (bf16[4,32,1152]{2,1,0:T(8,128)(2,1)S(1)}, bf16[4,32,1152]{2,1,0:T(8,128)(2,1)S(1)}, u32[]{:S(2)}, u32[]{:S(2)}) collective-permute-start(bf16[4,32,1152]{2,1,0:T(8,128)(2,1)S(1)} %get-tuple-element.173), channel_id=1, source_target_pairs={{0,4},{1,5},{2,6},{3,7},{4,0},{5,1},{6,2},{7,3},{8,12},{9,13},{10,... | collective-permute-start | bytes 884744 | tf_op jit(solution)/shard_map/ppermute | solution.py:648
  479.8 28.5 %collective-permute-start.3 = (bf16[4,32,1152]{2,1,0:T(8,128)(2,1)S(1)}, bf16[4,32,1152]{2,1,0:T(8,128)(2,1)S(1)}, u32[]{:S(2)}, u32[]{:S(2)}) collective-permute-start(bf16[4,32,1152]{2,1,0:T(8,128)(2,1)S(1)} %get-tuple-element.172), channel_id=1, source_target_pairs={{0,6},{1,7},{2,4},{3,5},{4,2},{5,3},{6,0},{7,1},{8,14},{9,15},{10,... | collective-permute-start | bytes 884744 | tf_op jit(solution)/shard_map/ppermute | solution.py:648
  536.5 25.4 %collective-permute-start.11 = (bf16[8,2,32,1536]{3,2,1,0:T(8,128)(2,1)}, bf16[8,2,32,1536]{3,2,1,0:T(8,128)(2,1)}, u32[]{:S(2)}, u32[]{:S(2)}) collective-permute-start(bf16[8,2,32,1536]{3,2,1,0:T(8,128)(2,1)} %dynamic-slice_bitcast_fusion), channel_id=1, source_target_pairs={{0,1},{1,0},{2,3},{3,2},{4,5},{5,4},{6,7},{7,6},{8,9},{9,8},{10,11... | collective-permute-start | bytes 4718600 | tf_op jit(solution)/shard_map/ppermute | solution.py:629
  536.9 9.6 %collective-permute-start.6 = (bf16[32,1152]{1,0:T(8,128)(2,1)S(1)}, bf16[32,1152]{1,0:T(8,128)(2,1)S(1)}, u32[]{:S(2)}, u32[]{:S(2)}) collective-permute-start(bf16[32,1152]{1,0:T(8,128)(2,1)S(1)} %get-tuple-element.182), channel_id=1, source_target_pairs={{0,16},{1,17},{2,18},{3,19},{4,20},{5,21},{6,22},{7,23},{8,24},{9,... | collective-permute-start | bytes 221192 | tf_op jit(solution)/shard_map/ppermute | solution.py:648
  540.2 7.5 %collective-permute-start.7 = (bf16[32,1152]{1,0:T(8,128)(2,1)S(1)}, bf16[32,1152]{1,0:T(8,128)(2,1)S(1)}, u32[]{:S(2)}, u32[]{:S(2)}) collective-permute-start(bf16[32,1152]{1,0:T(8,128)(2,1)S(1)} %get-tuple-element.181), channel_id=1, source_target_pairs={{0,24},{1,25},{2,26},{3,27},{4,28},{5,29},{6,30},{7,31},{8,16},{9,... | collective-permute-start | bytes 221192 | tf_op jit(solution)/shard_map/ppermute | solution.py:648
  541.4 13.0 %collective-permute-start.10 = (bf16[4,32,1536]{2,1,0:T(8,128)(2,1)S(1)}, bf16[4,32,1536]{2,1,0:T(8,128)(2,1)S(1)}, u32[]{:S(2)}, u32[]{:S(2)}) collective-permute-start(bf16[4,32,1536]{2,1,0:T(8,128)(2,1)S(1)} %get-tuple-element.169), channel_id=1, source_target_pairs={{0,6},{1,7},{2,4},{3,5},{4,2},{5,3},{6,0},{7,1},{8,14},{9,15},{10,... | collective-permute-start | bytes 1179656 | tf_op jit(solution)/shard_map/ppermute | solution.py:648
  543.7 18.0 %collective-permute-start.8 = (bf16[4,32,1536]{2,1,0:T(8,128)(2,1)S(1)}, bf16[4,32,1536]{2,1,0:T(8,128)(2,1)S(1)}, u32[]{:S(2)}, u32[]{:S(2)}) collective-permute-start(bf16[4,32,1536]{2,1,0:T(8,128)(2,1)S(1)} %get-tuple-element.168), channel_id=1, source_target_pairs={{0,2},{1,3},{2,0},{3,1},{4,6},{5,7},{6,4},{7,5},{8,10},{9,11},{10,... | collective-permute-start | bytes 1179656 | tf_op jit(solution)/shard_map/ppermute | solution.py:648
  546.5 15.2 %collective-permute-start.9 = (bf16[4,32,1536]{2,1,0:T(8,128)(2,1)S(1)}, bf16[4,32,1536]{2,1,0:T(8,128)(2,1)S(1)}, u32[]{:S(2)}, u32[]{:S(2)}) collective-permute-start(bf16[4,32,1536]{2,1,0:T(8,128)(2,1)S(1)} %get-tuple-element.170), channel_id=1, source_target_pairs={{0,4},{1,5},{2,6},{3,7},{4,0},{5,1},{6,2},{7,3},{8,12},{9,13},{10,... | collective-permute-start | bytes 1179656 | tf_op jit(solution)/shard_map/ppermute | solution.py:648
  564.1 22.6 %collective-permute-start.15 = (bf16[4,32,1536]{2,1,0:T(8,128)(2,1)S(1)}, bf16[4,32,1536]{2,1,0:T(8,128)(2,1)S(1)}, u32[]{:S(2)}, u32[]{:S(2)}) collective-permute-start(bf16[4,32,1536]{2,1,0:T(8,128)(2,1)S(1)} %get-tuple-element.165), channel_id=1, source_target_pairs={{0,2},{1,3},{2,0},{3,1},{4,6},{5,7},{6,4},{7,5},{8,10},{9,11},{10,... | collective-permute-start | bytes 1179656 | tf_op jit(solution)/shard_map/ppermute | solution.py:648
  565.3 21.3 %collective-permute-start.16 = (bf16[4,32,1536]{2,1,0:T(8,128)(2,1)S(1)}, bf16[4,32,1536]{2,1,0:T(8,128)(2,1)S(1)}, u32[]{:S(2)}, u32[]{:S(2)}) collective-permute-start(bf16[4,32,1536]{2,1,0:T(8,128)(2,1)S(1)} %get-tuple-element.167), channel_id=1, source_target_pairs={{0,4},{1,5},{2,6},{3,7},{4,0},{5,1},{6,2},{7,3},{8,12},{9,13},{10,... | collective-permute-start | bytes 1179656 | tf_op jit(solution)/shard_map/ppermute | solution.py:648
  566.8 18.3 %collective-permute-start.12 = (bf16[32,1536]{1,0:T(8,128)(2,1)S(1)}, bf16[32,1536]{1,0:T(8,128)(2,1)S(1)}, u32[]{:S(2)}, u32[]{:S(2)}) collective-permute-start(bf16[32,1536]{1,0:T(8,128)(2,1)S(1)} %get-tuple-element.177), channel_id=1, source_target_pairs={{0,8},{1,9},{2,10},{3,11},{4,12},{5,13},{6,14},{7,15},{8,0},{9,1},... | collective-permute-start | bytes 294920 | tf_op jit(solution)/shard_map/ppermute | solution.py:648
  566.8 19.1 %collective-permute-start.13 = (bf16[32,1536]{1,0:T(8,128)(2,1)S(1)}, bf16[32,1536]{1,0:T(8,128)(2,1)S(1)}, u32[]{:S(2)}, u32[]{:S(2)}) collective-permute-start(bf16[32,1536]{1,0:T(8,128)(2,1)S(1)} %get-tuple-element.179), channel_id=1, source_target_pairs={{0,16},{1,17},{2,18},{3,19},{4,20},{5,21},{6,22},{7,23},{8,24},{9,... | collective-permute-start | bytes 294920 | tf_op jit(solution)/shard_map/ppermute | solution.py:648
  569.5 16.4 %collective-permute-start.14 = (bf16[32,1536]{1,0:T(8,128)(2,1)S(1)}, bf16[32,1536]{1,0:T(8,128)(2,1)S(1)}, u32[]{:S(2)}, u32[]{:S(2)}) collective-permute-start(bf16[32,1536]{1,0:T(8,128)(2,1)S(1)} %get-tuple-element.178), channel_id=1, source_target_pairs={{0,24},{1,25},{2,26},{3,27},{4,28},{5,29},{6,30},{7,31},{8,16},{9,... | collective-permute-start | bytes 294920 | tf_op jit(solution)/shard_map/ppermute | solution.py:648
  585.0 10.5 %collective-permute-start.17 = (bf16[4,32,1536]{2,1,0:T(8,128)(2,1)S(1)}, bf16[4,32,1536]{2,1,0:T(8,128)(2,1)S(1)}, u32[]{:S(2)}, u32[]{:S(2)}) collective-permute-start(bf16[4,32,1536]{2,1,0:T(8,128)(2,1)S(1)} %get-tuple-element.166), channel_id=1, source_target_pairs={{0,6},{1,7},{2,4},{3,5},{4,2},{5,3},{6,0},{7,1},{8,14},{9,15},{10,... | collective-permute-start | bytes 1179656 | tf_op jit(solution)/shard_map/ppermute | solution.py:648
  596.6 18.6 %all-to-all-start.7 = ((f32[32,1,64]{2,1,0:T(1,128)}), f32[32,1,64]{2,1,0:T(1,128)S(1)}, u32[]{:S(2)}, u32[]{:S(2)}) async-start(f32[32,1,64]{2,1,0:T(1,128)} %bitcast.64), calls=%async_computation.7 | async-start | bytes 32768 | tf_op jit(solution)/shard_map/all_to_all | solution.py:893
  600.1 15.8 %collective-permute-start.18 = (bf16[32,1536]{1,0:T(8,128)(2,1)S(1)}, bf16[32,1536]{1,0:T(8,128)(2,1)S(1)}, u32[]{:S(2)}, u32[]{:S(2)}) collective-permute-start(bf16[32,1536]{1,0:T(8,128)(2,1)S(1)} %get-tuple-element.174), channel_id=1, source_target_pairs={{0,8},{1,9},{2,10},{3,11},{4,12},{5,13},{6,14},{7,15},{8,0},{9,1},... | collective-permute-start | bytes 294920 | tf_op jit(solution)/shard_map/ppermute | solution.py:648
  602.1 13.9 %collective-permute-start.19 = (bf16[32,1536]{1,0:T(8,128)(2,1)S(1)}, bf16[32,1536]{1,0:T(8,128)(2,1)S(1)}, u32[]{:S(2)}, u32[]{:S(2)}) collective-permute-start(bf16[32,1536]{1,0:T(8,128)(2,1)S(1)} %get-tuple-element.176), channel_id=1, source_target_pairs={{0,16},{1,17},{2,18},{3,19},{4,20},{5,21},{6,22},{7,23},{8,24},{9,... | collective-permute-start | bytes 294920 | tf_op jit(solution)/shard_map/ppermute | solution.py:648
  604.5 11.5 %collective-permute-start.20 = (bf16[32,1536]{1,0:T(8,128)(2,1)S(1)}, bf16[32,1536]{1,0:T(8,128)(2,1)S(1)}, u32[]{:S(2)}, u32[]{:S(2)}) collective-permute-start(bf16[32,1536]{1,0:T(8,128)(2,1)S(1)} %get-tuple-element.175), channel_id=1, source_target_pairs={{0,24},{1,25},{2,26},{3,27},{4,28},{5,29},{6,30},{7,31},{8,16},{9,... | collective-permute-start | bytes 294920 | tf_op jit(solution)/shard_map/ppermute | solution.py:648
  (60 other events, 685.2 us)
Sparse Core Ops, SparseCore 0:
  11.5 81.1 all-gather.3
  94.8 56.8 all-gather.5
  153.9 59.3 all-gather.7
  341.8 70.3 reduce-scatter.4
  437.2 84.6 reduce-scatter.2

commit v3 on v2

--- a/solution.py
+++ b/solution.py
@@ -34,6 +34,12 @@
     0.35459055762612957,
     -0.10013360714943426,
 )
+
+
+def hint(microseconds):
+    return pl.CostEstimate(
+        flops=int(microseconds * 1.9e8), bytes_accessed=0, transcendentals=0
+    )
 
 
 def dot_rows(left, right):
@@ -119,9 +125,7 @@
         ],
         scratch_shapes=[pltpu.VMEM((SEQ, SEQ), f32)],
         compiler_params=pltpu.CompilerParams(vmem_limit_bytes=48 * 2**20),
-        cost_estimate=pl.CostEstimate(
-            flops=4 * count * SEQ * width, bytes_accessed=8 * count * width, transcendentals=0
-        ),
+        cost_estimate=hint(29),
         name="attend",
     )(packed, packed, packed, doc_col, doc_row)
 
@@ -197,11 +201,7 @@
         out_shape=jax.ShapeDtypeStruct((tokens, 3 * count * LANES), low),
         scratch_shapes=[pltpu.VMEM((SEQ, SEQ), f32), pltpu.VMEM((LANES, SEQ), f32)],
         compiler_params=pltpu.CompilerParams(vmem_limit_bytes=48 * 2**20),
-        cost_estimate=pl.CostEstimate(
-            flops=20 * tokens * SEQ * count * LANES,
-            bytes_accessed=16 * tokens * count * LANES,
-            transcendentals=0,
-        ),
+        cost_estimate=hint(4.8 * count),
         name="attend_back",
     )(packed, packed, packed, grad_mixed, mixed, lse, doc_col, doc_row)
 
@@ -292,11 +292,7 @@
         + [jax.ShapeDtypeStruct((rows, width), low) for rows in chunk_rows],
         scratch_shapes=[pltpu.VMEM((count, width), low)],
         compiler_params=pltpu.CompilerParams(vmem_limit_bytes=48 * 2**20),
-        cost_estimate=pl.CostEstimate(
-            flops=2 * count * width * (width + sum(chunk_rows)),
-            bytes_accessed=12 * count * width,
-            transcendentals=0,
-        ),
+        cost_estimate=hint(13),
         name="after_attend",
     )(*mixed, proj, tokens, out_grad, norms, centres, routes, slot_row)
 
@@ -362,9 +358,7 @@
             jax.ShapeDtypeStruct((16, width), f32),
         ],
         compiler_params=pltpu.CompilerParams(vmem_limit_bytes=48 * 2**20),
-        cost_estimate=pl.CostEstimate(
-            flops=5 * count * width * width, bytes_accessed=16 * count * width, transcendentals=0
-        ),
+        cost_estimate=hint(12),
         name="before_attend_back",
     )(*rows, slot_col, after, out_grad, norms, proj)
 
@@ -416,9 +410,7 @@
             jax.ShapeDtypeStruct((16, width), f32),
         ],
         compiler_params=pltpu.CompilerParams(vmem_limit_bytes=48 * 2**20),
-        cost_estimate=pl.CostEstimate(
-            flops=6 * count * width * width, bytes_accessed=16 * count * width, transcendentals=0
-        ),
+        cost_estimate=hint(14),
         name="input_gradient",
     )(*grads, dense, tokens, norms, grad_after)
 
@@ -445,9 +437,7 @@
         out_specs=tile,
         out_shape=jax.ShapeDtypeStruct((count, width), low),
         compiler_params=pltpu.CompilerParams(vmem_limit_bytes=48 * 2**20),
-        cost_estimate=pl.CostEstimate(
-            flops=3 * count * width * width, bytes_accessed=10 * count * width, transcendentals=0
-        ),
+        cost_estimate=hint(7.5),
         name="activations_of",
     )(*rows, slot_col, gate, after)
 
@@ -500,11 +490,7 @@
         ],
         input_output_aliases={} if buffer is None else {2: 0},
         compiler_params=pltpu.CompilerParams(vmem_limit_bytes=56 * 2**20),
-        cost_estimate=pl.CostEstimate(
-            flops=4 * experts * each * width * inner,
-            bytes_accessed=4 * (experts * each + width) * inner,
-            transcendentals=0,
-        ),
+        cost_estimate=hint(21),
         name="expert_forward",
     )(arrived, weight_in, *([] if buffer is None else [buffer]))
 
@@ -606,11 +592,7 @@
         ],
         input_output_aliases={} if buffer is None else {7: 0},
         compiler_params=pltpu.CompilerParams(vmem_limit_bytes=58 * 2**20),
-        cost_estimate=pl.CostEstimate(
-            flops=4 * experts * each * width * inner,
-            bytes_accessed=4 * (experts * each + width) * inner,
-            transcendentals=0,
-        ),
+        cost_estimate=hint(23),
         name="expert_back",
     )(
         grad_arrived,
@@ -624,17 +606,134 @@
     )
 
 
+def weight_grads_kernel(chunks, refs):
+    x_refs, grad_refs = refs[:chunks], refs[chunks : 2 * chunks]
+    grad_preact_ref, hidden_ref, in_out_ref, out_out_ref, turned = refs[2 * chunks :]
+    step = pl.program_id(0)
+    half = pl.num_programs(0) // 2
+
+    def turn_rows(chunk_refs):
+        for c, ref in enumerate(chunk_refs):
+            experts, each, width = ref.shape
+            group, size = row_groups(experts, each)
+            for e in range(0, experts, group):
+                turned[c, :, e * each : e * each + size] = (
+                    ref[e : e + group].reshape(size, width).T
+                )
+
+    pl.when(step == 0)(lambda: turn_rows(x_refs))
+    pl.when(step == half)(lambda: turn_rows(grad_refs))
+
+    def multiply(ref, out_ref):
+        experts, slots, tile = ref.shape
+        each = slots // chunks
+        right = [
+            ref[:, c * each : (c + 1) * each, :].reshape(experts * each, tile)
+            for c in range(chunks)
+        ]
+        for row in range(0, turned.shape[1], BLOCK):
+            rows = slice(row, row + BLOCK)
+            total = dot_rows(turned[0, rows, :], right[0])
+            for c in range(1, chunks):
+                total = total + dot_rows(turned[c, rows, :], right[c])
+            out_ref[rows, :] = total.astype(low)
+
+    pl.when(step < half)(lambda: multiply(grad_preact_ref, in_out_ref))
+    pl.when(step >= half)(lambda: multiply(hidden_ref, out_out_ref))
+
+
+def weight_grads(arrived, grad_arrived, grad_preact, hidden, tile=1024):
+    chunks = len(arrived)
+    experts, each, width = arrived[0].shape
+    slots, inner = hidden.shape[1:]
+    half = inner // tile
+    whole = pl.BlockSpec((experts, each, width), lambda j: (0, 0, 0))
+
+    def first(j):
+        return jnp.minimum(j, half - 1)
+
+    def second(j):
+        return jnp.maximum(j - half, 0)
+
+    return pl.pallas_call(
+        lambda *refs: weight_grads_kernel(chunks, refs),
+        grid=(2 * half,),
+        in_specs=[whole] * (2 * chunks)
+        + [
+            pl.BlockSpec((experts, slots, tile), lambda j: (0, 0, first(j))),
+            pl.BlockSpec((experts, slots, tile), lambda j: (0, 0, second(j))),
+        ],
+        out_specs=[
+            pl.BlockSpec((width, tile), lambda j: (0, first(j))),
+            pl.BlockSpec((width, tile), lambda j: (0, second(j))),
+        ],
+        out_shape=[jax.ShapeDtypeStruct((width, inner), low)] * 2,
+        scratch_shapes=[pltpu.VMEM((chunks, width, experts * each), low)],
+        compiler_params=pltpu.CompilerParams(vmem_limit_bytes=58 * 2**20),
+        cost_estimate=hint(38),
+        name="weight_grads",
+    )(*arrived, *grad_arrived, grad_preact, hidden)
+
+
+def turn_kernel(in_ref, out_ref, square_ref):
+    values = in_ref[...].astype(f32)
+    out_ref[...] = in_ref[...].T.astype(f32)
+    square = sum_slabs(values * values)
+
+    @pl.when(pl.program_id(0) == 0)
+    def _():
+        square_ref[...] = square
+
+    @pl.when(pl.program_id(0) > 0)
+    def _():
+        square_ref[...] += square
+
+
+def turn(values, tile=512):
+    rows, columns = values.shape
+    turned, square = pl.pallas_call(
+        turn_kernel,
+        grid=(columns // tile,),
+        in_specs=[pl.BlockSpec((rows, tile), lambda j: (0, j))],
+        out_specs=[
+            pl.BlockSpec((tile, rows), lambda j: (j, 0)),
+            pl.BlockSpec((8, tile), lambda j: (0, 0)),
+        ],
+        out_shape=[
+            jax.ShapeDtypeStruct((columns, rows), f32),
+            jax.ShapeDtypeStruct((8, tile), f32),
+        ],
+        cost_estimate=hint(3),
+        name="turn",
+    )(values)
+    return turned, jnp.sum(square)
+
+
 def swap(values, axis, distance):
     size = lax.axis_size(axis)
     return lax.ppermute(values, axis, [(i, i ^ distance) for i in range(size)])
 
 
-def sum_over_cores(held):
-    bit = lax.axis_index("dp") % 2
-    halves = held.reshape((held.shape[0], held.shape[1] // 2, 2) + held.shape[2:])
-    mine = lax.dynamic_index_in_dim(halves, bit, 2, keepdims=False)
-    theirs = lax.dynamic_index_in_dim(halves, 1 - bit, 2, keepdims=False)
-    return (mine.astype(f32) + swap(theirs, "dp", 1).astype(f32)).astype(low)
+def sum_halves(parts, axis, bit, at):
+    own = (lax.axis_index(axis) // bit) % 2
+
+    def side(which):
+        picked = []
+        for part in parts:
+            shape = part.shape
+            halves = part.reshape(shape[:at] + (shape[at] // 2, 2) + shape[at + 1 :])
+            picked.append(lax.dynamic_index_in_dim(halves, which, at + 1, keepdims=False))
+        return jnp.concatenate(picked, axis=-1)
+
+    return (side(own).astype(f32) + swap(side(1 - own), axis, bit).astype(f32)).astype(low)
+
+
+def sum_over_cores(parts):
+    return sum_halves(parts, "dp", 1, 1)
+
+
+def sum_over_neighbours(held):
+    return sum_halves([held], "expert", 1, 0)
 
 
 def sum_over_pairs(held, partners, keep):
@@ -650,16 +749,21 @@
 
 
 def sum_near(held):
-    far = held.shape[1]
-    held = held.reshape((held.shape[0] // 2, 2 * far) + held.shape[2:]).swapaxes(0, 1)
-    partners = [(i // far, i % far * 2) for i in range(1, 2 * far)]
-    keep = lax.axis_index("expert") % 2 * far + lax.axis_index("dp") // 2
+    near = held.shape[1]
+    held = held.reshape((held.shape[0] // 2, 2 * near) + held.shape[2:]).swapaxes(0, 1)
+    partners = [(i // near, i % near * 2) for i in range(1, 2 * near)]
+    keep = lax.axis_index("expert") % 2 * near + lax.axis_index("dp") // 2
     return sum_over_pairs(held, partners, keep).astype(low)
 
 
 def sum_far(held):
     partners = [(2 * i, 0) for i in range(1, held.shape[0])]
     return sum_over_pairs(held, partners, lax.axis_index("expert") // 2)
+
+
+def sum_across(held):
+    partners = [(0, 2 * i) for i in range(1, held.shape[0])]
+    return sum_over_pairs(held, partners, lax.axis_index("dp") // 2)
 
 
 def in_order(*values):
@@ -746,6 +850,7 @@
     doc_row = documents[None, :]
 
     normed_low = layer_norm(tokens.astype(f32), norms[0], norms[1]).astype(low)
+    normed_low, dense = in_order(normed_low, dense)
     packed = jnp.dot(normed_low, dense[:, : 3 * width], preferred_element_type=f32).astype(low)
     mixed, lse = attend(packed, doc_col, doc_row)
     after, grad_rows, gate, *outgoing = after_attend(
@@ -772,7 +877,9 @@
     arrived, slope, hidden = [], [], None
     for c in range(chunks):
         if c:
-            arrived[c - 1], outgoing[c] = in_order(arrived[c - 1], outgoing[c])
+            arrived[c - 1], outgoing[c], *grad_outgoing = in_order(
+                arrived[c - 1], outgoing[c], *grad_outgoing
+            )
         arrived.append(exchange(outgoing[c]))
     for c in range(chunks):
         if c == chunks - 1:
@@ -791,18 +898,10 @@
         )
         grad_arrived.append(exchange(grad_outgoing[c]))
     centre_row = lax.dynamic_slice_in_dim(centre_table, lax.axis_index("expert"), 1, 0)
-    grad_preact = grad_weight_out = None
+    grad_preact = None
     grad_input, grad_centre = [], 0.0
     for c in range(chunks):
         last = c == chunks - 1
-        if last:
-            grad_weight_out = lax.dot_general(
-                hidden,
-                jnp.concatenate(grad_arrived, axis=1).reshape(slots, width),
-                (((0,), (0,)), ((), ())),
-                preferred_element_type=f32,
-            ).astype(low)
-            grad_arrived[c], grad_weight_out = in_order(grad_arrived[c], grad_weight_out)
         grad_preact, rows_c, centre_c = expert_back(
             grad_arrived[c],
             slope[c],
@@ -821,18 +920,18 @@
             rows_c, grad_input[-1] = in_order(rows_c, grad_input[-1])
         grad_input.append(exchange(rows_c).reshape(slots // chunks, width))
         grad_centre = grad_centre + jnp.sum(centre_c, axis=0)
-    out_grad_w = lax.psum_scatter(grad_weight_out[None], "dp", scatter_dimension=2, tiled=True)
-    arrived = jnp.concatenate(arrived, axis=1)
-    grad_weight_in = lax.dot_general(
-        arrived.reshape(slots, width),
-        grad_preact.reshape(slots, -1),
-        (((0,), (0,)), ((), ())),
-        preferred_element_type=f32,
-    ).astype(low)
-    out_grad_w = out_grad_w.astype(f32)
-    result, grad_input[-1], grad_weight_in = in_order(result, grad_input[-1], grad_weight_in)
-    in_grad = lax.psum_scatter(grad_weight_in[None], "dp", scatter_dimension=1, tiled=True)
+    if chunks > 1:
+        hidden, arrived[0], grad_input[0] = in_order(hidden, arrived[0], grad_input[0])
+    grad_in, grad_out_turned = weight_grads(
+        arrived, grad_arrived, grad_preact, hidden.reshape(experts, slot_cap, -1)
+    )
+    result, grad_input[-1], grad_in, grad_out_turned = in_order(
+        result, grad_input[-1], grad_in, grad_out_turned
+    )
+    in_grad = lax.psum_scatter(grad_in[None], "dp", scatter_dimension=1, tiled=True)
+    out_turned = lax.psum_scatter(grad_out_turned[None], "dp", scatter_dimension=1, tiled=True)
     in_grad = in_grad.astype(f32)
+    in_square = jnp.sum(in_grad * in_grad)
     returned = exchange(result).reshape(slots, width)
 
     grad_after, grad_low, grad_mixed, sums_two = before_attend_back(
@@ -852,9 +951,8 @@
     each = width // LANES // groups
     wide = each * LANES
 
-    def begin(parts):
-        joined = jnp.concatenate(parts, axis=1)
-        return joined.reshape(experts, dp, rows_own, joined.shape[1])
+    def by_owner(values):
+        return values.reshape(experts, dp, rows_own, values.shape[1])
 
     def back_group(g):
         part = attend_back(packed, grad_mixed, mixed, lse, doc_col, doc_row, g * each, each)
@@ -864,40 +962,48 @@
         return part, grad.astype(low)
 
     parts, grads = [], []
-    rest = begin([grad_proj, extra])
+    rest = by_owner(jnp.concatenate([grad_proj, extra], axis=1))
     for g in range(groups):
         if g == 1:
-            rest = sum_over_cores(rest)
+            rest = sum_over_cores([rest])
             rest, grad_mixed = in_order(rest, grad_mixed)
         if g == groups - 1:
-            first = sum_over_cores(begin(grads[: groups // 2]))
-            rest = sum_near(rest)
+            rest = sum_over_neighbours(rest)
+            first = sum_over_cores([by_owner(v) for v in grads[: groups // 2]])
             rest, first, grad_mixed, returned = in_order(rest, first, grad_mixed, returned)
         part, grad = back_group(g)
         grad, grad_mixed = in_order(grad, grad_mixed)
         parts.append(part)
         grads.append(grad)
-    first = sum_near(first)
-    second = sum_over_cores(begin(grads[groups // 2 :]))
-    first, second, grad_after = in_order(first, second, grad_after)
+    second = sum_over_cores([by_owner(v) for v in grads[groups // 2 :]])
+    second, first, grad_after = in_order(second, first, grad_after)
     second = sum_near(second)
+    first = sum_over_neighbours(first)
     input_grad, sums_one = input_gradient(
         [(g * wide, wide) for g in range(groups)], parts, dense, tokens, norms, grad_after
     )
-    rest, first = sum_far(rest), sum_far(first)
-    rest, first, second, sums_one, gate = in_order(rest, first, second, sums_one, gate)
-    activations = activations_of([returned], slot_col, gate, after)
-    second = sum_far(second)
+    first, second, sums_one, gate, out_turned = in_order(
+        first, second, sums_one, gate, out_turned
+    )
     norm_one = jnp.sum(sums_one.reshape(2, 8, width), axis=1)
     norm_one = norm_one.reshape(2, devices, norm_own).transpose(1, 0, 2).reshape(devices, -1)
     norm_one = lax.all_to_all(norm_one, everywhere, split_axis=0, concat_axis=0, tiled=True)
     norm_one = jnp.sum(norm_one, axis=0).reshape(2, norm_own)
-
-    proj_grad = rest[:, :width]
-    extra = rest[:, width:].reshape(-1)
+    out_grad_w, out_square = turn(out_turned[0])
+    out_grad_w = out_grad_w[None]
+    activations = activations_of([returned], slot_col, gate, after)
+    second = sum_far(second)
+    first = sum_far(jnp.concatenate([rest, first], axis=-1)).astype(low)
+    first, second, in_square, out_square, norm_one, activations = in_order(
+        first, second, in_square, out_square, norm_one, activations
+    )
+    first = sum_across(first)
+
+    proj_grad = first[:, :width]
+    extra = first[:, width : width + LANES].reshape(-1)
     norm_grad = jnp.concatenate([norm_one, extra[: 2 * norm_own].reshape(2, norm_own)], axis=0)
     centre_grad = extra[2 * norm_own : 2 * norm_own + centre_own].reshape(centroids.shape)
-    owned = [first, second]
+    owned = [first[:, width + LANES :], second]
     qkv_grad = jnp.concatenate(
         [
             half[:, (3 * k + s) * wide : (3 * k + s + 1) * wide]
@@ -912,8 +1018,8 @@
         + jnp.sum(proj_grad * proj_grad)
         + jnp.sum(norm_grad * norm_grad)
         + jnp.sum(centre_grad * centre_grad)
-        + jnp.sum(in_grad * in_grad)
-        + jnp.sum(out_grad_w * out_grad_w)
+        + in_square
+        + out_square
     )
     grad_norm = jnp.sqrt(sum_everywhere(square_sum))
     factor = clip_limit / jnp.maximum(grad_norm, clip_limit)

time: 692 us -> 694 us (level)
  Pallas kernels: 205 us -> 248 us
  blocking collectives: 41.1 us -> 0 us
  matrix products: 91.1 us -> 51.7 us
  waiting for transfers between devices: 170 us -> 198 us
  other arithmetic: 65.1 us -> 74.7 us
    pallas_call x0 -> x2, Pallas kernels: none -> 44.4 us  [the longest x1 38 us: weight_grads(): pl.pallas_call(lambda *refs: weight_grads_kernel(chunks, refs), grid=(2 *...]
    all_to_all x1 -> x0, blocking collectives: 41.1 us -> none  [exchange(): lax.all_to_all(rows, 'expert', split_axis=0, concat_axis=0, tiled=True)]
    dot_general x2 -> x0, matrix products: 38.9 us -> none  [the longest x1 19.5 us: shards(): lax.dot_general(arrived.reshape(slots, width), grad_preact.reshape(slots,...]
    all_to_all x6 -> x7, waiting for transfers between devices: 57.1 us -> 79.3 us  [exchange(): lax.all_to_all(rows, 'expert', split_axis=0, concat_axis=0, tiled=True)]
    ppermute x8 -> x10, waiting for transfers between devices: 3 us -> 15.2 us  [swap(): return lax.ppermute(values, axis, [(i, i ^ distance) for i in range(size)])]
    ppermute x18 -> x10, starting transfers between devices: 24.9 us -> 15.2 us  [sum_over_pairs(): total = total + lax.ppermute(block, everywhere, perm).astype(f32)]
    all_to_all x6 -> x7, starting transfers between devices: 26.9 us -> 32.8 us  [exchange(): lax.all_to_all(rows, 'expert', split_axis=0, concat_axis=0, tiled=True)]
    ppermute x18 -> x10, waiting for transfers between devices: 40.1 us -> 37.1 us  [sum_over_pairs(): total = total + lax.ppermute(block, everywhere, perm).astype(f32)]
  transfers between devices with their start and end apart: 38 -> 33, of which waited for: 17 -> 18; matrix products, arithmetic and copies ran while one was open for 16% -> 15% of each run, Pallas kernels for 30% -> 36%
where the time goes in v3:
time: 694 us; the launch traced here: 684 us
  Pallas kernels  248 us (36%)
  waiting for transfers between devices  198 us (29%)
  other arithmetic  74.7 us (11%)
  starting transfers between devices  66.3 us (10%)
  matrix products  51.7 us (7%)
  between operations  23.5 us (3%)
  local copies, waits for them, and re-layouts  22.3 us (3%)
    all_to_all x7, waiting for transfers between devices, exchange(): lax.all_to_all(rows, 'expert', split_axis=0, concat_axis=0, tiled=True)  79.3 us
    all_gather x1, waiting for transfers between devices, shards(): dense = lax.all_gather(dense, everywhere, axis=0, tiled=True)  65.3 us
    pallas_call x2, Pallas kernels, expert_back(): pl.pallas_call(expert_back_kernel, grid=(count + width // columns,), in_s...  44.9 us
    pallas_call x2, Pallas kernels, expert_forward(): pl.pallas_call(expert_kernel, grid=(inner // tile,), in_specs=[pl.BlockSp...  42.6 us
    pallas_call x4, Pallas kernels, attend_back(): pl.pallas_call(attend_back_kernel, grid=(tokens // SEQ, count), in_specs=...  38.7 us
    pallas_call x1, Pallas kernels, weight_grads(): pl.pallas_call(lambda *refs: weight_grads_kernel(chunks, refs), grid=(2 *...  38 us
    ppermute x10, waiting for transfers between devices, sum_over_pairs(): total = total + lax.ppermute(block, everywhere, perm).astype(f32)  37.1 us
    all_to_all x7, starting transfers between devices, exchange(): lax.all_to_all(rows, 'expert', split_axis=0, concat_axis=0, tiled=True)  32.8 us
  transfers between devices with their start and end apart: 33, of which 18 were waited for; matrix products, arithmetic and copies ran while one was open for 15% of the time, Pallas kernels for 36%

profile of v3, /device:TPU:0, one launch (start us, length us, event | category | flops | bytes accessed | tf_op | source)
XLA Modules:
  0.0 683.7 jit_solution(1365557321478982690)
XLA Ops:
  27.4 65.3 %all-gather.4.cloned.1.call-done.refs_1_.refs_6_.refs_4_ = bf16[1024,4224]{1,0:T(8,128)(2,1)} async-done(((bf16[32,4224]{1,0:T(8,128)(2,1)}), bf16[1024,4224]{1,0:T(8,128)(2,1)}) %all-gather.4.cloned.1.call-update) | async-done | bytes 8650768 | tf_op jit(solution)/shard_map/all_gather | solution.py:831
  98.0 11.7 %fusion.2.q_ref.k_ref.v_ref = bf16[1024,3072]{1,0:T(8,128)(2,1)} fusion(bf16[1024,1024]{1,0:T(8,128)(2,1)} %fusion.14, bf16[1024,4224]{1,0:T(8,128)(2,1)} %all-gather.4.cloned.1.call-done.refs_1_.refs_6_.refs_4_), kind=kOutput, calls=%fused_computation.2 | convolution fusion | flops 6445596672 | bytes 14680064 | tf_op jit(solution)/shard_map/dot_general | solution.py:854
  109.7 29.1 %attend.1 = (bf16[1024,1024]{1,0:T(8,128)(2,1)S(1)}, f32[64,1024]{1,0:T(8,128)S(1)}) custom-call(bf16[1024,3072]{1,0:T(8,128)(2,1)} %fusion.2.q_ref.k_ref.v_ref, bf16[1024,3072]{1,0:T(8,128)(2,1)} %fusion.2.q_ref.k_ref.v_ref, bf16[1024,3072]{1,0:T(8,128)(2,1)} %fusion.2.q_ref.k_ref.v_ref, s32[1024,1]{1,0:T(8,128)S(1)} %copy.116.doc_col, s32[1,1024]{1,0:T(1,128)S(1)} %bitcast.168), custom_call_target="tpu_custom_call" | custom-call | flops 5510000128 | tf_op jit(solution)/shard_map/attend/pallas_call | solution.py:108
  140.2 13.6 %after_attend.1 = (f32[1024,1024]{1,0:T(8,128)}, bf16[1024,1024]{1,0:T(8,128)(2,1)}, f32[1024,128]{1,0:T(8,128)S(1)}, bf16[768,1024]{1,0:T(8,128)(2,1)}, bf16[768,1024]{1,0:T(8,128)(2,1)}) custom-call(bf16[1024,1024]{1,0:T(8,128)(2,1)} %copy-done, bf16[1024,4224]{1,0:T(8,128)(2,1)} %all-gather.4.cloned.1.call-done.refs_1_.refs_6_.refs_4_, ...), custom_call_target="tpu_custom_call" | custom-call | flops 2470000128 | tf_op jit(solution)/shard_map/after_attend/pallas_call | solution.py:272
  153.8 4.4 all-to-all-start
  158.2 4.8 fusion.22
  166.0 29.4 %all-to-all-done.x_ref.refs_0_ = bf16[8,96,1024]{2,1,0:T(8,128)(2,1)S(1)} async-done(((bf16[8,96,1024]{2,1,0:T(8,128)(2,1)}), bf16[8,96,1024]{2,1,0:T(8,128)(2,1)S(1)}, u32[]{:S(2)}, u32[]{:S(2)}) %all-to-all-start) | async-done | bytes 1572896 | tf_op jit(solution)/shard_map/all_to_all | solution.py:870
  200.3 21.3 %expert_forward.2 = (bf16[8,192,4096]{2,1,0:T(8,128)(2,1)}, bf16[8,96,4096]{2,1,0:T(8,128)(2,1)}) custom-call(bf16[8,96,1024]{2,1,0:T(8,128)(2,1)} %copy-done.14, bf16[1024,4096]{1,0:T(8,128)(2,1)} %bitcast.173), custom_call_target="tpu_custom_call" | custom-call | flops 3990000128 | tf_op jit(solution)/shard_map/expert_forward/pallas_call | solution.py:475
  221.6 15.9 %all-to-all-done.1.x_ref.refs_1_ = bf16[8,96,1024]{2,1,0:T(8,128)(2,1)S(1)} async-done(((bf16[8,96,1024]{2,1,0:T(8,128)(2,1)}), bf16[8,96,1024]{2,1,0:T(8,128)(2,1)S(1)}, u32[]{:S(2)}, u32[]{:S(2)}) %all-to-all-start.1) | async-done | bytes 1572896 | tf_op jit(solution)/shard_map/all_to_all | solution.py:870
  241.7 21.3 %expert_forward.3 = (bf16[8,192,4096]{2,1,0:T(8,128)(2,1)}, bf16[8,96,4096]{2,1,0:T(8,128)(2,1)}) custom-call(bf16[8,96,1024]{2,1,0:T(8,128)(2,1)} %copy-done.12, bf16[1024,4096]{1,0:T(8,128)(2,1)} %bitcast.174, bf16[8,192,4096]{2,1,0:T(8,128)(2,1)} %get-tuple-element.111.rest_0_), custom_call_target="tpu_custom_call", output_to_operand_aliasing={{0}: (2, {})} | custom-call | flops 3990000128 | tf_op jit(solution)/shard_map/expert_forward/pallas_call | solution.py:475
  263.1 19.1 %convolution_convert_fusion = bf16[1536,1024]{1,0:T(8,128)(2,1)} fusion(bf16[1536,4096]{1,0:T(8,128)(2,1)} %bitcast.177, bf16[1,4096,1024]{2,1,0:T(8,128)(2,1)} %all-gather.8.cloned.1.call-done), kind=kOutput, calls=%fused_computation.24 | convolution fusion | flops 12886474752 | bytes 24117248 | tf_op jit(solution)/shard_map/dot_general | solution.py:893
  282.2 6.1 all-to-all-start.3
  288.9 22.4 %expert_back.2 = (bf16[8,192,4096]{2,1,0:T(8,128)(2,1)}, bf16[8,96,1024]{2,1,0:T(8,128)(2,1)}, f32[8,1024]{1,0:T(8,128)}) custom-call(bf16[8,96,1024]{2,1,0:T(8,128)(2,1)} %all-to-all-done.2.grad_ref.refs_2_, bf16[8,96,4096]{2,1,0:T(8,128)(2,1)} %get-tuple-element.116.slope_ref, bf16[1024,4096]{1,0:T(8,128)(2,1)} %bitcast.175, bf16[4096,1024]{1,0:T(8,128)(2,1)} %bitcast.178, ...), custom_call_target="tpu_custom_call" | custom-call | flops 4369999872 | tf_op jit(solution)/shard_map/expert_back/pallas_call | solution.py:566
  311.3 13.1 %all-to-all-done.3.grad_ref.refs_3_ = bf16[8,96,1024]{2,1,0:T(8,128)(2,1)S(1)} async-done(((bf16[8,96,1024]{2,1,0:T(8,128)(2,1)}), bf16[8,96,1024]{2,1,0:T(8,128)(2,1)S(1)}, u32[]{:S(2)}, u32[]{:S(2)}) %all-to-all-start.3) | async-done | bytes 1572896 | tf_op jit(solution)/shard_map/all_to_all | solution.py:870
  329.1 22.5 %expert_back.3 = (bf16[8,192,4096]{2,1,0:T(8,128)(2,1)}, bf16[8,96,1024]{2,1,0:T(8,128)(2,1)}, f32[8,1024]{1,0:T(8,128)}) custom-call(bf16[8,96,1024]{2,1,0:T(8,128)(2,1)} %copy-done.13, bf16[8,96,4096]{2,1,0:T(8,128)(2,1)} %get-tuple-element.121.slope_ref, bf16[1024,4096]{1,0:T(8,128)(2,1)} %bitcast.176, ...), custom_call_target="tpu_custom_call", output_to_operand_aliasing={{0}: (7, {})} | custom-call | flops 4369999872 | tf_op jit(solution)/shard_map/expert_back/pallas_call | solution.py:566
  351.7 14.5 %all-to-all-done.4 = bf16[8,96,1024]{2,1,0:T(8,128)(2,1)S(1)} async-done(((bf16[8,96,1024]{2,1,0:T(8,128)(2,1)}), bf16[8,96,1024]{2,1,0:T(8,128)(2,1)S(1)}, u32[]{:S(2)}, u32[]{:S(2)}) %all-to-all-start.4) | async-done | bytes 1572896 | tf_op jit(solution)/shard_map/all_to_all | solution.py:870
  370.8 38.0 %weight_grads.1 = (bf16[1024,4096]{1,0:T(8,128)(2,1)}, bf16[1024,4096]{1,0:T(8,128)(2,1)}) custom-call(bf16[8,96,1024]{2,1,0:T(8,128)(2,1)} %copy-done.14, bf16[8,96,1024]{2,1,0:T(8,128)(2,1)} %copy-done.12, bf16[8,96,1024]{2,1,0:T(8,128)(2,1)} %all-to-all-done.2.grad_ref.refs_2_, bf16[8,96,1024]{2,1,0:T(8,128)(2,1)} %copy-done.13, ...), custom_call_target="tpu_custom_call" | custom-call | flops 7219999744 | tf_op jit(solution)/shard_map/weight_grads/pallas_call | solution.py:658
  414.9 12.6 %before_attend_back.1 = (f32[1024,1024]{1,0:T(8,128)}, bf16[1024,1024]{1,0:T(8,128)(2,1)S(1)}, bf16[1024,1024]{1,0:T(8,128)(2,1)}, f32[16,1024]{1,0:T(8,128)S(1)}) custom-call(bf16[768,1024]{1,0:T(8,128)(2,1)S(1)} %bitcast.166, bf16[768,1024]{1,0:T(8,128)(2,1)} %bitcast.19.refs_1_, s32[1024,1]{1,0:T(8,128)S(1)} %fusion.41.refs_2_, ...), custom_call_target="tpu_custom_call" | custom-call | flops 2280000000 | tf_op jit(solution)/shard_map/before_attend_back/pallas_call | solution.py:342
  429.9 6.5 all-to-all-start.6
  442.9 9.6 %attend_back.4.refs_0_ = bf16[1024,768]{1,0:T(8,128)(2,1)S(1)} custom-call(bf16[1024,3072]{1,0:T(8,128)(2,1)} %fusion.2.q_ref.k_ref.v_ref, bf16[1024,3072]{1,0:T(8,128)(2,1)} %fusion.2.q_ref.k_ref.v_ref, bf16[1024,3072]{1,0:T(8,128)(2,1)} %fusion.2.q_ref.k_ref.v_ref, bf16[1024,1024]{1,0:T(8,128)(2,1)S(1)} %copy-done.2, bf16[1024,1024]{1,0:T(8,128)(2,1)} %copy-done, ...), custom_call_target="tpu_custom_call" | custom-call | flops 1824000000 | tf_op jit(solution)/shard_map/attend_back/pallas_call | solution.py:187
  459.1 9.7 %attend_back.5.refs_1_ = bf16[1024,768]{1,0:T(8,128)(2,1)S(1)} custom-call(bf16[1024,3072]{1,0:T(8,128)(2,1)} %fusion.2.q_ref.k_ref.v_ref, bf16[1024,3072]{1,0:T(8,128)(2,1)} %fusion.2.q_ref.k_ref.v_ref, bf16[1024,3072]{1,0:T(8,128)(2,1)} %fusion.2.q_ref.k_ref.v_ref, bf16[1024,1024]{1,0:T(8,128)(2,1)S(1)} %copy-done.2, bf16[1024,1024]{1,0:T(8,128)(2,1)} %copy-done, ...), custom_call_target="tpu_custom_call" | custom-call | flops 1824000000 | tf_op jit(solution)/shard_map/attend_back/pallas_call | solution.py:187
  476.7 9.7 %attend_back.6.refs_2_ = bf16[1024,768]{1,0:T(8,128)(2,1)S(1)} custom-call(bf16[1024,3072]{1,0:T(8,128)(2,1)} %fusion.2.q_ref.k_ref.v_ref, bf16[1024,3072]{1,0:T(8,128)(2,1)} %fusion.2.q_ref.k_ref.v_ref, bf16[1024,3072]{1,0:T(8,128)(2,1)} %fusion.2.q_ref.k_ref.v_ref, bf16[1024,1024]{1,0:T(8,128)(2,1)S(1)} %copy-done.2, bf16[1024,1024]{1,0:T(8,128)(2,1)} %copy-done, ...), custom_call_target="tpu_custom_call" | custom-call | flops 1824000000 | tf_op jit(solution)/shard_map/attend_back/pallas_call | solution.py:187
  489.6 6.1 collective-permute-done.1
  500.1 6.3 all-to-all-done.6
  506.5 9.8 %attend_back.7.refs_3_ = bf16[1024,768]{1,0:T(8,128)(2,1)S(1)} custom-call(bf16[1024,3072]{1,0:T(8,128)(2,1)} %fusion.2.q_ref.k_ref.v_ref, bf16[1024,3072]{1,0:T(8,128)(2,1)} %fusion.2.q_ref.k_ref.v_ref, bf16[1024,3072]{1,0:T(8,128)(2,1)} %fusion.2.q_ref.k_ref.v_ref, bf16[1024,1024]{1,0:T(8,128)(2,1)S(1)} %copy-done.2, bf16[1024,1024]{1,0:T(8,128)(2,1)} %copy-done, ...), custom_call_target="tpu_custom_call" | custom-call | flops 1824000000 | tf_op jit(solution)/shard_map/attend_back/pallas_call | solution.py:187
  531.0 14.1 %input_gradient.1 = (f32[1024,1024]{1,0:T(8,128)}, f32[16,1024]{1,0:T(8,128)S(1)}) custom-call(bf16[1024,768]{1,0:T(8,128)(2,1)S(1)} %copy-done.4, bf16[1024,768]{1,0:T(8,128)(2,1)S(1)} %copy-done.6, bf16[1024,768]{1,0:T(8,128)(2,1)S(1)} %copy-done.8, bf16[1024,768]{1,0:T(8,128)(2,1)} %copy-done.9, ...), custom_call_target="tpu_custom_call" | custom-call | flops 2660000000 | tf_op jit(solution)/shard_map/input_gradient/pallas_call | solution.py:397
  546.2 17.4 %collective-permute-done.7 = bf16[4,32,1536]{2,1,0:T(8,128)(2,1)S(1)} collective-permute-done((bf16[4,32,1536]{2,1,0:T(8,128)(2,1)S(1)}, bf16[4,32,1536]{2,1,0:T(8,128)(2,1)S(1)}, u32[]{:S(2)}, u32[]{:S(2)}) %collective-permute-start.7) | collective-permute-done | bytes 393248 | tf_op jit(solution)/shard_map/ppermute | solution.py:747
  580.9 7.6 %activations_of.1 = bf16[1024,1024]{1,0:T(8,128)(2,1)} custom-call(bf16[1536,1024]{1,0:T(8,128)(2,1)} %bitcast.36.refs_0_, s32[1024,1]{1,0:T(8,128)S(1)} %copy.135.refs_1_, f32[1024,128]{1,0:T(8,128)S(1)} %get-tuple-element.168.refs_2_, f32[1024,1024]{1,0:T(8,128)} %get-tuple-element.134.refs_3_), custom_call_target="tpu_custom_call" | custom-call | flops 1424999936 | tf_op jit(solution)/shard_map/activations_of/pallas_call | solution.py:428
  588.5 6.4 turn.1
  601.7 12.2 %collective-permute-done.8 = bf16[2,32,2688]{2,1,0:T(8,128)(2,1)S(1)} collective-permute-done((bf16[2,32,2688]{2,1,0:T(8,128)(2,1)}, bf16[2,32,2688]{2,1,0:T(8,128)(2,1)S(1)}, u32[]{:S(2)}, u32[]{:S(2)}) %collective-permute-start.8) | collective-permute-done | bytes 344096 | tf_op jit(solution)/shard_map/ppermute | solution.py:747
  651.8 11.8 %multiply_add_fusion = (f32[1,4096,256]{2,1,0:T(8,128)}, f32[1,4096,256]{2,1,0:T(8,128)}, f32[1,4096,256]{2,1,0:T(8,128)}) fusion(f32[1,4096,256]{2,1,0:T(8,128)} %param.43, f32[1,4096,256]{2,1,0:T(8,128)} %param.31, f32[4096,256]{1,0:T(8,128)} %get-tuple-element.176, f32[]{:T(128)S(6)} %div.68, f32[1,4096,256]{2,1,0:T(8,128)} %param.37), kind=kLoop, calls=%fused_computation.22 | loop fusion | flops 10485760 | bytes 29360132 | tf_op jit(solution)/shard_map/add | solution.py:787
  664.2 11.3 %multiply_add_fusion.1 = (f32[1,256,4096]{2,1,0:T(8,128)}, f32[1,256,4096]{2,1,0:T(8,128)}, f32[1,256,4096]{2,1,0:T(8,128)}) fusion(f32[1,256,4096]{2,1,0:T(8,128)} %param.42, f32[1,256,4096]{2,1,0:T(8,128)} %param.30, f32[]{:T(128)S(6)} %div.68, bf16[1,256,4096]{2,1,0:T(8,128)(2,1)S(1)} %copy-done.15, f32[1,256,4096]{2,1,0:T(8,128)} %param.36), kind=kLoop, calls=%fused_computation.23 | loop fusion | flops 11534336 | bytes 27262980 | tf_op jit(solution)/shard_map/add | solution.py:787
  (273 shorter events, 156.5 us)
Async XLA Ops:
  7.2 85.5 %all-gather.4.cloned.1.call-start = ((), (), s32[]{:S(2)}) async-start(), calls=%async_computation.10 | async-start | bytes 8921088 | tf_op jit(solution)/shard_map/all_gather | solution.py:831
  11.4 188.8 %all-gather.6.cloned.1.call-start = ((), (), s32[]{:S(2)}) async-start(), calls=%async_computation.11 | async-start | bytes 10485760 | tf_op jit(solution)/shard_map/all_gather | solution.py:832
  15.3 247.8 %all-gather.8.cloned.1.call-start = ((), (), s32[]{:S(2)}) async-start(), calls=%async_computation.12 | async-start | bytes 10485760 | tf_op jit(solution)/shard_map/all_gather | solution.py:833
  153.8 41.7 %all-to-all-start = ((bf16[8,96,1024]{2,1,0:T(8,128)(2,1)}), bf16[8,96,1024]{2,1,0:T(8,128)(2,1)S(1)}, u32[]{:S(2)}, u32[]{:S(2)}) async-start(bf16[8,96,1024]{2,1,0:T(8,128)(2,1)} %bitcast.10), calls=%async_computation | async-start | bytes 3145728 | tf_op jit(solution)/shard_map/all_to_all | solution.py:870
  196.6 40.8 %all-to-all-start.1 = ((bf16[8,96,1024]{2,1,0:T(8,128)(2,1)}), bf16[8,96,1024]{2,1,0:T(8,128)(2,1)S(1)}, u32[]{:S(2)}, u32[]{:S(2)}) async-start(bf16[8,96,1024]{2,1,0:T(8,128)(2,1)} %bitcast.11), calls=%async_computation.1 | async-start | bytes 3145728 | tf_op jit(solution)/shard_map/all_to_all | solution.py:870
  237.4 44.8 %all-to-all-start.2 = ((bf16[8,96,1024]{2,1,0:T(8,128)(2,1)}), bf16[8,96,1024]{2,1,0:T(8,128)(2,1)}, u32[]{:S(2)}, u32[]{:S(2)}) async-start(bf16[8,96,1024]{2,1,0:T(8,128)(2,1)} %bitcast.196), calls=%async_computation.2 | async-start | bytes 3145728 | tf_op jit(solution)/shard_map/all_to_all | solution.py:870
  282.2 42.2 %all-to-all-start.3 = ((bf16[8,96,1024]{2,1,0:T(8,128)(2,1)}), bf16[8,96,1024]{2,1,0:T(8,128)(2,1)S(1)}, u32[]{:S(2)}, u32[]{:S(2)}) async-start(bf16[8,96,1024]{2,1,0:T(8,128)(2,1)} %bitcast.195), calls=%async_computation.3 | async-start | bytes 3145728 | tf_op jit(solution)/shard_map/all_to_all | solution.py:870
  325.6 40.7 %all-to-all-start.4 = ((bf16[8,96,1024]{2,1,0:T(8,128)(2,1)}), bf16[8,96,1024]{2,1,0:T(8,128)(2,1)S(1)}, u32[]{:S(2)}, u32[]{:S(2)}) async-start(bf16[8,96,1024]{2,1,0:T(8,128)(2,1)} %get-tuple-element.124), calls=%async_computation.4 | async-start | bytes 3145728 | tf_op jit(solution)/shard_map/all_to_all | solution.py:870
  366.2 42.5 %all-to-all-start.5 = ((bf16[8,96,1024]{2,1,0:T(8,128)(2,1)}), bf16[8,96,1024]{2,1,0:T(8,128)(2,1)}, u32[]{:S(2)}, u32[]{:S(2)}) async-start(bf16[8,96,1024]{2,1,0:T(8,128)(2,1)} %get-tuple-element.127), calls=%async_computation.5 | async-start | bytes 3145728 | tf_op jit(solution)/shard_map/all_to_all | solution.py:870
  370.5 194.3 %reduce-scatter.3.cloned.1.call-start = ((), (), s32[]{:S(2)}) async-start(), calls=%async_computation.13 | async-start | bytes 10485760 | tf_op jit(solution)/shard_map/reduce_scatter | solution.py:932
  408.8 168.8 %reduce-scatter.5.cloned.1.call-start = ((), (), s32[]{:S(2)}) async-start(), calls=%async_computation.14 | async-start | bytes 10485760 | tf_op jit(solution)/shard_map/reduce_scatter | solution.py:931
  429.9 76.6 %all-to-all-start.6 = ((bf16[8,192,1024]{2,1,0:T(8,128)(2,1)}), bf16[8,192,1024]{2,1,0:T(8,128)(2,1)}, u32[]{:S(2)}, u32[]{:S(2)}) async-start(bf16[8,192,1024]{2,1,0:T(8,128)(2,1)} %bitcast.182), calls=%async_computation.6 | async-start | bytes 6291456 | tf_op jit(solution)/shard_map/all_to_all | solution.py:870
  442.9 12.6 %collective-permute-start = (bf16[8,2,32,1152]{3,2,1,0:T(8,128)(2,1)}, bf16[8,2,32,1152]{3,2,1,0:T(8,128)(2,1)}, u32[]{:S(2)}, u32[]{:S(2)}) collective-permute-start(bf16[8,2,32,1152]{3,2,1,0:T(8,128)(2,1)} %fusion.31), channel_id=1, source_target_pairs={{0,1},{1,0},{2,3},{3,2},{4,5},{5,4},{6,7},{7,6},{8,9},{9,8},{10,11... | collective-permute-start | bytes 3538952 | tf_op jit(solution)/shard_map/ppermute | solution.py:714
  473.1 23.7 %collective-permute-start.2 = (bf16[8,2,32,1536]{3,2,1,0:T(8,128)(2,1)}, bf16[8,2,32,1536]{3,2,1,0:T(8,128)(2,1)}, u32[]{:S(2)}, u32[]{:S(2)}) collective-permute-start(bf16[8,2,32,1536]{3,2,1,0:T(8,128)(2,1)} %pad_maximum_fusion), channel_id=1, source_target_pairs={{0,1},{1,0},{2,3},{3,2},{4,5},{5,4},{6,7},{7,6},{8,9},{9,8},{10,11... | collective-permute-start | bytes 4718600 | tf_op jit(solution)/shard_map/ppermute | solution.py:714
  474.6 21.1 %collective-permute-start.1 = (bf16[4,2,32,1152]{3,2,1,0:T(8,128)(2,1)S(1)}, bf16[4,2,32,1152]{3,2,1,0:T(8,128)(2,1)S(1)}, u32[]{:S(2)}, u32[]{:S(2)}) collective-permute-start(bf16[4,2,32,1152]{3,2,1,0:T(8,128)(2,1)S(1)} %dynamic-slice_bitcast_fusion.9), channel_id=1, source_target_pairs={{0,4},{4,0},{8,12},{12,8},{16,20},{20,16},{24,28},{28,24},{1,5},{5... | collective-permute-start | bytes 1769480 | tf_op jit(solution)/shard_map/ppermute | solution.py:714
  519.9 3.8 collective-permute-start.3
  525.8 20.4 %collective-permute-start.5 = (bf16[4,32,1536]{2,1,0:T(8,128)(2,1)S(1)}, bf16[4,32,1536]{2,1,0:T(8,128)(2,1)S(1)}, u32[]{:S(2)}, u32[]{:S(2)}) collective-permute-start(bf16[4,32,1536]{2,1,0:T(8,128)(2,1)S(1)} %get-tuple-element.197), channel_id=1, source_target_pairs={{0,2},{1,3},{2,0},{3,1},{4,6},{5,7},{6,4},{7,5},{8,10},{9,11},{10,... | collective-permute-start | bytes 1179656 | tf_op jit(solution)/shard_map/ppermute | solution.py:747
  526.9 19.4 %collective-permute-start.6 = (bf16[4,32,1536]{2,1,0:T(8,128)(2,1)S(1)}, bf16[4,32,1536]{2,1,0:T(8,128)(2,1)S(1)}, u32[]{:S(2)}, u32[]{:S(2)}) collective-permute-start(bf16[4,32,1536]{2,1,0:T(8,128)(2,1)S(1)} %get-tuple-element.199), channel_id=1, source_target_pairs={{0,4},{1,5},{2,6},{3,7},{4,0},{5,1},{6,2},{7,3},{8,12},{9,13},{10,... | collective-permute-start | bytes 1179656 | tf_op jit(solution)/shard_map/ppermute | solution.py:747
  528.4 35.2 %collective-permute-start.7 = (bf16[4,32,1536]{2,1,0:T(8,128)(2,1)S(1)}, bf16[4,32,1536]{2,1,0:T(8,128)(2,1)S(1)}, u32[]{:S(2)}, u32[]{:S(2)}) collective-permute-start(bf16[4,32,1536]{2,1,0:T(8,128)(2,1)S(1)} %get-tuple-element.198), channel_id=1, source_target_pairs={{0,6},{1,7},{2,4},{3,5},{4,2},{5,3},{6,0},{7,1},{8,14},{9,15},{10,... | collective-permute-start | bytes 1179656 | tf_op jit(solution)/shard_map/ppermute | solution.py:747
  529.4 35.1 %collective-permute-start.4 = (bf16[4,2,32,1536]{3,2,1,0:T(8,128)(2,1)S(1)}, bf16[4,2,32,1536]{3,2,1,0:T(8,128)(2,1)S(1)}, u32[]{:S(2)}, u32[]{:S(2)}) collective-permute-start(bf16[4,2,32,1536]{3,2,1,0:T(8,128)(2,1)S(1)} %dynamic-slice_bitcast_fusion), channel_id=1, source_target_pairs={{0,4},{4,0},{8,12},{12,8},{16,20},{20,16},{24,28},{28,24},{1,5},{5... | collective-permute-start | bytes 2359304 | tf_op jit(solution)/shard_map/ppermute | solution.py:714
  566.5 31.6 %collective-permute-start.11 = (bf16[32,1536]{1,0:T(8,128)(2,1)}, bf16[32,1536]{1,0:T(8,128)(2,1)S(1)}, u32[]{:S(2)}, u32[]{:S(2)}) collective-permute-start(bf16[32,1536]{1,0:T(8,128)(2,1)} %get-tuple-element.211), channel_id=1, source_target_pairs={{0,8},{1,9},{2,10},{3,11},{4,12},{5,13},{6,14},{7,15},{8,0},{9,1},... | collective-permute-start | bytes 294920 | tf_op jit(solution)/shard_map/ppermute | solution.py:747
  566.5 34.1 %collective-permute-start.12 = (bf16[32,1536]{1,0:T(8,128)(2,1)}, bf16[32,1536]{1,0:T(8,128)(2,1)}, u32[]{:S(2)}, u32[]{:S(2)}) collective-permute-start(bf16[32,1536]{1,0:T(8,128)(2,1)} %get-tuple-element.213), channel_id=1, source_target_pairs={{0,16},{1,17},{2,18},{3,19},{4,20},{5,21},{6,22},{7,23},{8,24},{9,... | collective-permute-start | bytes 294920 | tf_op jit(solution)/shard_map/ppermute | solution.py:747
  568.6 32.0 %collective-permute-start.13 = (bf16[32,1536]{1,0:T(8,128)(2,1)S(1)}, bf16[32,1536]{1,0:T(8,128)(2,1)}, u32[]{:S(2)}, u32[]{:S(2)}) collective-permute-start(bf16[32,1536]{1,0:T(8,128)(2,1)S(1)} %get-tuple-element.212), channel_id=1, source_target_pairs={{0,24},{1,25},{2,26},{3,27},{4,28},{5,29},{6,30},{7,31},{8,16},{9,... | collective-permute-start | bytes 294920 | tf_op jit(solution)/shard_map/ppermute | solution.py:747
  571.9 29.7 %collective-permute-start.10 = (bf16[2,32,2688]{2,1,0:T(8,128)(2,1)}, bf16[2,32,2688]{2,1,0:T(8,128)(2,1)S(1)}, u32[]{:S(2)}, u32[]{:S(2)}) collective-permute-start(bf16[2,32,2688]{2,1,0:T(8,128)(2,1)} %get-tuple-element.209), channel_id=1, source_target_pairs={{0,24},{1,25},{2,26},{3,27},{4,28},{5,29},{6,30},{7,31},{8,16},{9,... | collective-permute-start | bytes 1032200 | tf_op jit(solution)/shard_map/ppermute | solution.py:747
  574.3 23.7 %all-to-all-start.7 = ((f32[32,1,64]{2,1,0:T(1,128)}), f32[32,1,64]{2,1,0:T(1,128)S(1)}, u32[]{:S(2)}, u32[]{:S(2)}) async-start(f32[32,1,64]{2,1,0:T(1,128)} %bitcast.64), calls=%async_computation.9 | async-start | bytes 32768 | tf_op jit(solution)/shard_map/all_to_all | solution.py:990
  596.2 17.6 %collective-permute-start.8 = (bf16[2,32,2688]{2,1,0:T(8,128)(2,1)}, bf16[2,32,2688]{2,1,0:T(8,128)(2,1)S(1)}, u32[]{:S(2)}, u32[]{:S(2)}) collective-permute-start(bf16[2,32,2688]{2,1,0:T(8,128)(2,1)} %get-tuple-element.208), channel_id=1, source_target_pairs={{0,8},{1,9},{2,10},{3,11},{4,12},{5,13},{6,14},{7,15},{8,0},{9,1},... | collective-permute-start | bytes 1032200 | tf_op jit(solution)/shard_map/ppermute | solution.py:747
  598.1 18.2 %collective-permute-start.9 = (bf16[2,32,2688]{2,1,0:T(8,128)(2,1)S(1)}, bf16[2,32,2688]{2,1,0:T(8,128)(2,1)S(1)}, u32[]{:S(2)}, u32[]{:S(2)}) collective-permute-start(bf16[2,32,2688]{2,1,0:T(8,128)(2,1)S(1)} %copy-done.34), channel_id=1, source_target_pairs={{0,16},{1,17},{2,18},{3,19},{4,20},{5,21},{6,22},{7,23},{8,24},{9,... | collective-permute-start | bytes 1032200 | tf_op jit(solution)/shard_map/ppermute | solution.py:747
  616.6 5.5 collective-permute-start.14
  630.6 3.6 collective-permute-start.16
  634.8 3.6 collective-permute-start.17
  639.0 3.6 collective-permute-start.18
  643.2 4.5 collective-permute-start.19
  (47 other events, 481.9 us)
Sparse Core Ops, SparseCore 0:
  11.5 81.0 all-gather.3
  94.8 56.8 all-gather.5
  153.8 59.3 all-gather.7
  408.9 72.8 reduce-scatter.2
  484.4 88.5 reduce-scatter.4

commit v4 on v3

--- a/solution.py
+++ b/solution.py
@@ -177,7 +177,7 @@
     out_ref[:, place[0]] = (grad_q_t[...] * scale_qk).T.astype(low)
 
 
-def attend_back(packed, grad_mixed, mixed, lse, doc_col, doc_row, first, count):
+def attend_back(packed, grad_mixed, mixed, lse, doc_col, doc_row, first, count, grad_first):
     tokens, wide = packed.shape
     pairs = wide // 3 // LANES
 
@@ -191,7 +191,7 @@
             part(0),
             part(1),
             part(2),
-            pl.BlockSpec((SEQ, LANES), lambda r, p: (r, first + p)),
+            pl.BlockSpec((SEQ, LANES), lambda r, p: (r, grad_first + p)),
             pl.BlockSpec((SEQ, LANES), lambda r, p: (r, first + p)),
             pl.BlockSpec((8, SEQ), lambda r, p: (first + p, r)),
             pl.BlockSpec((SEQ, 1), lambda r, p: (r, 0)),
@@ -274,7 +274,7 @@
         grid=(count // BLOCK,),
         in_specs=[pl.BlockSpec((BLOCK, m.shape[1]), lambda i: (i, 0)) for m in mixed]
         + [
-            pl.BlockSpec((width, width), lambda i: (0, 3)),
+            pl.BlockSpec((width, width), lambda i: (0, 0)),
             tile,
             tile,
             pl.BlockSpec(norms.shape, lambda i: (0, 0)),
@@ -348,7 +348,7 @@
             tile,
             tile,
             pl.BlockSpec(norms.shape, lambda i: (0, 0)),
-            pl.BlockSpec((width, width), lambda i: (0, 3)),
+            pl.BlockSpec((width, width), lambda i: (0, 0)),
         ],
         out_specs=[tile, tile, tile, pl.BlockSpec((16, width), lambda i: (0, 0))],
         out_shape=[
@@ -363,15 +363,14 @@
     )(*rows, slot_col, after, out_grad, norms, proj)
 
 
-def input_grad_kernel(plan, grad_refs, weight_ref, x_ref, norm_ref, grad_after_ref, outs):
+def input_grad_kernel(plan, grad_refs, weight_refs, x_ref, norm_ref, grad_after_ref, outs):
     out_ref, sums_ref = outs
     grad_normed = 0.0
-    each = weight_ref.shape[1] // 3
-    for grad, (offset, wide) in zip(grad_refs, plan):
+    for grad, (strip, offset, wide) in zip(grad_refs, plan):
         for s in range(3):
-            start = s * each + offset
+            weight = weight_refs[3 * strip + s]
             grad_normed = grad_normed + dot_cols(
-                grad[:, s * wide : (s + 1) * wide], weight_ref[:, start : start + wide]
+                grad[:, s * wide : (s + 1) * wide], weight[:, offset : offset + wide]
             )
     normal, scale = norm_parts(x_ref[...].astype(f32))
     out_ref[...] = grad_after_ref[...] + norm_back(grad_normed, normal, scale, norm_ref[0:1, :])
@@ -386,20 +385,23 @@
         sums_ref[...] += sums
 
 
-def input_gradient(plan, grads, dense, tokens, norms, grad_after):
+def input_gradient(plan, grads, weights, tokens, norms, grad_after):
     count, width = tokens.shape
     tile = pl.BlockSpec((BLOCK, width), lambda i: (i, 0))
 
     def kernel(*refs):
-        n = len(grads)
-        input_grad_kernel(plan, refs[:n], *refs[n : n + 4], refs[n + 4 :])
+        n, m = len(grads), len(grads) + len(weights)
+        input_grad_kernel(plan, refs[:n], refs[n:m], *refs[m : m + 3], refs[m + 3 :])
 
     return pl.pallas_call(
         kernel,
         grid=(count // BLOCK,),
         in_specs=[pl.BlockSpec((BLOCK, g.shape[1]), lambda i: (i, 0)) for g in grads]
         + [
-            pl.BlockSpec((width, 3 * width), lambda i: (0, 0)),
+            pl.BlockSpec((width, columns), lambda i, block=block: (0, block))
+            for _, block, columns in weights
+        ]
+        + [
             tile,
             pl.BlockSpec(norms.shape, lambda i: (0, 0)),
             tile,
@@ -412,7 +414,7 @@
         compiler_params=pltpu.CompilerParams(vmem_limit_bytes=48 * 2**20),
         cost_estimate=hint(14),
         name="input_gradient",
-    )(*grads, dense, tokens, norms, grad_after)
+    )(*grads, *[array for array, _, _ in weights], tokens, norms, grad_after)
 
 
 def activations_of(rows, slot_col, gate, after):
@@ -712,6 +714,30 @@
 def swap(values, axis, distance):
     size = lax.axis_size(axis)
     return lax.ppermute(values, axis, [(i, i ^ distance) for i in range(size)])
+
+
+def assemble_kernel(me_ref, *refs):
+    pieces, out_ref = refs[:-1], refs[-1]
+    experts, rows = pieces[0].shape[0], pieces[0].shape[1]
+    for t, piece in enumerate(pieces):
+        for e in range(experts):
+            owner = e * len(pieces) + (me_ref[0] ^ t)
+            out_ref[pl.ds(pl.multiple_of(owner * rows, rows), rows), :] = piece[e]
+
+
+def assemble(pieces):
+    experts, rows, columns = pieces[0].shape
+    dp = len(pieces)
+    return pl.pallas_call(
+        assemble_kernel,
+        in_specs=[pl.BlockSpec(memory_space=pltpu.SMEM)]
+        + [pl.BlockSpec(memory_space=pltpu.VMEM)] * dp,
+        out_specs=pl.BlockSpec(memory_space=pltpu.VMEM),
+        out_shape=jax.ShapeDtypeStruct((experts * dp * rows, columns), pieces[0].dtype),
+        compiler_params=pltpu.CompilerParams(vmem_limit_bytes=32 * 2**20),
+        cost_estimate=hint(4),
+        name="assemble",
+    )(lax.axis_index("dp").astype(jnp.int32).reshape(1), *pieces)
 
 
 def sum_halves(parts, axis, bit, at):
@@ -825,18 +851,19 @@
     centre_own = centroids.shape[1]
     groups = 4
 
+    strips = 2
+    strip = width // strips
     small = jnp.concatenate([norm_params.reshape(-1), centroids.reshape(-1)]).astype(low)
     small = jnp.pad(small, (0, rows_own * LANES - small.shape[0])).reshape(rows_own, LANES)
-    dense = jnp.concatenate([qkv_weight.astype(low), proj_weight.astype(low), small], axis=1)
-    dense = lax.all_gather(dense, everywhere, axis=0, tiled=True)
-    weight_in = lax.all_gather(expert_in.astype(low), "dp", axis=1, tiled=True)[0]
-    weight_out = lax.all_gather(expert_out.astype(low), "dp", axis=2, tiled=True)[0]
-
-    small_full = dense[:, 4 * width :].reshape(devices, rows_own * LANES)
-    norms = (
-        small_full[:, : 4 * norm_own].reshape(devices, 4, norm_own).transpose(1, 0, 2)
-    ).reshape(4, width).astype(f32)
-    centre_table = small_full[:, 4 * norm_own : 4 * norm_own + centre_own].reshape(experts, width)
+    qkv_low = qkv_weight.astype(low)
+    qkv_own = [
+        [qkv_low[:, s * width + h * strip : s * width + (h + 1) * strip] for s in range(3)]
+        for h in range(strips)
+    ]
+    front = jnp.concatenate([*qkv_own[0], small], axis=1)
+    later = jnp.concatenate([proj_weight.astype(low), *qkv_own[1]], axis=1)
+    later = lax.all_gather(later, everywhere, axis=0, tiled=True)
+    in_low, out_low = expert_in.astype(low), expert_out.astype(low)
 
     route_ids = routes[:, 0]
     onehot = route_ids[:, None] == jnp.arange(experts, dtype=jnp.int32)[None, :]
@@ -849,13 +876,41 @@
     doc_col = documents[:, None]
     doc_row = documents[None, :]
 
+    if rows_own % 16:
+        front = lax.all_gather(front, everywhere, axis=0, tiled=True)
+    else:
+        spread = jnp.broadcast_to(front[None], (experts,) + front.shape)
+        spread = lax.all_to_all(spread, "expert", split_axis=0, concat_axis=0, tiled=True)
+        spread, in_low, out_low, slot_row, slot_col, chunked_row, chunked_col = in_order(
+            spread, in_low, out_low, slot_row, slot_col, chunked_row, chunked_col
+        )
+        pieces = {0: spread}
+        distance = dp // 2
+        while distance:
+            for t in list(pieces):
+                pieces[t | distance] = swap(pieces[t], "dp", distance)
+            distance //= 2
+        front = assemble([pieces[t] for t in range(dp)])
+    weight_in = lax.all_gather(in_low, "dp", axis=1, tiled=True)[0]
+    weight_out = lax.all_gather(out_low, "dp", axis=2, tiled=True)[0]
+    small_full = front[:, 3 * strip :].reshape(devices, rows_own * LANES)
+    norms = (
+        small_full[:, : 4 * norm_own].reshape(devices, 4, norm_own).transpose(1, 0, 2)
+    ).reshape(4, width).astype(f32)
+    centre_table = small_full[:, 4 * norm_own : 4 * norm_own + centre_own].reshape(experts, width)
+
     normed_low = layer_norm(tokens.astype(f32), norms[0], norms[1]).astype(low)
-    normed_low, dense = in_order(normed_low, dense)
-    packed = jnp.dot(normed_low, dense[:, : 3 * width], preferred_element_type=f32).astype(low)
-    mixed, lse = attend(packed, doc_col, doc_row)
+    normed_low, front = in_order(normed_low, front)
+    packed, mixed, lse = [], [], []
+    for weight in (front[:, : 3 * strip], later[:, width:]):
+        packed_h = jnp.dot(normed_low, weight, preferred_element_type=f32).astype(low)
+        mixed_h, lse_h = attend(packed_h, doc_col, doc_row)
+        packed.append(packed_h)
+        mixed.append(mixed_h)
+        lse.append(lse_h)
     after, grad_rows, gate, *outgoing = after_attend(
-        [mixed],
-        dense,
+        mixed,
+        later,
         tokens,
         out_grad,
         norms,
@@ -930,16 +985,18 @@
     )
     in_grad = lax.psum_scatter(grad_in[None], "dp", scatter_dimension=1, tiled=True)
     out_turned = lax.psum_scatter(grad_out_turned[None], "dp", scatter_dimension=1, tiled=True)
-    in_grad = in_grad.astype(f32)
-    in_square = jnp.sum(in_grad * in_grad)
     returned = exchange(result).reshape(slots, width)
 
     grad_after, grad_low, grad_mixed, sums_two = before_attend_back(
-        grad_input, chunked_col, after, out_grad, norms, dense
-    )
-
-    grad_proj = lax.dot_general(
-        mixed, grad_low, (((0,), (0,)), ((), ())), preferred_element_type=f32
+        grad_input, chunked_col, after, out_grad, norms, later
+    )
+
+    grad_proj = jnp.concatenate(
+        [
+            lax.dot_general(m, grad_low, (((0,), (0,)), ((), ())), preferred_element_type=f32)
+            for m in mixed
+        ],
+        axis=0,
     ).astype(low)
     norm_two = jnp.sum(sums_two.reshape(2, 8, width), axis=1)
     norm_two = norm_two.reshape(2, devices, norm_own).transpose(1, 0, 2).reshape(devices, -1)
@@ -954,12 +1011,16 @@
     def by_owner(values):
         return values.reshape(experts, dp, rows_own, values.shape[1])
 
-    def back_group(g):
-        part = attend_back(packed, grad_mixed, mixed, lse, doc_col, doc_row, g * each, each)
+    def back_group(g, *beside):
+        h, k = g // (groups // strips), g % (groups // strips)
+        part = attend_back(
+            packed[h], grad_mixed, mixed[h], lse[h], doc_col, doc_row, k * each, each, g * each
+        )
+        part, *beside = in_order(part, *beside)
         grad = lax.dot_general(
             normed_low, part, (((0,), (0,)), ((), ())), preferred_element_type=f32
         )
-        return part, grad.astype(low)
+        return part, grad.astype(low), *beside
 
     parts, grads = [], []
     rest = by_owner(jnp.concatenate([grad_proj, extra], axis=1))
@@ -970,51 +1031,56 @@
         if g == groups - 1:
             rest = sum_over_neighbours(rest)
             first = sum_over_cores([by_owner(v) for v in grads[: groups // 2]])
-            rest, first, grad_mixed, returned = in_order(rest, first, grad_mixed, returned)
-        part, grad = back_group(g)
+            out_grad_w, out_square = turn(out_turned[0])
+            rest, first, grad_mixed, returned, out_grad_w, out_square = in_order(
+                rest, first, grad_mixed, returned, out_grad_w, out_square
+            )
+            out_grad_w = out_grad_w[None]
+            first = sum_over_neighbours(first)
+            part, grad, first = back_group(g, first)
+        else:
+            part, grad = back_group(g)
         grad, grad_mixed = in_order(grad, grad_mixed)
         parts.append(part)
         grads.append(grad)
     second = sum_over_cores([by_owner(v) for v in grads[groups // 2 :]])
     second, first, grad_after = in_order(second, first, grad_after)
     second = sum_near(second)
-    first = sum_over_neighbours(first)
+    first = sum_far(jnp.concatenate([rest, first], axis=-1)).astype(low)
+    per_strip = groups // strips
+    weights = [(front, s, strip) for s in range(3)]
+    weights += [(later, width // strip + s, strip) for s in range(3)]
     input_grad, sums_one = input_gradient(
-        [(g * wide, wide) for g in range(groups)], parts, dense, tokens, norms, grad_after
-    )
-    first, second, sums_one, gate, out_turned = in_order(
-        first, second, sums_one, gate, out_turned
-    )
+        [(g // per_strip, g % per_strip * wide, wide) for g in range(groups)],
+        parts,
+        weights,
+        tokens,
+        norms,
+        grad_after,
+    )
+    first, second, sums_one, gate = in_order(first, second, sums_one, gate)
     norm_one = jnp.sum(sums_one.reshape(2, 8, width), axis=1)
     norm_one = norm_one.reshape(2, devices, norm_own).transpose(1, 0, 2).reshape(devices, -1)
     norm_one = lax.all_to_all(norm_one, everywhere, split_axis=0, concat_axis=0, tiled=True)
+    norm_one, in_grad = in_order(norm_one, in_grad)
+    in_grad = in_grad.astype(f32)
+    in_square = jnp.sum(in_grad * in_grad)
     norm_one = jnp.sum(norm_one, axis=0).reshape(2, norm_own)
-    out_grad_w, out_square = turn(out_turned[0])
-    out_grad_w = out_grad_w[None]
     activations = activations_of([returned], slot_col, gate, after)
     second = sum_far(second)
-    first = sum_far(jnp.concatenate([rest, first], axis=-1)).astype(low)
+    first = sum_across(first)
     first, second, in_square, out_square, norm_one, activations = in_order(
         first, second, in_square, out_square, norm_one, activations
     )
-    first = sum_across(first)
 
     proj_grad = first[:, :width]
     extra = first[:, width : width + LANES].reshape(-1)
     norm_grad = jnp.concatenate([norm_one, extra[: 2 * norm_own].reshape(2, norm_own)], axis=0)
     centre_grad = extra[2 * norm_own : 2 * norm_own + centre_own].reshape(centroids.shape)
-    owned = [first[:, width + LANES :], second]
-    qkv_grad = jnp.concatenate(
-        [
-            half[:, (3 * k + s) * wide : (3 * k + s + 1) * wide]
-            for s in range(3)
-            for half in owned
-            for k in range(groups // 2)
-        ],
-        axis=1,
-    )
+    owned = jnp.concatenate([first[:, width + LANES :], second], axis=1)
+    qkv_grad = owned.reshape(rows_own, groups, 3, wide).swapaxes(1, 2).reshape(rows_own, 3 * width)
     square_sum = (
-        jnp.sum(qkv_grad * qkv_grad)
+        jnp.sum(owned * owned)
         + jnp.sum(proj_grad * proj_grad)
         + jnp.sum(norm_grad * norm_grad)
         + jnp.sum(centre_grad * centre_grad)

time: 694 us -> 649 us (0.935)
  waiting for transfers between devices: 198 us -> 141 us
  starting transfers between devices: 66.3 us -> 77.9 us
  local copies, waits for them, and re-layouts: 22.3 us -> 31.7 us
    all_gather x3, waiting for transfers between devices: 65.3 us -> 0.02 us  [the longest x1 0.01 us: shards(): weight_in = lax.all_gather(in_low, 'dp', axis=1, tiled=True)[0]]
    ppermute x10 -> x13, waiting for transfers between devices: 15.2 us -> 41.9 us  [swap(): return lax.ppermute(values, axis, [(i, i ^ distance) for i in range(size)])]
    ppermute x10, waiting for transfers between devices: 37.1 us -> 11.7 us  [sum_over_pairs(): total = total + lax.ppermute(block, everywhere, perm).astype(f32)]
    all_to_all x0 -> x1, waiting for transfers between devices: none -> 12.1 us  [shards(): lax.all_to_all(spread, 'expert', split_axis=0, concat_axis=0, tiled=True)]
    all_to_all x0 -> x1, starting transfers between devices: none -> 7.28 us  [shards(): lax.all_to_all(spread, 'expert', split_axis=0, concat_axis=0, tiled=True)]
    unnamed x106 -> x147, local copies, waits for them, and re-layouts: 9.13 us -> 16.1 us
    ppermute x10 -> x13, starting transfers between devices: 14.6 us -> 17.5 us  [swap(): return lax.ppermute(values, axis, [(i, i ^ distance) for i in range(size)])]
    dot_general x2 -> x4, matrix products: 15.8 us -> 15.3 us  [the longest x2 11 us: shards(): jnp.dot(normed_low, weight, preferred_element_type=f32).astype(low)]
  transfers between devices with their start and end apart: 33 -> 37, of which waited for: 18 -> 16; matrix products, arithmetic and copies ran while one was open for 15% -> 16% of each run, Pallas kernels for 36% -> 38%
where the time goes in v4:
time: 649 us; the launch traced here: 642 us
  Pallas kernels  247 us (38%)
  waiting for transfers between devices  141 us (22%)
  starting transfers between devices  77.9 us (12%)
  other arithmetic  70.8 us (11%)
  matrix products  50.8 us (8%)
  local copies, waits for them, and re-layouts  31.7 us (5%)
  between operations  23.1 us (4%)
    all_to_all x7, waiting for transfers between devices, exchange(): lax.all_to_all(rows, 'expert', split_axis=0, concat_axis=0, tiled=True)  73.6 us
    pallas_call x2, Pallas kernels, expert_back(): pl.pallas_call(expert_back_kernel, grid=(count + width // columns,), in_s...  45 us
    pallas_call x2, Pallas kernels, expert_forward(): pl.pallas_call(expert_kernel, grid=(inner // tile,), in_specs=[pl.BlockSp...  42.7 us
    ppermute x13, waiting for transfers between devices, swap(): return lax.ppermute(values, axis, [(i, i ^ distance) for i in range(size)])  41.9 us
    pallas_call x4, Pallas kernels, attend_back(): pl.pallas_call(attend_back_kernel, grid=(tokens // SEQ, count), in_specs=...  38.4 us
    pallas_call x1, Pallas kernels, weight_grads(): pl.pallas_call(lambda *refs: weight_grads_kernel(chunks, refs), grid=(2 *...  38.1 us
    all_to_all x7, starting transfers between devices, exchange(): lax.all_to_all(rows, 'expert', split_axis=0, concat_axis=0, tiled=True)  32.1 us
    pallas_call x2, Pallas kernels, attend(): pl.pallas_call(attend_kernel, grid=(count // SEQ, pairs), in_specs=[part(...  29.3 us
  transfers between devices with their start and end apart: 37, of which 16 were waited for; matrix products, arithmetic and copies ran while one was open for 16% of the time, Pallas kernels for 38%

profile of v4, /device:TPU:0, one launch (start us, length us, event | category | flops | bytes accessed | tf_op | source)
XLA Modules:
  0.0 642.0 jit_solution(6571932513326418234)
XLA Ops:
  12.4 7.3 %all-to-all-start = ((bf16[8,32,1664]{2,1,0:T(8,128)(2,1)}), bf16[8,32,1664]{2,1,0:T(8,128)(2,1)S(1)}, u32[]{:S(2)}, u32[]{:S(2)}) async-start(bf16[8,32,1664]{2,1,0:T(8,128)(2,1)} %broadcast_in_dim.55), calls=%async_computation | async-start | bytes 1703936 | tf_op jit(solution)/shard_map/all_to_all | solution.py:883
  32.7 12.1 %all-to-all-done.refs_0_ = bf16[8,32,1664]{2,1,0:T(8,128)(2,1)S(1)} async-done(((bf16[8,32,1664]{2,1,0:T(8,128)(2,1)}), bf16[8,32,1664]{2,1,0:T(8,128)(2,1)S(1)}, u32[]{:S(2)}, u32[]{:S(2)}) %all-to-all-start) | async-done | bytes 852000 | tf_op jit(solution)/shard_map/all_to_all | solution.py:883
  49.2 20.7 %collective-permute-done.1.refs_2_ = bf16[8,32,1664]{2,1,0:T(8,128)(2,1)S(1)} collective-permute-done((bf16[8,32,1664]{2,1,0:T(8,128)(2,1)S(1)}, bf16[8,32,1664]{2,1,0:T(8,128)(2,1)S(1)}, u32[]{:S(2)}, u32[]{:S(2)}) %collective-permute-start.1) | collective-permute-done | bytes 852000 | tf_op jit(solution)/shard_map/ppermute | solution.py:716
  88.1 14.7 %attend.2 = (bf16[1024,512]{1,0:T(8,128)(2,1)S(1)}, f32[32,1024]{1,0:T(8,128)S(1)}) custom-call(bf16[1024,1536]{1,0:T(8,128)(2,1)S(1)} %convolution_convert_fusion.2.q_ref.k_ref.v_ref, bf16[1024,1536]{1,0:T(8,128)(2,1)S(1)} %convolution_convert_fusion.2.q_ref.k_ref.v_ref, bf16[1024,1536]{1,0:T(8,128)(2,1)S(1)} %convolution_convert_fusion.2.q_ref.k_ref.v_ref, ...), custom_call_target="tpu_custom_call" | custom-call | flops 5510000128 | tf_op jit(solution)/shard_map/attend/pallas_call | solution.py:108
  105.4 5.6 convolution_convert_fusion.1.q_ref.k_ref.v_ref
  111.1 14.7 %attend.3 = (bf16[1024,512]{1,0:T(8,128)(2,1)S(1)}, f32[32,1024]{1,0:T(8,128)S(1)}) custom-call(bf16[1024,1536]{1,0:T(8,128)(2,1)S(1)} %convolution_convert_fusion.1.q_ref.k_ref.v_ref, bf16[1024,1536]{1,0:T(8,128)(2,1)S(1)} %convolution_convert_fusion.1.q_ref.k_ref.v_ref, bf16[1024,1536]{1,0:T(8,128)(2,1)S(1)} %convolution_convert_fusion.1.q_ref.k_ref.v_ref, ...), custom_call_target="tpu_custom_call" | custom-call | flops 5510000128 | tf_op jit(solution)/shard_map/attend/pallas_call | solution.py:108
  125.8 13.4 %after_attend.1 = (f32[1024,1024]{1,0:T(8,128)}, bf16[1024,1024]{1,0:T(8,128)(2,1)}, f32[1024,128]{1,0:T(8,128)S(1)}, bf16[768,1024]{1,0:T(8,128)(2,1)}, bf16[768,1024]{1,0:T(8,128)(2,1)}) custom-call(bf16[1024,512]{1,0:T(8,128)(2,1)S(1)} %copy-done.7, bf16[1024,512]{1,0:T(8,128)(2,1)S(1)} %get-tuple-element.116.refs_1_.mixed_ref, ...), custom_call_target="tpu_custom_call" | custom-call | flops 2470000128 | tf_op jit(solution)/shard_map/after_attend/pallas_call | solution.py:272
  152.6 29.7 %all-to-all-done.1.x_ref.refs_0_ = bf16[8,96,1024]{2,1,0:T(8,128)(2,1)S(1)} async-done(((bf16[8,96,1024]{2,1,0:T(8,128)(2,1)}), bf16[8,96,1024]{2,1,0:T(8,128)(2,1)S(1)}, u32[]{:S(2)}, u32[]{:S(2)}) %all-to-all-start.1) | async-done | bytes 1572896 | tf_op jit(solution)/shard_map/all_to_all | solution.py:925
  185.9 21.4 %expert_forward.2 = (bf16[8,192,4096]{2,1,0:T(8,128)(2,1)}, bf16[8,96,4096]{2,1,0:T(8,128)(2,1)}) custom-call(bf16[8,96,1024]{2,1,0:T(8,128)(2,1)} %copy-done.39, bf16[1024,4096]{1,0:T(8,128)(2,1)} %bitcast.184), custom_call_target="tpu_custom_call" | custom-call | flops 3990000128 | tf_op jit(solution)/shard_map/expert_forward/pallas_call | solution.py:477
  207.4 15.7 %all-to-all-done.2.x_ref.refs_1_ = bf16[8,96,1024]{2,1,0:T(8,128)(2,1)S(1)} async-done(((bf16[8,96,1024]{2,1,0:T(8,128)(2,1)}), bf16[8,96,1024]{2,1,0:T(8,128)(2,1)S(1)}, u32[]{:S(2)}, u32[]{:S(2)}) %all-to-all-start.2) | async-done | bytes 1572896 | tf_op jit(solution)/shard_map/all_to_all | solution.py:925
  227.2 21.3 %expert_forward.3 = (bf16[8,192,4096]{2,1,0:T(8,128)(2,1)}, bf16[8,96,4096]{2,1,0:T(8,128)(2,1)}) custom-call(bf16[8,96,1024]{2,1,0:T(8,128)(2,1)} %copy-done.35, bf16[1024,4096]{1,0:T(8,128)(2,1)} %bitcast.185, bf16[8,192,4096]{2,1,0:T(8,128)(2,1)} %get-tuple-element.128.rest_0_), custom_call_target="tpu_custom_call", output_to_operand_aliasing={{0}: (2, {})} | custom-call | flops 3990000128 | tf_op jit(solution)/shard_map/expert_forward/pallas_call | solution.py:477
  248.5 19.1 %convolution_convert_fusion = bf16[1536,1024]{1,0:T(8,128)(2,1)} fusion(bf16[1536,4096]{1,0:T(8,128)(2,1)} %bitcast.188, bf16[1,4096,1024]{2,1,0:T(8,128)(2,1)} %all-gather.8.cloned.1.call-done), kind=kOutput, calls=%fused_computation.21 | convolution fusion | flops 12886474752 | bytes 24117248 | tf_op jit(solution)/shard_map/dot_general | solution.py:948
  267.6 6.0 all-to-all-start.4
  274.2 22.5 %expert_back.2 = (bf16[8,192,4096]{2,1,0:T(8,128)(2,1)}, bf16[8,96,1024]{2,1,0:T(8,128)(2,1)}, f32[8,1024]{1,0:T(8,128)}) custom-call(bf16[8,96,1024]{2,1,0:T(8,128)(2,1)} %copy-done.40, bf16[8,96,4096]{2,1,0:T(8,128)(2,1)} %get-tuple-element.134.slope_ref, bf16[1024,4096]{1,0:T(8,128)(2,1)} %bitcast.186, bf16[4096,1024]{1,0:T(8,128)(2,1)} %bitcast.189, ...), custom_call_target="tpu_custom_call" | custom-call | flops 4369999872 | tf_op jit(solution)/shard_map/expert_back/pallas_call | solution.py:568
  296.7 13.5 %all-to-all-done.4.grad_ref.refs_3_ = bf16[8,96,1024]{2,1,0:T(8,128)(2,1)S(1)} async-done(((bf16[8,96,1024]{2,1,0:T(8,128)(2,1)}), bf16[8,96,1024]{2,1,0:T(8,128)(2,1)S(1)}, u32[]{:S(2)}, u32[]{:S(2)}) %all-to-all-start.4) | async-done | bytes 1572896 | tf_op jit(solution)/shard_map/all_to_all | solution.py:925
  314.1 22.5 %expert_back.3 = (bf16[8,192,4096]{2,1,0:T(8,128)(2,1)}, bf16[8,96,1024]{2,1,0:T(8,128)(2,1)}, f32[8,1024]{1,0:T(8,128)}) custom-call(bf16[8,96,1024]{2,1,0:T(8,128)(2,1)} %copy-done.38, bf16[8,96,4096]{2,1,0:T(8,128)(2,1)} %get-tuple-element.139.slope_ref, bf16[1024,4096]{1,0:T(8,128)(2,1)} %bitcast.187, ...), custom_call_target="tpu_custom_call", output_to_operand_aliasing={{0}: (7, {})} | custom-call | flops 4369999872 | tf_op jit(solution)/shard_map/expert_back/pallas_call | solution.py:568
  336.5 14.7 %all-to-all-done.5 = bf16[8,96,1024]{2,1,0:T(8,128)(2,1)S(1)} async-done(((bf16[8,96,1024]{2,1,0:T(8,128)(2,1)}), bf16[8,96,1024]{2,1,0:T(8,128)(2,1)S(1)}, u32[]{:S(2)}, u32[]{:S(2)}) %all-to-all-start.5) | async-done | bytes 1572896 | tf_op jit(solution)/shard_map/all_to_all | solution.py:925
  354.9 38.1 %weight_grads.1 = (bf16[1024,4096]{1,0:T(8,128)(2,1)}, bf16[1024,4096]{1,0:T(8,128)(2,1)}) custom-call(bf16[8,96,1024]{2,1,0:T(8,128)(2,1)} %copy-done.39, bf16[8,96,1024]{2,1,0:T(8,128)(2,1)} %copy-done.35, bf16[8,96,1024]{2,1,0:T(8,128)(2,1)} %copy-done.40, bf16[8,96,1024]{2,1,0:T(8,128)(2,1)} %copy-done.38, ...), custom_call_target="tpu_custom_call" | custom-call | flops 7219999744 | tf_op jit(solution)/shard_map/weight_grads/pallas_call | solution.py:660
  395.1 11.8 %before_attend_back.1 = (f32[1024,1024]{1,0:T(8,128)}, bf16[1024,1024]{1,0:T(8,128)(2,1)S(1)}, bf16[1024,1024]{1,0:T(8,128)(2,1)}, f32[16,1024]{1,0:T(8,128)S(1)}) custom-call(bf16[768,1024]{1,0:T(8,128)(2,1)S(1)} %bitcast.173, bf16[768,1024]{1,0:T(8,128)(2,1)S(1)} %bitcast.174, s32[1024,1]{1,0:T(8,128)S(1)} %copy-done.27, ...), custom_call_target="tpu_custom_call" | custom-call | flops 2280000000 | tf_op jit(solution)/shard_map/before_attend_back/pallas_call | solution.py:342
  408.4 6.1 all-to-all-start.7
  423.9 9.5 %attend_back.4.refs_0_ = bf16[1024,768]{1,0:T(8,128)(2,1)S(1)} custom-call(bf16[1024,1536]{1,0:T(8,128)(2,1)} %copy-done.1, bf16[1024,1536]{1,0:T(8,128)(2,1)} %copy-done.1, bf16[1024,1536]{1,0:T(8,128)(2,1)} %copy-done.1, bf16[1024,1024]{1,0:T(8,128)(2,1)S(1)} %copy-done.3, bf16[1024,512]{1,0:T(8,128)(2,1)S(1)} %copy-done.9, ...), custom_call_target="tpu_custom_call" | custom-call | flops 1824000000 | tf_op jit(solution)/shard_map/attend_back/pallas_call | solution.py:187
  439.8 9.8 %attend_back.5.refs_1_ = bf16[1024,768]{1,0:T(8,128)(2,1)S(1)} custom-call(bf16[1024,1536]{1,0:T(8,128)(2,1)} %copy-done.1, bf16[1024,1536]{1,0:T(8,128)(2,1)} %copy-done.1, bf16[1024,1536]{1,0:T(8,128)(2,1)} %copy-done.1, bf16[1024,1024]{1,0:T(8,128)(2,1)S(1)} %copy-done.3, bf16[1024,512]{1,0:T(8,128)(2,1)S(1)} %copy-done.9, ...), custom_call_target="tpu_custom_call" | custom-call | flops 1824000000 | tf_op jit(solution)/shard_map/attend_back/pallas_call | solution.py:187
  458.6 9.7 %attend_back.6.refs_2_ = bf16[1024,768]{1,0:T(8,128)(2,1)S(1)} custom-call(bf16[1024,1536]{1,0:T(8,128)(2,1)} %copy-done, bf16[1024,1536]{1,0:T(8,128)(2,1)} %copy-done, bf16[1024,1536]{1,0:T(8,128)(2,1)} %copy-done, bf16[1024,1024]{1,0:T(8,128)(2,1)S(1)} %copy-done.3, bf16[1024,512]{1,0:T(8,128)(2,1)S(1)} %copy-done.5, ...), custom_call_target="tpu_custom_call" | custom-call | flops 1824000000 | tf_op jit(solution)/shard_map/attend_back/pallas_call | solution.py:187
  471.4 5.7 collective-permute-done.4
  481.4 6.5 %turn.1 = (f32[4096,256]{1,0:T(8,128)}, f32[8,512]{1,0:T(8,128)}) custom-call(bf16[256,4096]{1,0:T(8,128)(2,1)} %bitcast.226), custom_call_target="tpu_custom_call" | custom-call | flops 570000000 | tf_op jit(solution)/shard_map/turn/pallas_call | solution.py:696
  494.2 9.5 %attend_back.7.refs_3_ = bf16[1024,768]{1,0:T(8,128)(2,1)S(1)} custom-call(bf16[1024,1536]{1,0:T(8,128)(2,1)} %copy-done, bf16[1024,1536]{1,0:T(8,128)(2,1)} %copy-done, bf16[1024,1536]{1,0:T(8,128)(2,1)} %copy-done, bf16[1024,1024]{1,0:T(8,128)(2,1)S(1)} %copy-done.3, bf16[1024,512]{1,0:T(8,128)(2,1)S(1)} %copy-done.5, ...), custom_call_target="tpu_custom_call" | custom-call | flops 1824000000 | tf_op jit(solution)/shard_map/attend_back/pallas_call | solution.py:187
  503.7 5.6 collective-permute-done.6
  531.9 13.9 %input_gradient.1 = (f32[1024,1024]{1,0:T(8,128)}, f32[16,1024]{1,0:T(8,128)S(1)}) custom-call(bf16[1024,768]{1,0:T(8,128)(2,1)S(1)} %copy-done.18, bf16[1024,768]{1,0:T(8,128)(2,1)S(1)} %copy-done.20, bf16[1024,768]{1,0:T(8,128)(2,1)S(1)} %copy-done.22, bf16[1024,768]{1,0:T(8,128)(2,1)} %copy-done.23, bf16[1024,1664]{1,0:T(8,128)(2,1)} %copy-done.2, ...), custom_call_target="tpu_custom_call" | custom-call | flops 2660000000 | tf_op jit(solution)/shard_map/input_gradient/pallas_call | solution.py:396
  545.9 11.5 %collective-permute-done.9 = bf16[2,32,2688]{2,1,0:T(8,128)(2,1)S(1)} collective-permute-done((bf16[2,32,2688]{2,1,0:T(8,128)(2,1)S(1)}, bf16[2,32,2688]{2,1,0:T(8,128)(2,1)S(1)}, u32[]{:S(2)}, u32[]{:S(2)}) %collective-permute-start.9) | collective-permute-done | bytes 344096 | tf_op jit(solution)/shard_map/ppermute | solution.py:773
  569.3 7.6 %activations_of.1 = bf16[1024,1024]{1,0:T(8,128)(2,1)} custom-call(bf16[1536,1024]{1,0:T(8,128)(2,1)} %bitcast.38.refs_0_, s32[1024,1]{1,0:T(8,128)S(1)} %copy-done.26, f32[1024,128]{1,0:T(8,128)S(1)} %copy-done.32, f32[1024,1024]{1,0:T(8,128)} %get-tuple-element.153.refs_3_), custom_call_target="tpu_custom_call" | custom-call | flops 1424999936 | tf_op jit(solution)/shard_map/activations_of/pallas_call | solution.py:430
  607.8 11.4 %multiply_add_fusion.1 = (f32[1,256,4096]{2,1,0:T(8,128)}, f32[1,256,4096]{2,1,0:T(8,128)}, f32[1,256,4096]{2,1,0:T(8,128)}) fusion(f32[1,256,4096]{2,1,0:T(8,128)} %param.42, f32[1,256,4096]{2,1,0:T(8,128)} %param.30, f32[]{:T(128)S(6)} %div.67, bf16[1,256,4096]{2,1,0:T(8,128)(2,1)S(1)} %copy-done.41, f32[1,256,4096]{2,1,0:T(8,128)} %param.36), kind=kLoop, calls=%fused_computation.20 | loop fusion | flops 11534336 | bytes 27262980 | tf_op jit(solution)/shard_map/add | solution.py:813
  620.6 11.8 %multiply_add_fusion = (f32[1,4096,256]{2,1,0:T(8,128)}, f32[1,4096,256]{2,1,0:T(8,128)}, f32[1,4096,256]{2,1,0:T(8,128)}) fusion(f32[1,4096,256]{2,1,0:T(8,128)} %param.43, f32[1,4096,256]{2,1,0:T(8,128)} %param.31, f32[4096,256]{1,0:T(8,128)} %get-tuple-element.202, f32[]{:T(128)S(6)} %div.67, f32[1,4096,256]{2,1,0:T(8,128)} %param.37), kind=kLoop, calls=%fused_computation.19 | loop fusion | flops 10485760 | bytes 29360132 | tf_op jit(solution)/shard_map/add | solution.py:813
  (335 shorter events, 175.6 us)
Async XLA Ops:
  7.2 98.2 %all-gather.4.cloned.1.call-start = ((), (), s32[]{:S(2)}) async-start(), calls=%async_computation.11 | async-start | bytes 5406720 | tf_op jit(solution)/shard_map/all_gather | solution.py:865
  12.4 32.4 %all-to-all-start = ((bf16[8,32,1664]{2,1,0:T(8,128)(2,1)}), bf16[8,32,1664]{2,1,0:T(8,128)(2,1)S(1)}, u32[]{:S(2)}, u32[]{:S(2)}) async-start(bf16[8,32,1664]{2,1,0:T(8,128)(2,1)} %broadcast_in_dim.55), calls=%async_computation | async-start | bytes 1703936 | tf_op jit(solution)/shard_map/all_to_all | solution.py:883
  19.6 166.3 %all-gather.6.cloned.1.call-start = ((), (), s32[]{:S(2)}) async-start(), calls=%async_computation.12 | async-start | bytes 10485760 | tf_op jit(solution)/shard_map/all_gather | solution.py:894
  44.8 203.7 %all-gather.8.cloned.1.call-start = ((), (), s32[]{:S(2)}) async-start(), calls=%async_computation.13 | async-start | bytes 10485760 | tf_op jit(solution)/shard_map/all_gather | solution.py:895
  45.5 24.3 %collective-permute-start.1 = (bf16[8,32,1664]{2,1,0:T(8,128)(2,1)S(1)}, bf16[8,32,1664]{2,1,0:T(8,128)(2,1)S(1)}, u32[]{:S(2)}, u32[]{:S(2)}) collective-permute-start(bf16[8,32,1664]{2,1,0:T(8,128)(2,1)S(1)} %all-to-all-done.refs_0_), channel_id=1, source_target_pairs={{0,2},{1,3},{2,0},{3,1},{4,6},{5,7},{6,4},{7,5},{8,10},{9,11},{10,... | collective-permute-start | bytes 2555912 | tf_op jit(solution)/shard_map/ppermute | solution.py:716
  49.2 23.7 %collective-permute-start = (bf16[8,32,1664]{2,1,0:T(8,128)(2,1)S(1)}, bf16[8,32,1664]{2,1,0:T(8,128)(2,1)S(1)}, u32[]{:S(2)}, u32[]{:S(2)}) collective-permute-start(bf16[8,32,1664]{2,1,0:T(8,128)(2,1)S(1)} %all-to-all-done.refs_0_), channel_id=1, source_target_pairs={{0,1},{1,0},{2,3},{3,2},{4,5},{5,4},{6,7},{7,6},{8,9},{9,8},{10,11... | collective-permute-start | bytes 2555912 | tf_op jit(solution)/shard_map/ppermute | solution.py:716
  140.0 42.3 %all-to-all-start.1 = ((bf16[8,96,1024]{2,1,0:T(8,128)(2,1)}), bf16[8,96,1024]{2,1,0:T(8,128)(2,1)S(1)}, u32[]{:S(2)}, u32[]{:S(2)}) async-start(bf16[8,96,1024]{2,1,0:T(8,128)(2,1)} %bitcast.12), calls=%async_computation.1 | async-start | bytes 3145728 | tf_op jit(solution)/shard_map/all_to_all | solution.py:925
  182.3 40.8 %all-to-all-start.2 = ((bf16[8,96,1024]{2,1,0:T(8,128)(2,1)}), bf16[8,96,1024]{2,1,0:T(8,128)(2,1)S(1)}, u32[]{:S(2)}, u32[]{:S(2)}) async-start(bf16[8,96,1024]{2,1,0:T(8,128)(2,1)} %bitcast.209), calls=%async_computation.2 | async-start | bytes 3145728 | tf_op jit(solution)/shard_map/all_to_all | solution.py:925
  223.1 44.5 %all-to-all-start.3 = ((bf16[8,96,1024]{2,1,0:T(8,128)(2,1)}), bf16[8,96,1024]{2,1,0:T(8,128)(2,1)S(1)}, u32[]{:S(2)}, u32[]{:S(2)}) async-start(bf16[8,96,1024]{2,1,0:T(8,128)(2,1)} %bitcast.208), calls=%async_computation.3 | async-start | bytes 3145728 | tf_op jit(solution)/shard_map/all_to_all | solution.py:925
  267.6 42.6 %all-to-all-start.4 = ((bf16[8,96,1024]{2,1,0:T(8,128)(2,1)}), bf16[8,96,1024]{2,1,0:T(8,128)(2,1)S(1)}, u32[]{:S(2)}, u32[]{:S(2)}) async-start(bf16[8,96,1024]{2,1,0:T(8,128)(2,1)} %bitcast.207), calls=%async_computation.4 | async-start | bytes 3145728 | tf_op jit(solution)/shard_map/all_to_all | solution.py:925
  310.2 41.0 %all-to-all-start.5 = ((bf16[8,96,1024]{2,1,0:T(8,128)(2,1)}), bf16[8,96,1024]{2,1,0:T(8,128)(2,1)S(1)}, u32[]{:S(2)}, u32[]{:S(2)}) async-start(bf16[8,96,1024]{2,1,0:T(8,128)(2,1)} %get-tuple-element.142), calls=%async_computation.5 | async-start | bytes 3145728 | tf_op jit(solution)/shard_map/all_to_all | solution.py:925
  351.2 41.8 %all-to-all-start.6 = ((bf16[8,96,1024]{2,1,0:T(8,128)(2,1)}), bf16[8,96,1024]{2,1,0:T(8,128)(2,1)S(1)}, u32[]{:S(2)}, u32[]{:S(2)}) async-start(bf16[8,96,1024]{2,1,0:T(8,128)(2,1)} %get-tuple-element.145), calls=%async_computation.6 | async-start | bytes 3145728 | tf_op jit(solution)/shard_map/all_to_all | solution.py:925
  354.9 126.5 %reduce-scatter.3.cloned.1.call-start = ((), (), s32[]{:S(2)}) async-start(), calls=%async_computation.14 | async-start | bytes 10485760 | tf_op jit(solution)/shard_map/reduce_scatter | solution.py:987
  393.0 183.9 %reduce-scatter.5.cloned.1.call-start = ((), (), s32[]{:S(2)}) async-start(), calls=%async_computation.15 | async-start | bytes 10485760 | tf_op jit(solution)/shard_map/reduce_scatter | solution.py:986
  408.4 80.9 %all-to-all-start.7 = ((bf16[8,192,1024]{2,1,0:T(8,128)(2,1)}), bf16[8,192,1024]{2,1,0:T(8,128)(2,1)}, u32[]{:S(2)}, u32[]{:S(2)}) async-start(bf16[8,192,1024]{2,1,0:T(8,128)(2,1)} %bitcast.193), calls=%async_computation.7 | async-start | bytes 6291456 | tf_op jit(solution)/shard_map/all_to_all | solution.py:925
  421.6 14.8 %collective-permute-start.3 = (bf16[8,2,32,1152]{3,2,1,0:T(8,128)(2,1)}, bf16[8,2,32,1152]{3,2,1,0:T(8,128)(2,1)}, u32[]{:S(2)}, u32[]{:S(2)}) collective-permute-start(bf16[8,2,32,1152]{3,2,1,0:T(8,128)(2,1)} %fusion.28), channel_id=1, source_target_pairs={{0,1},{1,0},{2,3},{3,2},{4,5},{5,4},{6,7},{7,6},{8,9},{9,8},{10,11... | collective-permute-start | bytes 3538952 | tf_op jit(solution)/shard_map/ppermute | solution.py:716
  453.8 24.3 %collective-permute-start.5 = (bf16[8,2,32,1536]{3,2,1,0:T(8,128)(2,1)}, bf16[8,2,32,1536]{3,2,1,0:T(8,128)(2,1)}, u32[]{:S(2)}, u32[]{:S(2)}) collective-permute-start(bf16[8,2,32,1536]{3,2,1,0:T(8,128)(2,1)} %pad_maximum_fusion.1), channel_id=1, source_target_pairs={{0,1},{1,0},{2,3},{3,2},{4,5},{5,4},{6,7},{7,6},{8,9},{9,8},{10,11... | collective-permute-start | bytes 4718600 | tf_op jit(solution)/shard_map/ppermute | solution.py:716
  455.4 21.6 %collective-permute-start.4 = (bf16[4,2,32,1152]{3,2,1,0:T(8,128)(2,1)S(1)}, bf16[4,2,32,1152]{3,2,1,0:T(8,128)(2,1)S(1)}, u32[]{:S(2)}, u32[]{:S(2)}) collective-permute-start(bf16[4,2,32,1152]{3,2,1,0:T(8,128)(2,1)S(1)} %dynamic-slice_bitcast_fusion.9), channel_id=1, source_target_pairs={{0,4},{4,0},{8,12},{12,8},{16,20},{20,16},{24,28},{28,24},{1,5},{5... | collective-permute-start | bytes 1769480 | tf_op jit(solution)/shard_map/ppermute | solution.py:716
  490.4 18.9 %collective-permute-start.6 = (bf16[4,2,32,1536]{3,2,1,0:T(8,128)(2,1)S(1)}, bf16[4,2,32,1536]{3,2,1,0:T(8,128)(2,1)S(1)}, u32[]{:S(2)}, u32[]{:S(2)}) collective-permute-start(bf16[4,2,32,1536]{3,2,1,0:T(8,128)(2,1)S(1)} %dynamic-slice_bitcast_fusion.3), channel_id=1, source_target_pairs={{0,4},{4,0},{8,12},{12,8},{16,20},{20,16},{24,28},{28,24},{1,5},{5... | collective-permute-start | bytes 2359304 | tf_op jit(solution)/shard_map/ppermute | solution.py:716
  521.5 24.4 %collective-permute-start.10 = (bf16[2,32,2688]{2,1,0:T(8,128)(2,1)S(1)}, bf16[2,32,2688]{2,1,0:T(8,128)(2,1)S(1)}, u32[]{:S(2)}, u32[]{:S(2)}) collective-permute-start(bf16[2,32,2688]{2,1,0:T(8,128)(2,1)S(1)} %get-tuple-element.235), channel_id=1, source_target_pairs={{0,24},{1,25},{2,26},{3,27},{4,28},{5,29},{6,30},{7,31},{8,16},{9,... | collective-permute-start | bytes 1032200 | tf_op jit(solution)/shard_map/ppermute | solution.py:773
  527.0 18.9 %collective-permute-start.8 = (bf16[2,32,2688]{2,1,0:T(8,128)(2,1)S(1)}, bf16[2,32,2688]{2,1,0:T(8,128)(2,1)S(1)}, u32[]{:S(2)}, u32[]{:S(2)}) collective-permute-start(bf16[2,32,2688]{2,1,0:T(8,128)(2,1)S(1)} %get-tuple-element.234), channel_id=1, source_target_pairs={{0,8},{1,9},{2,10},{3,11},{4,12},{5,13},{6,14},{7,15},{8,0},{9,1},... | collective-permute-start | bytes 1032200 | tf_op jit(solution)/shard_map/ppermute | solution.py:773
  527.0 30.5 %collective-permute-start.9 = (bf16[2,32,2688]{2,1,0:T(8,128)(2,1)S(1)}, bf16[2,32,2688]{2,1,0:T(8,128)(2,1)S(1)}, u32[]{:S(2)}, u32[]{:S(2)}) collective-permute-start(bf16[2,32,2688]{2,1,0:T(8,128)(2,1)S(1)} %get-tuple-element.236), channel_id=1, source_target_pairs={{0,16},{1,17},{2,18},{3,19},{4,20},{5,21},{6,22},{7,23},{8,24},{9,... | collective-permute-start | bytes 1032200 | tf_op jit(solution)/shard_map/ppermute | solution.py:773
  527.7 29.9 %collective-permute-start.11 = (bf16[4,32,1536]{2,1,0:T(8,128)(2,1)S(1)}, bf16[4,32,1536]{2,1,0:T(8,128)(2,1)S(1)}, u32[]{:S(2)}, u32[]{:S(2)}) collective-permute-start(bf16[4,32,1536]{2,1,0:T(8,128)(2,1)S(1)} %get-tuple-element.223), channel_id=1, source_target_pairs={{0,2},{1,3},{2,0},{3,1},{4,6},{5,7},{6,4},{7,5},{8,10},{9,11},{10,... | collective-permute-start | bytes 1179656 | tf_op jit(solution)/shard_map/ppermute | solution.py:773
  530.1 27.5 %collective-permute-start.12 = (bf16[4,32,1536]{2,1,0:T(8,128)(2,1)S(1)}, bf16[4,32,1536]{2,1,0:T(8,128)(2,1)S(1)}, u32[]{:S(2)}, u32[]{:S(2)}) collective-permute-start(bf16[4,32,1536]{2,1,0:T(8,128)(2,1)S(1)} %get-tuple-element.225), channel_id=1, source_target_pairs={{0,4},{1,5},{2,6},{3,7},{4,0},{5,1},{6,2},{7,3},{8,12},{9,13},{10,... | collective-permute-start | bytes 1179656 | tf_op jit(solution)/shard_map/ppermute | solution.py:773
  545.8 12.0 %collective-permute-start.13 = (bf16[4,32,1536]{2,1,0:T(8,128)(2,1)S(1)}, bf16[4,32,1536]{2,1,0:T(8,128)(2,1)S(1)}, u32[]{:S(2)}, u32[]{:S(2)}) collective-permute-start(bf16[4,32,1536]{2,1,0:T(8,128)(2,1)S(1)} %get-tuple-element.224), channel_id=1, source_target_pairs={{0,6},{1,7},{2,4},{3,5},{4,2},{5,3},{6,0},{7,1},{8,14},{9,15},{10,... | collective-permute-start | bytes 1179656 | tf_op jit(solution)/shard_map/ppermute | solution.py:773
  558.9 18.0 %all-to-all-start.8 = ((f32[32,1,64]{2,1,0:T(1,128)}), f32[32,1,64]{2,1,0:T(1,128)S(1)}, u32[]{:S(2)}, u32[]{:S(2)}) async-start(f32[32,1,64]{2,1,0:T(1,128)} %bitcast.67), calls=%async_computation.9 | async-start | bytes 32768 | tf_op jit(solution)/shard_map/all_to_all | solution.py:1064
  563.0 17.3 %collective-permute-start.15 = (bf16[32,1536]{1,0:T(8,128)(2,1)S(1)}, bf16[32,1536]{1,0:T(8,128)(2,1)S(1)}, u32[]{:S(2)}, u32[]{:S(2)}) collective-permute-start(bf16[32,1536]{1,0:T(8,128)(2,1)S(1)} %get-tuple-element.239), channel_id=1, source_target_pairs={{0,8},{1,9},{2,10},{3,11},{4,12},{5,13},{6,14},{7,15},{8,0},{9,1},... | collective-permute-start | bytes 294920 | tf_op jit(solution)/shard_map/ppermute | solution.py:773
  564.8 15.5 %collective-permute-start.16 = (bf16[32,1536]{1,0:T(8,128)(2,1)S(1)}, bf16[32,1536]{1,0:T(8,128)(2,1)S(1)}, u32[]{:S(2)}, u32[]{:S(2)}) collective-permute-start(bf16[32,1536]{1,0:T(8,128)(2,1)S(1)} %get-tuple-element.241), channel_id=1, source_target_pairs={{0,16},{1,17},{2,18},{3,19},{4,20},{5,21},{6,22},{7,23},{8,24},{9,... | collective-permute-start | bytes 294920 | tf_op jit(solution)/shard_map/ppermute | solution.py:773
  567.2 13.1 %collective-permute-start.17 = (bf16[32,1536]{1,0:T(8,128)(2,1)S(1)}, bf16[32,1536]{1,0:T(8,128)(2,1)S(1)}, u32[]{:S(2)}, u32[]{:S(2)}) collective-permute-start(bf16[32,1536]{1,0:T(8,128)(2,1)S(1)} %get-tuple-element.240), channel_id=1, source_target_pairs={{0,24},{1,25},{2,26},{3,27},{4,28},{5,29},{6,30},{7,31},{8,16},{9,... | collective-permute-start | bytes 294920 | tf_op jit(solution)/shard_map/ppermute | solution.py:773
  567.4 12.9 %collective-permute-start.14 = (bf16[32,2688]{1,0:T(8,128)(2,1)S(1)}, bf16[32,2688]{1,0:T(8,128)(2,1)S(1)}, u32[]{:S(2)}, u32[]{:S(2)}) collective-permute-start(bf16[32,2688]{1,0:T(8,128)(2,1)S(1)} %dynamic-slice_bitcast_fusion.16), channel_id=1, source_target_pairs={{0,2},{1,3},{2,0},{3,1},{4,6},{5,7},{6,4},{7,5},{8,10},{9,11},{10,... | collective-permute-start | bytes 516104 | tf_op jit(solution)/shard_map/ppermute | solution.py:773
  588.9 3.7 collective-permute-start.19
  601.8 4.6 collective-permute-start.22
  (78 other events, 583.8 us)
Sparse Core Ops, SparseCore 0:
  11.5 76.9 all-gather.3
  90.6 57.7 all-gather.5
  150.6 59.3 all-gather.7
  393.1 73.8 reduce-scatter.2
  469.7 80.6 reduce-scatter.4

commit v5 on v4

--- a/solution.py
+++ b/solution.py
@@ -78,18 +78,27 @@
     def _():
         fill_bias(bias, doc_col, doc_row, False)
 
+    def scores_of(block):
+        seen = block + BLOCK
+        query = q_ref[block:seen, :] * jnp.asarray(scale_qk, low)
+        return [dot_cols(keep_head(query, head), k_ref[:seen, :]) for head in range(2)]
+
+    following = scores_of(0)
     for block in range(0, SEQ, BLOCK):
         seen = block + BLOCK
-        query = q_ref[block:seen, :] * jnp.asarray(scale_qk, low)
-        outs, stats = [], []
+        current = following
+        if seen < SEQ:
+            following = scores_of(seen)
+        weights, outs, stats = [], [], []
         for head in range(2):
-            scores = dot_cols(keep_head(query, head), k_ref[:seen, :])
-            scores = jnp.minimum(scores, bias[block:seen, :seen])
+            scores = jnp.minimum(current[head], bias[block:seen, :seen])
             top = jnp.max(scores, axis=-1, keepdims=True)
             exponent = jnp.exp(scores - top)
             total = jnp.sum(exponent, axis=-1, keepdims=True)
-            outs.append(dot_rows(exponent.astype(low), v_ref[:seen, :]) / total)
+            weights.append((exponent.astype(low), total))
             stats.append(top + jnp.log(total))
+        for exponent, total in weights:
+            outs.append(dot_rows(exponent, v_ref[:seen, :]) / total)
         first = in_head((BLOCK, LANES), 0, 1)
         mixed_ref[block:seen, :] = jnp.where(first, outs[0], outs[1]).astype(low)
         lane = lax.broadcasted_iota(jnp.int32, (BLOCK, LANES), 1)
@@ -677,38 +686,47 @@
     )(*arrived, *grad_arrived, grad_preact, hidden)
 
 
-def turn_kernel(in_ref, out_ref, square_ref):
-    values = in_ref[...].astype(f32)
-    out_ref[...] = in_ref[...].T.astype(f32)
-    square = sum_slabs(values * values)
-
-    @pl.when(pl.program_id(0) == 0)
-    def _():
-        square_ref[...] = square
-
-    @pl.when(pl.program_id(0) > 0)
-    def _():
-        square_ref[...] += square
-
-
-def turn(values, tile=512):
-    rows, columns = values.shape
-    turned, square = pl.pallas_call(
-        turn_kernel,
+def update(weight, moment, average, gradient, factor, rate):
+    clipped = gradient * factor
+    moment_new = momentum_rate * moment + clipped
+    weight_new = weight - rate * (clipped + momentum_rate * moment_new)
+    average_new = average_rate * average + (1.0 - average_rate) * weight_new
+    return (weight_new, moment_new, average_new)
+
+
+def step_kernel(factor_ref, *refs):
+    inputs, outputs = refs[:8], refs[8:]
+    factor = factor_ref[0]
+    for which in range(2):
+        weight, moment, average, gradient = inputs[4 * which : 4 * which + 4]
+        gradient = gradient[...] if which == 0 else gradient[...].T
+        stepped = update(
+            weight[0], moment[0], average[0], gradient.astype(f32), factor, learn_rate
+        )
+        for out, value in zip(outputs[3 * which : 3 * which + 3], stepped):
+            out[0] = value
+
+
+def step_experts(factor, first, second, tile=256):
+    rows, columns = first[0].shape[1:]
+    along = pl.BlockSpec((1, rows, tile), lambda j: (0, 0, j))
+    down = pl.BlockSpec((1, tile, rows), lambda j: (0, j, 0))
+    gradient = pl.BlockSpec((rows, tile), lambda j: (0, j))
+    return pl.pallas_call(
+        step_kernel,
         grid=(columns // tile,),
-        in_specs=[pl.BlockSpec((rows, tile), lambda j: (0, j))],
-        out_specs=[
-            pl.BlockSpec((tile, rows), lambda j: (j, 0)),
-            pl.BlockSpec((8, tile), lambda j: (0, 0)),
-        ],
-        out_shape=[
-            jax.ShapeDtypeStruct((columns, rows), f32),
-            jax.ShapeDtypeStruct((8, tile), f32),
-        ],
-        cost_estimate=hint(3),
-        name="turn",
-    )(values)
-    return turned, jnp.sum(square)
+        in_specs=[pl.BlockSpec(memory_space=pltpu.SMEM)]
+        + [along] * 3
+        + [gradient]
+        + [down] * 3
+        + [gradient],
+        out_specs=[along] * 3 + [down] * 3,
+        out_shape=[jax.ShapeDtypeStruct(first[0].shape, f32)] * 3
+        + [jax.ShapeDtypeStruct(second[0].shape, f32)] * 3,
+        compiler_params=pltpu.CompilerParams(vmem_limit_bytes=48 * 2**20),
+        cost_estimate=hint(20),
+        name="step_experts",
+    )(factor.reshape(1), *first, *second)
 
 
 def swap(values, axis, distance):
@@ -762,16 +780,22 @@
     return sum_halves([held], "expert", 1, 0)
 
 
-def sum_over_pairs(held, partners, keep):
+def sum_over_pairs(held, partners, keep, *beside):
     experts, dp = lax.axis_size("expert"), lax.axis_size("dp")
     total = lax.dynamic_index_in_dim(held, keep, 0, keepdims=False).astype(f32)
+    received = []
     for offset, (far, near) in enumerate(partners, 1):
         block = lax.dynamic_index_in_dim(held, jnp.bitwise_xor(keep, offset), 0, keepdims=False)
         perm = [
             (e * dp + d, (e ^ far) * dp + (d ^ near)) for e in range(experts) for d in range(dp)
         ]
-        total = total + lax.ppermute(block, everywhere, perm).astype(f32)
-    return total
+        received.append(lax.ppermute(block, everywhere, perm))
+    if beside:
+        moved = in_order(*received, *beside)
+        received, beside = moved[: len(received)], moved[len(received) :]
+    for block in received:
+        total = total + block.astype(f32)
+    return (total, *beside) if beside else total
 
 
 def sum_near(held):
@@ -782,9 +806,9 @@
     return sum_over_pairs(held, partners, keep).astype(low)
 
 
-def sum_far(held):
+def sum_far(held, *beside):
     partners = [(2 * i, 0) for i in range(1, held.shape[0])]
-    return sum_over_pairs(held, partners, lax.axis_index("expert") // 2)
+    return sum_over_pairs(held, partners, lax.axis_index("expert") // 2, *beside)
 
 
 def sum_across(held):
@@ -804,14 +828,6 @@
             held = held + swap(held, axis, distance)
             distance *= 2
     return held[0, 0]
-
-
-def update(weight, moment, average, gradient, factor, rate):
-    clipped = gradient * factor
-    moment_new = momentum_rate * moment + clipped
-    weight_new = weight - rate * (clipped + momentum_rate * moment_new)
-    average_new = average_rate * average + (1.0 - average_rate) * weight_new
-    return (weight_new, moment_new, average_new)
 
 
 def shards(
@@ -1031,11 +1047,7 @@
         if g == groups - 1:
             rest = sum_over_neighbours(rest)
             first = sum_over_cores([by_owner(v) for v in grads[: groups // 2]])
-            out_grad_w, out_square = turn(out_turned[0])
-            rest, first, grad_mixed, returned, out_grad_w, out_square = in_order(
-                rest, first, grad_mixed, returned, out_grad_w, out_square
-            )
-            out_grad_w = out_grad_w[None]
+            rest, first, grad_mixed, returned = in_order(rest, first, grad_mixed, returned)
             first = sum_over_neighbours(first)
             part, grad, first = back_group(g, first)
         else:
@@ -1062,12 +1074,14 @@
     norm_one = jnp.sum(sums_one.reshape(2, 8, width), axis=1)
     norm_one = norm_one.reshape(2, devices, norm_own).transpose(1, 0, 2).reshape(devices, -1)
     norm_one = lax.all_to_all(norm_one, everywhere, split_axis=0, concat_axis=0, tiled=True)
-    norm_one, in_grad = in_order(norm_one, in_grad)
-    in_grad = in_grad.astype(f32)
-    in_square = jnp.sum(in_grad * in_grad)
+    norm_one, in_grad, out_turned = in_order(norm_one, in_grad, out_turned)
+    in_square = jnp.sum(jnp.square(in_grad.astype(f32)))
+    out_square = jnp.sum(jnp.square(out_turned.astype(f32)))
+    activations = activations_of([returned], slot_col, gate, after)
     norm_one = jnp.sum(norm_one, axis=0).reshape(2, norm_own)
-    activations = activations_of([returned], slot_col, gate, after)
-    second = sum_far(second)
+    second, activations, in_square, out_square = sum_far(
+        second, activations, in_square, out_square
+    )
     first = sum_across(first)
     first, second, in_square, out_square, norm_one, activations = in_order(
         first, second, in_square, out_square, norm_one, activations
@@ -1095,8 +1109,12 @@
     centre_new = update(
         centroids, centroid_moment, centroid_average, centre_grad, factor, learn_rate
     )
-    in_new = update(expert_in, in_moment, in_average, in_grad, factor, learn_rate)
-    out_new = update(expert_out, out_moment, out_average, out_grad_w, factor, learn_rate)
+    stepped = step_experts(
+        factor,
+        (expert_in, in_moment, in_average, in_grad[0]),
+        (expert_out, out_moment, out_average, out_turned[0]),
+    )
+    in_new, out_new = stepped[:3], stepped[3:]
     return (
         activations,
         input_grad,

time: 649 us -> 640 us (0.986)
  other arithmetic: 70.8 us -> 50.8 us
  Pallas kernels: 247 us -> 254 us
  waiting for transfers between devices: 141 us -> 148 us
    add x6 -> x4, other arithmetic: 26.2 us -> 5.4 us  [update(): average_new = average_rate * average + (1.0 - average_rate) * weight_new]
    pallas_call x1, Pallas kernels: 6.51 us -> 21.9 us  [step_experts(): pl.pallas_call(step_kernel, grid=(columns // tile,), in_specs=[pl.BlockSp...]
    pallas_call x2, Pallas kernels: 29.3 us -> 20.6 us  [attend(): pl.pallas_call(attend_kernel, grid=(count // SEQ, pairs), in_specs=[part(...]
    ppermute x10, waiting for transfers between devices: 11.7 us -> 19.8 us  [sum_over_pairs(): received.append(lax.ppermute(block, everywhere, perm))]
    unnamed x147 -> x137, local copies, waits for them, and re-layouts: 16.1 us -> 15.4 us
  transfers between devices with their start and end apart: 37 -> 37, of which waited for: 16 -> 16; matrix products, arithmetic and copies ran while one was open for 16% -> 17% of each run, Pallas kernels for 38% -> 37%
where the time goes in v5:
time: 640 us; the launch traced here: 634 us
  Pallas kernels  254 us (40%)
  waiting for transfers between devices  148 us (23%)
  starting transfers between devices  75.1 us (12%)
  other arithmetic  50.8 us (8%)
  matrix products  49.6 us (8%)
  local copies, waits for them, and re-layouts  32 us (5%)
  between operations  23.6 us (4%)
    all_to_all x7, waiting for transfers between devices, exchange(): lax.all_to_all(rows, 'expert', split_axis=0, concat_axis=0, tiled=True)  73.6 us
    pallas_call x2, Pallas kernels, expert_back(): pl.pallas_call(expert_back_kernel, grid=(count + width // columns,), in_s...  45.1 us
    pallas_call x2, Pallas kernels, expert_forward(): pl.pallas_call(expert_kernel, grid=(inner // tile,), in_specs=[pl.BlockSp...  42.5 us
    ppermute x13, waiting for transfers between devices, swap(): return lax.ppermute(values, axis, [(i, i ^ distance) for i in range(size)])  41.7 us
    pallas_call x4, Pallas kernels, attend_back(): pl.pallas_call(attend_back_kernel, grid=(tokens // SEQ, count), in_specs=...  38.8 us
    pallas_call x1, Pallas kernels, weight_grads(): pl.pallas_call(lambda *refs: weight_grads_kernel(chunks, refs), grid=(2 *...  37.9 us
    all_to_all x7, starting transfers between devices, exchange(): lax.all_to_all(rows, 'expert', split_axis=0, concat_axis=0, tiled=True)  32.3 us
    pallas_call x1, Pallas kernels, step_experts(): pl.pallas_call(step_kernel, grid=(columns // tile,), in_specs=[pl.BlockSp...  21.9 us
  transfers between devices with their start and end apart: 37, of which 16 were waited for; matrix products, arithmetic and copies ran while one was open for 17% of the time, Pallas kernels for 37%

profile of v5, /device:TPU:0, one launch (start us, length us, event | category | flops | bytes accessed | tf_op | source)
XLA Modules:
  0.0 633.7 jit_solution(7346781484794570108)
XLA Ops:
  12.4 7.3 %all-to-all-start = ((bf16[8,32,1664]{2,1,0:T(8,128)(2,1)}), bf16[8,32,1664]{2,1,0:T(8,128)(2,1)S(1)}, u32[]{:S(2)}, u32[]{:S(2)}) async-start(bf16[8,32,1664]{2,1,0:T(8,128)(2,1)} %broadcast_in_dim.54), calls=%async_computation | async-start | bytes 1703936 | tf_op jit(solution)/shard_map/all_to_all | solution.py:899
  32.6 12.1 %all-to-all-done.refs_0_ = bf16[8,32,1664]{2,1,0:T(8,128)(2,1)S(1)} async-done(((bf16[8,32,1664]{2,1,0:T(8,128)(2,1)}), bf16[8,32,1664]{2,1,0:T(8,128)(2,1)S(1)}, u32[]{:S(2)}, u32[]{:S(2)}) %all-to-all-start) | async-done | bytes 852000 | tf_op jit(solution)/shard_map/all_to_all | solution.py:899
  49.2 20.7 %collective-permute-done.1.refs_2_ = bf16[8,32,1664]{2,1,0:T(8,128)(2,1)S(1)} collective-permute-done((bf16[8,32,1664]{2,1,0:T(8,128)(2,1)S(1)}, bf16[8,32,1664]{2,1,0:T(8,128)(2,1)S(1)}, u32[]{:S(2)}, u32[]{:S(2)}) %collective-permute-start.1) | collective-permute-done | bytes 852000 | tf_op jit(solution)/shard_map/ppermute | solution.py:734
  82.7 5.8 convolution_convert_fusion.2.q_ref.k_ref.v_ref
  88.5 10.3 %attend.2 = (bf16[1024,512]{1,0:T(8,128)(2,1)S(1)}, f32[32,1024]{1,0:T(8,128)S(1)}) custom-call(bf16[1024,1536]{1,0:T(8,128)(2,1)S(1)} %convolution_convert_fusion.2.q_ref.k_ref.v_ref, bf16[1024,1536]{1,0:T(8,128)(2,1)S(1)} %convolution_convert_fusion.2.q_ref.k_ref.v_ref, bf16[1024,1536]{1,0:T(8,128)(2,1)S(1)} %convolution_convert_fusion.2.q_ref.k_ref.v_ref, ...), custom_call_target="tpu_custom_call" | custom-call | flops 5510000128 | tf_op jit(solution)/shard_map/attend/pallas_call | solution.py:117
  101.5 5.8 convolution_convert_fusion.1.q_ref.k_ref.v_ref
  107.3 10.3 %attend.3 = (bf16[1024,512]{1,0:T(8,128)(2,1)S(1)}, f32[32,1024]{1,0:T(8,128)S(1)}) custom-call(bf16[1024,1536]{1,0:T(8,128)(2,1)S(1)} %convolution_convert_fusion.1.q_ref.k_ref.v_ref, bf16[1024,1536]{1,0:T(8,128)(2,1)S(1)} %convolution_convert_fusion.1.q_ref.k_ref.v_ref, bf16[1024,1536]{1,0:T(8,128)(2,1)S(1)} %convolution_convert_fusion.1.q_ref.k_ref.v_ref, ...), custom_call_target="tpu_custom_call" | custom-call | flops 5510000128 | tf_op jit(solution)/shard_map/attend/pallas_call | solution.py:117
  117.7 13.4 %after_attend.1 = (f32[1024,1024]{1,0:T(8,128)}, bf16[1024,1024]{1,0:T(8,128)(2,1)}, f32[1024,128]{1,0:T(8,128)S(1)}, bf16[768,1024]{1,0:T(8,128)(2,1)}, bf16[768,1024]{1,0:T(8,128)(2,1)}) custom-call(bf16[1024,512]{1,0:T(8,128)(2,1)S(1)} %copy-done.7, bf16[1024,512]{1,0:T(8,128)(2,1)S(1)} %get-tuple-element.125.refs_1_.mixed_ref, ...), custom_call_target="tpu_custom_call" | custom-call | flops 2470000128 | tf_op jit(solution)/shard_map/after_attend/pallas_call | solution.py:281
  131.9 5.4 all-to-all-start.1
  145.0 29.7 %all-to-all-done.1.x_ref.refs_0_ = bf16[8,96,1024]{2,1,0:T(8,128)(2,1)S(1)} async-done(((bf16[8,96,1024]{2,1,0:T(8,128)(2,1)}), bf16[8,96,1024]{2,1,0:T(8,128)(2,1)S(1)}, u32[]{:S(2)}, u32[]{:S(2)}) %all-to-all-start.1) | async-done | bytes 1572896 | tf_op jit(solution)/shard_map/all_to_all | solution.py:941
  178.4 21.3 %expert_forward.2 = (bf16[8,192,4096]{2,1,0:T(8,128)(2,1)}, bf16[8,96,4096]{2,1,0:T(8,128)(2,1)}) custom-call(bf16[8,96,1024]{2,1,0:T(8,128)(2,1)} %copy-done.39, bf16[1024,4096]{1,0:T(8,128)(2,1)} %bitcast.179), custom_call_target="tpu_custom_call" | custom-call | flops 3990000128 | tf_op jit(solution)/shard_map/expert_forward/pallas_call | solution.py:486
  199.7 15.8 %all-to-all-done.2.x_ref.refs_1_ = bf16[8,96,1024]{2,1,0:T(8,128)(2,1)S(1)} async-done(((bf16[8,96,1024]{2,1,0:T(8,128)(2,1)}), bf16[8,96,1024]{2,1,0:T(8,128)(2,1)S(1)}, u32[]{:S(2)}, u32[]{:S(2)}) %all-to-all-start.2) | async-done | bytes 1572896 | tf_op jit(solution)/shard_map/all_to_all | solution.py:941
  219.2 21.2 %expert_forward.3 = (bf16[8,192,4096]{2,1,0:T(8,128)(2,1)}, bf16[8,96,4096]{2,1,0:T(8,128)(2,1)}) custom-call(bf16[8,96,1024]{2,1,0:T(8,128)(2,1)} %copy-done.35, bf16[1024,4096]{1,0:T(8,128)(2,1)} %bitcast.180, bf16[8,192,4096]{2,1,0:T(8,128)(2,1)} %get-tuple-element.137.rest_0_), custom_call_target="tpu_custom_call", output_to_operand_aliasing={{0}: (2, {})} | custom-call | flops 3990000128 | tf_op jit(solution)/shard_map/expert_forward/pallas_call | solution.py:486
  240.4 19.1 %convolution_convert_fusion = bf16[1536,1024]{1,0:T(8,128)(2,1)} fusion(bf16[1536,4096]{1,0:T(8,128)(2,1)} %bitcast.183, bf16[1,4096,1024]{2,1,0:T(8,128)(2,1)} %all-gather.8.cloned.1.call-done), kind=kOutput, calls=%fused_computation.10 | convolution fusion | flops 12886474752 | bytes 24117248 | tf_op jit(solution)/shard_map/dot_general | solution.py:964
  259.5 6.2 all-to-all-start.4
  266.4 22.6 %expert_back.2 = (bf16[8,192,4096]{2,1,0:T(8,128)(2,1)}, bf16[8,96,1024]{2,1,0:T(8,128)(2,1)}, f32[8,1024]{1,0:T(8,128)}) custom-call(bf16[8,96,1024]{2,1,0:T(8,128)(2,1)} %copy-done.40, bf16[8,96,4096]{2,1,0:T(8,128)(2,1)} %get-tuple-element.143.slope_ref, bf16[1024,4096]{1,0:T(8,128)(2,1)} %bitcast.181, bf16[4096,1024]{1,0:T(8,128)(2,1)} %bitcast.184, ...), custom_call_target="tpu_custom_call" | custom-call | flops 4369999872 | tf_op jit(solution)/shard_map/expert_back/pallas_call | solution.py:577
  288.9 13.4 %all-to-all-done.4.grad_ref.refs_3_ = bf16[8,96,1024]{2,1,0:T(8,128)(2,1)S(1)} async-done(((bf16[8,96,1024]{2,1,0:T(8,128)(2,1)}), bf16[8,96,1024]{2,1,0:T(8,128)(2,1)S(1)}, u32[]{:S(2)}, u32[]{:S(2)}) %all-to-all-start.4) | async-done | bytes 1572896 | tf_op jit(solution)/shard_map/all_to_all | solution.py:941
  306.0 22.5 %expert_back.3 = (bf16[8,192,4096]{2,1,0:T(8,128)(2,1)}, bf16[8,96,1024]{2,1,0:T(8,128)(2,1)}, f32[8,1024]{1,0:T(8,128)}) custom-call(bf16[8,96,1024]{2,1,0:T(8,128)(2,1)} %copy-done.38, bf16[8,96,4096]{2,1,0:T(8,128)(2,1)} %get-tuple-element.148.slope_ref, bf16[1024,4096]{1,0:T(8,128)(2,1)} %bitcast.182, ...), custom_call_target="tpu_custom_call", output_to_operand_aliasing={{0}: (7, {})} | custom-call | flops 4369999872 | tf_op jit(solution)/shard_map/expert_back/pallas_call | solution.py:577
  328.5 14.7 %all-to-all-done.5 = bf16[8,96,1024]{2,1,0:T(8,128)(2,1)S(1)} async-done(((bf16[8,96,1024]{2,1,0:T(8,128)(2,1)}), bf16[8,96,1024]{2,1,0:T(8,128)(2,1)S(1)}, u32[]{:S(2)}, u32[]{:S(2)}) %all-to-all-start.5) | async-done | bytes 1572896 | tf_op jit(solution)/shard_map/all_to_all | solution.py:941
  347.3 37.9 %weight_grads.1 = (bf16[1024,4096]{1,0:T(8,128)(2,1)}, bf16[1024,4096]{1,0:T(8,128)(2,1)}) custom-call(bf16[8,96,1024]{2,1,0:T(8,128)(2,1)} %copy-done.39, bf16[8,96,1024]{2,1,0:T(8,128)(2,1)} %copy-done.35, bf16[8,96,1024]{2,1,0:T(8,128)(2,1)} %copy-done.40, bf16[8,96,1024]{2,1,0:T(8,128)(2,1)} %copy-done.38, ...), custom_call_target="tpu_custom_call" | custom-call | flops 7219999744 | tf_op jit(solution)/shard_map/weight_grads/pallas_call | solution.py:669
  386.2 6.2 all-to-all-start.7
  393.4 12.3 %before_attend_back.1 = (f32[1024,1024]{1,0:T(8,128)}, bf16[1024,1024]{1,0:T(8,128)(2,1)S(1)}, bf16[1024,1024]{1,0:T(8,128)(2,1)}, f32[16,1024]{1,0:T(8,128)S(1)}) custom-call(bf16[768,1024]{1,0:T(8,128)(2,1)S(1)} %bitcast.168, bf16[768,1024]{1,0:T(8,128)(2,1)S(1)} %bitcast.169, s32[1024,1]{1,0:T(8,128)S(1)} %copy-done.27, ...), custom_call_target="tpu_custom_call" | custom-call | flops 2280000000 | tf_op jit(solution)/shard_map/before_attend_back/pallas_call | solution.py:351
  414.1 9.5 %attend_back.4.refs_0_ = bf16[1024,768]{1,0:T(8,128)(2,1)S(1)} custom-call(bf16[1024,1536]{1,0:T(8,128)(2,1)} %copy-done.1, bf16[1024,1536]{1,0:T(8,128)(2,1)} %copy-done.1, bf16[1024,1536]{1,0:T(8,128)(2,1)} %copy-done.1, bf16[1024,1024]{1,0:T(8,128)(2,1)S(1)} %copy-done.3, bf16[1024,512]{1,0:T(8,128)(2,1)S(1)} %copy-done.9, ...), custom_call_target="tpu_custom_call" | custom-call | flops 1824000000 | tf_op jit(solution)/shard_map/attend_back/pallas_call | solution.py:196
  430.0 9.7 %attend_back.5.refs_1_ = bf16[1024,768]{1,0:T(8,128)(2,1)S(1)} custom-call(bf16[1024,1536]{1,0:T(8,128)(2,1)} %copy-done.1, bf16[1024,1536]{1,0:T(8,128)(2,1)} %copy-done.1, bf16[1024,1536]{1,0:T(8,128)(2,1)} %copy-done.1, bf16[1024,1024]{1,0:T(8,128)(2,1)S(1)} %copy-done.3, bf16[1024,512]{1,0:T(8,128)(2,1)S(1)} %copy-done.9, ...), custom_call_target="tpu_custom_call" | custom-call | flops 1824000000 | tf_op jit(solution)/shard_map/attend_back/pallas_call | solution.py:196
  448.3 9.9 %attend_back.6.refs_2_ = bf16[1024,768]{1,0:T(8,128)(2,1)S(1)} custom-call(bf16[1024,1536]{1,0:T(8,128)(2,1)} %copy-done, bf16[1024,1536]{1,0:T(8,128)(2,1)} %copy-done, bf16[1024,1536]{1,0:T(8,128)(2,1)} %copy-done, bf16[1024,1024]{1,0:T(8,128)(2,1)S(1)} %copy-done.3, bf16[1024,512]{1,0:T(8,128)(2,1)S(1)} %copy-done.5, ...), custom_call_target="tpu_custom_call" | custom-call | flops 1824000000 | tf_op jit(solution)/shard_map/attend_back/pallas_call | solution.py:196
  474.7 9.7 %attend_back.7.refs_3_ = bf16[1024,768]{1,0:T(8,128)(2,1)S(1)} custom-call(bf16[1024,1536]{1,0:T(8,128)(2,1)} %copy-done, bf16[1024,1536]{1,0:T(8,128)(2,1)} %copy-done, bf16[1024,1536]{1,0:T(8,128)(2,1)} %copy-done, bf16[1024,1024]{1,0:T(8,128)(2,1)S(1)} %copy-done.3, bf16[1024,512]{1,0:T(8,128)(2,1)S(1)} %copy-done.5, ...), custom_call_target="tpu_custom_call" | custom-call | flops 1824000000 | tf_op jit(solution)/shard_map/attend_back/pallas_call | solution.py:196
  484.4 7.0 %collective-permute-done.6 = bf16[4,2,32,1536]{3,2,1,0:T(8,128)(2,1)S(1)} collective-permute-done((bf16[4,2,32,1536]{3,2,1,0:T(8,128)(2,1)S(1)}, bf16[4,2,32,1536]{3,2,1,0:T(8,128)(2,1)S(1)}, u32[]{:S(2)}, u32[]{:S(2)}) %collective-permute-start.6) | collective-permute-done | bytes 786464 | tf_op jit(solution)/shard_map/ppermute | solution.py:734
  511.8 13.8 %input_gradient.1 = (f32[1024,1024]{1,0:T(8,128)}, f32[16,1024]{1,0:T(8,128)S(1)}) custom-call(bf16[1024,768]{1,0:T(8,128)(2,1)S(1)} %copy-done.18, bf16[1024,768]{1,0:T(8,128)(2,1)S(1)} %copy-done.20, bf16[1024,768]{1,0:T(8,128)(2,1)S(1)} %copy-done.22, bf16[1024,768]{1,0:T(8,128)(2,1)} %copy-done.23, bf16[1024,1664]{1,0:T(8,128)(2,1)} %copy-done.2, ...), custom_call_target="tpu_custom_call" | custom-call | flops 2660000000 | tf_op jit(solution)/shard_map/input_gradient/pallas_call | solution.py:405
  525.7 11.2 %collective-permute-done.9 = bf16[2,32,2688]{2,1,0:T(8,128)(2,1)S(1)} collective-permute-done((bf16[2,32,2688]{2,1,0:T(8,128)(2,1)S(1)}, bf16[2,32,2688]{2,1,0:T(8,128)(2,1)S(1)}, u32[]{:S(2)}, u32[]{:S(2)}) %collective-permute-start.9) | collective-permute-done | bytes 344096 | tf_op jit(solution)/shard_map/ppermute | solution.py:792
  537.9 8.5 %collective-permute-done.13 = bf16[4,32,1536]{2,1,0:T(8,128)(2,1)S(1)} collective-permute-done((bf16[4,32,1536]{2,1,0:T(8,128)(2,1)S(1)}, bf16[4,32,1536]{2,1,0:T(8,128)(2,1)S(1)}, u32[]{:S(2)}, u32[]{:S(2)}) %collective-permute-start.13) | collective-permute-done | bytes 393248 | tf_op jit(solution)/shard_map/ppermute | solution.py:792
  558.3 7.6 %activations_of.1 = bf16[1024,1024]{1,0:T(8,128)(2,1)} custom-call(bf16[1536,1024]{1,0:T(8,128)(2,1)} %bitcast.38.refs_0_, s32[1024,1]{1,0:T(8,128)S(1)} %copy-done.26, f32[1024,128]{1,0:T(8,128)S(1)} %copy-done.32, f32[1024,1024]{1,0:T(8,128)} %get-tuple-element.162.refs_3_), custom_call_target="tpu_custom_call" | custom-call | flops 1424999936 | tf_op jit(solution)/shard_map/activations_of/pallas_call | solution.py:439
  604.0 21.9 %step_experts.1 = (f32[1,256,4096]{2,1,0:T(8,128)}, f32[1,256,4096]{2,1,0:T(8,128)}, f32[1,256,4096]{2,1,0:T(8,128)}, f32[1,4096,256]{2,1,0:T(8,128)}, f32[1,4096,256]{2,1,0:T(8,128)}, /*index=5*/f32[1,4096,256]{2,1,0:T(8,128)}) custom-call(f32[1]{0:T(128)} %bitcast.74.factor_ref, f32[1,256,4096]{2,1,0:T(8,128)} %refs_0_.1, f32[1,256,4096]{2,1,0:T(8,128)} %refs_1_.1, ...), custom_call_target="tpu_custom_call" | custom-call | flops 3800000000 | tf_op jit(solution)/shard_map/step_experts/pallas_call | solution.py:715
  (323 shorter events, 167.2 us)
Async XLA Ops:
  7.2 94.3 %all-gather.4.cloned.1.call-start = ((), (), s32[]{:S(2)}) async-start(), calls=%async_computation.11 | async-start | bytes 5406720 | tf_op jit(solution)/shard_map/all_gather | solution.py:881
  12.4 32.4 %all-to-all-start = ((bf16[8,32,1664]{2,1,0:T(8,128)(2,1)}), bf16[8,32,1664]{2,1,0:T(8,128)(2,1)S(1)}, u32[]{:S(2)}, u32[]{:S(2)}) async-start(bf16[8,32,1664]{2,1,0:T(8,128)(2,1)} %broadcast_in_dim.54), calls=%async_computation | async-start | bytes 1703936 | tf_op jit(solution)/shard_map/all_to_all | solution.py:899
  19.7 158.7 %all-gather.6.cloned.1.call-start = ((), (), s32[]{:S(2)}) async-start(), calls=%async_computation.12 | async-start | bytes 10485760 | tf_op jit(solution)/shard_map/all_gather | solution.py:910
  44.8 195.6 %all-gather.8.cloned.1.call-start = ((), (), s32[]{:S(2)}) async-start(), calls=%async_computation.13 | async-start | bytes 10485760 | tf_op jit(solution)/shard_map/all_gather | solution.py:911
  45.5 24.3 %collective-permute-start.1 = (bf16[8,32,1664]{2,1,0:T(8,128)(2,1)S(1)}, bf16[8,32,1664]{2,1,0:T(8,128)(2,1)S(1)}, u32[]{:S(2)}, u32[]{:S(2)}) collective-permute-start(bf16[8,32,1664]{2,1,0:T(8,128)(2,1)S(1)} %all-to-all-done.refs_0_), channel_id=1, source_target_pairs={{0,2},{1,3},{2,0},{3,1},{4,6},{5,7},{6,4},{7,5},{8,10},{9,11},{10,... | collective-permute-start | bytes 2555912 | tf_op jit(solution)/shard_map/ppermute | solution.py:734
  49.2 23.7 %collective-permute-start = (bf16[8,32,1664]{2,1,0:T(8,128)(2,1)S(1)}, bf16[8,32,1664]{2,1,0:T(8,128)(2,1)S(1)}, u32[]{:S(2)}, u32[]{:S(2)}) collective-permute-start(bf16[8,32,1664]{2,1,0:T(8,128)(2,1)S(1)} %all-to-all-done.refs_0_), channel_id=1, source_target_pairs={{0,1},{1,0},{2,3},{3,2},{4,5},{5,4},{6,7},{7,6},{8,9},{9,8},{10,11... | collective-permute-start | bytes 2555912 | tf_op jit(solution)/shard_map/ppermute | solution.py:734
  131.9 42.8 %all-to-all-start.1 = ((bf16[8,96,1024]{2,1,0:T(8,128)(2,1)}), bf16[8,96,1024]{2,1,0:T(8,128)(2,1)S(1)}, u32[]{:S(2)}, u32[]{:S(2)}) async-start(bf16[8,96,1024]{2,1,0:T(8,128)(2,1)} %bitcast.12), calls=%async_computation.1 | async-start | bytes 3145728 | tf_op jit(solution)/shard_map/all_to_all | solution.py:941
  174.7 40.8 %all-to-all-start.2 = ((bf16[8,96,1024]{2,1,0:T(8,128)(2,1)}), bf16[8,96,1024]{2,1,0:T(8,128)(2,1)S(1)}, u32[]{:S(2)}, u32[]{:S(2)}) async-start(bf16[8,96,1024]{2,1,0:T(8,128)(2,1)} %bitcast.204), calls=%async_computation.2 | async-start | bytes 3145728 | tf_op jit(solution)/shard_map/all_to_all | solution.py:941
  215.5 44.0 %all-to-all-start.3 = ((bf16[8,96,1024]{2,1,0:T(8,128)(2,1)}), bf16[8,96,1024]{2,1,0:T(8,128)(2,1)S(1)}, u32[]{:S(2)}, u32[]{:S(2)}) async-start(bf16[8,96,1024]{2,1,0:T(8,128)(2,1)} %bitcast.203), calls=%async_computation.3 | async-start | bytes 3145728 | tf_op jit(solution)/shard_map/all_to_all | solution.py:941
  259.5 42.8 %all-to-all-start.4 = ((bf16[8,96,1024]{2,1,0:T(8,128)(2,1)}), bf16[8,96,1024]{2,1,0:T(8,128)(2,1)S(1)}, u32[]{:S(2)}, u32[]{:S(2)}) async-start(bf16[8,96,1024]{2,1,0:T(8,128)(2,1)} %bitcast.202), calls=%async_computation.4 | async-start | bytes 3145728 | tf_op jit(solution)/shard_map/all_to_all | solution.py:941
  302.3 40.8 %all-to-all-start.5 = ((bf16[8,96,1024]{2,1,0:T(8,128)(2,1)}), bf16[8,96,1024]{2,1,0:T(8,128)(2,1)S(1)}, u32[]{:S(2)}, u32[]{:S(2)}) async-start(bf16[8,96,1024]{2,1,0:T(8,128)(2,1)} %get-tuple-element.151), calls=%async_computation.5 | async-start | bytes 3145728 | tf_op jit(solution)/shard_map/all_to_all | solution.py:941
  343.2 42.0 %all-to-all-start.6 = ((bf16[8,96,1024]{2,1,0:T(8,128)(2,1)}), bf16[8,96,1024]{2,1,0:T(8,128)(2,1)S(1)}, u32[]{:S(2)}, u32[]{:S(2)}) async-start(bf16[8,96,1024]{2,1,0:T(8,128)(2,1)} %get-tuple-element.154), calls=%async_computation.6 | async-start | bytes 3145728 | tf_op jit(solution)/shard_map/all_to_all | solution.py:941
  346.8 219.2 %reduce-scatter.3.cloned.1.call-start = ((), (), s32[]{:S(2)}) async-start(), calls=%async_computation.14 | async-start | bytes 10485760 | tf_op jit(solution)/shard_map/reduce_scatter | solution.py:1002
  385.2 180.9 %reduce-scatter.5.cloned.1.call-start = ((), (), s32[]{:S(2)}) async-start(), calls=%async_computation.15 | async-start | bytes 10485760 | tf_op jit(solution)/shard_map/reduce_scatter | solution.py:1003
  386.2 83.7 %all-to-all-start.7 = ((bf16[8,192,1024]{2,1,0:T(8,128)(2,1)}), bf16[8,192,1024]{2,1,0:T(8,128)(2,1)}, u32[]{:S(2)}, u32[]{:S(2)}) async-start(bf16[8,192,1024]{2,1,0:T(8,128)(2,1)} %bitcast.188), calls=%async_computation.7 | async-start | bytes 6291456 | tf_op jit(solution)/shard_map/all_to_all | solution.py:941
  411.3 15.3 %collective-permute-start.3 = (bf16[8,2,32,1152]{3,2,1,0:T(8,128)(2,1)}, bf16[8,2,32,1152]{3,2,1,0:T(8,128)(2,1)}, u32[]{:S(2)}, u32[]{:S(2)}) collective-permute-start(bf16[8,2,32,1152]{3,2,1,0:T(8,128)(2,1)} %fusion.21), channel_id=1, source_target_pairs={{0,1},{1,0},{2,3},{3,2},{4,5},{5,4},{6,7},{7,6},{8,9},{9,8},{10,11... | collective-permute-start | bytes 3538952 | tf_op jit(solution)/shard_map/ppermute | solution.py:734
  443.9 22.9 %collective-permute-start.5 = (bf16[8,2,32,1536]{3,2,1,0:T(8,128)(2,1)}, bf16[8,2,32,1536]{3,2,1,0:T(8,128)(2,1)}, u32[]{:S(2)}, u32[]{:S(2)}) collective-permute-start(bf16[8,2,32,1536]{3,2,1,0:T(8,128)(2,1)} %pad_maximum_fusion.1), channel_id=1, source_target_pairs={{0,1},{1,0},{2,3},{3,2},{4,5},{5,4},{6,7},{7,6},{8,9},{9,8},{10,11... | collective-permute-start | bytes 4718600 | tf_op jit(solution)/shard_map/ppermute | solution.py:734
  445.0 20.8 %collective-permute-start.4 = (bf16[4,2,32,1152]{3,2,1,0:T(8,128)(2,1)S(1)}, bf16[4,2,32,1152]{3,2,1,0:T(8,128)(2,1)S(1)}, u32[]{:S(2)}, u32[]{:S(2)}) collective-permute-start(bf16[4,2,32,1152]{3,2,1,0:T(8,128)(2,1)S(1)} %dynamic-slice_bitcast_fusion.9), channel_id=1, source_target_pairs={{0,4},{4,0},{8,12},{12,8},{16,20},{20,16},{24,28},{28,24},{1,5},{5... | collective-permute-start | bytes 1769480 | tf_op jit(solution)/shard_map/ppermute | solution.py:734
  471.1 20.3 %collective-permute-start.6 = (bf16[4,2,32,1536]{3,2,1,0:T(8,128)(2,1)S(1)}, bf16[4,2,32,1536]{3,2,1,0:T(8,128)(2,1)S(1)}, u32[]{:S(2)}, u32[]{:S(2)}) collective-permute-start(bf16[4,2,32,1536]{3,2,1,0:T(8,128)(2,1)S(1)} %dynamic-slice_bitcast_fusion.3), channel_id=1, source_target_pairs={{0,4},{4,0},{8,12},{12,8},{16,20},{20,16},{24,28},{28,24},{1,5},{5... | collective-permute-start | bytes 2359304 | tf_op jit(solution)/shard_map/ppermute | solution.py:734
  496.2 3.6 collective-permute-start.7
  503.5 22.1 %collective-permute-start.10 = (bf16[2,32,2688]{2,1,0:T(8,128)(2,1)S(1)}, bf16[2,32,2688]{2,1,0:T(8,128)(2,1)S(1)}, u32[]{:S(2)}, u32[]{:S(2)}) collective-permute-start(bf16[2,32,2688]{2,1,0:T(8,128)(2,1)S(1)} %get-tuple-element.247), channel_id=1, source_target_pairs={{0,24},{1,25},{2,26},{3,27},{4,28},{5,29},{6,30},{7,31},{8,16},{9,... | collective-permute-start | bytes 1032200 | tf_op jit(solution)/shard_map/ppermute | solution.py:792
  506.2 19.5 %collective-permute-start.8 = (bf16[2,32,2688]{2,1,0:T(8,128)(2,1)S(1)}, bf16[2,32,2688]{2,1,0:T(8,128)(2,1)S(1)}, u32[]{:S(2)}, u32[]{:S(2)}) collective-permute-start(bf16[2,32,2688]{2,1,0:T(8,128)(2,1)S(1)} %get-tuple-element.246), channel_id=1, source_target_pairs={{0,8},{1,9},{2,10},{3,11},{4,12},{5,13},{6,14},{7,15},{8,0},{9,1},... | collective-permute-start | bytes 1032200 | tf_op jit(solution)/shard_map/ppermute | solution.py:792
  506.2 30.7 %collective-permute-start.9 = (bf16[2,32,2688]{2,1,0:T(8,128)(2,1)S(1)}, bf16[2,32,2688]{2,1,0:T(8,128)(2,1)S(1)}, u32[]{:S(2)}, u32[]{:S(2)}) collective-permute-start(bf16[2,32,2688]{2,1,0:T(8,128)(2,1)S(1)} %get-tuple-element.248), channel_id=1, source_target_pairs={{0,16},{1,17},{2,18},{3,19},{4,20},{5,21},{6,22},{7,23},{8,24},{9,... | collective-permute-start | bytes 1032200 | tf_op jit(solution)/shard_map/ppermute | solution.py:792
  508.0 29.8 %collective-permute-start.11 = (bf16[4,32,1536]{2,1,0:T(8,128)(2,1)S(1)}, bf16[4,32,1536]{2,1,0:T(8,128)(2,1)S(1)}, u32[]{:S(2)}, u32[]{:S(2)}) collective-permute-start(bf16[4,32,1536]{2,1,0:T(8,128)(2,1)S(1)} %get-tuple-element.235), channel_id=1, source_target_pairs={{0,2},{1,3},{2,0},{3,1},{4,6},{5,7},{6,4},{7,5},{8,10},{9,11},{10,... | collective-permute-start | bytes 1179656 | tf_op jit(solution)/shard_map/ppermute | solution.py:792
  510.0 27.8 %collective-permute-start.12 = (bf16[4,32,1536]{2,1,0:T(8,128)(2,1)S(1)}, bf16[4,32,1536]{2,1,0:T(8,128)(2,1)S(1)}, u32[]{:S(2)}, u32[]{:S(2)}) collective-permute-start(bf16[4,32,1536]{2,1,0:T(8,128)(2,1)S(1)} %get-tuple-element.237), channel_id=1, source_target_pairs={{0,4},{1,5},{2,6},{3,7},{4,0},{5,1},{6,2},{7,3},{8,12},{9,13},{10,... | collective-permute-start | bytes 1179656 | tf_op jit(solution)/shard_map/ppermute | solution.py:792
  525.6 20.7 %collective-permute-start.13 = (bf16[4,32,1536]{2,1,0:T(8,128)(2,1)S(1)}, bf16[4,32,1536]{2,1,0:T(8,128)(2,1)S(1)}, u32[]{:S(2)}, u32[]{:S(2)}) collective-permute-start(bf16[4,32,1536]{2,1,0:T(8,128)(2,1)S(1)} %get-tuple-element.236), channel_id=1, source_target_pairs={{0,6},{1,7},{2,4},{3,5},{4,2},{5,3},{6,0},{7,1},{8,14},{9,15},{10,... | collective-permute-start | bytes 1179656 | tf_op jit(solution)/shard_map/ppermute | solution.py:792
  547.4 18.6 %all-to-all-start.8 = ((f32[32,1,64]{2,1,0:T(1,128)}), f32[32,1,64]{2,1,0:T(1,128)S(1)}, u32[]{:S(2)}, u32[]{:S(2)}) async-start(f32[32,1,64]{2,1,0:T(1,128)} %bitcast.65), calls=%async_computation.8 | async-start | bytes 32768 | tf_op jit(solution)/shard_map/all_to_all | solution.py:1076
  552.0 13.9 %collective-permute-start.14 = (bf16[32,2688]{1,0:T(8,128)(2,1)S(1)}, bf16[32,2688]{1,0:T(8,128)(2,1)S(1)}, u32[]{:S(2)}, u32[]{:S(2)}) collective-permute-start(bf16[32,2688]{1,0:T(8,128)(2,1)S(1)} %dynamic-slice_bitcast_fusion.16), channel_id=1, source_target_pairs={{0,2},{1,3},{2,0},{3,1},{4,6},{5,7},{6,4},{7,5},{8,10},{9,11},{10,... | collective-permute-start | bytes 516104 | tf_op jit(solution)/shard_map/ppermute | solution.py:792
  553.9 17.3 %collective-permute-start.15 = (bf16[32,1536]{1,0:T(8,128)(2,1)S(1)}, bf16[32,1536]{1,0:T(8,128)(2,1)S(1)}, u32[]{:S(2)}, u32[]{:S(2)}) collective-permute-start(bf16[32,1536]{1,0:T(8,128)(2,1)S(1)} %get-tuple-element.253), channel_id=1, source_target_pairs={{0,8},{1,9},{2,10},{3,11},{4,12},{5,13},{6,14},{7,15},{8,0},{9,1},... | collective-permute-start | bytes 294920 | tf_op jit(solution)/shard_map/ppermute | solution.py:792
  555.4 15.8 %collective-permute-start.16 = (bf16[32,1536]{1,0:T(8,128)(2,1)S(1)}, bf16[32,1536]{1,0:T(8,128)(2,1)S(1)}, u32[]{:S(2)}, u32[]{:S(2)}) collective-permute-start(bf16[32,1536]{1,0:T(8,128)(2,1)S(1)} %get-tuple-element.252), channel_id=1, source_target_pairs={{0,16},{1,17},{2,18},{3,19},{4,20},{5,21},{6,22},{7,23},{8,24},{9,... | collective-permute-start | bytes 294920 | tf_op jit(solution)/shard_map/ppermute | solution.py:792
  557.8 13.4 %collective-permute-start.17 = (bf16[32,1536]{1,0:T(8,128)(2,1)S(1)}, bf16[32,1536]{1,0:T(8,128)(2,1)S(1)}, u32[]{:S(2)}, u32[]{:S(2)}) collective-permute-start(bf16[32,1536]{1,0:T(8,128)(2,1)S(1)} %get-tuple-element.251), channel_id=1, source_target_pairs={{0,24},{1,25},{2,26},{3,27},{4,28},{5,29},{6,30},{7,31},{8,16},{9,... | collective-permute-start | bytes 294920 | tf_op jit(solution)/shard_map/ppermute | solution.py:792
  592.5 4.5 collective-permute-start.22
  (73 other events, 460.0 us)
Sparse Core Ops, SparseCore 0:
  11.5 77.0 all-gather.3
  90.6 57.7 all-gather.5
  150.6 59.3 all-gather.7
  385.3 73.4 reduce-scatter.2
  461.4 88.5 reduce-scatter.4

commit v6 on v5

--- a/solution.py
+++ b/solution.py
@@ -48,12 +48,6 @@
 
 def dot_cols(left, right):
     return lax.dot_general(left, right, (((1,), (1,)), ((), ())), preferred_element_type=f32)
-
-
-def layer_norm(values, norm_gain, norm_bias):
-    centre = values - jnp.mean(values, axis=-1, keepdims=True)
-    spread = jnp.mean(centre * centre, axis=-1, keepdims=True)
-    return centre * lax.rsqrt(spread + eps) * norm_gain + norm_bias
 
 
 def fill_bias(bias, doc_of_rows, doc_of_cols, rows_are_keys):
@@ -161,18 +155,33 @@
     ).astype(low)
     inner = dot_cols(chooser, upper) + dot_cols(chooser, lower)
     key_t = k_ref[...].T
+    def products(block):
+        after = block + BLOCK
+        return [
+            (
+                dot_cols(keep_head(k_ref[block:after, :], head), query[block:, :]),
+                dot_cols(keep_head(v_ref[block:after, :], head), grad[block:, :]),
+            )
+            for head in range(2)
+        ]
+
+    following = products(0)
     for block in range(0, SEQ, BLOCK):
         after = block + BLOCK
-        key = k_ref[block:after, :]
-        value = v_ref[block:after, :]
+        current = following
+        if after < SEQ:
+            following = products(after)
+        factors = []
+        for head in range(2):
+            scores, grad_w = current[head]
+            scores = jnp.minimum(scores, bias[block:after, block:])
+            weights = jnp.exp(scores - lse_ref[head : head + 1, block:])
+            grad_s = (weights * (grad_w - inner[head : head + 1, block:])).astype(low)
+            factors.append((weights.astype(low), grad_s))
         grad_k, grad_v = [], []
         for head in range(2):
-            scores = dot_cols(keep_head(key, head), query[block:, :])
-            scores = jnp.minimum(scores, bias[block:after, block:])
-            weights = jnp.exp(scores - lse_ref[head : head + 1, block:])
-            grad_w = dot_cols(keep_head(value, head), grad[block:, :])
-            grad_s = (weights * (grad_w - inner[head : head + 1, block:])).astype(low)
-            grad_v.append(dot_rows(weights.astype(low), grad[block:, :]))
+            weights, grad_s = factors[head]
+            grad_v.append(dot_rows(weights, grad[block:, :]))
             grad_k.append(dot_rows(grad_s, query[block:, :]))
             rows = slice(head * HEAD_DIM, (head + 1) * HEAD_DIM)
             moved = dot_rows(key_t[rows, block:after], grad_s)
@@ -707,7 +716,7 @@
             out[0] = value
 
 
-def step_experts(factor, first, second, tile=256):
+def step_experts(factor, first, second, tile=1024):
     rows, columns = first[0].shape[1:]
     along = pl.BlockSpec((1, rows, tile), lambda j: (0, 0, j))
     down = pl.BlockSpec((1, tile, rows), lambda j: (0, j, 0))
@@ -892,13 +901,14 @@
     doc_col = documents[:, None]
     doc_row = documents[None, :]
 
+    normal_one, _ = norm_parts(tokens.astype(f32))
     if rows_own % 16:
         front = lax.all_gather(front, everywhere, axis=0, tiled=True)
     else:
         spread = jnp.broadcast_to(front[None], (experts,) + front.shape)
         spread = lax.all_to_all(spread, "expert", split_axis=0, concat_axis=0, tiled=True)
-        spread, in_low, out_low, slot_row, slot_col, chunked_row, chunked_col = in_order(
-            spread, in_low, out_low, slot_row, slot_col, chunked_row, chunked_col
+        spread, normal_one, in_low, out_low, slot_row, slot_col, chunked_row, chunked_col = in_order(
+            spread, normal_one, in_low, out_low, slot_row, slot_col, chunked_row, chunked_col
         )
         pieces = {0: spread}
         distance = dp // 2
@@ -915,7 +925,7 @@
     ).reshape(4, width).astype(f32)
     centre_table = small_full[:, 4 * norm_own : 4 * norm_own + centre_own].reshape(experts, width)
 
-    normed_low = layer_norm(tokens.astype(f32), norms[0], norms[1]).astype(low)
+    normed_low = (normal_one * norms[0] + norms[1]).astype(low)
     normed_low, front = in_order(normed_low, front)
     packed, mixed, lse = [], [], []
     for weight in (front[:, : 3 * strip], later[:, width:]):

time: 640 us -> 640 us (level)
  local copies, waits for them, and re-layouts: 32 us -> 40.2 us
  Pallas kernels: 254 us -> 246 us
    all_to_all x1, waiting for transfers between devices: 12.1 us -> 3.75 us  [shards(): lax.all_to_all(spread, 'expert', split_axis=0, concat_axis=0, tiled=True)]
    unnamed x137 -> x147, local copies, waits for them, and re-layouts: 15.4 us -> 20.8 us
  transfers between devices with their start and end apart: 37 -> 37, of which waited for: 16 -> 16; matrix products, arithmetic and copies ran while one was open for 17% -> 18% of each run, Pallas kernels for 37% -> 36%
where the time goes in v6:
time: 640 us; the launch traced here: 633 us
  Pallas kernels  246 us (38%)
  waiting for transfers between devices  145 us (23%)
  starting transfers between devices  75.4 us (12%)
  other arithmetic  54.2 us (8%)
  matrix products  49 us (8%)
  local copies, waits for them, and re-layouts  40.2 us (6%)
  between operations  23.3 us (4%)
    all_to_all x7, waiting for transfers between devices, exchange(): lax.all_to_all(rows, 'expert', split_axis=0, concat_axis=0, tiled=True)  73.9 us
    ppermute x13, waiting for transfers between devices, swap(): return lax.ppermute(values, axis, [(i, i ^ distance) for i in range(size)])  46.1 us
    pallas_call x2, Pallas kernels, expert_back(): pl.pallas_call(expert_back_kernel, grid=(count + width // columns,), in_s...  45 us
    pallas_call x2, Pallas kernels, expert_forward(): pl.pallas_call(expert_kernel, grid=(inner // tile,), in_specs=[pl.BlockSp...  42.5 us
    pallas_call x1, Pallas kernels, weight_grads(): pl.pallas_call(lambda *refs: weight_grads_kernel(chunks, refs), grid=(2 *...  37.9 us
    pallas_call x4, Pallas kernels, attend_back(): pl.pallas_call(attend_back_kernel, grid=(tokens // SEQ, count), in_specs=...  36 us
    all_to_all x7, starting transfers between devices, exchange(): lax.all_to_all(rows, 'expert', split_axis=0, concat_axis=0, tiled=True)  32.1 us
    unnamed x147, local copies, waits for them, and re-layouts  20.8 us
  transfers between devices with their start and end apart: 37, of which 16 were waited for; matrix products, arithmetic and copies ran while one was open for 18% of the time, Pallas kernels for 36%

profile of v6, /device:TPU:0, one launch (start us, length us, event | category | flops | bytes accessed | tf_op | source)
XLA Modules:
  0.0 632.8 jit_solution(18144742970401046990)
XLA Ops:
  12.4 7.4 %all-to-all-start = ((bf16[8,32,1664]{2,1,0:T(8,128)(2,1)}), bf16[8,32,1664]{2,1,0:T(8,128)(2,1)S(1)}, u32[]{:S(2)}, u32[]{:S(2)}) async-start(bf16[8,32,1664]{2,1,0:T(8,128)(2,1)} %broadcast_in_dim.54), calls=%async_computation | async-start | bytes 1703936 | tf_op jit(solution)/shard_map/all_to_all | solution.py:909
  47.2 22.7 %collective-permute-done.1.refs_2_ = bf16[8,32,1664]{2,1,0:T(8,128)(2,1)S(1)} collective-permute-done((bf16[8,32,1664]{2,1,0:T(8,128)(2,1)S(1)}, bf16[8,32,1664]{2,1,0:T(8,128)(2,1)S(1)}, u32[]{:S(2)}, u32[]{:S(2)}) %collective-permute-start.1) | collective-permute-done | bytes 852000 | tf_op jit(solution)/shard_map/ppermute | solution.py:743
  87.5 5.4 convolution_convert_fusion.2.q_ref.k_ref.v_ref
  93.0 10.3 %attend.2 = (bf16[1024,512]{1,0:T(8,128)(2,1)S(1)}, f32[32,1024]{1,0:T(8,128)S(1)}) custom-call(bf16[1024,1536]{1,0:T(8,128)(2,1)S(1)} %convolution_convert_fusion.2.q_ref.k_ref.v_ref, bf16[1024,1536]{1,0:T(8,128)(2,1)S(1)} %convolution_convert_fusion.2.q_ref.k_ref.v_ref, bf16[1024,1536]{1,0:T(8,128)(2,1)S(1)} %convolution_convert_fusion.2.q_ref.k_ref.v_ref, ...), custom_call_target="tpu_custom_call" | custom-call | flops 5510000128 | tf_op jit(solution)/shard_map/attend/pallas_call | solution.py:111
  106.0 5.6 convolution_convert_fusion.1.q_ref.k_ref.v_ref
  111.6 10.3 %attend.3 = (bf16[1024,512]{1,0:T(8,128)(2,1)S(1)}, f32[32,1024]{1,0:T(8,128)S(1)}) custom-call(bf16[1024,1536]{1,0:T(8,128)(2,1)S(1)} %convolution_convert_fusion.1.q_ref.k_ref.v_ref, bf16[1024,1536]{1,0:T(8,128)(2,1)S(1)} %convolution_convert_fusion.1.q_ref.k_ref.v_ref, bf16[1024,1536]{1,0:T(8,128)(2,1)S(1)} %convolution_convert_fusion.1.q_ref.k_ref.v_ref, ...), custom_call_target="tpu_custom_call" | custom-call | flops 5510000128 | tf_op jit(solution)/shard_map/attend/pallas_call | solution.py:111
  122.0 13.4 %after_attend.1 = (f32[1024,1024]{1,0:T(8,128)}, bf16[1024,1024]{1,0:T(8,128)(2,1)}, f32[1024,128]{1,0:T(8,128)S(1)}, bf16[768,1024]{1,0:T(8,128)(2,1)}, bf16[768,1024]{1,0:T(8,128)(2,1)}) custom-call(bf16[1024,512]{1,0:T(8,128)(2,1)S(1)} %copy-done.7, bf16[1024,512]{1,0:T(8,128)(2,1)S(1)} %get-tuple-element.127.refs_1_.mixed_ref, ...), custom_call_target="tpu_custom_call" | custom-call | flops 2470000128 | tf_op jit(solution)/shard_map/after_attend/pallas_call | solution.py:290
  136.2 4.8 all-to-all-start.1
  148.8 30.0 %all-to-all-done.1.x_ref.refs_0_ = bf16[8,96,1024]{2,1,0:T(8,128)(2,1)S(1)} async-done(((bf16[8,96,1024]{2,1,0:T(8,128)(2,1)}), bf16[8,96,1024]{2,1,0:T(8,128)(2,1)S(1)}, u32[]{:S(2)}, u32[]{:S(2)}) %all-to-all-start.1) | async-done | bytes 1572896 | tf_op jit(solution)/shard_map/all_to_all | solution.py:951
  182.4 21.3 %expert_forward.2 = (bf16[8,192,4096]{2,1,0:T(8,128)(2,1)}, bf16[8,96,4096]{2,1,0:T(8,128)(2,1)}) custom-call(bf16[8,96,1024]{2,1,0:T(8,128)(2,1)} %copy-done.43, bf16[1024,4096]{1,0:T(8,128)(2,1)} %bitcast.179), custom_call_target="tpu_custom_call" | custom-call | flops 3990000128 | tf_op jit(solution)/shard_map/expert_forward/pallas_call | solution.py:495
  203.7 15.8 %all-to-all-done.2.x_ref.refs_1_ = bf16[8,96,1024]{2,1,0:T(8,128)(2,1)S(1)} async-done(((bf16[8,96,1024]{2,1,0:T(8,128)(2,1)}), bf16[8,96,1024]{2,1,0:T(8,128)(2,1)S(1)}, u32[]{:S(2)}, u32[]{:S(2)}) %all-to-all-start.2) | async-done | bytes 1572896 | tf_op jit(solution)/shard_map/all_to_all | solution.py:951
  223.2 21.2 %expert_forward.3 = (bf16[8,192,4096]{2,1,0:T(8,128)(2,1)}, bf16[8,96,4096]{2,1,0:T(8,128)(2,1)}) custom-call(bf16[8,96,1024]{2,1,0:T(8,128)(2,1)} %copy-done.39, bf16[1024,4096]{1,0:T(8,128)(2,1)} %bitcast.180, bf16[8,192,4096]{2,1,0:T(8,128)(2,1)} %get-tuple-element.139.rest_0_), custom_call_target="tpu_custom_call", output_to_operand_aliasing={{0}: (2, {})} | custom-call | flops 3990000128 | tf_op jit(solution)/shard_map/expert_forward/pallas_call | solution.py:495
  244.4 19.1 %convolution_convert_fusion = bf16[1536,1024]{1,0:T(8,128)(2,1)} fusion(bf16[1536,4096]{1,0:T(8,128)(2,1)} %bitcast.183, bf16[1,4096,1024]{2,1,0:T(8,128)(2,1)} %all-gather.8.cloned.1.call-done), kind=kOutput, calls=%fused_computation.8 | convolution fusion | flops 12886474752 | bytes 24117248 | tf_op jit(solution)/shard_map/dot_general | solution.py:974
  263.5 6.4 %all-to-all-start.4 = ((bf16[8,96,1024]{2,1,0:T(8,128)(2,1)}), bf16[8,96,1024]{2,1,0:T(8,128)(2,1)S(1)}, u32[]{:S(2)}, u32[]{:S(2)}) async-start(bf16[8,96,1024]{2,1,0:T(8,128)(2,1)} %bitcast.202), calls=%async_computation.4 | async-start | bytes 3145728 | tf_op jit(solution)/shard_map/all_to_all | solution.py:951
  270.6 22.5 %expert_back.2 = (bf16[8,192,4096]{2,1,0:T(8,128)(2,1)}, bf16[8,96,1024]{2,1,0:T(8,128)(2,1)}, f32[8,1024]{1,0:T(8,128)}) custom-call(bf16[8,96,1024]{2,1,0:T(8,128)(2,1)} %copy-done.44, bf16[8,96,4096]{2,1,0:T(8,128)(2,1)} %get-tuple-element.145.slope_ref, bf16[1024,4096]{1,0:T(8,128)(2,1)} %bitcast.181, bf16[4096,1024]{1,0:T(8,128)(2,1)} %bitcast.184, ...), custom_call_target="tpu_custom_call" | custom-call | flops 4369999872 | tf_op jit(solution)/shard_map/expert_back/pallas_call | solution.py:586
  293.1 13.4 %all-to-all-done.4.grad_ref.refs_3_ = bf16[8,96,1024]{2,1,0:T(8,128)(2,1)S(1)} async-done(((bf16[8,96,1024]{2,1,0:T(8,128)(2,1)}), bf16[8,96,1024]{2,1,0:T(8,128)(2,1)S(1)}, u32[]{:S(2)}, u32[]{:S(2)}) %all-to-all-start.4) | async-done | bytes 1572896 | tf_op jit(solution)/shard_map/all_to_all | solution.py:951
  310.2 22.5 %expert_back.3 = (bf16[8,192,4096]{2,1,0:T(8,128)(2,1)}, bf16[8,96,1024]{2,1,0:T(8,128)(2,1)}, f32[8,1024]{1,0:T(8,128)}) custom-call(bf16[8,96,1024]{2,1,0:T(8,128)(2,1)} %copy-done.42, bf16[8,96,4096]{2,1,0:T(8,128)(2,1)} %get-tuple-element.150.slope_ref, bf16[1024,4096]{1,0:T(8,128)(2,1)} %bitcast.182, ...), custom_call_target="tpu_custom_call", output_to_operand_aliasing={{0}: (7, {})} | custom-call | flops 4369999872 | tf_op jit(solution)/shard_map/expert_back/pallas_call | solution.py:586
  332.7 14.7 %all-to-all-done.5 = bf16[8,96,1024]{2,1,0:T(8,128)(2,1)S(1)} async-done(((bf16[8,96,1024]{2,1,0:T(8,128)(2,1)}), bf16[8,96,1024]{2,1,0:T(8,128)(2,1)S(1)}, u32[]{:S(2)}, u32[]{:S(2)}) %all-to-all-start.5) | async-done | bytes 1572896 | tf_op jit(solution)/shard_map/all_to_all | solution.py:951
  351.2 37.9 %weight_grads.1 = (bf16[1024,4096]{1,0:T(8,128)(2,1)}, bf16[1024,4096]{1,0:T(8,128)(2,1)}) custom-call(bf16[8,96,1024]{2,1,0:T(8,128)(2,1)} %copy-done.43, bf16[8,96,1024]{2,1,0:T(8,128)(2,1)} %copy-done.39, bf16[8,96,1024]{2,1,0:T(8,128)(2,1)} %copy-done.44, bf16[8,96,1024]{2,1,0:T(8,128)(2,1)} %copy-done.42, ...), custom_call_target="tpu_custom_call" | custom-call | flops 7219999744 | tf_op jit(solution)/shard_map/weight_grads/pallas_call | solution.py:678
  390.2 6.2 all-to-all-start.7
  397.6 12.1 %before_attend_back.1 = (f32[1024,1024]{1,0:T(8,128)}, bf16[1024,1024]{1,0:T(8,128)(2,1)S(1)}, bf16[1024,1024]{1,0:T(8,128)(2,1)}, f32[16,1024]{1,0:T(8,128)S(1)}) custom-call(bf16[768,1024]{1,0:T(8,128)(2,1)S(1)} %bitcast.168, bf16[768,1024]{1,0:T(8,128)(2,1)S(1)} %bitcast.169, s32[1024,1]{1,0:T(8,128)S(1)} %copy-done.27, ...), custom_call_target="tpu_custom_call" | custom-call | flops 2280000000 | tf_op jit(solution)/shard_map/before_attend_back/pallas_call | solution.py:360
  417.8 8.8 %attend_back.4.refs_0_ = bf16[1024,768]{1,0:T(8,128)(2,1)S(1)} custom-call(bf16[1024,1536]{1,0:T(8,128)(2,1)} %copy-done.1, bf16[1024,1536]{1,0:T(8,128)(2,1)} %copy-done.1, bf16[1024,1536]{1,0:T(8,128)(2,1)} %copy-done.1, bf16[1024,1024]{1,0:T(8,128)(2,1)S(1)} %copy-done.3, bf16[1024,512]{1,0:T(8,128)(2,1)S(1)} %copy-done.9, ...), custom_call_target="tpu_custom_call" | custom-call | flops 1824000000 | tf_op jit(solution)/shard_map/attend_back/pallas_call | solution.py:205
  433.1 9.1 %attend_back.5.refs_1_ = bf16[1024,768]{1,0:T(8,128)(2,1)S(1)} custom-call(bf16[1024,1536]{1,0:T(8,128)(2,1)} %copy-done.1, bf16[1024,1536]{1,0:T(8,128)(2,1)} %copy-done.1, bf16[1024,1536]{1,0:T(8,128)(2,1)} %copy-done.1, bf16[1024,1024]{1,0:T(8,128)(2,1)S(1)} %copy-done.3, bf16[1024,512]{1,0:T(8,128)(2,1)S(1)} %copy-done.9, ...), custom_call_target="tpu_custom_call" | custom-call | flops 1824000000 | tf_op jit(solution)/shard_map/attend_back/pallas_call | solution.py:205
  451.2 9.1 %attend_back.6.refs_2_ = bf16[1024,768]{1,0:T(8,128)(2,1)S(1)} custom-call(bf16[1024,1536]{1,0:T(8,128)(2,1)} %copy-done, bf16[1024,1536]{1,0:T(8,128)(2,1)} %copy-done, bf16[1024,1536]{1,0:T(8,128)(2,1)} %copy-done, bf16[1024,1024]{1,0:T(8,128)(2,1)S(1)} %copy-done.3, bf16[1024,512]{1,0:T(8,128)(2,1)S(1)} %copy-done.5, ...), custom_call_target="tpu_custom_call" | custom-call | flops 1824000000 | tf_op jit(solution)/shard_map/attend_back/pallas_call | solution.py:205
  463.3 6.6 %collective-permute-done.4 = bf16[4,2,32,1152]{3,2,1,0:T(8,128)(2,1)S(1)} collective-permute-done((bf16[4,2,32,1152]{3,2,1,0:T(8,128)(2,1)S(1)}, bf16[4,2,32,1152]{3,2,1,0:T(8,128)(2,1)S(1)}, u32[]{:S(2)}, u32[]{:S(2)}) %collective-permute-start.4) | collective-permute-done | bytes 589856 | tf_op jit(solution)/shard_map/ppermute | solution.py:743
  479.0 9.0 %attend_back.7.refs_3_ = bf16[1024,768]{1,0:T(8,128)(2,1)S(1)} custom-call(bf16[1024,1536]{1,0:T(8,128)(2,1)} %copy-done, bf16[1024,1536]{1,0:T(8,128)(2,1)} %copy-done, bf16[1024,1536]{1,0:T(8,128)(2,1)} %copy-done, bf16[1024,1024]{1,0:T(8,128)(2,1)S(1)} %copy-done.3, bf16[1024,512]{1,0:T(8,128)(2,1)S(1)} %copy-done.5, ...), custom_call_target="tpu_custom_call" | custom-call | flops 1824000000 | tf_op jit(solution)/shard_map/attend_back/pallas_call | solution.py:205
  488.0 7.5 %collective-permute-done.6 = bf16[4,2,32,1536]{3,2,1,0:T(8,128)(2,1)S(1)} collective-permute-done((bf16[4,2,32,1536]{3,2,1,0:T(8,128)(2,1)S(1)}, bf16[4,2,32,1536]{3,2,1,0:T(8,128)(2,1)S(1)}, u32[]{:S(2)}, u32[]{:S(2)}) %collective-permute-start.6) | collective-permute-done | bytes 786464 | tf_op jit(solution)/shard_map/ppermute | solution.py:743
  516.3 13.9 %input_gradient.1 = (f32[1024,1024]{1,0:T(8,128)}, f32[16,1024]{1,0:T(8,128)S(1)}) custom-call(bf16[1024,768]{1,0:T(8,128)(2,1)S(1)} %copy-done.18, bf16[1024,768]{1,0:T(8,128)(2,1)S(1)} %copy-done.20, bf16[1024,768]{1,0:T(8,128)(2,1)S(1)} %copy-done.22, bf16[1024,768]{1,0:T(8,128)(2,1)} %copy-done.23, bf16[1024,1664]{1,0:T(8,128)(2,1)} %copy-done.2, ...), custom_call_target="tpu_custom_call" | custom-call | flops 2660000000 | tf_op jit(solution)/shard_map/input_gradient/pallas_call | solution.py:414
  530.3 10.7 %collective-permute-done.9 = bf16[2,32,2688]{2,1,0:T(8,128)(2,1)S(1)} collective-permute-done((bf16[2,32,2688]{2,1,0:T(8,128)(2,1)S(1)}, bf16[2,32,2688]{2,1,0:T(8,128)(2,1)S(1)}, u32[]{:S(2)}, u32[]{:S(2)}) %collective-permute-start.9) | collective-permute-done | bytes 344096 | tf_op jit(solution)/shard_map/ppermute | solution.py:801
  541.9 9.0 %collective-permute-done.13 = bf16[4,32,1536]{2,1,0:T(8,128)(2,1)S(1)} collective-permute-done((bf16[4,32,1536]{2,1,0:T(8,128)(2,1)S(1)}, bf16[4,32,1536]{2,1,0:T(8,128)(2,1)S(1)}, u32[]{:S(2)}, u32[]{:S(2)}) %collective-permute-start.13) | collective-permute-done | bytes 393248 | tf_op jit(solution)/shard_map/ppermute | solution.py:801
  562.9 7.6 %activations_of.1 = bf16[1024,1024]{1,0:T(8,128)(2,1)} custom-call(bf16[1536,1024]{1,0:T(8,128)(2,1)} %bitcast.38.refs_0_, s32[1024,1]{1,0:T(8,128)S(1)} %copy-done.26, f32[1024,128]{1,0:T(8,128)S(1)} %copy-done.36, f32[1024,1024]{1,0:T(8,128)} %get-tuple-element.164.refs_3_), custom_call_target="tpu_custom_call" | custom-call | flops 1424999936 | tf_op jit(solution)/shard_map/activations_of/pallas_call | solution.py:448
  608.3 16.6 %step_experts.1 = (f32[1,256,4096]{2,1,0:T(8,128)}, f32[1,256,4096]{2,1,0:T(8,128)}, f32[1,256,4096]{2,1,0:T(8,128)}, f32[1,4096,256]{2,1,0:T(8,128)}, f32[1,4096,256]{2,1,0:T(8,128)}, /*index=5*/f32[1,4096,256]{2,1,0:T(8,128)}) custom-call(f32[1]{0:T(128)} %bitcast.74.factor_ref, f32[1,256,4096]{2,1,0:T(8,128)} %refs_0_.1, f32[1,256,4096]{2,1,0:T(8,128)} %refs_1_.1, ...), custom_call_target="tpu_custom_call" | custom-call | flops 3800000000 | tf_op jit(solution)/shard_map/step_experts/pallas_call | solution.py:724
  (334 shorter events, 178.4 us)
Async XLA Ops:
  7.2 98.8 %all-gather.4.cloned.1.call-start = ((), (), s32[]{:S(2)}) async-start(), calls=%async_computation.11 | async-start | bytes 5406720 | tf_op jit(solution)/shard_map/all_gather | solution.py:890
  12.4 32.5 %all-to-all-start = ((bf16[8,32,1664]{2,1,0:T(8,128)(2,1)}), bf16[8,32,1664]{2,1,0:T(8,128)(2,1)S(1)}, u32[]{:S(2)}, u32[]{:S(2)}) async-start(bf16[8,32,1664]{2,1,0:T(8,128)(2,1)} %broadcast_in_dim.54), calls=%async_computation | async-start | bytes 1703936 | tf_op jit(solution)/shard_map/all_to_all | solution.py:909
  19.8 162.6 %all-gather.6.cloned.1.call-start = ((), (), s32[]{:S(2)}) async-start(), calls=%async_computation.12 | async-start | bytes 10485760 | tf_op jit(solution)/shard_map/all_gather | solution.py:920
  45.0 199.4 %all-gather.8.cloned.1.call-start = ((), (), s32[]{:S(2)}) async-start(), calls=%async_computation.13 | async-start | bytes 10485760 | tf_op jit(solution)/shard_map/all_gather | solution.py:921
  45.7 24.2 %collective-permute-start.1 = (bf16[8,32,1664]{2,1,0:T(8,128)(2,1)S(1)}, bf16[8,32,1664]{2,1,0:T(8,128)(2,1)S(1)}, u32[]{:S(2)}, u32[]{:S(2)}) collective-permute-start(bf16[8,32,1664]{2,1,0:T(8,128)(2,1)S(1)} %all-to-all-done.refs_0_), channel_id=1, source_target_pairs={{0,2},{1,3},{2,0},{3,1},{4,6},{5,7},{6,4},{7,5},{8,10},{9,11},{10,... | collective-permute-start | bytes 2555912 | tf_op jit(solution)/shard_map/ppermute | solution.py:743
  47.2 24.8 %collective-permute-start = (bf16[8,32,1664]{2,1,0:T(8,128)(2,1)S(1)}, bf16[8,32,1664]{2,1,0:T(8,128)(2,1)S(1)}, u32[]{:S(2)}, u32[]{:S(2)}) collective-permute-start(bf16[8,32,1664]{2,1,0:T(8,128)(2,1)S(1)} %all-to-all-done.refs_0_), channel_id=1, source_target_pairs={{0,1},{1,0},{2,3},{3,2},{4,5},{5,4},{6,7},{7,6},{8,9},{9,8},{10,11... | collective-permute-start | bytes 2555912 | tf_op jit(solution)/shard_map/ppermute | solution.py:743
  136.2 42.6 %all-to-all-start.1 = ((bf16[8,96,1024]{2,1,0:T(8,128)(2,1)}), bf16[8,96,1024]{2,1,0:T(8,128)(2,1)S(1)}, u32[]{:S(2)}, u32[]{:S(2)}) async-start(bf16[8,96,1024]{2,1,0:T(8,128)(2,1)} %bitcast.12), calls=%async_computation.1 | async-start | bytes 3145728 | tf_op jit(solution)/shard_map/all_to_all | solution.py:951
  178.8 40.8 %all-to-all-start.2 = ((bf16[8,96,1024]{2,1,0:T(8,128)(2,1)}), bf16[8,96,1024]{2,1,0:T(8,128)(2,1)S(1)}, u32[]{:S(2)}, u32[]{:S(2)}) async-start(bf16[8,96,1024]{2,1,0:T(8,128)(2,1)} %bitcast.204), calls=%async_computation.2 | async-start | bytes 3145728 | tf_op jit(solution)/shard_map/all_to_all | solution.py:951
  219.5 44.0 %all-to-all-start.3 = ((bf16[8,96,1024]{2,1,0:T(8,128)(2,1)}), bf16[8,96,1024]{2,1,0:T(8,128)(2,1)S(1)}, u32[]{:S(2)}, u32[]{:S(2)}) async-start(bf16[8,96,1024]{2,1,0:T(8,128)(2,1)} %bitcast.203), calls=%async_computation.3 | async-start | bytes 3145728 | tf_op jit(solution)/shard_map/all_to_all | solution.py:951
  263.5 43.0 %all-to-all-start.4 = ((bf16[8,96,1024]{2,1,0:T(8,128)(2,1)}), bf16[8,96,1024]{2,1,0:T(8,128)(2,1)S(1)}, u32[]{:S(2)}, u32[]{:S(2)}) async-start(bf16[8,96,1024]{2,1,0:T(8,128)(2,1)} %bitcast.202), calls=%async_computation.4 | async-start | bytes 3145728 | tf_op jit(solution)/shard_map/all_to_all | solution.py:951
  306.5 40.8 %all-to-all-start.5 = ((bf16[8,96,1024]{2,1,0:T(8,128)(2,1)}), bf16[8,96,1024]{2,1,0:T(8,128)(2,1)S(1)}, u32[]{:S(2)}, u32[]{:S(2)}) async-start(bf16[8,96,1024]{2,1,0:T(8,128)(2,1)} %get-tuple-element.153), calls=%async_computation.5 | async-start | bytes 3145728 | tf_op jit(solution)/shard_map/all_to_all | solution.py:951
  347.4 41.8 %all-to-all-start.6 = ((bf16[8,96,1024]{2,1,0:T(8,128)(2,1)}), bf16[8,96,1024]{2,1,0:T(8,128)(2,1)S(1)}, u32[]{:S(2)}, u32[]{:S(2)}) async-start(bf16[8,96,1024]{2,1,0:T(8,128)(2,1)} %get-tuple-element.156), calls=%async_computation.6 | async-start | bytes 3145728 | tf_op jit(solution)/shard_map/all_to_all | solution.py:951
  351.0 219.6 %reduce-scatter.3.cloned.1.call-start = ((), (), s32[]{:S(2)}) async-start(), calls=%async_computation.14 | async-start | bytes 10485760 | tf_op jit(solution)/shard_map/reduce_scatter | solution.py:1012
  389.2 181.5 %reduce-scatter.5.cloned.1.call-start = ((), (), s32[]{:S(2)}) async-start(), calls=%async_computation.15 | async-start | bytes 10485760 | tf_op jit(solution)/shard_map/reduce_scatter | solution.py:1013
  390.2 83.9 %all-to-all-start.7 = ((bf16[8,192,1024]{2,1,0:T(8,128)(2,1)}), bf16[8,192,1024]{2,1,0:T(8,128)(2,1)}, u32[]{:S(2)}, u32[]{:S(2)}) async-start(bf16[8,192,1024]{2,1,0:T(8,128)(2,1)} %bitcast.188), calls=%async_computation.7 | async-start | bytes 6291456 | tf_op jit(solution)/shard_map/all_to_all | solution.py:951
  415.2 14.3 %collective-permute-start.3 = (bf16[8,2,32,1152]{3,2,1,0:T(8,128)(2,1)}, bf16[8,2,32,1152]{3,2,1,0:T(8,128)(2,1)}, u32[]{:S(2)}, u32[]{:S(2)}) collective-permute-start(bf16[8,2,32,1152]{3,2,1,0:T(8,128)(2,1)} %fusion.18), channel_id=1, source_target_pairs={{0,1},{1,0},{2,3},{3,2},{4,5},{5,4},{6,7},{7,6},{8,9},{9,8},{10,11... | collective-permute-start | bytes 3538952 | tf_op jit(solution)/shard_map/ppermute | solution.py:743
  446.5 24.4 %collective-permute-start.5 = (bf16[8,2,32,1536]{3,2,1,0:T(8,128)(2,1)}, bf16[8,2,32,1536]{3,2,1,0:T(8,128)(2,1)}, u32[]{:S(2)}, u32[]{:S(2)}) collective-permute-start(bf16[8,2,32,1536]{3,2,1,0:T(8,128)(2,1)} %pad_maximum_fusion.1), channel_id=1, source_target_pairs={{0,1},{1,0},{2,3},{3,2},{4,5},{5,4},{6,7},{7,6},{8,9},{9,8},{10,11... | collective-permute-start | bytes 4718600 | tf_op jit(solution)/shard_map/ppermute | solution.py:743
  447.9 22.0 %collective-permute-start.4 = (bf16[4,2,32,1152]{3,2,1,0:T(8,128)(2,1)S(1)}, bf16[4,2,32,1152]{3,2,1,0:T(8,128)(2,1)S(1)}, u32[]{:S(2)}, u32[]{:S(2)}) collective-permute-start(bf16[4,2,32,1152]{3,2,1,0:T(8,128)(2,1)S(1)} %dynamic-slice_bitcast_fusion.9), channel_id=1, source_target_pairs={{0,4},{4,0},{8,12},{12,8},{16,20},{20,16},{24,28},{28,24},{1,5},{5... | collective-permute-start | bytes 1769480 | tf_op jit(solution)/shard_map/ppermute | solution.py:743
  475.5 20.0 %collective-permute-start.6 = (bf16[4,2,32,1536]{3,2,1,0:T(8,128)(2,1)S(1)}, bf16[4,2,32,1536]{3,2,1,0:T(8,128)(2,1)S(1)}, u32[]{:S(2)}, u32[]{:S(2)}) collective-permute-start(bf16[4,2,32,1536]{3,2,1,0:T(8,128)(2,1)S(1)} %dynamic-slice_bitcast_fusion.3), channel_id=1, source_target_pairs={{0,4},{4,0},{8,12},{12,8},{16,20},{20,16},{24,28},{28,24},{1,5},{5... | collective-permute-start | bytes 2359304 | tf_op jit(solution)/shard_map/ppermute | solution.py:743
  500.3 3.6 collective-permute-start.7
  507.6 22.6 %collective-permute-start.10 = (bf16[2,32,2688]{2,1,0:T(8,128)(2,1)S(1)}, bf16[2,32,2688]{2,1,0:T(8,128)(2,1)S(1)}, u32[]{:S(2)}, u32[]{:S(2)}) collective-permute-start(bf16[2,32,2688]{2,1,0:T(8,128)(2,1)S(1)} %get-tuple-element.249), channel_id=1, source_target_pairs={{0,24},{1,25},{2,26},{3,27},{4,28},{5,29},{6,30},{7,31},{8,16},{9,... | collective-permute-start | bytes 1032200 | tf_op jit(solution)/shard_map/ppermute | solution.py:801
  510.4 19.9 %collective-permute-start.8 = (bf16[2,32,2688]{2,1,0:T(8,128)(2,1)S(1)}, bf16[2,32,2688]{2,1,0:T(8,128)(2,1)S(1)}, u32[]{:S(2)}, u32[]{:S(2)}) collective-permute-start(bf16[2,32,2688]{2,1,0:T(8,128)(2,1)S(1)} %get-tuple-element.248), channel_id=1, source_target_pairs={{0,8},{1,9},{2,10},{3,11},{4,12},{5,13},{6,14},{7,15},{8,0},{9,1},... | collective-permute-start | bytes 1032200 | tf_op jit(solution)/shard_map/ppermute | solution.py:801
  510.4 30.7 %collective-permute-start.9 = (bf16[2,32,2688]{2,1,0:T(8,128)(2,1)S(1)}, bf16[2,32,2688]{2,1,0:T(8,128)(2,1)S(1)}, u32[]{:S(2)}, u32[]{:S(2)}) collective-permute-start(bf16[2,32,2688]{2,1,0:T(8,128)(2,1)S(1)} %get-tuple-element.250), channel_id=1, source_target_pairs={{0,16},{1,17},{2,18},{3,19},{4,20},{5,21},{6,22},{7,23},{8,24},{9,... | collective-permute-start | bytes 1032200 | tf_op jit(solution)/shard_map/ppermute | solution.py:801
  512.1 29.8 %collective-permute-start.11 = (bf16[4,32,1536]{2,1,0:T(8,128)(2,1)S(1)}, bf16[4,32,1536]{2,1,0:T(8,128)(2,1)S(1)}, u32[]{:S(2)}, u32[]{:S(2)}) collective-permute-start(bf16[4,32,1536]{2,1,0:T(8,128)(2,1)S(1)} %get-tuple-element.237), channel_id=1, source_target_pairs={{0,2},{1,3},{2,0},{3,1},{4,6},{5,7},{6,4},{7,5},{8,10},{9,11},{10,... | collective-permute-start | bytes 1179656 | tf_op jit(solution)/shard_map/ppermute | solution.py:801
  514.6 27.4 %collective-permute-start.12 = (bf16[4,32,1536]{2,1,0:T(8,128)(2,1)S(1)}, bf16[4,32,1536]{2,1,0:T(8,128)(2,1)S(1)}, u32[]{:S(2)}, u32[]{:S(2)}) collective-permute-start(bf16[4,32,1536]{2,1,0:T(8,128)(2,1)S(1)} %get-tuple-element.239), channel_id=1, source_target_pairs={{0,4},{1,5},{2,6},{3,7},{4,0},{5,1},{6,2},{7,3},{8,12},{9,13},{10,... | collective-permute-start | bytes 1179656 | tf_op jit(solution)/shard_map/ppermute | solution.py:801
  530.2 20.7 %collective-permute-start.13 = (bf16[4,32,1536]{2,1,0:T(8,128)(2,1)S(1)}, bf16[4,32,1536]{2,1,0:T(8,128)(2,1)S(1)}, u32[]{:S(2)}, u32[]{:S(2)}) collective-permute-start(bf16[4,32,1536]{2,1,0:T(8,128)(2,1)S(1)} %get-tuple-element.238), channel_id=1, source_target_pairs={{0,6},{1,7},{2,4},{3,5},{4,2},{5,3},{6,0},{7,1},{8,14},{9,15},{10,... | collective-permute-start | bytes 1179656 | tf_op jit(solution)/shard_map/ppermute | solution.py:801
  552.0 18.6 %all-to-all-start.8 = ((f32[32,1,64]{2,1,0:T(1,128)}), f32[32,1,64]{2,1,0:T(1,128)S(1)}, u32[]{:S(2)}, u32[]{:S(2)}) async-start(f32[32,1,64]{2,1,0:T(1,128)} %bitcast.65), calls=%async_computation.8 | async-start | bytes 32768 | tf_op jit(solution)/shard_map/all_to_all | solution.py:1086
  556.6 13.9 %collective-permute-start.14 = (bf16[32,2688]{1,0:T(8,128)(2,1)S(1)}, bf16[32,2688]{1,0:T(8,128)(2,1)S(1)}, u32[]{:S(2)}, u32[]{:S(2)}) collective-permute-start(bf16[32,2688]{1,0:T(8,128)(2,1)S(1)} %dynamic-slice_bitcast_fusion.16), channel_id=1, source_target_pairs={{0,2},{1,3},{2,0},{3,1},{4,6},{5,7},{6,4},{7,5},{8,10},{9,11},{10,... | collective-permute-start | bytes 516104 | tf_op jit(solution)/shard_map/ppermute | solution.py:801
  558.5 17.3 %collective-permute-start.15 = (bf16[32,1536]{1,0:T(8,128)(2,1)S(1)}, bf16[32,1536]{1,0:T(8,128)(2,1)S(1)}, u32[]{:S(2)}, u32[]{:S(2)}) collective-permute-start(bf16[32,1536]{1,0:T(8,128)(2,1)S(1)} %get-tuple-element.255), channel_id=1, source_target_pairs={{0,8},{1,9},{2,10},{3,11},{4,12},{5,13},{6,14},{7,15},{8,0},{9,1},... | collective-permute-start | bytes 294920 | tf_op jit(solution)/shard_map/ppermute | solution.py:801
  560.0 15.8 %collective-permute-start.16 = (bf16[32,1536]{1,0:T(8,128)(2,1)S(1)}, bf16[32,1536]{1,0:T(8,128)(2,1)S(1)}, u32[]{:S(2)}, u32[]{:S(2)}) collective-permute-start(bf16[32,1536]{1,0:T(8,128)(2,1)S(1)} %get-tuple-element.254), channel_id=1, source_target_pairs={{0,16},{1,17},{2,18},{3,19},{4,20},{5,21},{6,22},{7,23},{8,24},{9,... | collective-permute-start | bytes 294920 | tf_op jit(solution)/shard_map/ppermute | solution.py:801
  562.4 13.4 %collective-permute-start.17 = (bf16[32,1536]{1,0:T(8,128)(2,1)S(1)}, bf16[32,1536]{1,0:T(8,128)(2,1)S(1)}, u32[]{:S(2)}, u32[]{:S(2)}) collective-permute-start(bf16[32,1536]{1,0:T(8,128)(2,1)S(1)} %get-tuple-element.253), channel_id=1, source_target_pairs={{0,24},{1,25},{2,26},{3,27},{4,28},{5,29},{6,30},{7,31},{8,16},{9,... | collective-permute-start | bytes 294920 | tf_op jit(solution)/shard_map/ppermute | solution.py:801
  596.9 4.5 collective-permute-start.22
  (78 other events, 463.4 us)
Sparse Core Ops, SparseCore 0:
  11.5 77.0 all-gather.3
  90.7 57.8 all-gather.5
  150.7 59.3 all-gather.7
  389.3 74.0 reduce-scatter.2
  466.0 88.5 reduce-scatter.4

commit v7 on v6

--- a/solution.py
+++ b/solution.py
@@ -901,14 +901,13 @@
     doc_col = documents[:, None]
     doc_row = documents[None, :]
 
-    normal_one, _ = norm_parts(tokens.astype(f32))
     if rows_own % 16:
         front = lax.all_gather(front, everywhere, axis=0, tiled=True)
     else:
         spread = jnp.broadcast_to(front[None], (experts,) + front.shape)
         spread = lax.all_to_all(spread, "expert", split_axis=0, concat_axis=0, tiled=True)
-        spread, normal_one, in_low, out_low, slot_row, slot_col, chunked_row, chunked_col = in_order(
-            spread, normal_one, in_low, out_low, slot_row, slot_col, chunked_row, chunked_col
+        spread, in_low, out_low, slot_row, slot_col, chunked_row, chunked_col = in_order(
+            spread, in_low, out_low, slot_row, slot_col, chunked_row, chunked_col
         )
         pieces = {0: spread}
         distance = dp // 2
@@ -925,6 +924,7 @@
     ).reshape(4, width).astype(f32)
     centre_table = small_full[:, 4 * norm_own : 4 * norm_own + centre_own].reshape(experts, width)
 
+    normal_one, _ = norm_parts(tokens.astype(f32))
     normed_low = (normal_one * norms[0] + norms[1]).astype(low)
     normed_low, front = in_order(normed_low, front)
     packed, mixed, lse = [], [], []

time: 640 us -> 635 us (level)
  local copies, waits for them, and re-layouts: 40.2 us -> 32.2 us
    all_to_all x1, waiting for transfers between devices: 3.75 us -> 12.1 us  [shards(): lax.all_to_all(spread, 'expert', split_axis=0, concat_axis=0, tiled=True)]
    unnamed x147 -> x137, local copies, waits for them, and re-layouts: 20.8 us -> 15.4 us
  transfers between devices with their start and end apart: 37 -> 37, of which waited for: 16 -> 16; matrix products, arithmetic and copies ran while one was open for 18% -> 17% of each run, Pallas kernels for 36% -> 37%
where the time goes in v7:
time: 635 us; the launch traced here: 628 us
  Pallas kernels  246 us (39%)
  waiting for transfers between devices  151 us (24%)
  starting transfers between devices  75 us (12%)
  other arithmetic  50.7 us (8%)
  matrix products  49.4 us (8%)
  local copies, waits for them, and re-layouts  32.2 us (5%)
  between operations  23.6 us (4%)
    all_to_all x7, waiting for transfers between devices, exchange(): lax.all_to_all(rows, 'expert', split_axis=0, concat_axis=0, tiled=True)  73.8 us
    pallas_call x2, Pallas kernels, expert_back(): pl.pallas_call(expert_back_kernel, grid=(count + width // columns,), in_s...  45.1 us
    ppermute x13, waiting for transfers between devices, swap(): return lax.ppermute(values, axis, [(i, i ^ distance) for i in range(size)])  44 us
    pallas_call x2, Pallas kernels, expert_forward(): pl.pallas_call(expert_kernel, grid=(inner // tile,), in_specs=[pl.BlockSp...  42.5 us
    pallas_call x1, Pallas kernels, weight_grads(): pl.pallas_call(lambda *refs: weight_grads_kernel(chunks, refs), grid=(2 *...  37.9 us
    pallas_call x4, Pallas kernels, attend_back(): pl.pallas_call(attend_back_kernel, grid=(tokens // SEQ, count), in_specs=...  36 us
    all_to_all x7, starting transfers between devices, exchange(): lax.all_to_all(rows, 'expert', split_axis=0, concat_axis=0, tiled=True)  32.3 us
    pallas_call x2, Pallas kernels, attend(): pl.pallas_call(attend_kernel, grid=(count // SEQ, pairs), in_specs=[part(...  20.6 us
  transfers between devices with their start and end apart: 37, of which 16 were waited for; matrix products, arithmetic and copies ran while one was open for 17% of the time, Pallas kernels for 37%

profile of v7, /device:TPU:0, one launch (start us, length us, event | category | flops | bytes accessed | tf_op | source)
XLA Modules:
  0.0 628.1 jit_solution(13695193784678834659)
XLA Ops:
  12.4 7.3 %all-to-all-start = ((bf16[8,32,1664]{2,1,0:T(8,128)(2,1)}), bf16[8,32,1664]{2,1,0:T(8,128)(2,1)S(1)}, u32[]{:S(2)}, u32[]{:S(2)}) async-start(bf16[8,32,1664]{2,1,0:T(8,128)(2,1)} %broadcast_in_dim.54), calls=%async_computation | async-start | bytes 1703936 | tf_op jit(solution)/shard_map/all_to_all | solution.py:908
  32.6 12.1 %all-to-all-done.refs_0_ = bf16[8,32,1664]{2,1,0:T(8,128)(2,1)S(1)} async-done(((bf16[8,32,1664]{2,1,0:T(8,128)(2,1)}), bf16[8,32,1664]{2,1,0:T(8,128)(2,1)S(1)}, u32[]{:S(2)}, u32[]{:S(2)}) %all-to-all-start) | async-done | bytes 852000 | tf_op jit(solution)/shard_map/all_to_all | solution.py:908
  49.2 20.7 %collective-permute-done.1.refs_2_ = bf16[8,32,1664]{2,1,0:T(8,128)(2,1)S(1)} collective-permute-done((bf16[8,32,1664]{2,1,0:T(8,128)(2,1)S(1)}, bf16[8,32,1664]{2,1,0:T(8,128)(2,1)S(1)}, u32[]{:S(2)}, u32[]{:S(2)}) %collective-permute-start.1) | collective-permute-done | bytes 852000 | tf_op jit(solution)/shard_map/ppermute | solution.py:743
  82.7 5.4 convolution_convert_fusion.2.q_ref.k_ref.v_ref
  88.1 10.3 %attend.2 = (bf16[1024,512]{1,0:T(8,128)(2,1)S(1)}, f32[32,1024]{1,0:T(8,128)S(1)}) custom-call(bf16[1024,1536]{1,0:T(8,128)(2,1)S(1)} %convolution_convert_fusion.2.q_ref.k_ref.v_ref, bf16[1024,1536]{1,0:T(8,128)(2,1)S(1)} %convolution_convert_fusion.2.q_ref.k_ref.v_ref, bf16[1024,1536]{1,0:T(8,128)(2,1)S(1)} %convolution_convert_fusion.2.q_ref.k_ref.v_ref, ...), custom_call_target="tpu_custom_call" | custom-call | flops 5510000128 | tf_op jit(solution)/shard_map/attend/pallas_call | solution.py:111
  101.1 6.1 convolution_convert_fusion.1.q_ref.k_ref.v_ref
  107.2 10.3 %attend.3 = (bf16[1024,512]{1,0:T(8,128)(2,1)S(1)}, f32[32,1024]{1,0:T(8,128)S(1)}) custom-call(bf16[1024,1536]{1,0:T(8,128)(2,1)S(1)} %convolution_convert_fusion.1.q_ref.k_ref.v_ref, bf16[1024,1536]{1,0:T(8,128)(2,1)S(1)} %convolution_convert_fusion.1.q_ref.k_ref.v_ref, bf16[1024,1536]{1,0:T(8,128)(2,1)S(1)} %convolution_convert_fusion.1.q_ref.k_ref.v_ref, ...), custom_call_target="tpu_custom_call" | custom-call | flops 5510000128 | tf_op jit(solution)/shard_map/attend/pallas_call | solution.py:111
  117.5 13.4 %after_attend.1 = (f32[1024,1024]{1,0:T(8,128)}, bf16[1024,1024]{1,0:T(8,128)(2,1)}, f32[1024,128]{1,0:T(8,128)S(1)}, bf16[768,1024]{1,0:T(8,128)(2,1)}, bf16[768,1024]{1,0:T(8,128)(2,1)}) custom-call(bf16[1024,512]{1,0:T(8,128)(2,1)S(1)} %copy-done.7, bf16[1024,512]{1,0:T(8,128)(2,1)S(1)} %get-tuple-element.125.refs_1_.mixed_ref, ...), custom_call_target="tpu_custom_call" | custom-call | flops 2470000128 | tf_op jit(solution)/shard_map/after_attend/pallas_call | solution.py:290
  144.6 29.9 %all-to-all-done.1.x_ref.refs_0_ = bf16[8,96,1024]{2,1,0:T(8,128)(2,1)S(1)} async-done(((bf16[8,96,1024]{2,1,0:T(8,128)(2,1)}), bf16[8,96,1024]{2,1,0:T(8,128)(2,1)S(1)}, u32[]{:S(2)}, u32[]{:S(2)}) %all-to-all-start.1) | async-done | bytes 1572896 | tf_op jit(solution)/shard_map/all_to_all | solution.py:951
  178.2 21.3 %expert_forward.2 = (bf16[8,192,4096]{2,1,0:T(8,128)(2,1)}, bf16[8,96,4096]{2,1,0:T(8,128)(2,1)}) custom-call(bf16[8,96,1024]{2,1,0:T(8,128)(2,1)} %copy-done.39, bf16[1024,4096]{1,0:T(8,128)(2,1)} %bitcast.179), custom_call_target="tpu_custom_call" | custom-call | flops 3990000128 | tf_op jit(solution)/shard_map/expert_forward/pallas_call | solution.py:495
  199.5 15.9 %all-to-all-done.2.x_ref.refs_1_ = bf16[8,96,1024]{2,1,0:T(8,128)(2,1)S(1)} async-done(((bf16[8,96,1024]{2,1,0:T(8,128)(2,1)}), bf16[8,96,1024]{2,1,0:T(8,128)(2,1)S(1)}, u32[]{:S(2)}, u32[]{:S(2)}) %all-to-all-start.2) | async-done | bytes 1572896 | tf_op jit(solution)/shard_map/all_to_all | solution.py:951
  219.0 21.2 %expert_forward.3 = (bf16[8,192,4096]{2,1,0:T(8,128)(2,1)}, bf16[8,96,4096]{2,1,0:T(8,128)(2,1)}) custom-call(bf16[8,96,1024]{2,1,0:T(8,128)(2,1)} %copy-done.35, bf16[1024,4096]{1,0:T(8,128)(2,1)} %bitcast.180, bf16[8,192,4096]{2,1,0:T(8,128)(2,1)} %get-tuple-element.137.rest_0_), custom_call_target="tpu_custom_call", output_to_operand_aliasing={{0}: (2, {})} | custom-call | flops 3990000128 | tf_op jit(solution)/shard_map/expert_forward/pallas_call | solution.py:495
  240.2 19.1 %convolution_convert_fusion = bf16[1536,1024]{1,0:T(8,128)(2,1)} fusion(bf16[1536,4096]{1,0:T(8,128)(2,1)} %bitcast.183, bf16[1,4096,1024]{2,1,0:T(8,128)(2,1)} %all-gather.8.cloned.1.call-done), kind=kOutput, calls=%fused_computation.10 | convolution fusion | flops 12886474752 | bytes 24117248 | tf_op jit(solution)/shard_map/dot_general | solution.py:974
  259.4 6.4 %all-to-all-start.4 = ((bf16[8,96,1024]{2,1,0:T(8,128)(2,1)}), bf16[8,96,1024]{2,1,0:T(8,128)(2,1)S(1)}, u32[]{:S(2)}, u32[]{:S(2)}) async-start(bf16[8,96,1024]{2,1,0:T(8,128)(2,1)} %bitcast.202), calls=%async_computation.4 | async-start | bytes 3145728 | tf_op jit(solution)/shard_map/all_to_all | solution.py:951
  266.4 22.6 %expert_back.2 = (bf16[8,192,4096]{2,1,0:T(8,128)(2,1)}, bf16[8,96,1024]{2,1,0:T(8,128)(2,1)}, f32[8,1024]{1,0:T(8,128)}) custom-call(bf16[8,96,1024]{2,1,0:T(8,128)(2,1)} %copy-done.40, bf16[8,96,4096]{2,1,0:T(8,128)(2,1)} %get-tuple-element.143.slope_ref, bf16[1024,4096]{1,0:T(8,128)(2,1)} %bitcast.181, bf16[4096,1024]{1,0:T(8,128)(2,1)} %bitcast.184, ...), custom_call_target="tpu_custom_call" | custom-call | flops 4369999872 | tf_op jit(solution)/shard_map/expert_back/pallas_call | solution.py:586
  289.0 13.4 %all-to-all-done.4.grad_ref.refs_3_ = bf16[8,96,1024]{2,1,0:T(8,128)(2,1)S(1)} async-done(((bf16[8,96,1024]{2,1,0:T(8,128)(2,1)}), bf16[8,96,1024]{2,1,0:T(8,128)(2,1)S(1)}, u32[]{:S(2)}, u32[]{:S(2)}) %all-to-all-start.4) | async-done | bytes 1572896 | tf_op jit(solution)/shard_map/all_to_all | solution.py:951
  306.0 22.5 %expert_back.3 = (bf16[8,192,4096]{2,1,0:T(8,128)(2,1)}, bf16[8,96,1024]{2,1,0:T(8,128)(2,1)}, f32[8,1024]{1,0:T(8,128)}) custom-call(bf16[8,96,1024]{2,1,0:T(8,128)(2,1)} %copy-done.38, bf16[8,96,4096]{2,1,0:T(8,128)(2,1)} %get-tuple-element.148.slope_ref, bf16[1024,4096]{1,0:T(8,128)(2,1)} %bitcast.182, ...), custom_call_target="tpu_custom_call", output_to_operand_aliasing={{0}: (7, {})} | custom-call | flops 4369999872 | tf_op jit(solution)/shard_map/expert_back/pallas_call | solution.py:586
  328.6 14.7 %all-to-all-done.5 = bf16[8,96,1024]{2,1,0:T(8,128)(2,1)S(1)} async-done(((bf16[8,96,1024]{2,1,0:T(8,128)(2,1)}), bf16[8,96,1024]{2,1,0:T(8,128)(2,1)S(1)}, u32[]{:S(2)}, u32[]{:S(2)}) %all-to-all-start.5) | async-done | bytes 1572896 | tf_op jit(solution)/shard_map/all_to_all | solution.py:951
  347.1 37.9 %weight_grads.1 = (bf16[1024,4096]{1,0:T(8,128)(2,1)}, bf16[1024,4096]{1,0:T(8,128)(2,1)}) custom-call(bf16[8,96,1024]{2,1,0:T(8,128)(2,1)} %copy-done.39, bf16[8,96,1024]{2,1,0:T(8,128)(2,1)} %copy-done.35, bf16[8,96,1024]{2,1,0:T(8,128)(2,1)} %copy-done.40, bf16[8,96,1024]{2,1,0:T(8,128)(2,1)} %copy-done.38, ...), custom_call_target="tpu_custom_call" | custom-call | flops 7219999744 | tf_op jit(solution)/shard_map/weight_grads/pallas_call | solution.py:678
  386.0 6.2 all-to-all-start.7
  393.3 12.6 %before_attend_back.1 = (f32[1024,1024]{1,0:T(8,128)}, bf16[1024,1024]{1,0:T(8,128)(2,1)S(1)}, bf16[1024,1024]{1,0:T(8,128)(2,1)}, f32[16,1024]{1,0:T(8,128)S(1)}) custom-call(bf16[768,1024]{1,0:T(8,128)(2,1)S(1)} %bitcast.168, bf16[768,1024]{1,0:T(8,128)(2,1)S(1)} %bitcast.169, s32[1024,1]{1,0:T(8,128)S(1)} %copy-done.27, ...), custom_call_target="tpu_custom_call" | custom-call | flops 2280000000 | tf_op jit(solution)/shard_map/before_attend_back/pallas_call | solution.py:360
  414.2 8.8 %attend_back.4.refs_0_ = bf16[1024,768]{1,0:T(8,128)(2,1)S(1)} custom-call(bf16[1024,1536]{1,0:T(8,128)(2,1)} %copy-done.1, bf16[1024,1536]{1,0:T(8,128)(2,1)} %copy-done.1, bf16[1024,1536]{1,0:T(8,128)(2,1)} %copy-done.1, bf16[1024,1024]{1,0:T(8,128)(2,1)S(1)} %copy-done.3, bf16[1024,512]{1,0:T(8,128)(2,1)S(1)} %copy-done.9, ...), custom_call_target="tpu_custom_call" | custom-call | flops 1824000000 | tf_op jit(solution)/shard_map/attend_back/pallas_call | solution.py:205
  429.4 9.2 %attend_back.5.refs_1_ = bf16[1024,768]{1,0:T(8,128)(2,1)S(1)} custom-call(bf16[1024,1536]{1,0:T(8,128)(2,1)} %copy-done.1, bf16[1024,1536]{1,0:T(8,128)(2,1)} %copy-done.1, bf16[1024,1536]{1,0:T(8,128)(2,1)} %copy-done.1, bf16[1024,1024]{1,0:T(8,128)(2,1)S(1)} %copy-done.3, bf16[1024,512]{1,0:T(8,128)(2,1)S(1)} %copy-done.9, ...), custom_call_target="tpu_custom_call" | custom-call | flops 1824000000 | tf_op jit(solution)/shard_map/attend_back/pallas_call | solution.py:205
  447.2 9.0 %attend_back.6.refs_2_ = bf16[1024,768]{1,0:T(8,128)(2,1)S(1)} custom-call(bf16[1024,1536]{1,0:T(8,128)(2,1)} %copy-done, bf16[1024,1536]{1,0:T(8,128)(2,1)} %copy-done, bf16[1024,1536]{1,0:T(8,128)(2,1)} %copy-done, bf16[1024,1024]{1,0:T(8,128)(2,1)S(1)} %copy-done.3, bf16[1024,512]{1,0:T(8,128)(2,1)S(1)} %copy-done.5, ...), custom_call_target="tpu_custom_call" | custom-call | flops 1824000000 | tf_op jit(solution)/shard_map/attend_back/pallas_call | solution.py:205
  459.2 6.4 %collective-permute-done.4 = bf16[4,2,32,1152]{3,2,1,0:T(8,128)(2,1)S(1)} collective-permute-done((bf16[4,2,32,1152]{3,2,1,0:T(8,128)(2,1)S(1)}, bf16[4,2,32,1152]{3,2,1,0:T(8,128)(2,1)S(1)}, u32[]{:S(2)}, u32[]{:S(2)}) %collective-permute-start.4) | collective-permute-done | bytes 589856 | tf_op jit(solution)/shard_map/ppermute | solution.py:743
  474.8 8.9 %attend_back.7.refs_3_ = bf16[1024,768]{1,0:T(8,128)(2,1)S(1)} custom-call(bf16[1024,1536]{1,0:T(8,128)(2,1)} %copy-done, bf16[1024,1536]{1,0:T(8,128)(2,1)} %copy-done, bf16[1024,1536]{1,0:T(8,128)(2,1)} %copy-done, bf16[1024,1024]{1,0:T(8,128)(2,1)S(1)} %copy-done.3, bf16[1024,512]{1,0:T(8,128)(2,1)S(1)} %copy-done.5, ...), custom_call_target="tpu_custom_call" | custom-call | flops 1824000000 | tf_op jit(solution)/shard_map/attend_back/pallas_call | solution.py:205
  483.7 7.5 %collective-permute-done.6 = bf16[4,2,32,1536]{3,2,1,0:T(8,128)(2,1)S(1)} collective-permute-done((bf16[4,2,32,1536]{3,2,1,0:T(8,128)(2,1)S(1)}, bf16[4,2,32,1536]{3,2,1,0:T(8,128)(2,1)S(1)}, u32[]{:S(2)}, u32[]{:S(2)}) %collective-permute-start.6) | collective-permute-done | bytes 786464 | tf_op jit(solution)/shard_map/ppermute | solution.py:743
  511.2 13.9 %input_gradient.1 = (f32[1024,1024]{1,0:T(8,128)}, f32[16,1024]{1,0:T(8,128)S(1)}) custom-call(bf16[1024,768]{1,0:T(8,128)(2,1)S(1)} %copy-done.18, bf16[1024,768]{1,0:T(8,128)(2,1)S(1)} %copy-done.20, bf16[1024,768]{1,0:T(8,128)(2,1)S(1)} %copy-done.22, bf16[1024,768]{1,0:T(8,128)(2,1)} %copy-done.23, bf16[1024,1664]{1,0:T(8,128)(2,1)} %copy-done.2, ...), custom_call_target="tpu_custom_call" | custom-call | flops 2660000000 | tf_op jit(solution)/shard_map/input_gradient/pallas_call | solution.py:414
  525.5 11.3 %collective-permute-done.9 = bf16[2,32,2688]{2,1,0:T(8,128)(2,1)S(1)} collective-permute-done((bf16[2,32,2688]{2,1,0:T(8,128)(2,1)S(1)}, bf16[2,32,2688]{2,1,0:T(8,128)(2,1)S(1)}, u32[]{:S(2)}, u32[]{:S(2)}) %collective-permute-start.9) | collective-permute-done | bytes 344096 | tf_op jit(solution)/shard_map/ppermute | solution.py:801
  537.7 8.2 %collective-permute-done.13 = bf16[4,32,1536]{2,1,0:T(8,128)(2,1)S(1)} collective-permute-done((bf16[4,32,1536]{2,1,0:T(8,128)(2,1)S(1)}, bf16[4,32,1536]{2,1,0:T(8,128)(2,1)S(1)}, u32[]{:S(2)}, u32[]{:S(2)}) %collective-permute-start.13) | collective-permute-done | bytes 393248 | tf_op jit(solution)/shard_map/ppermute | solution.py:801
  558.0 7.6 %activations_of.1 = bf16[1024,1024]{1,0:T(8,128)(2,1)} custom-call(bf16[1536,1024]{1,0:T(8,128)(2,1)} %bitcast.38.refs_0_, s32[1024,1]{1,0:T(8,128)S(1)} %copy-done.26, f32[1024,128]{1,0:T(8,128)S(1)} %copy-done.32, f32[1024,1024]{1,0:T(8,128)} %get-tuple-element.162.refs_3_), custom_call_target="tpu_custom_call" | custom-call | flops 1424999936 | tf_op jit(solution)/shard_map/activations_of/pallas_call | solution.py:448
  603.6 16.6 %step_experts.1 = (f32[1,256,4096]{2,1,0:T(8,128)}, f32[1,256,4096]{2,1,0:T(8,128)}, f32[1,256,4096]{2,1,0:T(8,128)}, f32[1,4096,256]{2,1,0:T(8,128)}, f32[1,4096,256]{2,1,0:T(8,128)}, /*index=5*/f32[1,4096,256]{2,1,0:T(8,128)}) custom-call(f32[1]{0:T(128)} %bitcast.74.factor_ref, f32[1,256,4096]{2,1,0:T(8,128)} %refs_0_.1, f32[1,256,4096]{2,1,0:T(8,128)} %refs_1_.1, ...), custom_call_target="tpu_custom_call" | custom-call | flops 3800000000 | tf_op jit(solution)/shard_map/step_experts/pallas_call | solution.py:724
  (323 shorter events, 167.8 us)
Async XLA Ops:
  7.2 93.9 %all-gather.4.cloned.1.call-start = ((), (), s32[]{:S(2)}) async-start(), calls=%async_computation.11 | async-start | bytes 5406720 | tf_op jit(solution)/shard_map/all_gather | solution.py:890
  12.4 32.4 %all-to-all-start = ((bf16[8,32,1664]{2,1,0:T(8,128)(2,1)}), bf16[8,32,1664]{2,1,0:T(8,128)(2,1)S(1)}, u32[]{:S(2)}, u32[]{:S(2)}) async-start(bf16[8,32,1664]{2,1,0:T(8,128)(2,1)} %broadcast_in_dim.54), calls=%async_computation | async-start | bytes 1703936 | tf_op jit(solution)/shard_map/all_to_all | solution.py:908
  19.7 158.5 %all-gather.6.cloned.1.call-start = ((), (), s32[]{:S(2)}) async-start(), calls=%async_computation.12 | async-start | bytes 10485760 | tf_op jit(solution)/shard_map/all_gather | solution.py:919
  44.8 195.4 %all-gather.8.cloned.1.call-start = ((), (), s32[]{:S(2)}) async-start(), calls=%async_computation.13 | async-start | bytes 10485760 | tf_op jit(solution)/shard_map/all_gather | solution.py:920
  45.5 24.3 %collective-permute-start.1 = (bf16[8,32,1664]{2,1,0:T(8,128)(2,1)S(1)}, bf16[8,32,1664]{2,1,0:T(8,128)(2,1)S(1)}, u32[]{:S(2)}, u32[]{:S(2)}) collective-permute-start(bf16[8,32,1664]{2,1,0:T(8,128)(2,1)S(1)} %all-to-all-done.refs_0_), channel_id=1, source_target_pairs={{0,2},{1,3},{2,0},{3,1},{4,6},{5,7},{6,4},{7,5},{8,10},{9,11},{10,... | collective-permute-start | bytes 2555912 | tf_op jit(solution)/shard_map/ppermute | solution.py:743
  49.2 23.7 %collective-permute-start = (bf16[8,32,1664]{2,1,0:T(8,128)(2,1)S(1)}, bf16[8,32,1664]{2,1,0:T(8,128)(2,1)S(1)}, u32[]{:S(2)}, u32[]{:S(2)}) collective-permute-start(bf16[8,32,1664]{2,1,0:T(8,128)(2,1)S(1)} %all-to-all-done.refs_0_), channel_id=1, source_target_pairs={{0,1},{1,0},{2,3},{3,2},{4,5},{5,4},{6,7},{7,6},{8,9},{9,8},{10,11... | collective-permute-start | bytes 2555912 | tf_op jit(solution)/shard_map/ppermute | solution.py:743
  131.8 42.7 %all-to-all-start.1 = ((bf16[8,96,1024]{2,1,0:T(8,128)(2,1)}), bf16[8,96,1024]{2,1,0:T(8,128)(2,1)S(1)}, u32[]{:S(2)}, u32[]{:S(2)}) async-start(bf16[8,96,1024]{2,1,0:T(8,128)(2,1)} %bitcast.12), calls=%async_computation.1 | async-start | bytes 3145728 | tf_op jit(solution)/shard_map/all_to_all | solution.py:951
  174.5 40.8 %all-to-all-start.2 = ((bf16[8,96,1024]{2,1,0:T(8,128)(2,1)}), bf16[8,96,1024]{2,1,0:T(8,128)(2,1)S(1)}, u32[]{:S(2)}, u32[]{:S(2)}) async-start(bf16[8,96,1024]{2,1,0:T(8,128)(2,1)} %bitcast.204), calls=%async_computation.2 | async-start | bytes 3145728 | tf_op jit(solution)/shard_map/all_to_all | solution.py:951
  215.4 44.0 %all-to-all-start.3 = ((bf16[8,96,1024]{2,1,0:T(8,128)(2,1)}), bf16[8,96,1024]{2,1,0:T(8,128)(2,1)S(1)}, u32[]{:S(2)}, u32[]{:S(2)}) async-start(bf16[8,96,1024]{2,1,0:T(8,128)(2,1)} %bitcast.203), calls=%async_computation.3 | async-start | bytes 3145728 | tf_op jit(solution)/shard_map/all_to_all | solution.py:951
  259.4 43.0 %all-to-all-start.4 = ((bf16[8,96,1024]{2,1,0:T(8,128)(2,1)}), bf16[8,96,1024]{2,1,0:T(8,128)(2,1)S(1)}, u32[]{:S(2)}, u32[]{:S(2)}) async-start(bf16[8,96,1024]{2,1,0:T(8,128)(2,1)} %bitcast.202), calls=%async_computation.4 | async-start | bytes 3145728 | tf_op jit(solution)/shard_map/all_to_all | solution.py:951
  302.4 40.8 %all-to-all-start.5 = ((bf16[8,96,1024]{2,1,0:T(8,128)(2,1)}), bf16[8,96,1024]{2,1,0:T(8,128)(2,1)S(1)}, u32[]{:S(2)}, u32[]{:S(2)}) async-start(bf16[8,96,1024]{2,1,0:T(8,128)(2,1)} %get-tuple-element.151), calls=%async_computation.5 | async-start | bytes 3145728 | tf_op jit(solution)/shard_map/all_to_all | solution.py:951
  343.2 41.8 %all-to-all-start.6 = ((bf16[8,96,1024]{2,1,0:T(8,128)(2,1)}), bf16[8,96,1024]{2,1,0:T(8,128)(2,1)S(1)}, u32[]{:S(2)}, u32[]{:S(2)}) async-start(bf16[8,96,1024]{2,1,0:T(8,128)(2,1)} %get-tuple-element.154), calls=%async_computation.6 | async-start | bytes 3145728 | tf_op jit(solution)/shard_map/all_to_all | solution.py:951
  346.9 218.9 %reduce-scatter.3.cloned.1.call-start = ((), (), s32[]{:S(2)}) async-start(), calls=%async_computation.14 | async-start | bytes 10485760 | tf_op jit(solution)/shard_map/reduce_scatter | solution.py:1012
  385.0 180.8 %reduce-scatter.5.cloned.1.call-start = ((), (), s32[]{:S(2)}) async-start(), calls=%async_computation.15 | async-start | bytes 10485760 | tf_op jit(solution)/shard_map/reduce_scatter | solution.py:1013
  386.0 83.7 %all-to-all-start.7 = ((bf16[8,192,1024]{2,1,0:T(8,128)(2,1)}), bf16[8,192,1024]{2,1,0:T(8,128)(2,1)}, u32[]{:S(2)}, u32[]{:S(2)}) async-start(bf16[8,192,1024]{2,1,0:T(8,128)(2,1)} %bitcast.188), calls=%async_computation.7 | async-start | bytes 6291456 | tf_op jit(solution)/shard_map/all_to_all | solution.py:951
  411.4 14.6 %collective-permute-start.3 = (bf16[8,2,32,1152]{3,2,1,0:T(8,128)(2,1)}, bf16[8,2,32,1152]{3,2,1,0:T(8,128)(2,1)}, u32[]{:S(2)}, u32[]{:S(2)}) collective-permute-start(bf16[8,2,32,1152]{3,2,1,0:T(8,128)(2,1)} %fusion.21), channel_id=1, source_target_pairs={{0,1},{1,0},{2,3},{3,2},{4,5},{5,4},{6,7},{7,6},{8,9},{9,8},{10,11... | collective-permute-start | bytes 3538952 | tf_op jit(solution)/shard_map/ppermute | solution.py:743
  442.8 23.8 %collective-permute-start.5 = (bf16[8,2,32,1536]{3,2,1,0:T(8,128)(2,1)}, bf16[8,2,32,1536]{3,2,1,0:T(8,128)(2,1)}, u32[]{:S(2)}, u32[]{:S(2)}) collective-permute-start(bf16[8,2,32,1536]{3,2,1,0:T(8,128)(2,1)} %pad_maximum_fusion.1), channel_id=1, source_target_pairs={{0,1},{1,0},{2,3},{3,2},{4,5},{5,4},{6,7},{7,6},{8,9},{9,8},{10,11... | collective-permute-start | bytes 4718600 | tf_op jit(solution)/shard_map/ppermute | solution.py:743
  443.9 21.7 %collective-permute-start.4 = (bf16[4,2,32,1152]{3,2,1,0:T(8,128)(2,1)S(1)}, bf16[4,2,32,1152]{3,2,1,0:T(8,128)(2,1)S(1)}, u32[]{:S(2)}, u32[]{:S(2)}) collective-permute-start(bf16[4,2,32,1152]{3,2,1,0:T(8,128)(2,1)S(1)} %dynamic-slice_bitcast_fusion.9), channel_id=1, source_target_pairs={{0,4},{4,0},{8,12},{12,8},{16,20},{20,16},{24,28},{28,24},{1,5},{5... | collective-permute-start | bytes 1769480 | tf_op jit(solution)/shard_map/ppermute | solution.py:743
  471.1 20.2 %collective-permute-start.6 = (bf16[4,2,32,1536]{3,2,1,0:T(8,128)(2,1)S(1)}, bf16[4,2,32,1536]{3,2,1,0:T(8,128)(2,1)S(1)}, u32[]{:S(2)}, u32[]{:S(2)}) collective-permute-start(bf16[4,2,32,1536]{3,2,1,0:T(8,128)(2,1)S(1)} %dynamic-slice_bitcast_fusion.3), channel_id=1, source_target_pairs={{0,4},{4,0},{8,12},{12,8},{16,20},{20,16},{24,28},{28,24},{1,5},{5... | collective-permute-start | bytes 2359304 | tf_op jit(solution)/shard_map/ppermute | solution.py:743
  496.0 3.6 collective-permute-start.7
  503.3 21.8 %collective-permute-start.10 = (bf16[2,32,2688]{2,1,0:T(8,128)(2,1)S(1)}, bf16[2,32,2688]{2,1,0:T(8,128)(2,1)S(1)}, u32[]{:S(2)}, u32[]{:S(2)}) collective-permute-start(bf16[2,32,2688]{2,1,0:T(8,128)(2,1)S(1)} %get-tuple-element.247), channel_id=1, source_target_pairs={{0,24},{1,25},{2,26},{3,27},{4,28},{5,29},{6,30},{7,31},{8,16},{9,... | collective-permute-start | bytes 1032200 | tf_op jit(solution)/shard_map/ppermute | solution.py:801
  505.9 19.6 %collective-permute-start.8 = (bf16[2,32,2688]{2,1,0:T(8,128)(2,1)S(1)}, bf16[2,32,2688]{2,1,0:T(8,128)(2,1)S(1)}, u32[]{:S(2)}, u32[]{:S(2)}) collective-permute-start(bf16[2,32,2688]{2,1,0:T(8,128)(2,1)S(1)} %get-tuple-element.246), channel_id=1, source_target_pairs={{0,8},{1,9},{2,10},{3,11},{4,12},{5,13},{6,14},{7,15},{8,0},{9,1},... | collective-permute-start | bytes 1032200 | tf_op jit(solution)/shard_map/ppermute | solution.py:801
  505.9 30.8 %collective-permute-start.9 = (bf16[2,32,2688]{2,1,0:T(8,128)(2,1)S(1)}, bf16[2,32,2688]{2,1,0:T(8,128)(2,1)S(1)}, u32[]{:S(2)}, u32[]{:S(2)}) collective-permute-start(bf16[2,32,2688]{2,1,0:T(8,128)(2,1)S(1)} %get-tuple-element.248), channel_id=1, source_target_pairs={{0,16},{1,17},{2,18},{3,19},{4,20},{5,21},{6,22},{7,23},{8,24},{9,... | collective-permute-start | bytes 1032200 | tf_op jit(solution)/shard_map/ppermute | solution.py:801
  507.8 29.8 %collective-permute-start.11 = (bf16[4,32,1536]{2,1,0:T(8,128)(2,1)S(1)}, bf16[4,32,1536]{2,1,0:T(8,128)(2,1)S(1)}, u32[]{:S(2)}, u32[]{:S(2)}) collective-permute-start(bf16[4,32,1536]{2,1,0:T(8,128)(2,1)S(1)} %get-tuple-element.235), channel_id=1, source_target_pairs={{0,2},{1,3},{2,0},{3,1},{4,6},{5,7},{6,4},{7,5},{8,10},{9,11},{10,... | collective-permute-start | bytes 1179656 | tf_op jit(solution)/shard_map/ppermute | solution.py:801
  509.4 28.2 %collective-permute-start.12 = (bf16[4,32,1536]{2,1,0:T(8,128)(2,1)S(1)}, bf16[4,32,1536]{2,1,0:T(8,128)(2,1)S(1)}, u32[]{:S(2)}, u32[]{:S(2)}) collective-permute-start(bf16[4,32,1536]{2,1,0:T(8,128)(2,1)S(1)} %get-tuple-element.237), channel_id=1, source_target_pairs={{0,4},{1,5},{2,6},{3,7},{4,0},{5,1},{6,2},{7,3},{8,12},{9,13},{10,... | collective-permute-start | bytes 1179656 | tf_op jit(solution)/shard_map/ppermute | solution.py:801
  525.1 20.8 %collective-permute-start.13 = (bf16[4,32,1536]{2,1,0:T(8,128)(2,1)S(1)}, bf16[4,32,1536]{2,1,0:T(8,128)(2,1)S(1)}, u32[]{:S(2)}, u32[]{:S(2)}) collective-permute-start(bf16[4,32,1536]{2,1,0:T(8,128)(2,1)S(1)} %get-tuple-element.236), channel_id=1, source_target_pairs={{0,6},{1,7},{2,4},{3,5},{4,2},{5,3},{6,0},{7,1},{8,14},{9,15},{10,... | collective-permute-start | bytes 1179656 | tf_op jit(solution)/shard_map/ppermute | solution.py:801
  546.9 18.8 %all-to-all-start.8 = ((f32[32,1,64]{2,1,0:T(1,128)}), f32[32,1,64]{2,1,0:T(1,128)S(1)}, u32[]{:S(2)}, u32[]{:S(2)}) async-start(f32[32,1,64]{2,1,0:T(1,128)} %bitcast.65), calls=%async_computation.8 | async-start | bytes 32768 | tf_op jit(solution)/shard_map/all_to_all | solution.py:1086
  551.7 13.9 %collective-permute-start.14 = (bf16[32,2688]{1,0:T(8,128)(2,1)S(1)}, bf16[32,2688]{1,0:T(8,128)(2,1)S(1)}, u32[]{:S(2)}, u32[]{:S(2)}) collective-permute-start(bf16[32,2688]{1,0:T(8,128)(2,1)S(1)} %dynamic-slice_bitcast_fusion.16), channel_id=1, source_target_pairs={{0,2},{1,3},{2,0},{3,1},{4,6},{5,7},{6,4},{7,5},{8,10},{9,11},{10,... | collective-permute-start | bytes 516104 | tf_op jit(solution)/shard_map/ppermute | solution.py:801
  553.6 17.3 %collective-permute-start.15 = (bf16[32,1536]{1,0:T(8,128)(2,1)S(1)}, bf16[32,1536]{1,0:T(8,128)(2,1)S(1)}, u32[]{:S(2)}, u32[]{:S(2)}) collective-permute-start(bf16[32,1536]{1,0:T(8,128)(2,1)S(1)} %get-tuple-element.253), channel_id=1, source_target_pairs={{0,8},{1,9},{2,10},{3,11},{4,12},{5,13},{6,14},{7,15},{8,0},{9,1},... | collective-permute-start | bytes 294920 | tf_op jit(solution)/shard_map/ppermute | solution.py:801
  555.1 15.8 %collective-permute-start.16 = (bf16[32,1536]{1,0:T(8,128)(2,1)S(1)}, bf16[32,1536]{1,0:T(8,128)(2,1)S(1)}, u32[]{:S(2)}, u32[]{:S(2)}) collective-permute-start(bf16[32,1536]{1,0:T(8,128)(2,1)S(1)} %get-tuple-element.252), channel_id=1, source_target_pairs={{0,16},{1,17},{2,18},{3,19},{4,20},{5,21},{6,22},{7,23},{8,24},{9,... | collective-permute-start | bytes 294920 | tf_op jit(solution)/shard_map/ppermute | solution.py:801
  557.5 13.4 %collective-permute-start.17 = (bf16[32,1536]{1,0:T(8,128)(2,1)S(1)}, bf16[32,1536]{1,0:T(8,128)(2,1)S(1)}, u32[]{:S(2)}, u32[]{:S(2)}) collective-permute-start(bf16[32,1536]{1,0:T(8,128)(2,1)S(1)} %get-tuple-element.251), channel_id=1, source_target_pairs={{0,24},{1,25},{2,26},{3,27},{4,28},{5,29},{6,30},{7,31},{8,16},{9,... | collective-permute-start | bytes 294920 | tf_op jit(solution)/shard_map/ppermute | solution.py:801
  592.2 4.5 collective-permute-start.22
  (73 other events, 464.4 us)
Sparse Core Ops, SparseCore 0:
  11.5 77.0 all-gather.3
  90.6 57.7 all-gather.5
  150.6 59.3 all-gather.7
  385.1 73.3 reduce-scatter.2
  461.1 88.5 reduce-scatter.4
